TPU v7x, 32 devices: a whole 2x2x4 slice. The times are simulated.
32 devices in a mesh: lat: 8 (over y, x, core), var: 4 (over z).
Axes of the slice: x: 2, y: 2, z: 4, core: 2. Of those that a mesh axis runs over, the one named last changes fastest.
Arguments:
- patches: bfloat16 [48, 96, 1024], P('lat', 'var'), may hold values from -6 to 6
- norm_gain: float32 [1024], replicated, may hold values from 0.25 to 1.75
- input_proj: bfloat16 [1024, 3072], replicated, may hold values from -7 to 7
- output_proj: bfloat16 [1024, 1024], replicated, may hold values from -0.1875 to 0.1875
- level_scale: float32 [40, 1024], P('var'), may hold values from 0.1 to 1.9
- level_shift: float32 [40, 1024], P('var'), may hold values from -3 to 3
- head_weight: bfloat16 [40, 1024, 320], P('var', 'lat'), may hold values from -0.1875 to 0.1875
- targets: bfloat16 [40, 48, 96, 320], P('var', 'lat'), may hold values from -6 to 6
- level_counts: int32 [4], replicated, may hold values from 13 to 37
- tile_dataset: int32 [8, 4], P('lat'), may hold values from 0 to 3
- slot_level: int32 [40], P('var'), may hold values from 0 to 39, as said below
Outputs:
- latent: bfloat16 [48, 96, 1024], P('lat', 'var')
- grad_latent: bfloat16 [48, 96, 1024], P('lat', 'var')
- grad_head: float32 [40, 1024, 320], P('var', 'lat')
Inputs may be any that keep to these rules, and one draw needn't show every extreme that they name: `slot_level`: for each j, slots j * 10 to (j + 1) * 10 - 1 hold the levels j * 10 to (j + 1) * 10 - 1 in some order.
All inputs are finite; a program needn't handle non-finite values.
Results may differ from a plain program's by a relative error of at most 0.012.
Values may be sent and summed in bfloat16 or wider, within the bound.
No kernel may reach another device: no remote copies, remote signals or barrier semaphores. Data moves between devices by JAX's collectives and lax.ppermute only.
A program may use at most 128 MiB of HBM per device.

v0:
```python
import math

import jax
import jax.numpy as jnp
from jax import lax
from jax.sharding import PartitionSpec as P

HEADS = 16
WH = 6
WW = 12


EPS = 1e-05


def padded(array, sides, width, wrap):
    for axis, dim in sides:
        size, length = (lax.axis_size(axis), array.shape[dim])
        up = [(i, (i + 1) % size) for i in range(size if wrap else size - 1)]
        down = [(j, i) for i, j in up]
        last = lax.slice_in_dim(array, length - width, length, axis=dim)
        initial = lax.slice_in_dim(array, 0, width, axis=dim)
        before = lax.ppermute(last, axis, up)
        after = lax.ppermute(initial, axis, down)
        array = jnp.concatenate([before, array, after], axis=dim)
    return array


def layer_norm(values, gain):
    wide = values.astype(jnp.float32)
    average = jnp.mean(wide, axis=-1, keepdims=True)
    centred = wide - average
    variance = jnp.mean(centred * centred, axis=-1, keepdims=True)
    return (centred * lax.rsqrt(variance + EPS) * gain).astype(jnp.bfloat16)


def window_attention(query_ext, keyval, row_valid, heads):
    ext_rows, ext_cols, width = query_ext.shape
    head_size = width // heads
    win_rows = ext_rows // WH
    win_cols = ext_cols // WW

    def split(values, parts):
        shaped = values.reshape(win_rows, WH, win_cols, WW, parts, heads, head_size)
        return shaped.transpose(0, 2, 1, 3, 4, 5, 6).reshape(
            win_rows * win_cols, WH * WW, parts, heads, head_size
        )

    query_win = split(query_ext, 1)[:, :, 0]
    pairs = split(keyval, 2)
    key_win = pairs[:, :, 0]
    value_win = pairs[:, :, 1]
    key_mask = jnp.broadcast_to(
        row_valid.reshape(win_rows, 1, WH, 1), (win_rows, win_cols, WH, WW)
    ).reshape(win_rows * win_cols, WH * WW)
    scores = jnp.einsum(
        "wqhd,wkhd->whqk", query_win, key_win, preferred_element_type=jnp.float32
    ) / math.sqrt(head_size)
    scores = jnp.where(key_mask[:, None, None, :], scores, -jnp.inf)
    peak = jnp.max(scores, axis=-1, keepdims=True)
    weights = jnp.exp(scores - peak)
    probs = (weights / jnp.sum(weights, axis=-1, keepdims=True)).astype(jnp.bfloat16)
    mixed = jnp.einsum("whqk,wkhd->wqhd", probs, value_win, preferred_element_type=jnp.float32)
    return (
        mixed.reshape(win_rows, win_cols, WH, WW, width)
        .transpose(0, 2, 1, 3, 4)
        .reshape(ext_rows, ext_cols, width)
    )


def slot_terms(piece, target_rows, live_cols, level_scale, level_shift, heads_full):
    piece_wide = piece.astype(jnp.float32)
    rows = (
        piece_wide[None] * level_scale[:, None, None, :] + level_shift[:, None, None, :]
    ).astype(jnp.bfloat16)
    predicted = jnp.einsum("krnd,kdo->krno", rows, heads_full, preferred_element_type=jnp.float32)
    errors = ((predicted - target_rows.astype(jnp.float32)) * live_cols[:, None, :, None]).astype(
        jnp.bfloat16
    )
    back_grad = jnp.einsum("krno,kdo->krnd", errors, heads_full, preferred_element_type=jnp.float32)
    piece_grad = jnp.sum(back_grad * level_scale[:, None, None, :], axis=0)
    head_add = jnp.einsum("krnd,krno->dko", rows, errors, preferred_element_type=jnp.float32)
    return (piece_grad, head_add)


def local(
    patches,
    norm_gain,
    input_proj,
    output_proj,
    level_scale,
    level_shift,
    head_weight,
    targets,
    level_counts,
    tile_dataset,
    slot_level,
):
    band_rows, band_cols, width = patches.shape
    half_rows = WH // 2
    half_cols = WW // 2
    lat_count = lax.axis_size("lat")
    var_count = lax.axis_size("var")
    lat_place = lax.axis_index("lat")
    ext_rows = band_rows + WH
    ext_cols = band_cols + WW
    extended = padded(patches, (("lat", 0),), half_rows, False)
    extended = padded(extended, (("var", 1),), half_cols, True)
    normed_ext = layer_norm(extended, norm_gain)
    keyval = jnp.dot(
        normed_ext.reshape(-1, width), input_proj[:, width:], preferred_element_type=jnp.float32
    )
    keyval = keyval.astype(jnp.bfloat16).reshape(ext_rows, ext_cols, 2 * width)
    normed = normed_ext[half_rows : half_rows + band_rows, half_cols : half_cols + band_cols]
    queries = jnp.dot(
        normed.reshape(-1, width), input_proj[:, :width], preferred_element_type=jnp.float32
    )
    queries = queries.astype(jnp.bfloat16).reshape(band_rows, band_cols, width)
    query_ext = jnp.pad(queries, ((half_rows, WH - half_rows), (half_cols, WW - half_cols), (0, 0)))
    global_row = lat_place * band_rows - half_rows + jnp.arange(ext_rows, dtype=jnp.int32)
    row_valid = (global_row >= 0) & (global_row < lat_count * band_rows)
    mixed = window_attention(query_ext, keyval, row_valid, HEADS)
    attn = mixed[half_rows : half_rows + band_rows, half_cols : half_cols + band_cols].astype(
        jnp.bfloat16
    )
    update = jnp.dot(
        attn.reshape(-1, width), output_proj, preferred_element_type=jnp.float32
    ).reshape(band_rows, band_cols, width)
    latent = (patches.astype(jnp.float32) + update).astype(jnp.bfloat16)
    dataset_row = tile_dataset[0]
    dataset_ids = jnp.arange(level_counts.shape[0], dtype=jnp.int32)
    tile_levels = jnp.sum(
        jnp.where(dataset_row[:, None] == dataset_ids[None, :], level_counts[None, :], 0), axis=1
    )
    live_tiles = (slot_level[None, :] < tile_levels[:, None]).astype(jnp.float32)
    heads_full = lax.all_gather(head_weight, "lat", axis=1, tiled=True)
    tile_ids = jnp.arange(var_count, dtype=jnp.int32)
    piece = lax.all_gather(latent, "var", axis=1, tiled=True)
    piece_cols = piece.shape[1]
    column_tile = jnp.arange(piece_cols, dtype=jnp.int32) // band_cols
    onehot = (column_tile[:, None] == tile_ids[None, :]).astype(jnp.float32)
    column_live = jnp.dot(onehot, live_tiles)
    piece_grad, head_add = slot_terms(
        piece, targets, column_live.T, level_scale, level_shift, heads_full
    )
    latent_terms = piece_grad
    latent_terms, head_terms = (latent_terms, head_add)
    grad_latent = lax.psum_scatter(
        latent_terms.astype(jnp.bfloat16), "var", scatter_dimension=1, tiled=True
    )
    head_terms = head_terms * (1.0 / math.sqrt(lat_count * band_rows * var_count * band_cols))
    mine = lax.psum_scatter(
        head_terms.astype(jnp.bfloat16), "lat", scatter_dimension=0, tiled=True
    ).astype(jnp.float32)
    grad_head = jnp.transpose(mine, (1, 0, 2))
    return (latent, grad_latent, grad_head)


def solution(mesh):
    in_specs = (
        P("lat", "var", None),
        P(),
        P(),
        P(),
        P("var", None),
        P("var", None),
        P("var", "lat", None),
        P("var", "lat", None, None),
        P(),
        P("lat", None),
        P("var"),
    )
    out_specs = (P("lat", "var", None), P("lat", "var", None), P("var", "lat", None))
    return jax.shard_map(local, mesh=mesh, in_specs=in_specs, out_specs=out_specs, check_vma=False)
```

profile of v0, /device:TPU:0, one launch (start us, length us, event | category | flops | bytes accessed | tf_op | source)
XLA Modules:
  0.0 298.6 jit_solution(14891887657996292141)
XLA Ops:
  7.2 1.1 fusion.63
  8.4 2.4 collective-permute-start
  10.8 1.3 collective-permute-start.1
  12.1 1.0 constant_dynamic-update-slice_fusion.1
  13.1 3.0 %collective-permute-done.1 = bf16[3,24,1024]{2,1,0:T(8,128)(2,1)S(1)} collective-permute-done((bf16[3,24,1024]{2,1,0:T(8,128)(2,1)S(1)}, bf16[3,24,1024]{2,1,0:T(8,128)(2,1)S(1)}, u32[]{:S(2)}, u32[]{:S(2)}) %collective-permute-start.1) | collective-permute-done | bytes 147488 | tf_op jit(solution)/shard_map/ppermute | solution.py:24
  16.2 3.7 %collective-permute-start.3 = (bf16[12,6,1024]{2,1,0:T(8,128)(2,1)S(1)}, bf16[12,6,1024]{2,1,0:T(8,128)(2,1)S(1)}, u32[]{:S(2)}, u32[]{:S(2)}) collective-permute-start(bf16[12,6,1024]{2,1,0:T(8,128)(2,1)S(1)} %get-tuple-element.8), channel_id=1, source_target_pairs={{1,0},{2,1},{3,2},{0,3},{5,4},{6,5},{7,6},{4,7},{9,8},{10,9},{11,1... | collective-permute-start | bytes 442376 | tf_op jit(solution)/shard_map/ppermute | solution.py:24
  20.0 3.1 %collective-permute-done.3 = bf16[12,6,1024]{2,1,0:T(8,128)(2,1)S(1)} collective-permute-done((bf16[12,6,1024]{2,1,0:T(8,128)(2,1)S(1)}, bf16[12,6,1024]{2,1,0:T(8,128)(2,1)S(1)}, u32[]{:S(2)}, u32[]{:S(2)}) %collective-permute-start.3) | collective-permute-done | bytes 147488 | tf_op jit(solution)/shard_map/ppermute | solution.py:24
  23.1 6.2 %collective-permute-done.2 = bf16[12,6,1024]{2,1,0:T(8,128)(2,1)S(1)} collective-permute-done((bf16[12,6,1024]{2,1,0:T(8,128)(2,1)S(1)}, bf16[12,6,1024]{2,1,0:T(8,128)(2,1)S(1)}, u32[]{:S(2)}, u32[]{:S(2)}) %collective-permute-start.2) | collective-permute-done | bytes 147488 | tf_op jit(solution)/shard_map/ppermute | solution.py:23
  29.3 0.4 fusion.60
  29.8 1.8 multiply_reduce_fusion.1
  31.9 1.3 fusion.52
  33.2 2.1 fusion.42
  35.3 1.1 pad.4
  36.4 3.6 %reshape.99 = bf16[2,6,3,12,1,16,64]{6,5,3,2,1,0,4:T(8,128)(2,1)} reshape(bf16[12,36,1024]{2,1,0:T(8,128)(2,1)} %pad.4) | data formatting | bytes 1769472 | tf_op jit(solution)/shard_map/reshape | solution.py:44
  39.9 3.1 %copy.43 = bf16[2,3,6,12,1,16,64]{6,5,3,2,1,0,4:T(8,128)(2,1)} copy(bf16[2,3,6,12,1,16,64]{6,5,3,1,2,0,4:T(8,128)(2,1)} %bitcast.60) | data formatting | bytes 1769472 | tf_op jit(solution)/shard_map/transpose | solution.py:45
  43.0 1.6 maximum_convert_fusion
  44.7 2.7 reshape.102
  47.3 6.1 %fusion.19 = bf16[432,2048]{1,0:T(8,128)(2,1)} fusion(bf16[1024,3072]{1,0:T(8,128)(2,1)} %param.13, f32[432,1024]{1,0:T(8,128)} %reshape.102, f32[1024]{0:T(1024)S(1)} %copy-done.3, f32[432]{0:T(512)S(1)} %rsqrt.13, f32[432]{0:T(512)S(1)} %div.33), kind=kOutput, calls=%fused_computation.22 | convolution fusion | flops 1814593536 | bytes 7740800 | tf_op jit(solution)/shard_map/dot_general | solution.py:110
  53.5 6.4 %reshape_reshape.3 = bf16[2,6,3,12,2,16,64]{6,5,4,3,2,1,0:T(8,128)(2,1)} reshape(bf16[432,2048]{1,0:T(8,128)(2,1)} %fusion.19) | data formatting | bytes 3538944 | tf_op jit(solution)/shard_map/reshape;reshape | solution.py:44
  59.8 2.6 copy.41
  62.4 2.6 fusion.61
  65.0 4.0 %copy.59 = bf16[6,72,1,16,64]{1,4,3,0,2:T(8,128)(2,1)} copy(bf16[6,72,1,16,64]{4,3,2,1,0:T(8,128)(2,1)} %get-tuple-element.4) | data formatting | bytes 1769472
  69.1 4.0 %copy.58 = bf16[6,72,1,16,64]{1,4,3,0,2:T(8,128)(2,1)} copy(bf16[6,72,1,16,64]{4,3,2,1,0:T(8,128)(2,1)} %get-tuple-element.3) | data formatting | bytes 1769472
  73.1 3.1 %fusion.27 = f32[6,16,72,72]{2,3,1,0:T(8,128)S(1)} fusion(bf16[6,72,16,64]{3,2,1,0:T(8,128)(2,1)} %bitcast.61, bf16[6,72,1,16,64]{1,4,3,0,2:T(8,128)(2,1)} %copy.59), kind=kOutput, calls=%fused_computation.29 | convolution fusion | flops 63700992 | bytes 3760128 | tf_op jit(solution)/shard_map/wqhd,wkhd->whqk/dot_general | solution.py:56
  76.2 1.8 fusion.64
  78.0 1.9 fusion.36
  79.9 4.0 %copy.47 = bf16[6,72,16,64]{3,2,1,0:T(8,128)(2,1)} copy(bf16[6,72,16,64]{1,3,2,0:T(8,128)(2,1)} %fusion.36) | data formatting | bytes 1769472 | tf_op jit(solution)/shard_map/whqk,wkhd->wqhd/transpose | solution.py:63
  83.9 3.9 %reshape.100 = bf16[2,3,6,12,1024]{4,3,2,1,0:T(8,128)(2,1)} reshape(bf16[6,72,16,64]{3,2,1,0:T(8,128)(2,1)} %copy.47) | data formatting | bytes 1769472 | tf_op jit(solution)/shard_map/reshape | solution.py:65
  87.9 1.4 copy.48
  89.3 1.0 reshape.101
  90.3 2.3 fusion.45
  92.7 0.7 all-gather.5.cloned.1.call-update
  93.4 0.2 select_reduce_fusion
  93.6 0.2 fusion.54
  93.9 31.5 %all-gather.3.cloned.1.call-done = bf16[6,96,1024]{2,1,0:T(8,128)(2,1)} async-done(((bf16[6,24,1024]{2,1,0:T(8,128)(2,1)}), bf16[6,96,1024]{2,1,0:T(8,128)(2,1)}) %all-gather.3.cloned.1.call-update) | async-done | bytes 1179664 | tf_op jit(solution)/shard_map/all_gather | solution.py:138
  125.3 3.1 %convert_element_type.67 = f32[6,96,1024]{2,1,0:T(8,128)} convert(bf16[6,96,1024]{2,1,0:T(8,128)(2,1)} %all-gather.3.cloned.1.call-done) | non-fusion elementwise | flops 589824 | bytes 3538944 | tf_op jit(solution)/shard_map/convert_element_type | solution.py:72
  128.4 45.8 %all-gather.5.cloned.1.call-done = bf16[10,1024,320]{1,2,0:T(8,128)(2,1)} async-done(((bf16[10,128,320]{1,2,0:T(8,128)(2,1)}), bf16[10,1024,320]{1,2,0:T(8,128)(2,1)}) %all-gather.5.cloned.1.call-update) | async-done | bytes 6553616 | tf_op jit(solution)/shard_map/all_gather | solution.py:136
  174.2 12.5 %multiply_convert_fusion = bf16[10,6,96,320]{3,2,1,0:T(8,128)(2,1)S(1)} fusion(bf16[10,6,96,320]{3,2,1,0:T(8,128)(2,1)} %param.18, f32[10,96]{1,0:T(8,128)S(1)} %fusion.54, bf16[10,1024,320]{1,2,0:T(8,128)(2,1)} %all-gather.5.cloned.1.call-done, f32[10,1024]{1,0:T(8,128)S(1)} %copy-done.6, f32[10,1024]{1,0:T(8,128)S(1)} %copy-done.5, ...), kind=kOutput, calls=%fused_computation.13 | convolution fusion | flops 3799941120 | bytes 16371456 | tf_op jit(solution)/shard_map/krnd,kdo->krno/dot_general | solution.py:76
  186.7 6.8 %multiply_reduce_fusion = bf16[6,96,1024]{2,1,0:T(8,128)(2,1)S(1)} fusion(f32[10,1024]{1,0:T(8,128)S(1)} %copy-done.5, bf16[10,6,96,320]{3,2,1,0:T(8,128)(2,1)S(1)} %multiply_convert_fusion, bf16[10,1024,320]{1,2,0:T(8,128)(2,1)S(1)} %copy-done.4), kind=kOutput, calls=%fused_computation.1 | convolution fusion | flops 3786080256 | bytes 11460608 | tf_op jit(solution)/shard_map/krno,kdo->krnd/dot_general | solution.py:80
  193.5 1.1 copy.60
  194.7 10.3 %fusion.3 = bf16[10,320,1024]{2,1,0:T(8,128)(2,1)} fusion(bf16[10,6,96,320]{3,2,1,0:T(8,128)(2,1)} %copy-done.10, f32[10,1024]{1,0:T(8,128)S(1)} %copy-done.6, f32[10,1024]{1,0:T(8,128)S(1)} %copy-done.5, f32[6,96,1024]{2,1,0:T(8,128)} %convert_element_type.67), kind=kOutput, calls=%fused_computation.6 | convolution fusion | flops 3799121920 | bytes 12681216 | tf_op jit(solution)/shard_map/krnd,krno->dko/dot_general | solution.py:82
  205.0 9.6 %copy.56 = bf16[1024,3200]{1,0:T(8,128)(2,1)} copy(bf16[1024,3200]{0,1:T(8,128)(2,1)} %bitcast.62) | data formatting | bytes 13107200
  214.6 9.4 %reduce-scatter.7.cloned.1.call-done = bf16[24,6144]{1,0:T(8,128)(2,1)} async-done(((bf16[96,6144]{1,0:T(8,128)(2,1)}), bf16[24,6144]{1,0:T(8,128)(2,1)}) %reduce-scatter.7.cloned.1.call-update) | async-done | bytes 294928
  224.0 1.3 reshape.107
  225.3 0.9 copy.53
  226.2 62.8 %reduce-scatter.9.cloned.1.call-done = bf16[128,3200]{1,0:T(8,128)(2,1)} async-done(((bf16[1024,3200]{1,0:T(8,128)(2,1)}), bf16[128,3200]{1,0:T(8,128)(2,1)}) %reduce-scatter.9.cloned.1.call-update) | async-done | bytes 819216
  289.0 1.7 copy.57
  290.7 1.3 convert_bitcast_fusion
  (43 shorter events, 0.8 us)
Async XLA Ops:
  7.2 83.1 %copy-start = (bf16[1024,1024]{1,0:T(8,128)(2,1)S(1)}, bf16[1024,1024]{1,0:T(8,128)(2,1)}, u32[]{:S(2)}) copy-start(bf16[1024,1024]{1,0:T(8,128)(2,1)} %param.14) | copy-start | bytes 6291460
  7.2 118.1 %all-gather.3.cloned.1.call-start = ((), (), s32[]{:S(2)}) async-start(), calls=%async_computation.2 | async-start | bytes 1474560 | tf_op jit(solution)/shard_map/all_gather | solution.py:138
  8.4 23.5 %copy-start.3 = (f32[1024]{0:T(1024)S(1)}, f32[1024]{0:T(1024)}, u32[]{:S(2)}) copy-start(f32[1024]{0:T(1024)} %param.12) | copy-start | bytes 12292
  8.4 3.7 %collective-permute-start = (bf16[3,24,1024]{2,1,0:T(8,128)(2,1)S(1)}, bf16[3,24,1024]{2,1,0:T(8,128)(2,1)S(1)}, u32[]{:S(2)}, u32[]{:S(2)}) collective-permute-start(bf16[3,24,1024]{2,1,0:T(8,128)(2,1)S(1)} %get-tuple-element.10), channel_id=1, source_target_pairs={{0,4},{4,8},{8,12},{12,16},{16,20},{20,24},{24,28},{1,5},{5,9},{9,... | collective-permute-start | bytes 442376 | tf_op jit(solution)/shard_map/ppermute | solution.py:23
  10.8 5.4 %collective-permute-start.1 = (bf16[3,24,1024]{2,1,0:T(8,128)(2,1)S(1)}, bf16[3,24,1024]{2,1,0:T(8,128)(2,1)S(1)}, u32[]{:S(2)}, u32[]{:S(2)}) collective-permute-start(bf16[3,24,1024]{2,1,0:T(8,128)(2,1)S(1)} %get-tuple-element.9), channel_id=1, source_target_pairs={{4,0},{8,4},{12,8},{16,12},{20,16},{24,20},{28,24},{5,1},{9,5},{13... | collective-permute-start | bytes 442376 | tf_op jit(solution)/shard_map/ppermute | solution.py:24
  16.2 6.9 %collective-permute-start.3 = (bf16[12,6,1024]{2,1,0:T(8,128)(2,1)S(1)}, bf16[12,6,1024]{2,1,0:T(8,128)(2,1)S(1)}, u32[]{:S(2)}, u32[]{:S(2)}) collective-permute-start(bf16[12,6,1024]{2,1,0:T(8,128)(2,1)S(1)} %get-tuple-element.8), channel_id=1, source_target_pairs={{1,0},{2,1},{3,2},{0,3},{5,4},{6,5},{7,6},{4,7},{9,8},{10,9},{11,1... | collective-permute-start | bytes 442376 | tf_op jit(solution)/shard_map/ppermute | solution.py:24
  19.9 9.5 %collective-permute-start.2 = (bf16[12,6,1024]{2,1,0:T(8,128)(2,1)S(1)}, bf16[12,6,1024]{2,1,0:T(8,128)(2,1)S(1)}, u32[]{:S(2)}, u32[]{:S(2)}) collective-permute-start(bf16[12,6,1024]{2,1,0:T(8,128)(2,1)S(1)} %get-tuple-element.7), channel_id=1, source_target_pairs={{0,1},{1,2},{2,3},{3,0},{4,5},{5,6},{6,7},{7,4},{8,9},{9,10},{10,1... | collective-permute-start | bytes 442376 | tf_op jit(solution)/shard_map/ppermute | solution.py:23
  76.2 1.8 copy-start.2
  89.2 4.2 %copy-start.7 = (s32[4]{0:T(128)S(1)}, s32[4]{0:T(128)}, u32[]{:S(2)}) copy-start(s32[4]{0:T(128)} %param.19) | copy-start | bytes 52
  89.2 4.2 %copy-start.8 = (s32[1,4]{1,0:T(1,128)S(1)}, s32[1,4]{1,0:T(1,128)}, u32[]{:S(2)}) copy-start(s32[1,4]{1,0:T(1,128)} %param.20) | copy-start | bytes 52
  89.2 4.4 %copy-start.9 = (s32[10]{0:T(128)S(1)}, s32[10]{0:T(128)}, u32[]{:S(2)}) copy-start(s32[10]{0:T(128)} %param.21) | copy-start | bytes 124
  92.6 81.6 %copy-start.5 = (f32[10,1024]{1,0:T(8,128)S(1)}, f32[10,1024]{1,0:T(8,128)}, u32[]{:S(2)}) copy-start(f32[10,1024]{1,0:T(8,128)} %param.15) | copy-start | bytes 122884
  92.6 81.6 %copy-start.6 = (f32[10,1024]{1,0:T(8,128)S(1)}, f32[10,1024]{1,0:T(8,128)}, u32[]{:S(2)}) copy-start(f32[10,1024]{1,0:T(8,128)} %param.16) | copy-start | bytes 122884
  92.6 81.6 %all-gather.5.cloned.1.call-start = ((), (), s32[]{:S(2)}) async-start(), calls=%async_computation.3 | async-start | bytes 7372800 | tf_op jit(solution)/shard_map/all_gather | solution.py:136
  93.4 130.6 %reduce-scatter.7.cloned.1.call-start = ((), (), s32[]{:S(2)}) async-start(), calls=%async_computation.4 | async-start | bytes 1474560
  174.2 12.5 %copy-start.4 = (bf16[10,1024,320]{1,2,0:T(8,128)(2,1)S(1)}, bf16[10,1024,320]{1,2,0:T(8,128)(2,1)}, u32[]{:S(2)}) copy-start(bf16[10,1024,320]{1,2,0:T(8,128)(2,1)} %all-gather.5.cloned.1.call-done) | copy-start | bytes 19660804
  186.7 6.8 %copy-start.10 = (bf16[10,6,96,320]{3,2,1,0:T(8,128)(2,1)}, bf16[10,6,96,320]{3,2,1,0:T(8,128)(2,1)S(1)}, u32[]{:S(2)}) copy-start(bf16[10,6,96,320]{3,2,1,0:T(8,128)(2,1)S(1)} %multiply_convert_fusion) | copy-start | bytes 11059204
  194.6 94.4 %reduce-scatter.9.cloned.1.call-start = ((), (), s32[]{:S(2)}) async-start(), calls=%async_computation.5 | async-start | bytes 7372800
  214.6 77.4 %copy-start.1 = (bf16[1024,1024]{1,0:T(8,128)(2,1)S(1)}, bf16[1024,1024]{1,0:T(8,128)(2,1)}, u32[]{:S(2)}) copy-start(bf16[1024,1024]{1,0:T(8,128)(2,1)} %param.14) | copy-start | bytes 6291460
Sparse Core Ops, SparseCore 0:
  92.7 32.5 all-gather.2
  127.2 46.9 all-gather.4
  194.8 29.1 reduce-scatter.6
  227.3 61.6 reduce-scatter.8
where the time goes:
time: 300 us; the launch traced here: 299 us
  waiting for transfers between devices  163 us (54%)
  local copies, waits for them, and re-layouts  57.8 us (19%)
  matrix products  45.2 us (15%)
  between operations  14 us (5%)
  other arithmetic  11.6 us (4%)
  starting transfers between devices  7.47 us (2%)
    unnamed x6, waiting for transfers between devices  72.9 us
    all_gather x1, waiting for transfers between devices, local(): heads_full = lax.all_gather(head_weight, 'lat', axis=1, tiled=True)  45.8 us
    all_gather x1, waiting for transfers between devices, local(): piece = lax.all_gather(latent, 'var', axis=1, tiled=True)  31.5 us
    unnamed x31, local copies, waits for them, and re-layouts  23.8 us
    dot_general x1, matrix products, slot_terms(): jnp.einsum('krnd,kdo->krno', rows, heads_full, preferred_element_type=jnp...  12.5 us
    dot_general x1, matrix products, slot_terms(): jnp.einsum('krnd,krno->dko', rows, errors, preferred_element_type=jnp.flo...  10.3 us
    another operation x2, local copies, waits for them, and re-layouts, split(): shaped = values.reshape(win_rows, WH, win_cols, WW, parts, heads, head_size)  8.98 us
    dot_general x1, matrix products, slot_terms(): jnp.einsum('krno,kdo->krnd', errors, heads_full, preferred_element_type=j...  6.78 us
  transfers between devices with their start and end apart: 8, of which 7 were waited for; matrix products, arithmetic and copies ran while one was open for 9% of the time, Pallas kernels for 0%

commit v1 on v0

--- a/solution.py
+++ b/solution.py
@@ -1,16 +1,433 @@
+import functools
 import math
 
 import jax
 import jax.numpy as jnp
+import numpy as np
 from jax import lax
+from jax.experimental import pallas as pl
+from jax.experimental.pallas import tpu as pltpu
 from jax.sharding import PartitionSpec as P
 
 HEADS = 16
 WH = 6
 WW = 12
-
-
 EPS = 1e-05
+HR = WH // 2
+HC = WW // 2
+QP = 48
+LEFT = 8
+VMEM_LIMIT = 48 * 1024 * 1024
+F32 = jnp.float32
+BF16 = jnp.bfloat16
+
+
+def source_base(cols):
+    own = 0
+    left = own + WH * cols
+    above = left + WH * LEFT
+    above_left = above + HR * cols
+    below = above_left + HR * LEFT
+    below_left = below + HR * cols
+    total = below_left + HR * LEFT
+    return own, left, above, above_left, below, below_left, total
+
+
+def gather_maps(cols):
+    own, left, above, above_left, below, below_left, total = source_base(cols)
+    win_cols = cols // WW
+    windows = 2 * win_cols
+
+    def source(part, win_row, row, col):
+        if part == 0:
+            r = win_row * HR + row
+            return left + r * LEFT + col if col < HC else own + r * cols + col - HC
+        if win_row == 0:
+            return above_left + row * LEFT + col if col < HC else above + row * cols + col - HC
+        return below_left + row * LEFT + col if col < HC else below + row * cols + col - HC
+
+    into = np.zeros((windows * 2 * QP, total), np.float32)
+    keep = np.zeros((WH * cols, total), np.float32)
+    back = np.zeros((WH * cols, windows * QP), np.float32)
+    for win in range(windows):
+        win_row, win_col = divmod(win, win_cols)
+        for part in range(2):
+            for row in range(HR):
+                for c in range(WW):
+                    at = source(part, win_row, row, win_col * WW + c)
+                    slot = row * WW + c
+                    into[win * 2 * QP + part * QP + slot, at] = 1
+                    if part == 0:
+                        natural = (win_row * HR + row) * cols + win_col * WW + c
+                        keep[natural, at] = 1
+                        back[natural, win * QP + slot] = 1
+    return into, keep, back
+
+
+def attention_kernel(
+    bands,
+    place,
+    own,
+    left,
+    above,
+    above_left,
+    below,
+    below_left,
+    gain,
+    into,
+    keep,
+    back,
+    proj_in,
+    proj_out,
+    out,
+    raw,
+    qkv,
+    attn,
+):
+    cols, width = own.shape[1], own.shape[2]
+    bases = source_base(cols)
+    windows = 2 * (cols // WW)
+    head_size = width // HEADS
+    quad = 256 // head_size
+    for base, ref in zip(bases, (own, left, above, above_left, below, below_left)):
+        count = ref.shape[0]
+        if ref.shape[1] == cols:
+            raw[base : base + count * cols, :] = ref[...].astype(F32).reshape(count * cols, width)
+        else:
+            for r in range(count):
+                raw[base + r * LEFT : base + (r + 1) * LEFT, :] = jnp.zeros((LEFT, width), F32)
+                raw[base + r * LEFT : base + r * LEFT + HC, :] = ref[r].astype(F32)
+    wide = raw[...]
+    average = jnp.mean(wide, axis=-1, keepdims=True)
+    centred = wide - average
+    variance = jnp.mean(centred * centred, axis=-1, keepdims=True)
+    normed = (centred * lax.rsqrt(variance + EPS) * gain[...]).astype(BF16)
+    win_x = jnp.dot(into[...], normed, preferred_element_type=F32).astype(BF16)
+    step = 512
+    for j in range(3 * width // step):
+        part = slice(j * step, (j + 1) * step)
+        qkv[:, part] = jnp.dot(win_x, proj_in[:, part], preferred_element_type=F32).astype(BF16)
+    lane = lax.broadcasted_iota(jnp.int32, (1, 256), 1) // head_size
+    heads = [jnp.where(lane == h, 1.0, 0.0) for h in range(quad)]
+    key_id = lax.broadcasted_iota(jnp.int32, (1, 2 * QP), 1)
+    scale = 1.0 / math.sqrt(head_size)
+    for win in range(windows):
+        win_row = win // (cols // WW)
+        edge = 0 if win_row == 0 else bands - 1
+        has_halo = place[0] != edge
+        halo_keys = jnp.logical_and(key_id >= QP, key_id < QP + HR * WW)
+        valid = jnp.logical_or(key_id < HR * WW, jnp.logical_and(halo_keys, has_halo))
+        bias = jnp.where(valid, 0.0, -1e30)
+        row0 = win * 2 * QP
+        for g in range(width // 256):
+            lanes = slice(g * 256, (g + 1) * 256)
+            query = qkv[row0 : row0 + QP, lanes].astype(F32) * scale
+            stacked = jnp.concatenate([query * h for h in heads], axis=0).astype(BF16)
+            key = qkv[row0 : row0 + 2 * QP, width + g * 256 : width + (g + 1) * 256]
+            value = qkv[row0 : row0 + 2 * QP, 2 * width + g * 256 : 2 * width + (g + 1) * 256]
+            scores = (
+                lax.dot_general(
+                    stacked, key, (((1,), (1,)), ((), ())), preferred_element_type=F32
+                )
+                + bias
+            )
+            weights = jnp.exp(scores - jnp.max(scores, axis=-1, keepdims=True))
+            probs = (weights / jnp.sum(weights, axis=-1, keepdims=True)).astype(BF16)
+            mixed = jnp.dot(probs, value, preferred_element_type=F32)
+            chosen = mixed[0:QP] * heads[0]
+            for h in range(1, quad):
+                chosen = chosen + mixed[h * QP : (h + 1) * QP] * heads[h]
+            attn[win * QP : (win + 1) * QP, lanes] = chosen.astype(BF16)
+    ordered = jnp.dot(back[...], attn[...], preferred_element_type=F32).astype(BF16)
+    update = jnp.dot(ordered, proj_out[...], preferred_element_type=F32)
+    residual = jnp.dot(keep[...], raw[...].astype(BF16), preferred_element_type=F32)
+    out[...] = (residual + update).astype(BF16)
+
+
+def attention(place, pieces, gain, proj_in, proj_out, bands):
+    rows, cols, width = pieces[0].shape
+    into, keep, back = gather_maps(cols)
+    total = source_base(cols)[-1]
+    windows = 2 * (cols // WW)
+    vmem = pl.BlockSpec(memory_space=pltpu.VMEM)
+    return pl.pallas_call(
+        functools.partial(attention_kernel, bands),
+        out_shape=jax.ShapeDtypeStruct((rows * cols, width), BF16),
+        in_specs=[pl.BlockSpec(memory_space=pltpu.SMEM)] + [vmem] * 12,
+        out_specs=vmem,
+        scratch_shapes=[
+            pltpu.VMEM((total, width), F32),
+            pltpu.VMEM((windows * 2 * QP, 3 * width), BF16),
+            pltpu.VMEM((windows * QP, width), BF16),
+        ],
+        compiler_params=pltpu.CompilerParams(vmem_limit_bytes=VMEM_LIMIT),
+        cost_estimate=pl.CostEstimate(
+            flops=6_000_000_000, bytes_accessed=12_000_000, transcendentals=400_000
+        ),
+        name="window_attention",
+    )(
+        place,
+        *pieces,
+        gain.reshape(1, width),
+        jnp.asarray(into, BF16),
+        jnp.asarray(keep, BF16),
+        jnp.asarray(back, BF16),
+        proj_in,
+        proj_out,
+    )
+
+
+def band_map(tiles, cols):
+    wide = tiles * cols
+    chosen = np.zeros((WH * wide, WH * wide), np.float32)
+    for r in range(WH):
+        for c in range(wide):
+            tile, at = divmod((c + HC) % wide, cols)
+            chosen[r * wide + c, tile * WH * cols + r * cols + at] = 1
+    return chosen
+
+
+def band_kernel(tiles, cols, place, chosen, *refs):
+    pieces, (band, latent, laid, wide) = refs[:tiles], refs[tiles:]
+    size = WH * cols
+    var = place[1]
+    for s in range(tiles):
+        tile = lax.rem(var + tiles - s, tiles)
+        laid[pl.ds(pl.multiple_of(tile * size, 16), size), :] = pieces[s][...]
+    wide[...] = jnp.dot(chosen[...], laid[...], preferred_element_type=F32)
+    band[...] = wide[...].astype(BF16)
+    for r in range(WH):
+        start = pl.multiple_of(r * tiles * cols + var * cols, 8)
+        latent[r] = wide[pl.ds(start, cols), :].astype(BF16)
+
+
+def band_latents(place, pieces, cols):
+    tiles = len(pieces)
+    width = pieces[0].shape[1]
+    total = WH * tiles * cols
+    vmem = pl.BlockSpec(memory_space=pltpu.VMEM)
+    return pl.pallas_call(
+        functools.partial(band_kernel, tiles, cols),
+        out_shape=(
+            jax.ShapeDtypeStruct((total, width), BF16),
+            jax.ShapeDtypeStruct((WH, cols, width), BF16),
+        ),
+        in_specs=[pl.BlockSpec(memory_space=pltpu.SMEM)] + [vmem] * (tiles + 1),
+        out_specs=(vmem, vmem),
+        scratch_shapes=[pltpu.VMEM((total, width), BF16), pltpu.VMEM((total, width), F32)],
+        compiler_params=pltpu.CompilerParams(vmem_limit_bytes=VMEM_LIMIT),
+        cost_estimate=pl.CostEstimate(
+            flops=2 * total * total * width, bytes_accessed=4_000_000, transcendentals=0
+        ),
+        name="band_latents",
+    )(place, jnp.asarray(band_map(tiles, cols), BF16), *pieces)
+
+
+def slot_kernel(
+    first_slot, lats, outer_bit, tile_count, place, counts, datasets, levels, tile_of, band, scale, shift,
+    weight, target, *refs
+):
+    keep, send, err, turned = refs[-4:]
+    slot = first_slot + pl.program_id(0)
+    rows = (band[...].astype(F32) * scale[0] + shift[0]).astype(BF16)
+    predicted = jnp.dot(rows, weight[0], preferred_element_type=F32)
+    total, outs = predicted.shape
+    diff = predicted - target[0].astype(F32).reshape(total, outs)
+    tile = tile_of[...]
+    live = jnp.zeros(tile.shape, F32)
+    for t in range(tile_count):
+        alive = levels[slot] < counts[datasets[0, t]]
+        live = live + jnp.where(jnp.logical_and(tile == t, alive), 1.0, 0.0)
+    errors = (diff * live).astype(BF16)
+    err[0] = errors
+    turned[...] = lax.dot_general(
+        errors, rows, (((0,), (0,)), ((), ())), preferred_element_type=F32
+    ).astype(BF16)
+    piece = turned.shape[1] // lats
+    for q in range(lats):
+        core, x, y = q & 1, (q >> 1) & 1, (q >> 2) & 1
+        outer, inner = (x, y) if outer_bit == 2 else (y, x)
+        start = pl.multiple_of(jnp.bitwise_xor(place[0], q) * piece, piece)
+        to = send if core else keep
+        to[outer, inner, 0] = turned[:, pl.ds(start, piece)]
+
+
+def slot_chunk(first_slot, count, outer_bit, lats, place, small, tile_of, band, scale, shift, heads, targets, errors):
+    total, width = band.shape
+    slots, _, outs = heads.shape
+    piece = width // lats
+    smem = pl.BlockSpec(memory_space=pltpu.SMEM)
+    halves = jax.ShapeDtypeStruct((2, 2, count, outs, piece), BF16)
+    half_spec = pl.BlockSpec((2, 2, 1, outs, piece), lambda k: (0, 0, k, 0, 0))
+    in_specs = [
+        smem, smem, smem, smem,
+        pl.BlockSpec((total, 1), lambda k: (0, 0)),
+        pl.BlockSpec((total, width), lambda k: (0, 0)),
+        pl.BlockSpec((1, 1, width), lambda k: (k + first_slot, 0, 0)),
+        pl.BlockSpec((1, 1, width), lambda k: (k + first_slot, 0, 0)),
+        pl.BlockSpec((1, width, outs), lambda k: (k + first_slot, 0, 0)),
+        pl.BlockSpec((1,) + targets.shape[1:], lambda k: (k + first_slot, 0, 0, 0)),
+    ]
+    args = [place, *small, tile_of, band, scale, shift, heads, targets]
+    aliases = {}
+    if errors is not None:
+        in_specs.append(pl.BlockSpec(memory_space=pl.ANY))
+        aliases = {len(args): 2}
+        args.append(errors)
+    return pl.pallas_call(
+        functools.partial(slot_kernel, first_slot, lats, outer_bit, total // (WH * tile_cols(targets, small))),
+        grid=(count,),
+        out_shape=(halves, halves, jax.ShapeDtypeStruct((slots, total, outs), BF16)),
+        in_specs=in_specs,
+        out_specs=(
+            half_spec,
+            half_spec,
+            pl.BlockSpec((1, total, outs), lambda k: (k + first_slot, 0, 0)),
+        ),
+        scratch_shapes=[pltpu.VMEM((outs, width), BF16)],
+        input_output_aliases=aliases,
+        compiler_params=pltpu.CompilerParams(vmem_limit_bytes=VMEM_LIMIT),
+        cost_estimate=pl.CostEstimate(
+            flops=count * 8 * total * width * outs, bytes_accessed=count * 2_500_000, transcendentals=0
+        ),
+        name="slot_errors",
+    )(*args)
+
+
+def tile_cols(targets, small):
+    return targets.shape[2] // small[1].shape[1]
+
+
+def back_kernel(tiles, cols, place, err, weight, scale, out, total):
+    slot = pl.program_id(0)
+    term = (
+        lax.dot_general(err[0], weight[0], (((1,), (1,)), ((), ())), preferred_element_type=F32)
+        * scale[0]
+    )
+
+    @pl.when(slot == 0)
+    def _():
+        total[...] = term
+
+    @pl.when(slot > 0)
+    def _():
+        total[...] += term
+
+    @pl.when(slot == pl.num_programs(0) - 1)
+    def _():
+        for s in range(tiles):
+            tile = lax.rem(place[1] + s, tiles)
+            for r in range(WH):
+                start = pl.multiple_of(r * tiles * cols + tile * cols, 8)
+                out[s, r] = total[pl.ds(start, cols), :].astype(BF16)
+
+
+def back_terms(place, errors, heads, scale, tiles, cols):
+    slots, total, outs = errors.shape
+    width = heads.shape[1]
+    shape = (tiles, WH, cols, width)
+    return pl.pallas_call(
+        functools.partial(back_kernel, tiles, cols),
+        grid=(slots,),
+        out_shape=jax.ShapeDtypeStruct(shape, BF16),
+        in_specs=[
+            pl.BlockSpec(memory_space=pltpu.SMEM),
+            pl.BlockSpec((1, total, outs), lambda k: (k, 0, 0)),
+            pl.BlockSpec((1, width, outs), lambda k: (k, 0, 0)),
+            pl.BlockSpec((1, 1, width), lambda k: (k, 0, 0)),
+        ],
+        out_specs=pl.BlockSpec(shape, lambda k: (0, 0, 0, 0)),
+        scratch_shapes=[pltpu.VMEM((total, width), F32)],
+        compiler_params=pltpu.CompilerParams(vmem_limit_bytes=VMEM_LIMIT),
+        cost_estimate=pl.CostEstimate(
+            flops=slots * 4 * total * width * outs, bytes_accessed=12_000_000, transcendentals=0
+        ),
+        name="latent_terms",
+    )(place, errors, heads, scale)
+
+
+def join_kernel(norm, *refs):
+    out = refs[-1]
+    pairs = refs[:-1]
+    slot = 0
+    for kept, came in zip(pairs[0::2], pairs[1::2]):
+        for k in range(kept.shape[0]):
+            total = (kept[k].astype(F32) + came[k].astype(F32)) * norm
+            out[slot] = total.T
+            slot += 1
+
+
+def join_heads(pairs, norm):
+    flat = [array for pair in pairs for array in pair]
+    slots = sum(kept.shape[0] for kept, _ in pairs)
+    _, outs, piece = flat[0].shape
+    vmem = pl.BlockSpec(memory_space=pltpu.VMEM)
+    return pl.pallas_call(
+        functools.partial(join_kernel, norm),
+        out_shape=jax.ShapeDtypeStruct((slots, piece, outs), F32),
+        in_specs=[vmem] * len(flat),
+        out_specs=vmem,
+        compiler_params=pltpu.CompilerParams(vmem_limit_bytes=VMEM_LIMIT),
+        cost_estimate=pl.CostEstimate(flops=1_000_000, bytes_accessed=4_000_000, transcendentals=0),
+        name="join_heads",
+    )(*flat)
+
+
+def fast_local(
+    patches, norm_gain, input_proj, output_proj, level_scale, level_shift, head_weight, targets,
+    level_counts, tile_dataset, slot_level,
+):
+    rows, cols, width = patches.shape
+    lats, tiles = lax.axis_size("lat"), lax.axis_size("var")
+    slots, _, outs = head_weight.shape
+    lat, var = lax.axis_index("lat"), lax.axis_index("var")
+    place = jnp.stack([lat, var]).astype(jnp.int32)
+    heads_full = lax.all_gather(head_weight, "lat", axis=1, tiled=True)
+
+    right = [(i, (i + 1) % tiles) for i in range(tiles)]
+    up = [(i, i + 1) for i in range(lats - 1)]
+    down = [(i + 1, i) for i in range(lats - 1)]
+    both = lambda pairs: [(a * tiles + c, b * tiles + d) for a, b in pairs for c, d in right]
+    low, high = patches[HR:], patches[:HR]
+    above = lax.ppermute(low, "lat", up)
+    below = lax.ppermute(high, "lat", down)
+    left = lax.ppermute(patches[:, cols - HC :], "var", right)
+    above_left = lax.ppermute(low[:, cols - HC :], ("lat", "var"), both(up))
+    below_left = lax.ppermute(high[:, cols - HC :], ("lat", "var"), both(down))
+    mine = attention(
+        place, (patches, left, above, above_left, below, below_left), norm_gain, input_proj, output_proj, lats
+    )
+    pieces = [mine]
+    for s in range(1, tiles):
+        pieces.append(lax.ppermute(mine, "var", [(i, (i + s) % tiles) for i in range(tiles)]))
+    band, latent = band_latents(place, pieces, cols)
+
+    tile_of = jnp.asarray(np.arange(rows * tiles * cols)[:, None] % (tiles * cols) // cols, jnp.int32)
+    scale3, shift3 = level_scale.reshape(slots, 1, width), level_shift.reshape(slots, 1, width)
+    small = (level_counts, tile_dataset, slot_level)
+    flip = lambda array, bit: lax.ppermute(array, "lat", [(i, i ^ bit) for i in range(lats)])
+    add = lambda a, b: (a.astype(F32) + b.astype(F32)).astype(BF16)
+    count = 2
+    errors, pairs = None, []
+    for index in range(slots // count):
+        outer_bit = 2 if index % 2 == 0 else 4
+        keep, send, errors = slot_chunk(
+            index * count, count, outer_bit, lats, place, small, tile_of, band, scale3, shift3,
+            heads_full, targets, errors,
+        )
+        came = flip(send, 1)
+        keep, send = add(keep[0], came[0]), add(keep[1], came[1])
+        came = flip(send, outer_bit)
+        keep, send = add(keep[0], came[0]), add(keep[1], came[1])
+        pairs.append((keep, flip(send, 6 - outer_bit)))
+    terms = back_terms(place, errors, heads_full, scale3, tiles, cols)
+    total = terms[0].astype(F32)
+    for s in range(1, tiles):
+        came = lax.ppermute(terms[s], "var", [(i, (i + s) % tiles) for i in range(tiles)])
+        total = total + came.astype(F32)
+    grad_latent = total.astype(BF16)
+    grad_head = join_heads(pairs, 1.0 / math.sqrt(lats * rows * tiles * cols))
+    return (latent, grad_latent, grad_head)
 
 
 def padded(array, sides, width, wrap):
@@ -170,5 +587,7 @@
         P("lat", None),
         P("var"),
     )
+    fast = mesh.shape["lat"] == 8 and mesh.shape["var"] == 4
+    body = fast_local if fast else local
     out_specs = (P("lat", "var", None), P("lat", "var", None), P("var", "lat", None))
-    return jax.shard_map(local, mesh=mesh, in_specs=in_specs, out_specs=out_specs, check_vma=False)
+    return jax.shard_map(body, mesh=mesh, in_specs=in_specs, out_specs=out_specs, check_vma=False)

time: 300 us -> 173 us (0.58)
  waiting for transfers between devices: 163 us -> 50.6 us
  Pallas kernels: 0 us -> 51 us
  matrix products: 45.2 us -> 0 us
  local copies, waits for them, and re-layouts: 57.8 us -> 15.1 us
  starting transfers between devices: 7.47 us -> 39 us
  other arithmetic: 11.6 us -> 2.3 us
    all_gather x2 -> x1, waiting for transfers between devices: 77.3 us -> 0.01 us  [fast_local(): heads_full = lax.all_gather(head_weight, 'lat', axis=1, tiled=True)]
    unnamed x6 -> x1, waiting for transfers between devices: 72.9 us -> 0.02 us
    pallas_call x0 -> x9, Pallas kernels: none -> 51 us  [the longest x5 27.1 us: slot_chunk(): pl.pallas_call(functools.partial(slot_kernel, first_slot, lats, outer_bit...]
    dot_general x9 -> x0, matrix products: 45.2 us -> none  [the longest x1 12.5 us: slot_terms(): jnp.einsum('krnd,kdo->krno', rows, heads_full, preferred_element_type=jnp...]
    ppermute x4 -> x26, waiting for transfers between devices: 12.3 us -> 50.6 us  [the longest x3 24.7 us: fast_local(): lax.ppermute(mine, 'var', [(i, (i + s) % tiles) for i in range(tiles)])]
    ppermute x4 -> x26, starting transfers between devices: 7.31 us -> 38.9 us  [the longest x15 17 us: fast_local(): lax.ppermute(array, 'lat', [(i, i ^ bit) for i in range(lats)])]
    unnamed x31 -> x30, local copies, waits for them, and re-layouts: 23.8 us -> 12.2 us
    another operation x2 -> x0, local copies, waits for them, and re-layouts: 8.98 us -> none  [split(): shaped = values.reshape(win_rows, WH, win_cols, WW, parts, heads, head_size)]
  transfers between devices with their start and end apart: 8 -> 27, of which waited for: 7 -> 9; matrix products, arithmetic and copies ran while one was open for 9% -> 3% of each run, Pallas kernels for 0% -> 26%
where the time goes in v1:
time: 173 us; the launch traced here: 172 us
  Pallas kernels  51 us (29%)
  waiting for transfers between devices  50.6 us (29%)
  starting transfers between devices  39 us (23%)
  local copies, waits for them, and re-layouts  15.1 us (9%)
  between operations  14.3 us (8%)
  other arithmetic  2.3 us (1%)
    pallas_call x5, Pallas kernels, slot_chunk(): pl.pallas_call(functools.partial(slot_kernel, first_slot, lats, outer_bit...  27.1 us
    ppermute x3, waiting for transfers between devices, fast_local(): lax.ppermute(mine, 'var', [(i, (i + s) % tiles) for i in range(tiles)])  24.7 us
    ppermute x15, waiting for transfers between devices, fast_local(): lax.ppermute(array, 'lat', [(i, i ^ bit) for i in range(lats)])  21.1 us
    ppermute x15, starting transfers between devices, fast_local(): lax.ppermute(array, 'lat', [(i, i ^ bit) for i in range(lats)])  17 us
    unnamed x30, local copies, waits for them, and re-layouts  12.2 us
    pallas_call x1, Pallas kernels, back_terms(): pl.pallas_call(functools.partial(back_kernel, tiles, cols), grid=(slots,)...  12.1 us
    pallas_call x1, Pallas kernels, attention(): pl.pallas_call(functools.partial(attention_kernel, bands), out_shape=jax....  8.6 us
    ppermute x1, starting transfers between devices, fast_local(): above_left = lax.ppermute(low[:, cols - HC:], ('lat', 'var'), both(up))  6.84 us
  transfers between devices with their start and end apart: 27, of which 9 were waited for; matrix products, arithmetic and copies ran while one was open for 3% of the time, Pallas kernels for 26%

profile of v1, /device:TPU:0, one launch (start us, length us, event | category | flops | bytes accessed | tf_op | source)
XLA Modules:
  0.0 172.2 jit_solution(13307644506606325949)
XLA Ops:
  7.2 2.2 %copy.23 = bf16[10,128,320]{2,1,0:T(8,128)(2,1)} copy(bf16[10,128,320]{1,2,0:T(8,128)(2,1)} %param.22) | data formatting | bytes 1638400 | tf_op args[6]
  9.4 1.0 fusion.29
  10.5 1.3 collective-permute-start.3
  11.8 3.0 %collective-permute-start.1 = (bf16[3,24,1024]{2,1,0:T(8,128)(2,1)S(1)}, bf16[3,24,1024]{2,1,0:T(8,128)(2,1)S(1)}, u32[]{:S(2)}, u32[]{:S(2)}) collective-permute-start(bf16[3,24,1024]{2,1,0:T(8,128)(2,1)S(1)} %get-tuple-element.66), channel_id=1, source_target_pairs={{0,4},{4,8},{8,12},{12,16},{16,20},{20,24},{24,28},{1,5},{5,9},{9,... | collective-permute-start | bytes 442376 | tf_op jit(solution)/shard_map/ppermute | solution.py:392
  14.8 0.9 fusion.28
  15.7 1.3 collective-permute-start.4
  17.0 6.8 %collective-permute-start.2 = (bf16[3,6,1024]{2,1,0:T(8,128)(2,1)S(1)}, bf16[3,6,1024]{2,1,0:T(8,128)(2,1)S(1)}, u32[]{:S(2)}, u32[]{:S(2)}) collective-permute-start(bf16[3,6,1024]{2,1,0:T(8,128)(2,1)S(1)} %get-tuple-element.64), channel_id=1, source_target_pairs={{0,5},{1,6},{2,7},{3,4},{4,9},{5,10},{6,11},{7,8},{8,13},{9,14},{1... | collective-permute-start | bytes 110600 | tf_op jit(solution)/shard_map/ppermute | solution.py:395
  23.8 0.9 slice.159
  24.7 1.6 collective-permute-start
  26.4 4.8 %collective-permute-done.left = bf16[6,6,1024]{2,1,0:T(8,128)(2,1)S(1)} collective-permute-done((bf16[6,6,1024]{2,1,0:T(8,128)(2,1)S(1)}, bf16[6,6,1024]{2,1,0:T(8,128)(2,1)S(1)}, u32[]{:S(2)}, u32[]{:S(2)}) %collective-permute-start) | collective-permute-done | bytes 73760 | tf_op jit(solution)/shard_map/ppermute | solution.py:394
  31.2 1.0 copy-done.2
  32.2 1.6 copy-done.6
  33.8 0.7 copy-done.7
  34.5 1.0 copy-done.9
  35.4 0.9 copy-done.10
  36.3 0.9 copy-done.11
  37.3 8.6 %window_attention.1.refs_0_ = bf16[144,1024]{1,0:T(8,128)(2,1)S(1)} custom-call(s32[2]{0:T(128)S(1)} %pad_add_fusion.place, bf16[6,24,1024]{2,1,0:T(8,128)(2,1)S(1)} %copy-done.2, bf16[6,6,1024]{2,1,0:T(8,128)(2,1)S(1)} %collective-permute-done.left, bf16[3,24,1024]{2,1,0:T(8,128)(2,1)S(1)} %collective-permute-done.1.above, ...), custom_call_target="tpu_custom_call" | custom-call | flops 6000000000 | bytes 12000000 | tf_op jit(solution)/shard_map/window_attention/pallas_call | solution.py:153
  46.4 0.8 collective-permute-start.6
  47.2 1.7 collective-permute-start.5
  49.0 7.6 %collective-permute-done.7.refs_3_ = bf16[144,1024]{1,0:T(8,128)(2,1)S(1)} collective-permute-done((bf16[144,1024]{1,0:T(8,128)(2,1)S(1)}, bf16[144,1024]{1,0:T(8,128)(2,1)S(1)}, u32[]{:S(2)}, u32[]{:S(2)}) %collective-permute-start.7) | collective-permute-done | bytes 294944 | tf_op jit(solution)/shard_map/ppermute | solution.py:402
  56.5 17.2 %collective-permute-done.6.refs_2_ = bf16[144,1024]{1,0:T(8,128)(2,1)S(1)} collective-permute-done((bf16[144,1024]{1,0:T(8,128)(2,1)S(1)}, bf16[144,1024]{1,0:T(8,128)(2,1)S(1)}, u32[]{:S(2)}, u32[]{:S(2)}) %collective-permute-start.6) | collective-permute-done | bytes 294944 | tf_op jit(solution)/shard_map/ppermute | solution.py:402
  73.7 2.6 %band_latents.1 = (bf16[576,1024]{1,0:T(8,128)(2,1)S(1)}, bf16[6,24,1024]{2,1,0:T(8,128)(2,1)}) custom-call(s32[2]{0:T(128)S(1)} %pad_add_fusion.place, bf16[576,576]{1,0:T(8,128)(2,1)S(1)} %copy-done.8, bf16[144,1024]{1,0:T(8,128)(2,1)S(1)} %window_attention.1.refs_0_, bf16[144,1024]{1,0:T(8,128)(2,1)S(1)} %collective-permute-done.5.refs_1_, ...), custom_call_target="tpu_custom_call" | custom-call | flops 679477248 | bytes 4000000 | tf_op jit(solution)/shard_map/band_latents/pallas_call | solution.py:209
  76.3 5.4 %slot_errors.5 = (bf16[2,2,2,320,128]{4,3,2,1,0:T(8,128)(2,1)S(1)}, bf16[2,2,2,320,128]{4,3,2,1,0:T(8,128)(2,1)S(1)}, bf16[10,576,320]{2,1,0:T(8,128)(2,1)}) custom-call(s32[2]{0:T(128)S(1)} %pad_add_fusion.place, s32[4]{0:T(128)S(1)} %copy-done.3, s32[1,4]{1,0:T(1,128)S(1)} %copy-done.4, s32[10]{0:T(128)S(1)} %copy-done.5, s32[576,1]{1,0:T(8,128)S(1)} %copy-done.1, ...), custom_call_target="tpu_custom_call" | custom-call | flops 3019898880 | bytes 5000000 | tf_op jit(solution)/shard_map/slot_errors/pallas_call | solution.py:277
  81.9 5.4 %slot_errors.6 = (bf16[2,2,2,320,128]{4,3,2,1,0:T(8,128)(2,1)S(1)}, bf16[2,2,2,320,128]{4,3,2,1,0:T(8,128)(2,1)S(1)}, bf16[10,576,320]{2,1,0:T(8,128)(2,1)}) custom-call(s32[2]{0:T(128)S(1)} %pad_add_fusion.place, s32[4]{0:T(128)S(1)} %copy-done.3, s32[1,4]{1,0:T(1,128)S(1)} %copy-done.4, s32[10]{0:T(128)S(1)} %copy-done.5, ...), custom_call_target="tpu_custom_call", output_to_operand_aliasing={{2}: (10, {})} | custom-call | flops 3019898880 | bytes 5000000 | tf_op jit(solution)/shard_map/slot_errors/pallas_call | solution.py:277
  87.6 5.4 %slot_errors.7 = (bf16[2,2,2,320,128]{4,3,2,1,0:T(8,128)(2,1)S(1)}, bf16[2,2,2,320,128]{4,3,2,1,0:T(8,128)(2,1)S(1)}, bf16[10,576,320]{2,1,0:T(8,128)(2,1)}) custom-call(s32[2]{0:T(128)S(1)} %pad_add_fusion.place, s32[4]{0:T(128)S(1)} %copy-done.3, s32[1,4]{1,0:T(1,128)S(1)} %copy-done.4, s32[10]{0:T(128)S(1)} %copy-done.5, ...), custom_call_target="tpu_custom_call", output_to_operand_aliasing={{2}: (10, {})} | custom-call | flops 3019898880 | bytes 5000000 | tf_op jit(solution)/shard_map/slot_errors/pallas_call | solution.py:277
  93.2 5.4 %slot_errors.8 = (bf16[2,2,2,320,128]{4,3,2,1,0:T(8,128)(2,1)S(1)}, bf16[2,2,2,320,128]{4,3,2,1,0:T(8,128)(2,1)S(1)}, bf16[10,576,320]{2,1,0:T(8,128)(2,1)}) custom-call(s32[2]{0:T(128)S(1)} %pad_add_fusion.place, s32[4]{0:T(128)S(1)} %copy-done.3, s32[1,4]{1,0:T(1,128)S(1)} %copy-done.4, s32[10]{0:T(128)S(1)} %copy-done.5, ...), custom_call_target="tpu_custom_call", output_to_operand_aliasing={{2}: (10, {})} | custom-call | flops 3019898880 | bytes 5000000 | tf_op jit(solution)/shard_map/slot_errors/pallas_call | solution.py:277
  98.6 5.4 %slot_errors.9 = (bf16[2,2,2,320,128]{4,3,2,1,0:T(8,128)(2,1)S(1)}, bf16[2,2,2,320,128]{4,3,2,1,0:T(8,128)(2,1)S(1)}, bf16[10,576,320]{2,1,0:T(8,128)(2,1)}) custom-call(s32[2]{0:T(128)S(1)} %pad_add_fusion.place, s32[4]{0:T(128)S(1)} %copy-done.3, s32[1,4]{1,0:T(1,128)S(1)} %copy-done.4, s32[10]{0:T(128)S(1)} %copy-done.5, ...), custom_call_target="tpu_custom_call", output_to_operand_aliasing={{2}: (10, {})} | custom-call | flops 3019898880 | bytes 5000000 | tf_op jit(solution)/shard_map/slot_errors/pallas_call | solution.py:277
  104.5 2.3 %copy-done = bf16[10,576,320]{2,1,0:T(8,128)(2,1)S(1)} copy-done((bf16[10,576,320]{2,1,0:T(8,128)(2,1)S(1)}, bf16[10,576,320]{2,1,0:T(8,128)(2,1)}, u32[]{:S(2)}) %copy-start) | copy-done | bytes 3686424
  106.8 12.1 %latent_terms.1 = bf16[4,6,24,1024]{3,2,1,0:T(8,128)(2,1)S(1)} custom-call(s32[2]{0:T(128)S(1)} %pad_add_fusion.place, bf16[10,576,320]{2,1,0:T(8,128)(2,1)S(1)} %copy-done, bf16[10,1024,320]{2,1,0:T(8,128)(2,1)} %all-gather.2.cloned.1.call-done.weight, f32[10,1,1024]{2,1,0:T(1,128)S(1)} %reshape.128.scale), custom_call_target="tpu_custom_call" | custom-call | flops 7549747200 | bytes 12000000 | tf_op jit(solution)/shard_map/latent_terms/pallas_call | solution.py:329
  119.7 3.6 %collective-permute-start.10 = (bf16[6,24,1024]{2,1,0:T(8,128)(2,1)S(1)}, bf16[6,24,1024]{2,1,0:T(8,128)(2,1)S(1)}, u32[]{:S(2)}, u32[]{:S(2)}) collective-permute-start(bf16[6,24,1024]{2,1,0:T(8,128)(2,1)S(1)} %get-tuple-element.51), channel_id=1, source_target_pairs={{0,3},{1,0},{2,1},{3,2},{4,7},{5,4},{6,5},{7,6},{8,11},{9,8},{10,9... | collective-permute-start | bytes 884744 | tf_op jit(solution)/shard_map/ppermute | solution.py:426
  124.4 2.4 %collective-permute-start.12 = (bf16[2,2,320,128]{3,2,1,0:T(8,128)(2,1)S(1)}, bf16[2,2,320,128]{3,2,1,0:T(8,128)(2,1)S(1)}, u32[]{:S(2)}, u32[]{:S(2)}) collective-permute-start(bf16[2,2,320,128]{3,2,1,0:T(8,128)(2,1)S(1)} %get-tuple-element.49), channel_id=1, source_target_pairs={{0,8},{4,12},{8,0},{12,4},{16,24},{20,28},{24,16},{28,20},{1,9},{5... | collective-permute-start | bytes 983048 | tf_op jit(solution)/shard_map/ppermute | solution.py:408
  126.9 0.9 collective-permute-start.15
  128.0 6.1 %collective-permute-done.12 = bf16[2,2,320,128]{3,2,1,0:T(8,128)(2,1)S(1)} collective-permute-done((bf16[2,2,320,128]{3,2,1,0:T(8,128)(2,1)S(1)}, bf16[2,2,320,128]{3,2,1,0:T(8,128)(2,1)S(1)}, u32[]{:S(2)}, u32[]{:S(2)}) %collective-permute-start.12) | collective-permute-done | bytes 327712 | tf_op jit(solution)/shard_map/ppermute | solution.py:408
  134.1 1.7 %collective-permute-start.18 = (bf16[2,2,320,128]{3,2,1,0:T(8,128)(2,1)S(1)}, bf16[2,2,320,128]{3,2,1,0:T(8,128)(2,1)S(1)}, u32[]{:S(2)}, u32[]{:S(2)}) collective-permute-start(bf16[2,2,320,128]{3,2,1,0:T(8,128)(2,1)S(1)} %get-tuple-element.45), channel_id=1, source_target_pairs={{0,8},{4,12},{8,0},{12,4},{16,24},{20,28},{24,16},{28,20},{1,9},{5... | collective-permute-start | bytes 983048 | tf_op jit(solution)/shard_map/ppermute | solution.py:408
  136.0 1.1 collective-permute-start.24
  137.2 7.6 %collective-permute-done.18 = bf16[2,2,320,128]{3,2,1,0:T(8,128)(2,1)S(1)} collective-permute-done((bf16[2,2,320,128]{3,2,1,0:T(8,128)(2,1)S(1)}, bf16[2,2,320,128]{3,2,1,0:T(8,128)(2,1)S(1)}, u32[]{:S(2)}, u32[]{:S(2)}) %collective-permute-start.18) | collective-permute-done | bytes 327712 | tf_op jit(solution)/shard_map/ppermute | solution.py:408
  144.8 2.7 %collective-permute-start.21 = (bf16[2,2,320,128]{3,2,1,0:T(8,128)(2,1)S(1)}, bf16[2,2,320,128]{3,2,1,0:T(8,128)(2,1)S(1)}, u32[]{:S(2)}, u32[]{:S(2)}) collective-permute-start(bf16[2,2,320,128]{3,2,1,0:T(8,128)(2,1)S(1)} %get-tuple-element.43), channel_id=1, source_target_pairs={{0,16},{4,20},{8,24},{12,28},{16,0},{20,4},{24,8},{28,12},{1,17},{... | collective-permute-start | bytes 983048 | tf_op jit(solution)/shard_map/ppermute | solution.py:408
  147.6 2.1 %collective-permute-done.24 = bf16[2,2,320,128]{3,2,1,0:T(8,128)(2,1)S(1)} collective-permute-done((bf16[2,2,320,128]{3,2,1,0:T(8,128)(2,1)S(1)}, bf16[2,2,320,128]{3,2,1,0:T(8,128)(2,1)S(1)}, u32[]{:S(2)}, u32[]{:S(2)}) %collective-permute-start.24) | collective-permute-done | bytes 327712 | tf_op jit(solution)/shard_map/ppermute | solution.py:408
  149.7 2.5 %collective-permute-start.13 = (bf16[2,320,128]{2,1,0:T(8,128)(2,1)S(1)}, bf16[2,320,128]{2,1,0:T(8,128)(2,1)S(1)}, u32[]{:S(2)}, u32[]{:S(2)}) collective-permute-start(bf16[2,320,128]{2,1,0:T(8,128)(2,1)S(1)} %get-tuple-element.61), channel_id=1, source_target_pairs={{0,16},{4,20},{8,24},{12,28},{16,0},{20,4},{24,8},{28,12},{1,17},{... | collective-permute-start | bytes 491528 | tf_op jit(solution)/shard_map/ppermute | solution.py:408
  152.3 1.8 %collective-permute-done.21 = bf16[2,2,320,128]{3,2,1,0:T(8,128)(2,1)S(1)} collective-permute-done((bf16[2,2,320,128]{3,2,1,0:T(8,128)(2,1)S(1)}, bf16[2,2,320,128]{3,2,1,0:T(8,128)(2,1)S(1)}, u32[]{:S(2)}, u32[]{:S(2)}) %collective-permute-start.21) | collective-permute-done | bytes 327712 | tf_op jit(solution)/shard_map/ppermute | solution.py:408
  154.1 1.2 collective-permute-start.16
  155.4 1.2 collective-permute-start.19
  156.6 0.9 collective-permute-start.25
  157.5 1.2 collective-permute-start.22
  158.7 0.9 fusion.2
  159.6 1.7 collective-permute-done.19.refs_5_
  161.3 1.8 %collective-permute-done.25.refs_9_ = bf16[2,320,128]{2,1,0:T(8,128)(2,1)S(1)} collective-permute-done((bf16[2,320,128]{2,1,0:T(8,128)(2,1)S(1)}, bf16[2,320,128]{2,1,0:T(8,128)(2,1)S(1)}, u32[]{:S(2)}, u32[]{:S(2)}) %collective-permute-start.25) | collective-permute-done | bytes 163872 | tf_op jit(solution)/shard_map/ppermute | solution.py:408
  163.7 1.7 copy.24
  (64 shorter events, 5.1 us)
Async XLA Ops:
  7.2 69.1 %all-gather.2.cloned.1.call-start = ((), (), s32[]{:S(2)}) async-start(), calls=%async_computation | async-start | bytes 8847360 | tf_op jit(solution)/shard_map/all_gather | solution.py:385
  10.5 20.8 %collective-permute-start.3 = (bf16[3,24,1024]{2,1,0:T(8,128)(2,1)S(1)}, bf16[3,24,1024]{2,1,0:T(8,128)(2,1)S(1)}, u32[]{:S(2)}, u32[]{:S(2)}) collective-permute-start(bf16[3,24,1024]{2,1,0:T(8,128)(2,1)S(1)} %get-tuple-element.65), channel_id=1, source_target_pairs={{4,0},{8,4},{12,8},{16,12},{20,16},{24,20},{28,24},{5,1},{9,5},{13... | collective-permute-start | bytes 442376 | tf_op jit(solution)/shard_map/ppermute | solution.py:393
  11.8 19.5 %collective-permute-start.1 = (bf16[3,24,1024]{2,1,0:T(8,128)(2,1)S(1)}, bf16[3,24,1024]{2,1,0:T(8,128)(2,1)S(1)}, u32[]{:S(2)}, u32[]{:S(2)}) collective-permute-start(bf16[3,24,1024]{2,1,0:T(8,128)(2,1)S(1)} %get-tuple-element.66), channel_id=1, source_target_pairs={{0,4},{4,8},{8,12},{12,16},{16,20},{20,24},{24,28},{1,5},{5,9},{9,... | collective-permute-start | bytes 442376 | tf_op jit(solution)/shard_map/ppermute | solution.py:392
  15.7 10.8 %collective-permute-start.4 = (bf16[3,6,1024]{2,1,0:T(8,128)(2,1)S(1)}, bf16[3,6,1024]{2,1,0:T(8,128)(2,1)S(1)}, u32[]{:S(2)}, u32[]{:S(2)}) collective-permute-start(bf16[3,6,1024]{2,1,0:T(8,128)(2,1)S(1)} %get-tuple-element.63), channel_id=1, source_target_pairs={{4,1},{5,2},{6,3},{7,0},{8,5},{9,6},{10,7},{11,4},{12,9},{13,10},{... | collective-permute-start | bytes 110600 | tf_op jit(solution)/shard_map/ppermute | solution.py:396
  17.0 9.5 %collective-permute-start.2 = (bf16[3,6,1024]{2,1,0:T(8,128)(2,1)S(1)}, bf16[3,6,1024]{2,1,0:T(8,128)(2,1)S(1)}, u32[]{:S(2)}, u32[]{:S(2)}) collective-permute-start(bf16[3,6,1024]{2,1,0:T(8,128)(2,1)S(1)} %get-tuple-element.64), channel_id=1, source_target_pairs={{0,5},{1,6},{2,7},{3,4},{4,9},{5,10},{6,11},{7,8},{8,13},{9,14},{1... | collective-permute-start | bytes 110600 | tf_op jit(solution)/shard_map/ppermute | solution.py:395
  24.7 6.5 %collective-permute-start = (bf16[6,6,1024]{2,1,0:T(8,128)(2,1)S(1)}, bf16[6,6,1024]{2,1,0:T(8,128)(2,1)S(1)}, u32[]{:S(2)}, u32[]{:S(2)}) collective-permute-start(bf16[6,6,1024]{2,1,0:T(8,128)(2,1)S(1)} %slice.159), channel_id=1, source_target_pairs={{0,1},{1,2},{2,3},{3,0},{4,5},{5,6},{6,7},{7,4},{8,9},{9,10},{10,1... | collective-permute-start | bytes 221192 | tf_op jit(solution)/shard_map/ppermute | solution.py:394
  31.2 1.0 copy-start.2
  32.2 1.6 copy-start.6
  33.8 0.7 copy-start.7
  34.5 1.0 copy-start.9
  35.4 0.9 copy-start.10
  36.3 0.9 copy-start.11
  37.2 11.7 %copy-start.12 = (f32[10,1024]{1,0:T(8,128)S(1)}, f32[10,1024]{1,0:T(8,128)}, u32[]{:S(2)}) copy-start(f32[10,1024]{1,0:T(8,128)} %param.20) | copy-start | bytes 122884
  37.2 11.7 %copy-start.13 = (f32[10,1024]{1,0:T(8,128)S(1)}, f32[10,1024]{1,0:T(8,128)}, u32[]{:S(2)}) copy-start(f32[10,1024]{1,0:T(8,128)} %param.21) | copy-start | bytes 122884
  37.2 36.5 %copy-start.8 = (bf16[576,576]{1,0:T(8,128)(2,1)S(1)}, bf16[576,576]{1,0:T(8,128)(2,1)}, u32[]{:S(2)}) copy-start(bf16[576,576]{1,0:T(8,128)(2,1)} %constant.22.clone.chosen) | copy-start | bytes 1990660
  37.2 39.1 %copy-start.1 = (s32[576,1]{1,0:T(8,128)S(1)}, s32[576,1]{1,0:T(8,128)}, u32[]{:S(2)}) copy-start(s32[576,1]{1,0:T(8,128)} %constant.23.clone.tile_of) | copy-start | bytes 6916
  37.2 39.1 %copy-start.3 = (s32[4]{0:T(128)S(1)}, s32[4]{0:T(128)}, u32[]{:S(2)}) copy-start(s32[4]{0:T(128)} %counts.9) | copy-start | bytes 52
  37.2 39.1 %copy-start.4 = (s32[1,4]{1,0:T(1,128)S(1)}, s32[1,4]{1,0:T(1,128)}, u32[]{:S(2)}) copy-start(s32[1,4]{1,0:T(1,128)} %datasets.9) | copy-start | bytes 52
  37.2 39.0 %copy-start.5 = (s32[10]{0:T(128)S(1)}, s32[10]{0:T(128)}, u32[]{:S(2)}) copy-start(s32[10]{0:T(128)} %levels.9) | copy-start | bytes 124
  45.9 10.6 %collective-permute-start.7 = (bf16[144,1024]{1,0:T(8,128)(2,1)S(1)}, bf16[144,1024]{1,0:T(8,128)(2,1)S(1)}, u32[]{:S(2)}, u32[]{:S(2)}) collective-permute-start(bf16[144,1024]{1,0:T(8,128)(2,1)S(1)} %window_attention.1.refs_0_), channel_id=1, source_target_pairs={{0,3},{1,0},{2,1},{3,2},{4,7},{5,4},{6,5},{7,6},{8,11},{9,8},{10,9... | collective-permute-start | bytes 884744 | tf_op jit(solution)/shard_map/ppermute | solution.py:402
  46.4 27.3 %collective-permute-start.6 = (bf16[144,1024]{1,0:T(8,128)(2,1)S(1)}, bf16[144,1024]{1,0:T(8,128)(2,1)S(1)}, u32[]{:S(2)}, u32[]{:S(2)}) collective-permute-start(bf16[144,1024]{1,0:T(8,128)(2,1)S(1)} %window_attention.1.refs_0_), channel_id=1, source_target_pairs={{0,2},{1,3},{2,0},{3,1},{4,6},{5,7},{6,4},{7,5},{8,10},{9,11},{10,... | collective-permute-start | bytes 884744 | tf_op jit(solution)/shard_map/ppermute | solution.py:402
  47.2 26.5 %collective-permute-start.5 = (bf16[144,1024]{1,0:T(8,128)(2,1)S(1)}, bf16[144,1024]{1,0:T(8,128)(2,1)S(1)}, u32[]{:S(2)}, u32[]{:S(2)}) collective-permute-start(bf16[144,1024]{1,0:T(8,128)(2,1)S(1)} %window_attention.1.refs_0_), channel_id=1, source_target_pairs={{0,1},{1,2},{2,3},{3,0},{4,5},{5,6},{6,7},{7,4},{8,9},{9,10},{10,1... | collective-permute-start | bytes 884744 | tf_op jit(solution)/shard_map/ppermute | solution.py:402
  81.7 37.2 %collective-permute-start.11 = (bf16[2,2,2,320,128]{4,3,2,1,0:T(8,128)(2,1)S(1)}, bf16[2,2,2,320,128]{4,3,2,1,0:T(8,128)(2,1)S(1)}, u32[]{:S(2)}, u32[]{:S(2)}) collective-permute-start(bf16[2,2,2,320,128]{4,3,2,1,0:T(8,128)(2,1)S(1)} %get-tuple-element.28), channel_id=1, source_target_pairs={{0,4},{4,0},{8,12},{12,8},{16,20},{20,16},{24,28},{28,24},{1,5},{5... | collective-permute-start | bytes 1966088 | tf_op jit(solution)/shard_map/ppermute | solution.py:408
  87.3 32.5 %collective-permute-start.14 = (bf16[2,2,2,320,128]{4,3,2,1,0:T(8,128)(2,1)S(1)}, bf16[2,2,2,320,128]{4,3,2,1,0:T(8,128)(2,1)S(1)}, u32[]{:S(2)}, u32[]{:S(2)}) collective-permute-start(bf16[2,2,2,320,128]{4,3,2,1,0:T(8,128)(2,1)S(1)} %get-tuple-element.30), channel_id=1, source_target_pairs={{0,4},{4,0},{8,12},{12,8},{16,20},{20,16},{24,28},{28,24},{1,5},{5... | collective-permute-start | bytes 1966088 | tf_op jit(solution)/shard_map/ppermute | solution.py:408
  93.1 30.5 %collective-permute-start.17 = (bf16[2,2,2,320,128]{4,3,2,1,0:T(8,128)(2,1)S(1)}, bf16[2,2,2,320,128]{4,3,2,1,0:T(8,128)(2,1)S(1)}, u32[]{:S(2)}, u32[]{:S(2)}) collective-permute-start(bf16[2,2,2,320,128]{4,3,2,1,0:T(8,128)(2,1)S(1)} %get-tuple-element.32), channel_id=1, source_target_pairs={{0,4},{4,0},{8,12},{12,8},{16,20},{20,16},{24,28},{28,24},{1,5},{5... | collective-permute-start | bytes 1966088 | tf_op jit(solution)/shard_map/ppermute | solution.py:408
  104.0 20.4 %collective-permute-start.23 = (bf16[2,2,2,320,128]{4,3,2,1,0:T(8,128)(2,1)S(1)}, bf16[2,2,2,320,128]{4,3,2,1,0:T(8,128)(2,1)S(1)}, u32[]{:S(2)}, u32[]{:S(2)}) collective-permute-start(bf16[2,2,2,320,128]{4,3,2,1,0:T(8,128)(2,1)S(1)} %get-tuple-element.36), channel_id=1, source_target_pairs={{0,4},{4,0},{8,12},{12,8},{16,20},{20,16},{24,28},{28,24},{1,5},{5... | collective-permute-start | bytes 1966088 | tf_op jit(solution)/shard_map/ppermute | solution.py:408
  104.4 22.5 %collective-permute-start.20 = (bf16[2,2,2,320,128]{4,3,2,1,0:T(8,128)(2,1)S(1)}, bf16[2,2,2,320,128]{4,3,2,1,0:T(8,128)(2,1)S(1)}, u32[]{:S(2)}, u32[]{:S(2)}) collective-permute-start(bf16[2,2,2,320,128]{4,3,2,1,0:T(8,128)(2,1)S(1)} %get-tuple-element.34), channel_id=1, source_target_pairs={{0,4},{4,0},{8,12},{12,8},{16,20},{20,16},{24,28},{28,24},{1,5},{5... | collective-permute-start | bytes 1966088 | tf_op jit(solution)/shard_map/ppermute | solution.py:408
  104.5 2.3 %copy-start = (bf16[10,576,320]{2,1,0:T(8,128)(2,1)S(1)}, bf16[10,576,320]{2,1,0:T(8,128)(2,1)}, u32[]{:S(2)}) copy-start(bf16[10,576,320]{2,1,0:T(8,128)(2,1)} %get-tuple-element.26.err) | copy-start | bytes 11059204
  119.0 36.4 %collective-permute-start.8 = (bf16[6,24,1024]{2,1,0:T(8,128)(2,1)S(1)}, bf16[6,24,1024]{2,1,0:T(8,128)(2,1)S(1)}, u32[]{:S(2)}, u32[]{:S(2)}) collective-permute-start(bf16[6,24,1024]{2,1,0:T(8,128)(2,1)S(1)} %get-tuple-element.50), channel_id=1, source_target_pairs={{0,1},{1,2},{2,3},{3,0},{4,5},{5,6},{6,7},{7,4},{8,9},{9,10},{10,1... | collective-permute-start | bytes 884744 | tf_op jit(solution)/shard_map/ppermute | solution.py:426
  119.7 36.9 %collective-permute-start.10 = (bf16[6,24,1024]{2,1,0:T(8,128)(2,1)S(1)}, bf16[6,24,1024]{2,1,0:T(8,128)(2,1)S(1)}, u32[]{:S(2)}, u32[]{:S(2)}) collective-permute-start(bf16[6,24,1024]{2,1,0:T(8,128)(2,1)S(1)} %get-tuple-element.51), channel_id=1, source_target_pairs={{0,3},{1,0},{2,1},{3,2},{4,7},{5,4},{6,5},{7,6},{8,11},{9,8},{10,9... | collective-permute-start | bytes 884744 | tf_op jit(solution)/shard_map/ppermute | solution.py:426
  123.5 34.0 %collective-permute-start.9 = (bf16[6,24,1024]{2,1,0:T(8,128)(2,1)S(1)}, bf16[6,24,1024]{2,1,0:T(8,128)(2,1)S(1)}, u32[]{:S(2)}, u32[]{:S(2)}) collective-permute-start(bf16[6,24,1024]{2,1,0:T(8,128)(2,1)S(1)} %get-tuple-element.52), channel_id=1, source_target_pairs={{0,2},{1,3},{2,0},{3,1},{4,6},{5,7},{6,4},{7,5},{8,10},{9,11},{10,... | collective-permute-start | bytes 884744 | tf_op jit(solution)/shard_map/ppermute | solution.py:426
  124.4 9.7 %collective-permute-start.12 = (bf16[2,2,320,128]{3,2,1,0:T(8,128)(2,1)S(1)}, bf16[2,2,320,128]{3,2,1,0:T(8,128)(2,1)S(1)}, u32[]{:S(2)}, u32[]{:S(2)}) collective-permute-start(bf16[2,2,320,128]{3,2,1,0:T(8,128)(2,1)S(1)} %get-tuple-element.49), channel_id=1, source_target_pairs={{0,8},{4,12},{8,0},{12,4},{16,24},{20,28},{24,16},{28,20},{1,9},{5... | collective-permute-start | bytes 983048 | tf_op jit(solution)/shard_map/ppermute | solution.py:408
  126.9 9.0 %collective-permute-start.15 = (bf16[2,2,320,128]{3,2,1,0:T(8,128)(2,1)S(1)}, bf16[2,2,320,128]{3,2,1,0:T(8,128)(2,1)S(1)}, u32[]{:S(2)}, u32[]{:S(2)}) collective-permute-start(bf16[2,2,320,128]{3,2,1,0:T(8,128)(2,1)S(1)} %get-tuple-element.47), channel_id=1, source_target_pairs={{0,16},{4,20},{8,24},{12,28},{16,0},{20,4},{24,8},{28,12},{1,17},{... | collective-permute-start | bytes 983048 | tf_op jit(solution)/shard_map/ppermute | solution.py:408
  134.1 10.6 %collective-permute-start.18 = (bf16[2,2,320,128]{3,2,1,0:T(8,128)(2,1)S(1)}, bf16[2,2,320,128]{3,2,1,0:T(8,128)(2,1)S(1)}, u32[]{:S(2)}, u32[]{:S(2)}) collective-permute-start(bf16[2,2,320,128]{3,2,1,0:T(8,128)(2,1)S(1)} %get-tuple-element.45), channel_id=1, source_target_pairs={{0,8},{4,12},{8,0},{12,4},{16,24},{20,28},{24,16},{28,20},{1,9},{5... | collective-permute-start | bytes 983048 | tf_op jit(solution)/shard_map/ppermute | solution.py:408
  136.0 13.7 %collective-permute-start.24 = (bf16[2,2,320,128]{3,2,1,0:T(8,128)(2,1)S(1)}, bf16[2,2,320,128]{3,2,1,0:T(8,128)(2,1)S(1)}, u32[]{:S(2)}, u32[]{:S(2)}) collective-permute-start(bf16[2,2,320,128]{3,2,1,0:T(8,128)(2,1)S(1)} %get-tuple-element.41), channel_id=1, source_target_pairs={{0,8},{4,12},{8,0},{12,4},{16,24},{20,28},{24,16},{28,20},{1,9},{5... | collective-permute-start | bytes 983048 | tf_op jit(solution)/shard_map/ppermute | solution.py:408
  144.8 9.3 %collective-permute-start.21 = (bf16[2,2,320,128]{3,2,1,0:T(8,128)(2,1)S(1)}, bf16[2,2,320,128]{3,2,1,0:T(8,128)(2,1)S(1)}, u32[]{:S(2)}, u32[]{:S(2)}) collective-permute-start(bf16[2,2,320,128]{3,2,1,0:T(8,128)(2,1)S(1)} %get-tuple-element.43), channel_id=1, source_target_pairs={{0,16},{4,20},{8,24},{12,28},{16,0},{20,4},{24,8},{28,12},{1,17},{... | collective-permute-start | bytes 983048 | tf_op jit(solution)/shard_map/ppermute | solution.py:408
  149.7 9.9 %collective-permute-start.13 = (bf16[2,320,128]{2,1,0:T(8,128)(2,1)S(1)}, bf16[2,320,128]{2,1,0:T(8,128)(2,1)S(1)}, u32[]{:S(2)}, u32[]{:S(2)}) collective-permute-start(bf16[2,320,128]{2,1,0:T(8,128)(2,1)S(1)} %get-tuple-element.61), channel_id=1, source_target_pairs={{0,16},{4,20},{8,24},{12,28},{16,0},{20,4},{24,8},{28,12},{1,17},{... | collective-permute-start | bytes 491528 | tf_op jit(solution)/shard_map/ppermute | solution.py:408
  154.1 5.5 %collective-permute-start.16 = (bf16[2,320,128]{2,1,0:T(8,128)(2,1)S(1)}, bf16[2,320,128]{2,1,0:T(8,128)(2,1)S(1)}, u32[]{:S(2)}, u32[]{:S(2)}) collective-permute-start(bf16[2,320,128]{2,1,0:T(8,128)(2,1)S(1)} %get-tuple-element.59), channel_id=1, source_target_pairs={{0,8},{4,12},{8,0},{12,4},{16,24},{20,28},{24,16},{28,20},{1,9},{5... | collective-permute-start | bytes 491528 | tf_op jit(solution)/shard_map/ppermute | solution.py:408
  155.4 5.9 %collective-permute-start.19 = (bf16[2,320,128]{2,1,0:T(8,128)(2,1)S(1)}, bf16[2,320,128]{2,1,0:T(8,128)(2,1)S(1)}, u32[]{:S(2)}, u32[]{:S(2)}) collective-permute-start(bf16[2,320,128]{2,1,0:T(8,128)(2,1)S(1)} %get-tuple-element.57), channel_id=1, source_target_pairs={{0,16},{4,20},{8,24},{12,28},{16,0},{20,4},{24,8},{28,12},{1,17},{... | collective-permute-start | bytes 491528 | tf_op jit(solution)/shard_map/ppermute | solution.py:408
  156.6 6.5 %collective-permute-start.25 = (bf16[2,320,128]{2,1,0:T(8,128)(2,1)S(1)}, bf16[2,320,128]{2,1,0:T(8,128)(2,1)S(1)}, u32[]{:S(2)}, u32[]{:S(2)}) collective-permute-start(bf16[2,320,128]{2,1,0:T(8,128)(2,1)S(1)} %get-tuple-element.53), channel_id=1, source_target_pairs={{0,16},{4,20},{8,24},{12,28},{16,0},{20,4},{24,8},{28,12},{1,17},{... | collective-permute-start | bytes 491528 | tf_op jit(solution)/shard_map/ppermute | solution.py:408
  157.5 5.6 %collective-permute-start.22 = (bf16[2,320,128]{2,1,0:T(8,128)(2,1)S(1)}, bf16[2,320,128]{2,1,0:T(8,128)(2,1)S(1)}, u32[]{:S(2)}, u32[]{:S(2)}) collective-permute-start(bf16[2,320,128]{2,1,0:T(8,128)(2,1)S(1)} %get-tuple-element.55), channel_id=1, source_target_pairs={{0,8},{4,12},{8,0},{12,4},{16,24},{20,28},{24,16},{28,20},{1,9},{5... | collective-permute-start | bytes 491528 | tf_op jit(solution)/shard_map/ppermute | solution.py:408
Sparse Core Ops, SparseCore 0:
  10.5 55.3 all-gather.1

commit v2 on v1

--- a/solution.py
+++ b/solution.py
@@ -67,30 +67,46 @@
 def attention_kernel(
     bands,
     place,
-    own,
     left,
     above,
     above_left,
     below,
     below_left,
+    own_hbm,
     gain,
-    into,
-    keep,
-    back,
-    proj_in,
-    proj_out,
+    maps_hbm,
+    in_hbm,
+    out_hbm,
     out,
     raw,
     qkv,
     attn,
+    own,
+    maps,
+    proj_in,
+    proj_out,
+    sems,
 ):
+    moves = [
+        pltpu.make_async_copy(src, dst, sems.at[i])
+        for i, (src, dst) in enumerate(
+            ((own_hbm, own), (maps_hbm, maps), (in_hbm, proj_in), (out_hbm, proj_out))
+        )
+    ]
+    for move in moves:
+        move.start()
     cols, width = own.shape[1], own.shape[2]
     bases = source_base(cols)
-    windows = 2 * (cols // WW)
+    total = bases[-1]
+    win_cols = cols // WW
+    windows = 2 * win_cols
+    slots = windows * 2 * QP
     head_size = width // HEADS
     quad = 256 // head_size
     for base, ref in zip(bases, (own, left, above, above_left, below, below_left)):
         count = ref.shape[0]
+        if ref is own:
+            moves[0].wait()
         if ref.shape[1] == cols:
             raw[base : base + count * cols, :] = ref[...].astype(F32).reshape(count * cols, width)
         else:
@@ -102,7 +118,9 @@
     centred = wide - average
     variance = jnp.mean(centred * centred, axis=-1, keepdims=True)
     normed = (centred * lax.rsqrt(variance + EPS) * gain[...]).astype(BF16)
-    win_x = jnp.dot(into[...], normed, preferred_element_type=F32).astype(BF16)
+    moves[1].wait()
+    win_x = jnp.dot(maps[0:slots, :], normed, preferred_element_type=F32).astype(BF16)
+    moves[2].wait()
     step = 512
     for j in range(3 * width // step):
         part = slice(j * step, (j + 1) * step)
@@ -112,7 +130,7 @@
     key_id = lax.broadcasted_iota(jnp.int32, (1, 2 * QP), 1)
     scale = 1.0 / math.sqrt(head_size)
     for win in range(windows):
-        win_row = win // (cols // WW)
+        win_row = win // win_cols
         edge = 0 if win_row == 0 else bands - 1
         has_halo = place[0] != edge
         halo_keys = jnp.logical_and(key_id >= QP, key_id < QP + HR * WW)
@@ -138,27 +156,39 @@
             for h in range(1, quad):
                 chosen = chosen + mixed[h * QP : (h + 1) * QP] * heads[h]
             attn[win * QP : (win + 1) * QP, lanes] = chosen.astype(BF16)
-    ordered = jnp.dot(back[...], attn[...], preferred_element_type=F32).astype(BF16)
+    size = WH * cols
+    keep = maps[slots : slots + size, :]
+    back = maps[slots + size : slots + 2 * size, 0 : windows * QP]
+    ordered = jnp.dot(back, attn[...], preferred_element_type=F32).astype(BF16)
+    residual = jnp.dot(keep, raw[...].astype(BF16), preferred_element_type=F32)
+    moves[3].wait()
     update = jnp.dot(ordered, proj_out[...], preferred_element_type=F32)
-    residual = jnp.dot(keep[...], raw[...].astype(BF16), preferred_element_type=F32)
     out[...] = (residual + update).astype(BF16)
 
 
-def attention(place, pieces, gain, proj_in, proj_out, bands):
-    rows, cols, width = pieces[0].shape
+def attention(place, patches, pieces, gain, proj_in, proj_out, bands):
+    rows, cols, width = patches.shape
     into, keep, back = gather_maps(cols)
     total = source_base(cols)[-1]
     windows = 2 * (cols // WW)
+    back = np.pad(back, ((0, 0), (0, total - back.shape[1])))
+    maps = np.concatenate([into, keep, back])
     vmem = pl.BlockSpec(memory_space=pltpu.VMEM)
+    hbm = pl.BlockSpec(memory_space=pltpu.HBM)
     return pl.pallas_call(
         functools.partial(attention_kernel, bands),
         out_shape=jax.ShapeDtypeStruct((rows * cols, width), BF16),
-        in_specs=[pl.BlockSpec(memory_space=pltpu.SMEM)] + [vmem] * 12,
+        in_specs=[pl.BlockSpec(memory_space=pltpu.SMEM)] + [vmem] * 5 + [hbm, vmem, hbm, hbm, hbm],
         out_specs=vmem,
         scratch_shapes=[
             pltpu.VMEM((total, width), F32),
             pltpu.VMEM((windows * 2 * QP, 3 * width), BF16),
             pltpu.VMEM((windows * QP, width), BF16),
+            pltpu.VMEM(patches.shape, BF16),
+            pltpu.VMEM(maps.shape, BF16),
+            pltpu.VMEM(proj_in.shape, BF16),
+            pltpu.VMEM(proj_out.shape, BF16),
+            pltpu.SemaphoreType.DMA((4,)),
         ],
         compiler_params=pltpu.CompilerParams(vmem_limit_bytes=VMEM_LIMIT),
         cost_estimate=pl.CostEstimate(
@@ -168,10 +198,9 @@
     )(
         place,
         *pieces,
+        patches,
         gain.reshape(1, width),
-        jnp.asarray(into, BF16),
-        jnp.asarray(keep, BF16),
-        jnp.asarray(back, BF16),
+        jnp.asarray(maps, BF16),
         proj_in,
         proj_out,
     )
@@ -223,66 +252,130 @@
     )(place, jnp.asarray(band_map(tiles, cols), BF16), *pieces)
 
 
+LANES = 384
+
+
+def scale_kernel(gathered, scale, shift, scaled, bias):
+    lats, _, outs, piece = gathered.shape
+    weight = jnp.concatenate([gathered[l, 0] for l in range(lats)], axis=1)
+    scaled[0, 0:outs, :] = (weight.astype(F32) * scale[0]).astype(BF16)
+    scaled[0, outs:, :] = jnp.zeros((scaled.shape[1] - outs, lats * piece), BF16)
+    rest = jnp.broadcast_to(shift[0], (8, lats * piece))
+    row = lax.broadcasted_iota(jnp.int32, rest.shape, 0)
+    split = jnp.zeros(rest.shape, F32)
+    for i in range(3):
+        part = rest.astype(BF16).astype(F32)
+        split = jnp.where(row == i, part, split)
+        rest = rest - part
+    terms = lax.dot_general(
+        split.astype(BF16), weight, (((1,), (1,)), ((), ())), preferred_element_type=F32
+    )
+    bias[0] = jnp.sum(terms, axis=0, keepdims=True)
+
+
+def scaled_heads(gathered, scale, shift):
+    lats, slots, outs, piece = gathered.shape
+    width = lats * piece
+    return pl.pallas_call(
+        scale_kernel,
+        grid=(slots,),
+        out_shape=(
+            jax.ShapeDtypeStruct((slots, LANES, width), BF16),
+            jax.ShapeDtypeStruct((slots, 1, outs), F32),
+        ),
+        in_specs=[
+            pl.BlockSpec((lats, 1, outs, piece), lambda k: (0, k, 0, 0)),
+            pl.BlockSpec((1, 1, width), lambda k: (k, 0, 0)),
+            pl.BlockSpec((1, 1, width), lambda k: (k, 0, 0)),
+        ],
+        out_specs=(
+            pl.BlockSpec((1, LANES, width), lambda k: (k, 0, 0)),
+            pl.BlockSpec((1, 1, outs), lambda k: (k, 0, 0)),
+        ),
+        compiler_params=pltpu.CompilerParams(vmem_limit_bytes=VMEM_LIMIT),
+        cost_estimate=pl.CostEstimate(
+            flops=100_000_000, bytes_accessed=16_000_000, transcendentals=0
+        ),
+        name="scaled_heads",
+    )(gathered, scale, shift)
+
+
 def slot_kernel(
-    first_slot, lats, outer_bit, tile_count, place, counts, datasets, levels, tile_of, band, scale, shift,
-    weight, target, *refs
+    first_slot, lats, outer_bit, tiles, place, counts, datasets, levels, tile_of, band, scale, shift,
+    bias, weight, target, *refs
 ):
     keep, send, err, turned = refs[-4:]
-    slot = first_slot + pl.program_id(0)
-    rows = (band[...].astype(F32) * scale[0] + shift[0]).astype(BF16)
-    predicted = jnp.dot(rows, weight[0], preferred_element_type=F32)
-    total, outs = predicted.shape
-    diff = predicted - target[0].astype(F32).reshape(total, outs)
+    count, outs = target.shape[0], target.shape[-1]
+    total, width = band.shape
+    piece = width // lats
+    latent = band[...]
+    predicted = lax.dot_general(
+        latent, weight[...].reshape(count * LANES, width), (((1,), (1,)), ((), ())),
+        preferred_element_type=F32,
+    )
     tile = tile_of[...]
-    live = jnp.zeros(tile.shape, F32)
-    for t in range(tile_count):
-        alive = levels[slot] < counts[datasets[0, t]]
-        live = live + jnp.where(jnp.logical_and(tile == t, alive), 1.0, 0.0)
-    errors = (diff * live).astype(BF16)
-    err[0] = errors
-    turned[...] = lax.dot_general(
-        errors, rows, (((0,), (0,)), ((), ())), preferred_element_type=F32
-    ).astype(BF16)
-    piece = turned.shape[1] // lats
-    for q in range(lats):
-        core, x, y = q & 1, (q >> 1) & 1, (q >> 2) & 1
-        outer, inner = (x, y) if outer_bit == 2 else (y, x)
-        start = pl.multiple_of(jnp.bitwise_xor(place[0], q) * piece, piece)
-        to = send if core else keep
-        to[outer, inner, 0] = turned[:, pl.ds(start, piece)]
-
-
-def slot_chunk(first_slot, count, outer_bit, lats, place, small, tile_of, band, scale, shift, heads, targets, errors):
+    for k in range(count):
+        live = jnp.zeros(tile.shape, F32)
+        for t in range(tiles):
+            alive = levels[first_slot + k] < counts[datasets[0, t]]
+            live = live + jnp.where(jnp.logical_and(tile == t, alive), 1.0, 0.0)
+        mine = predicted[:, k * LANES : k * LANES + outs]
+        diff = mine + bias[k] - target[k].astype(F32).reshape(total, outs)
+        err[:, k * LANES : k * LANES + outs] = (diff * live).astype(BF16)
+        err[:, k * LANES + outs : (k + 1) * LANES] = jnp.zeros((total, LANES - outs), BF16)
+        errors = err[:, k * LANES : (k + 1) * LANES]
+        sums = jnp.sum(errors.astype(F32), axis=0, keepdims=True)
+        column = jnp.transpose(jnp.broadcast_to(sums, (128, LANES)))[0:outs]
+        grad = lax.dot_general(
+            errors, latent, (((0,), (0,)), ((), ())), preferred_element_type=F32
+        )[0:outs]
+        for j in range(lats):
+            lanes = slice(j * piece, (j + 1) * piece)
+            turned[:, lanes] = (
+                grad[:, lanes] * scale[k][:, lanes] + column[:, 0:piece] * shift[k][:, lanes]
+            ).astype(BF16)
+        for q in range(lats):
+            core, x, y = q & 1, (q >> 1) & 1, (q >> 2) & 1
+            outer, inner = (x, y) if outer_bit == 2 else (y, x)
+            start = pl.multiple_of(jnp.bitwise_xor(place[0], q) * piece, piece)
+            to = send if core else keep
+            to[outer, inner, k] = turned[:, pl.ds(start, piece)]
+
+
+def slot_chunk(index, count, outer_bit, lats, place, small, tile_of, band, scale, shift, bias, heads, targets, errors, after):
     total, width = band.shape
-    slots, _, outs = heads.shape
+    slots, _, _, outs = targets.shape
+    tiles = small[1].shape[1]
     piece = width // lats
     smem = pl.BlockSpec(memory_space=pltpu.SMEM)
     halves = jax.ShapeDtypeStruct((2, 2, count, outs, piece), BF16)
-    half_spec = pl.BlockSpec((2, 2, 1, outs, piece), lambda k: (0, 0, k, 0, 0))
+    half_spec = pl.BlockSpec(halves.shape, lambda i: (0, 0, 0, 0, 0))
     in_specs = [
         smem, smem, smem, smem,
-        pl.BlockSpec((total, 1), lambda k: (0, 0)),
-        pl.BlockSpec((total, width), lambda k: (0, 0)),
-        pl.BlockSpec((1, 1, width), lambda k: (k + first_slot, 0, 0)),
-        pl.BlockSpec((1, 1, width), lambda k: (k + first_slot, 0, 0)),
-        pl.BlockSpec((1, width, outs), lambda k: (k + first_slot, 0, 0)),
-        pl.BlockSpec((1,) + targets.shape[1:], lambda k: (k + first_slot, 0, 0, 0)),
+        pl.BlockSpec((total, 1), lambda i: (0, 0)),
+        pl.BlockSpec((total, width), lambda i: (0, 0)),
+        pl.BlockSpec((count, 1, width), lambda i: (index, 0, 0)),
+        pl.BlockSpec((count, 1, width), lambda i: (index, 0, 0)),
+        pl.BlockSpec((count, 1, outs), lambda i: (index, 0, 0)),
+        pl.BlockSpec((count, LANES, width), lambda i: (index, 0, 0)),
+        pl.BlockSpec((count,) + targets.shape[1:], lambda i: (index, 0, 0, 0)),
     ]
-    args = [place, *small, tile_of, band, scale, shift, heads, targets]
+    args = [place, *small, tile_of, band, scale, shift, bias, heads, targets]
     aliases = {}
     if errors is not None:
-        in_specs.append(pl.BlockSpec(memory_space=pl.ANY))
         aliases = {len(args): 2}
         args.append(errors)
+    args.extend(after)
+    in_specs.extend([pl.BlockSpec(memory_space=pl.ANY)] * (len(args) - len(in_specs)))
     return pl.pallas_call(
-        functools.partial(slot_kernel, first_slot, lats, outer_bit, total // (WH * tile_cols(targets, small))),
-        grid=(count,),
-        out_shape=(halves, halves, jax.ShapeDtypeStruct((slots, total, outs), BF16)),
+        functools.partial(slot_kernel, index * count, lats, outer_bit, tiles),
+        grid=(1,),
+        out_shape=(halves, halves, jax.ShapeDtypeStruct((total, slots * LANES), BF16)),
         in_specs=in_specs,
         out_specs=(
             half_spec,
             half_spec,
-            pl.BlockSpec((1, total, outs), lambda k: (k + first_slot, 0, 0)),
+            pl.BlockSpec((total, count * LANES), lambda i: (0, index)),
         ),
         scratch_shapes=[pltpu.VMEM((outs, width), BF16)],
         input_output_aliases=aliases,
@@ -294,26 +387,21 @@
     )(*args)
 
 
-def tile_cols(targets, small):
-    return targets.shape[2] // small[1].shape[1]
-
-
-def back_kernel(tiles, cols, place, err, weight, scale, out, total):
-    slot = pl.program_id(0)
-    term = (
-        lax.dot_general(err[0], weight[0], (((1,), (1,)), ((), ())), preferred_element_type=F32)
-        * scale[0]
-    )
-
-    @pl.when(slot == 0)
+def back_kernel(tiles, cols, place, err, weight, *refs):
+    out, total = refs[-2:]
+    step = pl.program_id(0)
+    width = weight.shape[-1]
+    term = jnp.dot(err[...], weight[...].reshape(-1, width), preferred_element_type=F32)
+
+    @pl.when(step == 0)
     def _():
         total[...] = term
 
-    @pl.when(slot > 0)
+    @pl.when(step > 0)
     def _():
         total[...] += term
 
-    @pl.when(slot == pl.num_programs(0) - 1)
+    @pl.when(step == pl.num_programs(0) - 1)
     def _():
         for s in range(tiles):
             tile = lax.rem(place[1] + s, tiles)
@@ -322,28 +410,28 @@
                 out[s, r] = total[pl.ds(start, cols), :].astype(BF16)
 
 
-def back_terms(place, errors, heads, scale, tiles, cols):
-    slots, total, outs = errors.shape
-    width = heads.shape[1]
+def back_terms(place, errors, heads, count, tiles, cols, after):
+    total = errors.shape[0]
+    slots, _, width = heads.shape
     shape = (tiles, WH, cols, width)
     return pl.pallas_call(
         functools.partial(back_kernel, tiles, cols),
-        grid=(slots,),
+        grid=(slots // count,),
         out_shape=jax.ShapeDtypeStruct(shape, BF16),
         in_specs=[
             pl.BlockSpec(memory_space=pltpu.SMEM),
-            pl.BlockSpec((1, total, outs), lambda k: (k, 0, 0)),
-            pl.BlockSpec((1, width, outs), lambda k: (k, 0, 0)),
-            pl.BlockSpec((1, 1, width), lambda k: (k, 0, 0)),
-        ],
-        out_specs=pl.BlockSpec(shape, lambda k: (0, 0, 0, 0)),
+            pl.BlockSpec((total, count * LANES), lambda i: (0, i)),
+            pl.BlockSpec((count, LANES, width), lambda i: (i, 0, 0)),
+        ]
+        + [pl.BlockSpec(memory_space=pl.ANY)] * len(after),
+        out_specs=pl.BlockSpec(shape, lambda i: (0, 0, 0, 0)),
         scratch_shapes=[pltpu.VMEM((total, width), F32)],
         compiler_params=pltpu.CompilerParams(vmem_limit_bytes=VMEM_LIMIT),
         cost_estimate=pl.CostEstimate(
-            flops=slots * 4 * total * width * outs, bytes_accessed=12_000_000, transcendentals=0
+            flops=slots * 2 * total * width * LANES, bytes_accessed=12_000_000, transcendentals=0
         ),
         name="latent_terms",
-    )(place, errors, heads, scale)
+    )(place, errors, heads, *after)
 
 
 def join_kernel(norm, *refs):
@@ -352,8 +440,7 @@
     slot = 0
     for kept, came in zip(pairs[0::2], pairs[1::2]):
         for k in range(kept.shape[0]):
-            total = (kept[k].astype(F32) + came[k].astype(F32)) * norm
-            out[slot] = total.T
+            out[slot] = (kept[k].astype(F32) + came[k].astype(F32)) * norm
             slot += 1
 
 
@@ -364,7 +451,7 @@
     vmem = pl.BlockSpec(memory_space=pltpu.VMEM)
     return pl.pallas_call(
         functools.partial(join_kernel, norm),
-        out_shape=jax.ShapeDtypeStruct((slots, piece, outs), F32),
+        out_shape=jax.ShapeDtypeStruct((slots, outs, piece), F32),
         in_specs=[vmem] * len(flat),
         out_specs=vmem,
         compiler_params=pltpu.CompilerParams(vmem_limit_bytes=VMEM_LIMIT),
@@ -379,10 +466,10 @@
 ):
     rows, cols, width = patches.shape
     lats, tiles = lax.axis_size("lat"), lax.axis_size("var")
-    slots, _, outs = head_weight.shape
+    slots = head_weight.shape[0]
     lat, var = lax.axis_index("lat"), lax.axis_index("var")
     place = jnp.stack([lat, var]).astype(jnp.int32)
-    heads_full = lax.all_gather(head_weight, "lat", axis=1, tiled=True)
+    gathered = lax.all_gather(jnp.transpose(head_weight, (0, 2, 1)), "lat", axis=0, tiled=False)
 
     right = [(i, (i + 1) % tiles) for i in range(tiles)]
     up = [(i, i + 1) for i in range(lats - 1)]
@@ -395,7 +482,7 @@
     above_left = lax.ppermute(low[:, cols - HC :], ("lat", "var"), both(up))
     below_left = lax.ppermute(high[:, cols - HC :], ("lat", "var"), both(down))
     mine = attention(
-        place, (patches, left, above, above_left, below, below_left), norm_gain, input_proj, output_proj, lats
+        place, patches, (left, above, above_left, below, below_left), norm_gain, input_proj, output_proj, lats
     )
     pieces = [mine]
     for s in range(1, tiles):
@@ -405,29 +492,42 @@
     tile_of = jnp.asarray(np.arange(rows * tiles * cols)[:, None] % (tiles * cols) // cols, jnp.int32)
     scale3, shift3 = level_scale.reshape(slots, 1, width), level_shift.reshape(slots, 1, width)
     small = (level_counts, tile_dataset, slot_level)
+    heads_full, bias = scaled_heads(gathered, scale3, shift3)
     flip = lambda array, bit: lax.ppermute(array, "lat", [(i, i ^ bit) for i in range(lats)])
     add = lambda a, b: (a.astype(F32) + b.astype(F32)).astype(BF16)
     count = 2
-    errors, pairs = None, []
-    for index in range(slots // count):
-        outer_bit = 2 if index % 2 == 0 else 4
-        keep, send, errors = slot_chunk(
-            index * count, count, outer_bit, lats, place, small, tile_of, band, scale3, shift3,
-            heads_full, targets, errors,
+    chunks = slots // count
+    kept, sent, errors = {}, {}, None
+
+    def advance(index, stage):
+        if index < 0 or index >= chunks:
+            return []
+        outer = 2 if index % 2 == 0 else 4
+        came = flip(sent[index], (1, outer)[stage])
+        kept[index], sent[index] = add(kept[index][0], came[0]), add(kept[index][1], came[1])
+        return [sent[index]]
+
+    for index in range(chunks):
+        after = advance(index - 3, 1) + advance(index - 2, 0)
+        kept[index], sent[index], errors = slot_chunk(
+            index, count, 2 if index % 2 == 0 else 4, lats, place, small, tile_of, band, scale3, shift3,
+            bias, heads_full, targets, errors, after,
         )
-        came = flip(send, 1)
-        keep, send = add(keep[0], came[0]), add(keep[1], came[1])
-        came = flip(send, outer_bit)
-        keep, send = add(keep[0], came[0]), add(keep[1], came[1])
-        pairs.append((keep, flip(send, 6 - outer_bit)))
-    terms = back_terms(place, errors, heads_full, scale3, tiles, cols)
+    after = advance(chunks - 3, 1) + advance(chunks - 2, 0)
+    terms = back_terms(place, errors, heads_full, count, tiles, cols, after)
+    advance(chunks - 1, 0)
+    advance(chunks - 2, 1)
+    advance(chunks - 1, 1)
+    pairs = [
+        (kept[i], flip(sent[i], 4 if i % 2 == 0 else 2)) for i in range(chunks)
+    ]
     total = terms[0].astype(F32)
     for s in range(1, tiles):
         came = lax.ppermute(terms[s], "var", [(i, (i + s) % tiles) for i in range(tiles)])
         total = total + came.astype(F32)
     grad_latent = total.astype(BF16)
     grad_head = join_heads(pairs, 1.0 / math.sqrt(lats * rows * tiles * cols))
-    return (latent, grad_latent, grad_head)
+    return (latent, grad_latent, jnp.transpose(grad_head, (0, 2, 1)))
 
 
 def padded(array, sides, width, wrap):

time: 173 us -> 179 us (1.035)
  Pallas kernels: 51 us -> 56.7 us
  local copies, waits for them, and re-layouts: 15.1 us -> 9.45 us
  waiting for transfers between devices: 50.6 us -> 55.6 us
    ppermute x3, waiting for transfers between devices: 0.01 us -> 21.3 us  [fast_local(): lax.ppermute(terms[s], 'var', [(i, (i + s) % tiles) for i in range(tiles)])]
    ppermute x15, waiting for transfers between devices: 21.1 us -> 9.18 us  [fast_local(): lax.ppermute(array, 'lat', [(i, i ^ bit) for i in range(lats)])]
    ppermute x3, waiting for transfers between devices: 24.7 us -> 18.6 us  [fast_local(): lax.ppermute(mine, 'var', [(i, (i + s) % tiles) for i in range(tiles)])]
    unnamed x30 -> x24, local copies, waits for them, and re-layouts: 12.2 us -> 6.55 us
    ppermute x1, waiting for transfers between devices: 0.01 us -> 5.47 us  [fast_local(): below_left = lax.ppermute(high[:, cols - HC:], ('lat', 'var'), both(down))]
    ppermute x1, waiting for transfers between devices: 4.77 us -> 0.01 us  [fast_local(): left = lax.ppermute(patches[:, cols - HC:], 'var', right)]
    pallas_call x6 -> x7, Pallas kernels: 39.2 us -> 43.8 us  [the longest x5 25.7 us: slot_chunk(): pl.pallas_call(functools.partial(slot_kernel, index * count, lats, outer_...]
    ppermute x3, starting transfers between devices: 4.83 us -> 7.57 us  [fast_local(): lax.ppermute(terms[s], 'var', [(i, (i + s) % tiles) for i in range(tiles)])]
  transfers between devices with their start and end apart: 27 -> 27, of which waited for: 9 -> 11; matrix products, arithmetic and copies ran while one was open for 3% -> 3% of each run, Pallas kernels for 26% -> 23%
where the time goes in v2:
time: 179 us; the launch traced here: 178 us
  Pallas kernels  56.7 us (32%)
  waiting for transfers between devices  55.6 us (31%)
  starting transfers between devices  39.4 us (22%)
  between operations  14.3 us (8%)
  local copies, waits for them, and re-layouts  9.45 us (5%)
  other arithmetic  2.53 us (1%)
    pallas_call x5, Pallas kernels, slot_chunk(): pl.pallas_call(functools.partial(slot_kernel, index * count, lats, outer_...  25.7 us
    ppermute x3, waiting for transfers between devices, fast_local(): lax.ppermute(terms[s], 'var', [(i, (i + s) % tiles) for i in range(tiles)])  21.3 us
    ppermute x3, waiting for transfers between devices, fast_local(): lax.ppermute(mine, 'var', [(i, (i + s) % tiles) for i in range(tiles)])  18.6 us
    ppermute x15, starting transfers between devices, fast_local(): lax.ppermute(array, 'lat', [(i, i ^ bit) for i in range(lats)])  15.1 us
    pallas_call x1, Pallas kernels, scaled_heads(): pl.pallas_call(scale_kernel, grid=(slots,), out_shape=(jax.ShapeDtypeStru...  9.74 us
    ppermute x15, waiting for transfers between devices, fast_local(): lax.ppermute(array, 'lat', [(i, i ^ bit) for i in range(lats)])  9.18 us
    pallas_call x1, Pallas kernels, attention(): pl.pallas_call(functools.partial(attention_kernel, bands), out_shape=jax....  8.92 us
    pallas_call x1, Pallas kernels, back_terms(): pl.pallas_call(functools.partial(back_kernel, tiles, cols), grid=(slots /...  8.37 us
  transfers between devices with their start and end apart: 27, of which 11 were waited for; matrix products, arithmetic and copies ran while one was open for 3% of the time, Pallas kernels for 23%

profile of v2, /device:TPU:0, one launch (start us, length us, event | category | flops | bytes accessed | tf_op | source)
XLA Modules:
  0.0 178.0 jit_solution(9600544738312793721)
XLA Ops:
  7.2 0.7 all-gather.3.cloned.1.call-update
  7.9 0.9 slice.159
  8.8 3.1 %collective-permute-start = (bf16[6,6,1024]{2,1,0:T(8,128)(2,1)S(1)}, bf16[6,6,1024]{2,1,0:T(8,128)(2,1)S(1)}, u32[]{:S(2)}, u32[]{:S(2)}) collective-permute-start(bf16[6,6,1024]{2,1,0:T(8,128)(2,1)S(1)} %slice.159), channel_id=1, source_target_pairs={{0,1},{1,2},{2,3},{3,0},{4,5},{5,6},{6,7},{7,4},{8,9},{9,10},{10,1... | collective-permute-start | bytes 221192 | tf_op jit(solution)/shard_map/ppermute | solution.py:481
  11.9 1.0 fusion.29
  12.9 1.5 collective-permute-start.1
  14.4 1.3 collective-permute-start.3
  15.7 0.9 fusion.28
  16.5 5.8 %collective-permute-start.2 = (bf16[3,6,1024]{2,1,0:T(8,128)(2,1)S(1)}, bf16[3,6,1024]{2,1,0:T(8,128)(2,1)S(1)}, u32[]{:S(2)}, u32[]{:S(2)}) collective-permute-start(bf16[3,6,1024]{2,1,0:T(8,128)(2,1)S(1)} %get-tuple-element.65), channel_id=1, source_target_pairs={{0,5},{1,6},{2,7},{3,4},{4,9},{5,10},{6,11},{7,8},{8,13},{9,14},{1... | collective-permute-start | bytes 110600 | tf_op jit(solution)/shard_map/ppermute | solution.py:482
  22.3 1.3 collective-permute-start.4
  24.0 5.5 %collective-permute-done.4.below_left = bf16[3,6,1024]{2,1,0:T(8,128)(2,1)S(1)} collective-permute-done((bf16[3,6,1024]{2,1,0:T(8,128)(2,1)S(1)}, bf16[3,6,1024]{2,1,0:T(8,128)(2,1)S(1)}, u32[]{:S(2)}, u32[]{:S(2)}) %collective-permute-start.4) | collective-permute-done | bytes 36896 | tf_op jit(solution)/shard_map/ppermute | solution.py:483
  29.5 1.0 copy-done.2
  30.5 1.6 copy-done.6
  32.1 0.7 copy-done.7
  32.8 1.0 copy-done.9
  33.8 8.9 %window_attention.1.refs_0_ = bf16[144,1024]{1,0:T(8,128)(2,1)S(1)} custom-call(s32[2]{0:T(128)S(1)} %pad_add_fusion.place, bf16[6,6,1024]{2,1,0:T(8,128)(2,1)S(1)} %collective-permute-done.left, bf16[3,24,1024]{2,1,0:T(8,128)(2,1)S(1)} %collective-permute-done.1.above, bf16[3,6,1024]{2,1,0:T(8,128)(2,1)S(1)} %collective-permute-done.2.above_left, ...), custom_call_target="tpu_custom_call" | custom-call | flops 6000000000 | bytes 12000000 | tf_op jit(solution)/shard_map/window_attention/pallas_call | solution.py:178
  42.8 1.0 collective-permute-start.6
  43.8 2.8 %collective-permute-start.7 = (bf16[144,1024]{1,0:T(8,128)(2,1)S(1)}, bf16[144,1024]{1,0:T(8,128)(2,1)S(1)}, u32[]{:S(2)}, u32[]{:S(2)}) collective-permute-start(bf16[144,1024]{1,0:T(8,128)(2,1)S(1)} %window_attention.1.refs_0_), channel_id=1, source_target_pairs={{0,3},{1,0},{2,1},{3,2},{4,7},{5,4},{6,5},{7,6},{8,11},{9,8},{10,9... | collective-permute-start | bytes 884744 | tf_op jit(solution)/shard_map/ppermute | solution.py:489
  46.8 5.3 %collective-permute-done.5.refs_1_ = bf16[144,1024]{1,0:T(8,128)(2,1)S(1)} collective-permute-done((bf16[144,1024]{1,0:T(8,128)(2,1)S(1)}, bf16[144,1024]{1,0:T(8,128)(2,1)S(1)}, u32[]{:S(2)}, u32[]{:S(2)}) %collective-permute-start.5) | collective-permute-done | bytes 294944 | tf_op jit(solution)/shard_map/ppermute | solution.py:489
  52.1 13.3 %collective-permute-done.6.refs_2_ = bf16[144,1024]{1,0:T(8,128)(2,1)S(1)} collective-permute-done((bf16[144,1024]{1,0:T(8,128)(2,1)S(1)}, bf16[144,1024]{1,0:T(8,128)(2,1)S(1)}, u32[]{:S(2)}, u32[]{:S(2)}) %collective-permute-start.6) | collective-permute-done | bytes 294944 | tf_op jit(solution)/shard_map/ppermute | solution.py:489
  65.4 2.6 %band_latents.1 = (bf16[576,1024]{1,0:T(8,128)(2,1)S(1)}, bf16[6,24,1024]{2,1,0:T(8,128)(2,1)}) custom-call(s32[2]{0:T(128)S(1)} %pad_add_fusion.place, bf16[576,576]{1,0:T(8,128)(2,1)S(1)} %copy-done.8, bf16[144,1024]{1,0:T(8,128)(2,1)S(1)} %window_attention.1.refs_0_, bf16[144,1024]{1,0:T(8,128)(2,1)S(1)} %collective-permute-done.5.refs_1_, ...), custom_call_target="tpu_custom_call" | custom-call | flops 679477248 | bytes 4000000 | tf_op jit(solution)/shard_map/band_latents/pallas_call | solution.py:238
  67.9 9.7 %scaled_heads.1 = (bf16[10,384,1024]{2,1,0:T(8,128)(2,1)}, f32[10,1,320]{2,1,0:T(1,128)S(1)}) custom-call(bf16[8,10,320,128]{3,2,1,0:T(8,128)(2,1)} %bitcast.98, f32[10,1,1024]{2,1,0:T(1,128)S(1)} %reshape.128.scale, f32[10,1,1024]{2,1,0:T(1,128)S(1)} %reshape.129.shift), custom_call_target="tpu_custom_call" | custom-call | flops 100000000 | bytes 16000000 | tf_op jit(solution)/shard_map/scaled_heads/pallas_call | solution.py:279
  77.7 4.8 %slot_errors.5 = (bf16[2,2,2,320,128]{4,3,2,1,0:T(8,128)(2,1)S(1)}, bf16[2,2,2,320,128]{4,3,2,1,0:T(8,128)(2,1)S(1)}, bf16[576,3840]{1,0:T(8,128)(2,1)}) custom-call(s32[2]{0:T(128)S(1)} %pad_add_fusion.place, s32[4]{0:T(128)S(1)} %copy-done.3, s32[1,4]{1,0:T(1,128)S(1)} %copy-done.4, s32[10]{0:T(128)S(1)} %copy-done.5, s32[576,1]{1,0:T(8,128)S(1)} %copy-done.1, ...), custom_call_target="tpu_custom_call" | custom-call | flops 3019898880 | bytes 5000000 | tf_op jit(solution)/shard_map/slot_errors/pallas_call | solution.py:370
  82.5 1.8 %collective-permute-start.8 = (bf16[2,2,2,320,128]{4,3,2,1,0:T(8,128)(2,1)S(1)}, bf16[2,2,2,320,128]{4,3,2,1,0:T(8,128)(2,1)S(1)}, u32[]{:S(2)}, u32[]{:S(2)}) collective-permute-start(bf16[2,2,2,320,128]{4,3,2,1,0:T(8,128)(2,1)S(1)} %get-tuple-element.29), channel_id=1, source_target_pairs={{0,4},{4,0},{8,12},{12,8},{16,20},{20,16},{24,28},{28,24},{1,5},{5... | collective-permute-start | bytes 1966088 | tf_op jit(solution)/shard_map/ppermute | solution.py:496
  84.3 5.2 %slot_errors.6 = (bf16[2,2,2,320,128]{4,3,2,1,0:T(8,128)(2,1)S(1)}, bf16[2,2,2,320,128]{4,3,2,1,0:T(8,128)(2,1)S(1)}, bf16[576,3840]{1,0:T(8,128)(2,1)}) custom-call(s32[2]{0:T(128)S(1)} %pad_add_fusion.place, s32[4]{0:T(128)S(1)} %copy-done.3, s32[1,4]{1,0:T(1,128)S(1)} %copy-done.4, s32[10]{0:T(128)S(1)} %copy-done.5, ...), custom_call_target="tpu_custom_call", output_to_operand_aliasing={{2}: (11, {})} | custom-call | flops 3019898880 | bytes 5000000 | tf_op jit(solution)/shard_map/slot_errors/pallas_call | solution.py:370
  89.7 2.4 %collective-permute-start.9 = (bf16[2,2,320,128]{3,2,1,0:T(8,128)(2,1)S(1)}, bf16[2,2,320,128]{3,2,1,0:T(8,128)(2,1)S(1)}, u32[]{:S(2)}, u32[]{:S(2)}) collective-permute-start(bf16[2,2,320,128]{3,2,1,0:T(8,128)(2,1)S(1)} %get-tuple-element.50.refs_1_), channel_id=1, source_target_pairs={{0,8},{4,12},{8,0},{12,4},{16,24},{20,28},{24,16},{28,20},{1,9},{5... | collective-permute-start | bytes 983048 | tf_op jit(solution)/shard_map/ppermute | solution.py:496
  92.3 2.1 %collective-permute-start.11 = (bf16[2,2,320,128]{3,2,1,0:T(8,128)(2,1)S(1)}, bf16[2,2,320,128]{3,2,1,0:T(8,128)(2,1)S(1)}, u32[]{:S(2)}, u32[]{:S(2)}) collective-permute-start(bf16[2,2,320,128]{3,2,1,0:T(8,128)(2,1)S(1)} %get-tuple-element.48.refs_2_), channel_id=1, source_target_pairs={{0,16},{4,20},{8,24},{12,28},{16,0},{20,4},{24,8},{28,12},{1,17},{... | collective-permute-start | bytes 983048 | tf_op jit(solution)/shard_map/ppermute | solution.py:496
  94.3 5.2 %slot_errors.7 = (bf16[2,2,2,320,128]{4,3,2,1,0:T(8,128)(2,1)S(1)}, bf16[2,2,2,320,128]{4,3,2,1,0:T(8,128)(2,1)S(1)}, bf16[576,3840]{1,0:T(8,128)(2,1)}) custom-call(s32[2]{0:T(128)S(1)} %pad_add_fusion.place, s32[4]{0:T(128)S(1)} %copy-done.3, s32[1,4]{1,0:T(1,128)S(1)} %copy-done.4, s32[10]{0:T(128)S(1)} %copy-done.5, ...), custom_call_target="tpu_custom_call", output_to_operand_aliasing={{2}: (11, {})} | custom-call | flops 3019898880 | bytes 5000000 | tf_op jit(solution)/shard_map/slot_errors/pallas_call | solution.py:370
  99.6 0.9 collective-permute-done.9
  100.6 2.0 %collective-permute-start.18 = (bf16[2,320,128]{2,1,0:T(8,128)(2,1)S(1)}, bf16[2,320,128]{2,1,0:T(8,128)(2,1)S(1)}, u32[]{:S(2)}, u32[]{:S(2)}) collective-permute-start(bf16[2,320,128]{2,1,0:T(8,128)(2,1)S(1)} %get-tuple-element.63.refs_1_), channel_id=1, source_target_pairs={{0,16},{4,20},{8,24},{12,28},{16,0},{20,4},{24,8},{28,12},{1,17},{... | collective-permute-start | bytes 491528 | tf_op jit(solution)/shard_map/ppermute | solution.py:496
  102.5 5.2 %slot_errors.8 = (bf16[2,2,2,320,128]{4,3,2,1,0:T(8,128)(2,1)S(1)}, bf16[2,2,2,320,128]{4,3,2,1,0:T(8,128)(2,1)S(1)}, bf16[576,3840]{1,0:T(8,128)(2,1)}) custom-call(s32[2]{0:T(128)S(1)} %pad_add_fusion.place, s32[4]{0:T(128)S(1)} %copy-done.3, s32[1,4]{1,0:T(1,128)S(1)} %copy-done.4, s32[10]{0:T(128)S(1)} %copy-done.5, ...), custom_call_target="tpu_custom_call", output_to_operand_aliasing={{2}: (11, {})} | custom-call | flops 3019898880 | bytes 5000000 | tf_op jit(solution)/shard_map/slot_errors/pallas_call | solution.py:370
  107.9 0.4 add_convert_fusion.4
  108.6 5.2 %slot_errors.9 = (bf16[2,2,2,320,128]{4,3,2,1,0:T(8,128)(2,1)S(1)}, bf16[2,2,2,320,128]{4,3,2,1,0:T(8,128)(2,1)S(1)}, bf16[576,3840]{1,0:T(8,128)(2,1)}) custom-call(s32[2]{0:T(128)S(1)} %pad_add_fusion.place, s32[4]{0:T(128)S(1)} %copy-done.3, s32[1,4]{1,0:T(1,128)S(1)} %copy-done.4, s32[10]{0:T(128)S(1)} %copy-done.5, ...), custom_call_target="tpu_custom_call", output_to_operand_aliasing={{2}: (11, {})} | custom-call | flops 3019898880 | bytes 5000000 | tf_op jit(solution)/shard_map/slot_errors/pallas_call | solution.py:370
  114.3 1.6 collective-permute-start.21
  115.9 2.6 %collective-permute-done.13 = bf16[2,2,320,128]{3,2,1,0:T(8,128)(2,1)S(1)} collective-permute-done((bf16[2,2,320,128]{3,2,1,0:T(8,128)(2,1)S(1)}, bf16[2,2,320,128]{3,2,1,0:T(8,128)(2,1)S(1)}, u32[]{:S(2)}, u32[]{:S(2)}) %collective-permute-start.13) | collective-permute-done | bytes 327712 | tf_op jit(solution)/shard_map/ppermute | solution.py:496
  118.6 2.2 %copy-done = bf16[576,3840]{1,0:T(8,128)(2,1)S(1)} copy-done((bf16[576,3840]{1,0:T(8,128)(2,1)S(1)}, bf16[576,3840]{1,0:T(8,128)(2,1)}, u32[]{:S(2)}) %copy-start) | copy-done | bytes 4423704
  120.8 8.4 %latent_terms.1 = bf16[4,6,24,1024]{3,2,1,0:T(8,128)(2,1)S(1)} custom-call(s32[2]{0:T(128)S(1)} %pad_add_fusion.place, bf16[576,3840]{1,0:T(8,128)(2,1)S(1)} %copy-done, bf16[10,384,1024]{2,1,0:T(8,128)(2,1)} %get-tuple-element.25.weight, bf16[2,320,128]{2,1,0:T(8,128)(2,1)S(1)} %get-tuple-element.59.refs_0_, ...), custom_call_target="tpu_custom_call" | custom-call | flops 4529848320 | bytes 12000000 | tf_op jit(solution)/shard_map/latent_terms/pallas_call | solution.py:417
  129.8 5.7 %collective-permute-start.17 = (bf16[6,24,1024]{2,1,0:T(8,128)(2,1)S(1)}, bf16[6,24,1024]{2,1,0:T(8,128)(2,1)S(1)}, u32[]{:S(2)}, u32[]{:S(2)}) collective-permute-start(bf16[6,24,1024]{2,1,0:T(8,128)(2,1)S(1)} %get-tuple-element.52), channel_id=1, source_target_pairs={{0,3},{1,0},{2,1},{3,2},{4,7},{5,4},{6,5},{7,6},{8,11},{9,8},{10,9... | collective-permute-start | bytes 884744 | tf_op jit(solution)/shard_map/ppermute | solution.py:526
  135.5 1.9 %collective-permute-start.16 = (bf16[6,24,1024]{2,1,0:T(8,128)(2,1)S(1)}, bf16[6,24,1024]{2,1,0:T(8,128)(2,1)S(1)}, u32[]{:S(2)}, u32[]{:S(2)}) collective-permute-start(bf16[6,24,1024]{2,1,0:T(8,128)(2,1)S(1)} %get-tuple-element.53), channel_id=1, source_target_pairs={{0,2},{1,3},{2,0},{3,1},{4,6},{5,7},{6,4},{7,5},{8,10},{9,11},{10,... | collective-permute-start | bytes 884744 | tf_op jit(solution)/shard_map/ppermute | solution.py:526
  137.5 1.3 collective-permute-done.24
  138.8 0.5 collective-permute-start.19
  139.4 3.7 %collective-permute-done.17 = bf16[6,24,1024]{2,1,0:T(8,128)(2,1)S(1)} collective-permute-done((bf16[6,24,1024]{2,1,0:T(8,128)(2,1)S(1)}, bf16[6,24,1024]{2,1,0:T(8,128)(2,1)S(1)}, u32[]{:S(2)}, u32[]{:S(2)}) %collective-permute-start.17) | collective-permute-done | bytes 294944 | tf_op jit(solution)/shard_map/ppermute | solution.py:526
  143.0 2.0 %collective-permute-start.20 = (bf16[2,320,128]{2,1,0:T(8,128)(2,1)S(1)}, bf16[2,320,128]{2,1,0:T(8,128)(2,1)S(1)}, u32[]{:S(2)}, u32[]{:S(2)}) collective-permute-start(bf16[2,320,128]{2,1,0:T(8,128)(2,1)S(1)} %get-tuple-element.59.refs_0_), channel_id=1, source_target_pairs={{0,16},{4,20},{8,24},{12,28},{16,0},{20,4},{24,8},{28,12},{1,17},{... | collective-permute-start | bytes 491528 | tf_op jit(solution)/shard_map/ppermute | solution.py:496
  145.0 17.6 %collective-permute-done.16 = bf16[6,24,1024]{2,1,0:T(8,128)(2,1)S(1)} collective-permute-done((bf16[6,24,1024]{2,1,0:T(8,128)(2,1)S(1)}, bf16[6,24,1024]{2,1,0:T(8,128)(2,1)S(1)}, u32[]{:S(2)}, u32[]{:S(2)}) %collective-permute-start.16) | collective-permute-done | bytes 294944 | tf_op jit(solution)/shard_map/ppermute | solution.py:526
  162.7 1.7 collective-permute-start.22
  164.4 0.9 fusion.2
  165.4 2.6 %collective-permute-done.22.refs_7_ = bf16[2,320,128]{2,1,0:T(8,128)(2,1)S(1)} collective-permute-done((bf16[2,320,128]{2,1,0:T(8,128)(2,1)S(1)}, bf16[2,320,128]{2,1,0:T(8,128)(2,1)S(1)}, u32[]{:S(2)}, u32[]{:S(2)}) %collective-permute-start.22) | collective-permute-done | bytes 163872 | tf_op jit(solution)/shard_map/ppermute | solution.py:496
  168.0 1.7 collective-permute-done.25.refs_9_
  169.7 1.4 join_heads.1
  (59 shorter events, 2.9 us)
Async XLA Ops:
  7.2 60.8 %all-gather.3.cloned.1.call-start = ((), (), s32[]{:S(2)}) async-start(), calls=%async_computation | async-start | bytes 7372800 | tf_op jit(solution)/shard_map/all_gather | solution.py:472
  8.8 20.7 %collective-permute-start = (bf16[6,6,1024]{2,1,0:T(8,128)(2,1)S(1)}, bf16[6,6,1024]{2,1,0:T(8,128)(2,1)S(1)}, u32[]{:S(2)}, u32[]{:S(2)}) collective-permute-start(bf16[6,6,1024]{2,1,0:T(8,128)(2,1)S(1)} %slice.159), channel_id=1, source_target_pairs={{0,1},{1,2},{2,3},{3,0},{4,5},{5,6},{6,7},{7,4},{8,9},{9,10},{10,1... | collective-permute-start | bytes 221192 | tf_op jit(solution)/shard_map/ppermute | solution.py:481
  12.9 16.6 %collective-permute-start.1 = (bf16[3,24,1024]{2,1,0:T(8,128)(2,1)S(1)}, bf16[3,24,1024]{2,1,0:T(8,128)(2,1)S(1)}, u32[]{:S(2)}, u32[]{:S(2)}) collective-permute-start(bf16[3,24,1024]{2,1,0:T(8,128)(2,1)S(1)} %get-tuple-element.67), channel_id=1, source_target_pairs={{0,4},{4,8},{8,12},{12,16},{16,20},{20,24},{24,28},{1,5},{5,9},{9,... | collective-permute-start | bytes 442376 | tf_op jit(solution)/shard_map/ppermute | solution.py:479
  14.4 15.1 %collective-permute-start.3 = (bf16[3,24,1024]{2,1,0:T(8,128)(2,1)S(1)}, bf16[3,24,1024]{2,1,0:T(8,128)(2,1)S(1)}, u32[]{:S(2)}, u32[]{:S(2)}) collective-permute-start(bf16[3,24,1024]{2,1,0:T(8,128)(2,1)S(1)} %get-tuple-element.66), channel_id=1, source_target_pairs={{4,0},{8,4},{12,8},{16,12},{20,16},{24,20},{28,24},{5,1},{9,5},{13... | collective-permute-start | bytes 442376 | tf_op jit(solution)/shard_map/ppermute | solution.py:480
  16.5 7.5 %collective-permute-start.2 = (bf16[3,6,1024]{2,1,0:T(8,128)(2,1)S(1)}, bf16[3,6,1024]{2,1,0:T(8,128)(2,1)S(1)}, u32[]{:S(2)}, u32[]{:S(2)}) collective-permute-start(bf16[3,6,1024]{2,1,0:T(8,128)(2,1)S(1)} %get-tuple-element.65), channel_id=1, source_target_pairs={{0,5},{1,6},{2,7},{3,4},{4,9},{5,10},{6,11},{7,8},{8,13},{9,14},{1... | collective-permute-start | bytes 110600 | tf_op jit(solution)/shard_map/ppermute | solution.py:482
  22.3 7.2 %collective-permute-start.4 = (bf16[3,6,1024]{2,1,0:T(8,128)(2,1)S(1)}, bf16[3,6,1024]{2,1,0:T(8,128)(2,1)S(1)}, u32[]{:S(2)}, u32[]{:S(2)}) collective-permute-start(bf16[3,6,1024]{2,1,0:T(8,128)(2,1)S(1)} %get-tuple-element.64), channel_id=1, source_target_pairs={{4,1},{5,2},{6,3},{7,0},{8,5},{9,6},{10,7},{11,4},{12,9},{13,10},{... | collective-permute-start | bytes 110600 | tf_op jit(solution)/shard_map/ppermute | solution.py:483
  29.5 1.0 copy-start.2
  30.5 1.6 copy-start.6
  32.1 0.7 copy-start.7
  32.8 1.0 copy-start.9
  33.8 12.8 %copy-start.10 = (f32[10,1024]{1,0:T(8,128)S(1)}, f32[10,1024]{1,0:T(8,128)}, u32[]{:S(2)}) copy-start(f32[10,1024]{1,0:T(8,128)} %param.18) | copy-start | bytes 122884
  33.8 12.8 %copy-start.11 = (f32[10,1024]{1,0:T(8,128)S(1)}, f32[10,1024]{1,0:T(8,128)}, u32[]{:S(2)}) copy-start(f32[10,1024]{1,0:T(8,128)} %param.19) | copy-start | bytes 122884
  33.8 31.5 %copy-start.8 = (bf16[576,576]{1,0:T(8,128)(2,1)S(1)}, bf16[576,576]{1,0:T(8,128)(2,1)}, u32[]{:S(2)}) copy-start(bf16[576,576]{1,0:T(8,128)(2,1)} %constant.16.clone.chosen) | copy-start | bytes 1990660
  42.7 9.3 %collective-permute-start.5 = (bf16[144,1024]{1,0:T(8,128)(2,1)S(1)}, bf16[144,1024]{1,0:T(8,128)(2,1)S(1)}, u32[]{:S(2)}, u32[]{:S(2)}) collective-permute-start(bf16[144,1024]{1,0:T(8,128)(2,1)S(1)} %window_attention.1.refs_0_), channel_id=1, source_target_pairs={{0,1},{1,2},{2,3},{3,0},{4,5},{5,6},{6,7},{7,4},{8,9},{9,10},{10,1... | collective-permute-start | bytes 884744 | tf_op jit(solution)/shard_map/ppermute | solution.py:489
  42.8 22.5 %collective-permute-start.6 = (bf16[144,1024]{1,0:T(8,128)(2,1)S(1)}, bf16[144,1024]{1,0:T(8,128)(2,1)S(1)}, u32[]{:S(2)}, u32[]{:S(2)}) collective-permute-start(bf16[144,1024]{1,0:T(8,128)(2,1)S(1)} %window_attention.1.refs_0_), channel_id=1, source_target_pairs={{0,2},{1,3},{2,0},{3,1},{4,6},{5,7},{6,4},{7,5},{8,10},{9,11},{10,... | collective-permute-start | bytes 884744 | tf_op jit(solution)/shard_map/ppermute | solution.py:489
  43.8 21.5 %collective-permute-start.7 = (bf16[144,1024]{1,0:T(8,128)(2,1)S(1)}, bf16[144,1024]{1,0:T(8,128)(2,1)S(1)}, u32[]{:S(2)}, u32[]{:S(2)}) collective-permute-start(bf16[144,1024]{1,0:T(8,128)(2,1)S(1)} %window_attention.1.refs_0_), channel_id=1, source_target_pairs={{0,3},{1,0},{2,1},{3,2},{4,7},{5,4},{6,5},{7,6},{8,11},{9,8},{10,9... | collective-permute-start | bytes 884744 | tf_op jit(solution)/shard_map/ppermute | solution.py:489
  46.7 31.0 %copy-start.1 = (s32[576,1]{1,0:T(8,128)S(1)}, s32[576,1]{1,0:T(8,128)}, u32[]{:S(2)}) copy-start(s32[576,1]{1,0:T(8,128)} %constant.17.clone.tile_of) | copy-start | bytes 6916
  46.7 31.0 %copy-start.3 = (s32[4]{0:T(128)S(1)}, s32[4]{0:T(128)}, u32[]{:S(2)}) copy-start(s32[4]{0:T(128)} %counts.9) | copy-start | bytes 52
  46.7 31.0 %copy-start.4 = (s32[1,4]{1,0:T(1,128)S(1)}, s32[1,4]{1,0:T(1,128)}, u32[]{:S(2)}) copy-start(s32[1,4]{1,0:T(1,128)} %datasets.9) | copy-start | bytes 52
  46.7 31.0 %copy-start.5 = (s32[10]{0:T(128)S(1)}, s32[10]{0:T(128)}, u32[]{:S(2)}) copy-start(s32[10]{0:T(128)} %levels.9) | copy-start | bytes 124
  82.5 7.0 %collective-permute-start.8 = (bf16[2,2,2,320,128]{4,3,2,1,0:T(8,128)(2,1)S(1)}, bf16[2,2,2,320,128]{4,3,2,1,0:T(8,128)(2,1)S(1)}, u32[]{:S(2)}, u32[]{:S(2)}) collective-permute-start(bf16[2,2,2,320,128]{4,3,2,1,0:T(8,128)(2,1)S(1)} %get-tuple-element.29), channel_id=1, source_target_pairs={{0,4},{4,0},{8,12},{12,8},{16,20},{20,16},{24,28},{28,24},{1,5},{5... | collective-permute-start | bytes 1966088 | tf_op jit(solution)/shard_map/ppermute | solution.py:496
  89.5 2.6 %collective-permute-start.10 = (bf16[2,2,2,320,128]{4,3,2,1,0:T(8,128)(2,1)S(1)}, bf16[2,2,2,320,128]{4,3,2,1,0:T(8,128)(2,1)S(1)}, u32[]{:S(2)}, u32[]{:S(2)}) collective-permute-start(bf16[2,2,2,320,128]{4,3,2,1,0:T(8,128)(2,1)S(1)} %get-tuple-element.32), channel_id=1, source_target_pairs={{0,4},{4,0},{8,12},{12,8},{16,20},{20,16},{24,28},{28,24},{1,5},{5... | collective-permute-start | bytes 1966088 | tf_op jit(solution)/shard_map/ppermute | solution.py:496
  89.7 10.7 %collective-permute-start.9 = (bf16[2,2,320,128]{3,2,1,0:T(8,128)(2,1)S(1)}, bf16[2,2,320,128]{3,2,1,0:T(8,128)(2,1)S(1)}, u32[]{:S(2)}, u32[]{:S(2)}) collective-permute-start(bf16[2,2,320,128]{3,2,1,0:T(8,128)(2,1)S(1)} %get-tuple-element.50.refs_1_), channel_id=1, source_target_pairs={{0,8},{4,12},{8,0},{12,4},{16,24},{20,28},{24,16},{28,20},{1,9},{5... | collective-permute-start | bytes 983048 | tf_op jit(solution)/shard_map/ppermute | solution.py:496
  92.3 15.5 %collective-permute-start.11 = (bf16[2,2,320,128]{3,2,1,0:T(8,128)(2,1)S(1)}, bf16[2,2,320,128]{3,2,1,0:T(8,128)(2,1)S(1)}, u32[]{:S(2)}, u32[]{:S(2)}) collective-permute-start(bf16[2,2,320,128]{3,2,1,0:T(8,128)(2,1)S(1)} %get-tuple-element.48.refs_2_), channel_id=1, source_target_pairs={{0,16},{4,20},{8,24},{12,28},{16,0},{20,4},{24,8},{28,12},{1,17},{... | collective-permute-start | bytes 983048 | tf_op jit(solution)/shard_map/ppermute | solution.py:496
  99.6 8.3 %collective-permute-start.12 = (bf16[2,2,2,320,128]{4,3,2,1,0:T(8,128)(2,1)S(1)}, bf16[2,2,2,320,128]{4,3,2,1,0:T(8,128)(2,1)S(1)}, u32[]{:S(2)}, u32[]{:S(2)}) collective-permute-start(bf16[2,2,2,320,128]{4,3,2,1,0:T(8,128)(2,1)S(1)} %get-tuple-element.35), channel_id=1, source_target_pairs={{0,4},{4,0},{8,12},{12,8},{16,20},{20,16},{24,28},{28,24},{1,5},{5... | collective-permute-start | bytes 1966088 | tf_op jit(solution)/shard_map/ppermute | solution.py:496
  100.6 64.8 %collective-permute-start.18 = (bf16[2,320,128]{2,1,0:T(8,128)(2,1)S(1)}, bf16[2,320,128]{2,1,0:T(8,128)(2,1)S(1)}, u32[]{:S(2)}, u32[]{:S(2)}) collective-permute-start(bf16[2,320,128]{2,1,0:T(8,128)(2,1)S(1)} %get-tuple-element.63.refs_1_), channel_id=1, source_target_pairs={{0,16},{4,20},{8,24},{12,28},{16,0},{20,4},{24,8},{28,12},{1,17},{... | collective-permute-start | bytes 491528 | tf_op jit(solution)/shard_map/ppermute | solution.py:496
  107.8 6.3 %collective-permute-start.14 = (bf16[2,2,2,320,128]{4,3,2,1,0:T(8,128)(2,1)S(1)}, bf16[2,2,2,320,128]{4,3,2,1,0:T(8,128)(2,1)S(1)}, u32[]{:S(2)}, u32[]{:S(2)}) collective-permute-start(bf16[2,2,2,320,128]{4,3,2,1,0:T(8,128)(2,1)S(1)} %get-tuple-element.38), channel_id=1, source_target_pairs={{0,4},{4,0},{8,12},{12,8},{16,20},{20,16},{24,28},{28,24},{1,5},{5... | collective-permute-start | bytes 1966088 | tf_op jit(solution)/shard_map/ppermute | solution.py:496
  108.3 10.2 %collective-permute-start.13 = (bf16[2,2,320,128]{3,2,1,0:T(8,128)(2,1)S(1)}, bf16[2,2,320,128]{3,2,1,0:T(8,128)(2,1)S(1)}, u32[]{:S(2)}, u32[]{:S(2)}) collective-permute-start(bf16[2,2,320,128]{3,2,1,0:T(8,128)(2,1)S(1)} %get-tuple-element.46.refs_2_), channel_id=1, source_target_pairs={{0,8},{4,12},{8,0},{12,4},{16,24},{20,28},{24,16},{28,20},{1,9},{5... | collective-permute-start | bytes 983048 | tf_op jit(solution)/shard_map/ppermute | solution.py:496
  113.8 15.4 %collective-permute-start.23 = (bf16[2,2,2,320,128]{4,3,2,1,0:T(8,128)(2,1)S(1)}, bf16[2,2,2,320,128]{4,3,2,1,0:T(8,128)(2,1)S(1)}, u32[]{:S(2)}, u32[]{:S(2)}) collective-permute-start(bf16[2,2,2,320,128]{4,3,2,1,0:T(8,128)(2,1)S(1)} %get-tuple-element.40), channel_id=1, source_target_pairs={{0,4},{4,0},{8,12},{12,8},{16,20},{20,16},{24,28},{28,24},{1,5},{5... | collective-permute-start | bytes 1966088 | tf_op jit(solution)/shard_map/ppermute | solution.py:496
  114.3 23.1 %collective-permute-start.21 = (bf16[2,2,320,128]{3,2,1,0:T(8,128)(2,1)S(1)}, bf16[2,2,320,128]{3,2,1,0:T(8,128)(2,1)S(1)}, u32[]{:S(2)}, u32[]{:S(2)}) collective-permute-start(bf16[2,2,320,128]{3,2,1,0:T(8,128)(2,1)S(1)} %get-tuple-element.44.refs_1_), channel_id=1, source_target_pairs={{0,16},{4,20},{8,24},{12,28},{16,0},{20,4},{24,8},{28,12},{1,17},{... | collective-permute-start | bytes 983048 | tf_op jit(solution)/shard_map/ppermute | solution.py:496
  118.6 2.3 %copy-start = (bf16[576,3840]{1,0:T(8,128)(2,1)S(1)}, bf16[576,3840]{1,0:T(8,128)(2,1)}, u32[]{:S(2)}) copy-start(bf16[576,3840]{1,0:T(8,128)(2,1)} %get-tuple-element.36.err) | copy-start | bytes 13271044
  129.4 9.4 %collective-permute-start.24 = (bf16[2,2,320,128]{3,2,1,0:T(8,128)(2,1)S(1)}, bf16[2,2,320,128]{3,2,1,0:T(8,128)(2,1)S(1)}, u32[]{:S(2)}, u32[]{:S(2)}) collective-permute-start(bf16[2,2,320,128]{3,2,1,0:T(8,128)(2,1)S(1)} %get-tuple-element.42), channel_id=1, source_target_pairs={{0,8},{4,12},{8,0},{12,4},{16,24},{20,28},{24,16},{28,20},{1,9},{5... | collective-permute-start | bytes 983048 | tf_op jit(solution)/shard_map/ppermute | solution.py:496
  129.8 13.2 %collective-permute-start.17 = (bf16[6,24,1024]{2,1,0:T(8,128)(2,1)S(1)}, bf16[6,24,1024]{2,1,0:T(8,128)(2,1)S(1)}, u32[]{:S(2)}, u32[]{:S(2)}) collective-permute-start(bf16[6,24,1024]{2,1,0:T(8,128)(2,1)S(1)} %get-tuple-element.52), channel_id=1, source_target_pairs={{0,3},{1,0},{2,1},{3,2},{4,7},{5,4},{6,5},{7,6},{8,11},{9,8},{10,9... | collective-permute-start | bytes 884744 | tf_op jit(solution)/shard_map/ppermute | solution.py:526
  135.5 27.1 %collective-permute-start.16 = (bf16[6,24,1024]{2,1,0:T(8,128)(2,1)S(1)}, bf16[6,24,1024]{2,1,0:T(8,128)(2,1)S(1)}, u32[]{:S(2)}, u32[]{:S(2)}) collective-permute-start(bf16[6,24,1024]{2,1,0:T(8,128)(2,1)S(1)} %get-tuple-element.53), channel_id=1, source_target_pairs={{0,2},{1,3},{2,0},{3,1},{4,6},{5,7},{6,4},{7,5},{8,10},{9,11},{10,... | collective-permute-start | bytes 884744 | tf_op jit(solution)/shard_map/ppermute | solution.py:526
  137.4 27.0 %collective-permute-start.15 = (bf16[6,24,1024]{2,1,0:T(8,128)(2,1)S(1)}, bf16[6,24,1024]{2,1,0:T(8,128)(2,1)S(1)}, u32[]{:S(2)}, u32[]{:S(2)}) collective-permute-start(bf16[6,24,1024]{2,1,0:T(8,128)(2,1)S(1)} %get-tuple-element.51), channel_id=1, source_target_pairs={{0,1},{1,2},{2,3},{3,0},{4,5},{5,6},{6,7},{7,4},{8,9},{9,10},{10,1... | collective-permute-start | bytes 884744 | tf_op jit(solution)/shard_map/ppermute | solution.py:526
  138.8 26.6 %collective-permute-start.19 = (bf16[2,320,128]{2,1,0:T(8,128)(2,1)S(1)}, bf16[2,320,128]{2,1,0:T(8,128)(2,1)S(1)}, u32[]{:S(2)}, u32[]{:S(2)}) collective-permute-start(bf16[2,320,128]{2,1,0:T(8,128)(2,1)S(1)} %get-tuple-element.61.refs_1_), channel_id=1, source_target_pairs={{0,8},{4,12},{8,0},{12,4},{16,24},{20,28},{24,16},{28,20},{1,9},{5... | collective-permute-start | bytes 491528 | tf_op jit(solution)/shard_map/ppermute | solution.py:496
  143.0 22.3 %collective-permute-start.20 = (bf16[2,320,128]{2,1,0:T(8,128)(2,1)S(1)}, bf16[2,320,128]{2,1,0:T(8,128)(2,1)S(1)}, u32[]{:S(2)}, u32[]{:S(2)}) collective-permute-start(bf16[2,320,128]{2,1,0:T(8,128)(2,1)S(1)} %get-tuple-element.59.refs_0_), channel_id=1, source_target_pairs={{0,16},{4,20},{8,24},{12,28},{16,0},{20,4},{24,8},{28,12},{1,17},{... | collective-permute-start | bytes 491528 | tf_op jit(solution)/shard_map/ppermute | solution.py:496
  162.7 5.3 %collective-permute-start.22 = (bf16[2,320,128]{2,1,0:T(8,128)(2,1)S(1)}, bf16[2,320,128]{2,1,0:T(8,128)(2,1)S(1)}, u32[]{:S(2)}, u32[]{:S(2)}) collective-permute-start(bf16[2,320,128]{2,1,0:T(8,128)(2,1)S(1)} %get-tuple-element.56), channel_id=1, source_target_pairs={{0,8},{4,12},{8,0},{12,4},{16,24},{20,28},{24,16},{28,20},{1,9},{5... | collective-permute-start | bytes 491528 | tf_op jit(solution)/shard_map/ppermute | solution.py:496
  164.4 5.3 %collective-permute-start.25 = (bf16[2,320,128]{2,1,0:T(8,128)(2,1)S(1)}, bf16[2,320,128]{2,1,0:T(8,128)(2,1)S(1)}, u32[]{:S(2)}, u32[]{:S(2)}) collective-permute-start(bf16[2,320,128]{2,1,0:T(8,128)(2,1)S(1)} %get-tuple-element.54), channel_id=1, source_target_pairs={{0,16},{4,20},{8,24},{12,28},{16,0},{20,4},{24,8},{28,12},{1,17},{... | collective-permute-start | bytes 491528 | tf_op jit(solution)/shard_map/ppermute | solution.py:496
Sparse Core Ops, SparseCore 0:
  9.9 50.2 all-gather.2

commit v3 on v2

--- a/solution.py
+++ b/solution.py
@@ -252,196 +252,118 @@
     )(place, jnp.asarray(band_map(tiles, cols), BF16), *pieces)
 
 
-LANES = 384
-
-
-def scale_kernel(gathered, scale, shift, scaled, bias):
-    lats, _, outs, piece = gathered.shape
-    weight = jnp.concatenate([gathered[l, 0] for l in range(lats)], axis=1)
-    scaled[0, 0:outs, :] = (weight.astype(F32) * scale[0]).astype(BF16)
-    scaled[0, outs:, :] = jnp.zeros((scaled.shape[1] - outs, lats * piece), BF16)
-    rest = jnp.broadcast_to(shift[0], (8, lats * piece))
-    row = lax.broadcasted_iota(jnp.int32, rest.shape, 0)
-    split = jnp.zeros(rest.shape, F32)
-    for i in range(3):
-        part = rest.astype(BF16).astype(F32)
-        split = jnp.where(row == i, part, split)
-        rest = rest - part
-    terms = lax.dot_general(
-        split.astype(BF16), weight, (((1,), (1,)), ((), ())), preferred_element_type=F32
-    )
-    bias[0] = jnp.sum(terms, axis=0, keepdims=True)
-
-
-def scaled_heads(gathered, scale, shift):
-    lats, slots, outs, piece = gathered.shape
-    width = lats * piece
-    return pl.pallas_call(
-        scale_kernel,
-        grid=(slots,),
-        out_shape=(
-            jax.ShapeDtypeStruct((slots, LANES, width), BF16),
-            jax.ShapeDtypeStruct((slots, 1, outs), F32),
-        ),
-        in_specs=[
-            pl.BlockSpec((lats, 1, outs, piece), lambda k: (0, k, 0, 0)),
-            pl.BlockSpec((1, 1, width), lambda k: (k, 0, 0)),
-            pl.BlockSpec((1, 1, width), lambda k: (k, 0, 0)),
-        ],
-        out_specs=(
-            pl.BlockSpec((1, LANES, width), lambda k: (k, 0, 0)),
-            pl.BlockSpec((1, 1, outs), lambda k: (k, 0, 0)),
-        ),
-        compiler_params=pltpu.CompilerParams(vmem_limit_bytes=VMEM_LIMIT),
-        cost_estimate=pl.CostEstimate(
-            flops=100_000_000, bytes_accessed=16_000_000, transcendentals=0
-        ),
-        name="scaled_heads",
-    )(gathered, scale, shift)
-
-
-def slot_kernel(
-    first_slot, lats, outer_bit, tiles, place, counts, datasets, levels, tile_of, band, scale, shift,
-    bias, weight, target, *refs
-):
-    keep, send, err, turned = refs[-4:]
-    count, outs = target.shape[0], target.shape[-1]
-    total, width = band.shape
+def slot_kernel(first_slot, lats, tiles, final, place, counts, datasets, levels, tile_of, band, scale, shift, gathered, target, *refs):
+    keep, send, out = refs[-8:-5] if final else refs[-7:-4]
+    rows, errs, turned = refs[-4:-2], refs[-2], refs[-1]
+    total = refs[-5] if final else out
+    step = pl.program_id(0)
+    outs = target.shape[-1]
+    places, width = band.shape
     piece = width // lats
-    latent = band[...]
-    predicted = lax.dot_general(
-        latent, weight[...].reshape(count * LANES, width), (((1,), (1,)), ((), ())),
-        preferred_element_type=F32,
-    )
+
+    @pl.when(step == 0)
+    def _():
+        total[...] = refs[0][...] if final else jnp.zeros_like(total)
+
     tile = tile_of[...]
-    for k in range(count):
+    for k in range(2):
+        rows[k][...] = (band[...].astype(F32) * scale[k] + shift[k]).astype(BF16)
+    for k in range(2):
+        weight = jnp.concatenate([gathered[l, k] for l in range(lats)], axis=1)
+        predicted = lax.dot_general(
+            rows[k][...], weight, (((1,), (1,)), ((), ())), preferred_element_type=F32
+        )
         live = jnp.zeros(tile.shape, F32)
         for t in range(tiles):
-            alive = levels[first_slot + k] < counts[datasets[0, t]]
+            alive = levels[first_slot + 2 * step + k] < counts[datasets[0, t]]
             live = live + jnp.where(jnp.logical_and(tile == t, alive), 1.0, 0.0)
-        mine = predicted[:, k * LANES : k * LANES + outs]
-        diff = mine + bias[k] - target[k].astype(F32).reshape(total, outs)
-        err[:, k * LANES : k * LANES + outs] = (diff * live).astype(BF16)
-        err[:, k * LANES + outs : (k + 1) * LANES] = jnp.zeros((total, LANES - outs), BF16)
-        errors = err[:, k * LANES : (k + 1) * LANES]
-        sums = jnp.sum(errors.astype(F32), axis=0, keepdims=True)
-        column = jnp.transpose(jnp.broadcast_to(sums, (128, LANES)))[0:outs]
-        grad = lax.dot_general(
-            errors, latent, (((0,), (0,)), ((), ())), preferred_element_type=F32
-        )[0:outs]
-        for j in range(lats):
-            lanes = slice(j * piece, (j + 1) * piece)
-            turned[:, lanes] = (
-                grad[:, lanes] * scale[k][:, lanes] + column[:, 0:piece] * shift[k][:, lanes]
-            ).astype(BF16)
+        diff = predicted - target[k].astype(F32).reshape(places, outs)
+        errs[k] = (diff * live).astype(BF16)
+    for k in range(2):
+        turned[k] = lax.dot_general(
+            errs[k], rows[k][...], (((0,), (0,)), ((), ())), preferred_element_type=F32
+        ).astype(BF16)
         for q in range(lats):
             core, x, y = q & 1, (q >> 1) & 1, (q >> 2) & 1
-            outer, inner = (x, y) if outer_bit == 2 else (y, x)
+            outer, inner = (x, y) if k == 0 else (y, x)
             start = pl.multiple_of(jnp.bitwise_xor(place[0], q) * piece, piece)
             to = send if core else keep
-            to[outer, inner, k] = turned[:, pl.ds(start, piece)]
-
-
-def slot_chunk(index, count, outer_bit, lats, place, small, tile_of, band, scale, shift, bias, heads, targets, errors, after):
-    total, width = band.shape
-    slots, _, _, outs = targets.shape
+            to[k, outer, inner, 0] = turned[k, :, pl.ds(start, piece)]
+    for l in range(0, lats, 2):
+        lanes = slice(l * piece, (l + 2) * piece)
+        term = 0.0
+        for k in range(2):
+            weight = jnp.concatenate([gathered[l, k], gathered[l + 1, k]], axis=1)
+            term = term + jnp.dot(errs[k], weight, preferred_element_type=F32) * scale[k][:, lanes]
+        total[:, lanes] += term
+
+    if final:
+
+        @pl.when(step == pl.num_programs(0) - 1)
+        def _():
+            cols = out.shape[2]
+            for s in range(tiles):
+                at = lax.rem(place[1] + s, tiles)
+                for r in range(WH):
+                    start = pl.multiple_of(r * tiles * cols + at * cols, 8)
+                    out[s, r] = total[pl.ds(start, cols), :].astype(BF16)
+
+
+def slot_group(pair, pairs, lats, place, small, tile_of, band, scale, shift, gathered, targets, before):
+    places, width = band.shape
+    outs = targets.shape[-1]
     tiles = small[1].shape[1]
     piece = width // lats
     smem = pl.BlockSpec(memory_space=pltpu.SMEM)
-    halves = jax.ShapeDtypeStruct((2, 2, count, outs, piece), BF16)
-    half_spec = pl.BlockSpec(halves.shape, lambda i: (0, 0, 0, 0, 0))
+    halves = jax.ShapeDtypeStruct((2, 2, 2, pairs, outs, piece), BF16)
+    half_spec = pl.BlockSpec((2, 2, 2, 1, outs, piece), lambda i: (0, 0, 0, i, 0, 0))
     in_specs = [
         smem, smem, smem, smem,
-        pl.BlockSpec((total, 1), lambda i: (0, 0)),
-        pl.BlockSpec((total, width), lambda i: (0, 0)),
-        pl.BlockSpec((count, 1, width), lambda i: (index, 0, 0)),
-        pl.BlockSpec((count, 1, width), lambda i: (index, 0, 0)),
-        pl.BlockSpec((count, 1, outs), lambda i: (index, 0, 0)),
-        pl.BlockSpec((count, LANES, width), lambda i: (index, 0, 0)),
-        pl.BlockSpec((count,) + targets.shape[1:], lambda i: (index, 0, 0, 0)),
+        pl.BlockSpec((places, 1), lambda i: (0, 0)),
+        pl.BlockSpec((places, width), lambda i: (0, 0)),
+        pl.BlockSpec((2, 1, width), lambda i: (i + pair, 0, 0)),
+        pl.BlockSpec((2, 1, width), lambda i: (i + pair, 0, 0)),
+        pl.BlockSpec((lats, 2, outs, piece), lambda i: (0, i + pair, 0, 0)),
+        pl.BlockSpec((2,) + targets.shape[1:], lambda i: (i + pair, 0, 0, 0)),
     ]
-    args = [place, *small, tile_of, band, scale, shift, bias, heads, targets]
-    aliases = {}
-    if errors is not None:
-        aliases = {len(args): 2}
-        args.append(errors)
-    args.extend(after)
-    in_specs.extend([pl.BlockSpec(memory_space=pl.ANY)] * (len(args) - len(in_specs)))
+    args = [place, *small, tile_of, band, scale, shift, gathered, targets]
+    final = before is not None
+    scratch = [
+        pltpu.VMEM((places, width), BF16),
+        pltpu.VMEM((places, width), BF16),
+        pltpu.VMEM((2, places, outs), BF16),
+        pltpu.VMEM((2, outs, width), BF16),
+    ]
+    sums = jax.ShapeDtypeStruct((places, width), F32)
+    if final:
+        in_specs.append(pl.BlockSpec((places, width), lambda i: (0, 0)))
+        args.append(before)
+        scratch.insert(0, pltpu.VMEM(sums.shape, F32))
+        sums = jax.ShapeDtypeStruct((tiles, WH, places // (WH * tiles), width), BF16)
     return pl.pallas_call(
-        functools.partial(slot_kernel, index * count, lats, outer_bit, tiles),
-        grid=(1,),
-        out_shape=(halves, halves, jax.ShapeDtypeStruct((total, slots * LANES), BF16)),
+        functools.partial(slot_kernel, 2 * pair, lats, tiles, final),
+        grid=(pairs,),
+        out_shape=(halves, halves, sums),
         in_specs=in_specs,
-        out_specs=(
-            half_spec,
-            half_spec,
-            pl.BlockSpec((total, count * LANES), lambda i: (0, index)),
-        ),
-        scratch_shapes=[pltpu.VMEM((outs, width), BF16)],
-        input_output_aliases=aliases,
+        out_specs=(half_spec, half_spec, pl.BlockSpec(sums.shape, lambda i: (0,) * len(sums.shape))),
+        scratch_shapes=scratch,
         compiler_params=pltpu.CompilerParams(vmem_limit_bytes=VMEM_LIMIT),
         cost_estimate=pl.CostEstimate(
-            flops=count * 8 * total * width * outs, bytes_accessed=count * 2_500_000, transcendentals=0
+            flops=pairs * 12 * places * width * outs, bytes_accessed=pairs * 5_000_000, transcendentals=0
         ),
-        name="slot_errors",
+        name="slot_group",
     )(*args)
-
-
-def back_kernel(tiles, cols, place, err, weight, *refs):
-    out, total = refs[-2:]
-    step = pl.program_id(0)
-    width = weight.shape[-1]
-    term = jnp.dot(err[...], weight[...].reshape(-1, width), preferred_element_type=F32)
-
-    @pl.when(step == 0)
-    def _():
-        total[...] = term
-
-    @pl.when(step > 0)
-    def _():
-        total[...] += term
-
-    @pl.when(step == pl.num_programs(0) - 1)
-    def _():
-        for s in range(tiles):
-            tile = lax.rem(place[1] + s, tiles)
-            for r in range(WH):
-                start = pl.multiple_of(r * tiles * cols + tile * cols, 8)
-                out[s, r] = total[pl.ds(start, cols), :].astype(BF16)
-
-
-def back_terms(place, errors, heads, count, tiles, cols, after):
-    total = errors.shape[0]
-    slots, _, width = heads.shape
-    shape = (tiles, WH, cols, width)
-    return pl.pallas_call(
-        functools.partial(back_kernel, tiles, cols),
-        grid=(slots // count,),
-        out_shape=jax.ShapeDtypeStruct(shape, BF16),
-        in_specs=[
-            pl.BlockSpec(memory_space=pltpu.SMEM),
-            pl.BlockSpec((total, count * LANES), lambda i: (0, i)),
-            pl.BlockSpec((count, LANES, width), lambda i: (i, 0, 0)),
-        ]
-        + [pl.BlockSpec(memory_space=pl.ANY)] * len(after),
-        out_specs=pl.BlockSpec(shape, lambda i: (0, 0, 0, 0)),
-        scratch_shapes=[pltpu.VMEM((total, width), F32)],
-        compiler_params=pltpu.CompilerParams(vmem_limit_bytes=VMEM_LIMIT),
-        cost_estimate=pl.CostEstimate(
-            flops=slots * 2 * total * width * LANES, bytes_accessed=12_000_000, transcendentals=0
-        ),
-        name="latent_terms",
-    )(place, errors, heads, *after)
 
 
 def join_kernel(norm, *refs):
     out = refs[-1]
     pairs = refs[:-1]
     slot = 0
-    for kept, came in zip(pairs[0::2], pairs[1::2]):
-        for k in range(kept.shape[0]):
-            out[slot] = (kept[k].astype(F32) + came[k].astype(F32)) * norm
-            slot += 1
+    for i in range(0, len(pairs), 4):
+        for k in range(pairs[i].shape[0]):
+            for kept, came in (pairs[i : i + 2], pairs[i + 2 : i + 4]):
+                out[slot] = (kept[k].astype(F32) + came[k].astype(F32)) * norm
+                slot += 1
 
 
 def join_heads(pairs, norm):
@@ -492,35 +414,21 @@
     tile_of = jnp.asarray(np.arange(rows * tiles * cols)[:, None] % (tiles * cols) // cols, jnp.int32)
     scale3, shift3 = level_scale.reshape(slots, 1, width), level_shift.reshape(slots, 1, width)
     small = (level_counts, tile_dataset, slot_level)
-    heads_full, bias = scaled_heads(gathered, scale3, shift3)
     flip = lambda array, bit: lax.ppermute(array, "lat", [(i, i ^ bit) for i in range(lats)])
     add = lambda a, b: (a.astype(F32) + b.astype(F32)).astype(BF16)
-    count = 2
-    chunks = slots // count
-    kept, sent, errors = {}, {}, None
-
-    def advance(index, stage):
-        if index < 0 or index >= chunks:
-            return []
-        outer = 2 if index % 2 == 0 else 4
-        came = flip(sent[index], (1, outer)[stage])
-        kept[index], sent[index] = add(kept[index][0], came[0]), add(kept[index][1], came[1])
-        return [sent[index]]
-
-    for index in range(chunks):
-        after = advance(index - 3, 1) + advance(index - 2, 0)
-        kept[index], sent[index], errors = slot_chunk(
-            index, count, 2 if index % 2 == 0 else 4, lats, place, small, tile_of, band, scale3, shift3,
-            bias, heads_full, targets, errors, after,
-        )
-    after = advance(chunks - 3, 1) + advance(chunks - 2, 0)
-    terms = back_terms(place, errors, heads_full, count, tiles, cols, after)
-    advance(chunks - 1, 0)
-    advance(chunks - 2, 1)
-    advance(chunks - 1, 1)
-    pairs = [
-        (kept[i], flip(sent[i], 4 if i % 2 == 0 else 2)) for i in range(chunks)
-    ]
+    common = (lats, place, small, tile_of, band, scale3, shift3, gathered, targets)
+    most = slots // 4 + 1
+    keep_a, send_a, so_far = slot_group(0, most, *common, None)
+    keep_b, send_b, terms = slot_group(most, slots // 2 - most, *common, so_far)
+    pairs = []
+    for keep, send in ((keep_a, send_a), (keep_b, send_b)):
+        came = flip(send, 1)
+        bits = (2, 4)
+        kept = [add(keep[k, 0], came[k, 0]) for k in range(2)]
+        sent = [flip(add(keep[k, 1], came[k, 1]), bits[k]) for k in range(2)]
+        for k in range(2):
+            last = flip(add(kept[k][1], sent[k][1]), bits[1 - k])
+            pairs.append((add(kept[k][0], sent[k][0]), last))
     total = terms[0].astype(F32)
     for s in range(1, tiles):
         came = lax.ppermute(terms[s], "var", [(i, (i + s) % tiles) for i in range(tiles)])

time: 179 us -> 147 us (0.82)
  Pallas kernels: 56.7 us -> 39.2 us
  starting transfers between devices: 39.4 us -> 32.9 us
  waiting for transfers between devices: 55.6 us -> 50.6 us
  local copies, waits for them, and re-layouts: 9.45 us -> 7.21 us
    pallas_call x7 -> x2, Pallas kernels: 43.8 us -> 26.3 us  [slot_group(): pl.pallas_call(functools.partial(slot_kernel, 2 * pair, lats, tiles, fina...]
    ppermute x3, waiting for transfers between devices: 21.3 us -> 7.39 us  [fast_local(): lax.ppermute(terms[s], 'var', [(i, (i + s) % tiles) for i in range(tiles)])]
    ppermute x3, waiting for transfers between devices: 18.6 us -> 24.7 us  [fast_local(): lax.ppermute(mine, 'var', [(i, (i + s) % tiles) for i in range(tiles)])]
    ppermute x15 -> x10, starting transfers between devices: 15.1 us -> 9.42 us  [fast_local(): lax.ppermute(array, 'lat', [(i, i ^ bit) for i in range(lats)])]
    ppermute x1, waiting for transfers between devices: 5.47 us -> 0.01 us  [fast_local(): below_left = lax.ppermute(high[:, cols - HC:], ('lat', 'var'), both(down))]
    ppermute x1, waiting for transfers between devices: 0.01 us -> 4.77 us  [fast_local(): left = lax.ppermute(patches[:, cols - HC:], 'var', right)]
    ppermute x15 -> x10, waiting for transfers between devices: 9.18 us -> 13 us  [fast_local(): lax.ppermute(array, 'lat', [(i, i ^ bit) for i in range(lats)])]
    unnamed x24 -> x22, local copies, waits for them, and re-layouts: 6.55 us -> 4.31 us
  transfers between devices with their start and end apart: 27 -> 22, of which waited for: 11 -> 8; matrix products, arithmetic and copies ran while one was open for 3% -> 4% of each run, Pallas kernels for 23% -> 15%
where the time goes in v3:
time: 147 us
  waiting for transfers between devices  50.6 us (34%)
  Pallas kernels  39.2 us (27%)
  starting transfers between devices  32.9 us (22%)
  between operations  14.2 us (10%)
  local copies, waits for them, and re-layouts  7.21 us (5%)
  other arithmetic  2.39 us (2%)
    pallas_call x2, Pallas kernels, slot_group(): pl.pallas_call(functools.partial(slot_kernel, 2 * pair, lats, tiles, fina...  26.3 us
    ppermute x3, waiting for transfers between devices, fast_local(): lax.ppermute(mine, 'var', [(i, (i + s) % tiles) for i in range(tiles)])  24.7 us
    ppermute x10, waiting for transfers between devices, fast_local(): lax.ppermute(array, 'lat', [(i, i ^ bit) for i in range(lats)])  13 us
    ppermute x10, starting transfers between devices, fast_local(): lax.ppermute(array, 'lat', [(i, i ^ bit) for i in range(lats)])  9.42 us
    pallas_call x1, Pallas kernels, attention(): pl.pallas_call(functools.partial(attention_kernel, bands), out_shape=jax....  8.92 us
    ppermute x3, waiting for transfers between devices, fast_local(): lax.ppermute(terms[s], 'var', [(i, (i + s) % tiles) for i in range(tiles)])  7.39 us
    ppermute x1, starting transfers between devices, fast_local(): above_left = lax.ppermute(low[:, cols - HC:], ('lat', 'var'), both(up))  6.84 us
    ppermute x3, starting transfers between devices, fast_local(): lax.ppermute(terms[s], 'var', [(i, (i + s) % tiles) for i in range(tiles)])  6.37 us
  transfers between devices with their start and end apart: 22, of which 8 were waited for; matrix products, arithmetic and copies ran while one was open for 4% of the time, Pallas kernels for 15%

profile of v3, /device:TPU:0, one launch (start us, length us, event | category | flops | bytes accessed | tf_op | source)
XLA Modules:
  0.0 146.6 jit_solution(11577010184494848360)
XLA Ops:
  7.2 0.7 all-gather.3.cloned.1.call-update
  7.9 1.0 fusion.24
  8.9 1.3 collective-permute-start.3
  10.2 3.0 %collective-permute-start.1 = (bf16[3,24,1024]{2,1,0:T(8,128)(2,1)S(1)}, bf16[3,24,1024]{2,1,0:T(8,128)(2,1)S(1)}, u32[]{:S(2)}, u32[]{:S(2)}) collective-permute-start(bf16[3,24,1024]{2,1,0:T(8,128)(2,1)S(1)} %get-tuple-element.41), channel_id=1, source_target_pairs={{0,4},{4,8},{8,12},{12,16},{16,20},{20,24},{24,28},{1,5},{5,9},{9,... | collective-permute-start | bytes 442376 | tf_op jit(solution)/shard_map/ppermute | solution.py:401
  13.3 0.9 fusion.23
  14.1 1.3 collective-permute-start.4
  15.4 6.8 %collective-permute-start.2 = (bf16[3,6,1024]{2,1,0:T(8,128)(2,1)S(1)}, bf16[3,6,1024]{2,1,0:T(8,128)(2,1)S(1)}, u32[]{:S(2)}, u32[]{:S(2)}) collective-permute-start(bf16[3,6,1024]{2,1,0:T(8,128)(2,1)S(1)} %get-tuple-element.39), channel_id=1, source_target_pairs={{0,5},{1,6},{2,7},{3,4},{4,9},{5,10},{6,11},{7,8},{8,13},{9,14},{1... | collective-permute-start | bytes 110600 | tf_op jit(solution)/shard_map/ppermute | solution.py:404
  22.3 0.9 slice.133
  23.2 1.6 %collective-permute-start = (bf16[6,6,1024]{2,1,0:T(8,128)(2,1)S(1)}, bf16[6,6,1024]{2,1,0:T(8,128)(2,1)S(1)}, u32[]{:S(2)}, u32[]{:S(2)}) collective-permute-start(bf16[6,6,1024]{2,1,0:T(8,128)(2,1)S(1)} %slice.133), channel_id=1, source_target_pairs={{0,1},{1,2},{2,3},{3,0},{4,5},{5,6},{6,7},{7,4},{8,9},{9,10},{10,1... | collective-permute-start | bytes 221192 | tf_op jit(solution)/shard_map/ppermute | solution.py:403
  24.9 4.8 %collective-permute-done.left = bf16[6,6,1024]{2,1,0:T(8,128)(2,1)S(1)} collective-permute-done((bf16[6,6,1024]{2,1,0:T(8,128)(2,1)S(1)}, bf16[6,6,1024]{2,1,0:T(8,128)(2,1)S(1)}, u32[]{:S(2)}, u32[]{:S(2)}) %collective-permute-start) | collective-permute-done | bytes 73760 | tf_op jit(solution)/shard_map/ppermute | solution.py:403
  29.7 1.0 copy-done
  30.6 1.6 %copy-done.1 = bf16[1024,1024]{1,0:T(8,128)(2,1)S(1)} copy-done((bf16[1024,1024]{1,0:T(8,128)(2,1)S(1)}, bf16[1024,1024]{1,0:T(8,128)(2,1)}, u32[]{:S(2)}) %copy-start.1) | copy-done | bytes 2097176
  32.2 0.7 copy-done.2
  32.9 1.0 copy-done.7
  34.0 8.9 %window_attention.1.refs_0_ = bf16[144,1024]{1,0:T(8,128)(2,1)S(1)} custom-call(s32[2]{0:T(128)S(1)} %pad_add_fusion.place, bf16[6,6,1024]{2,1,0:T(8,128)(2,1)S(1)} %collective-permute-done.left, bf16[3,24,1024]{2,1,0:T(8,128)(2,1)S(1)} %collective-permute-done.1.above, bf16[3,6,1024]{2,1,0:T(8,128)(2,1)S(1)} %collective-permute-done.2.above_left, ...), custom_call_target="tpu_custom_call" | custom-call | flops 6000000000 | bytes 12000000 | tf_op jit(solution)/shard_map/window_attention/pallas_call | solution.py:178
  42.9 0.5 collective-permute-start.7
  43.5 0.8 collective-permute-start.6
  44.2 1.7 %collective-permute-start.5 = (bf16[144,1024]{1,0:T(8,128)(2,1)S(1)}, bf16[144,1024]{1,0:T(8,128)(2,1)S(1)}, u32[]{:S(2)}, u32[]{:S(2)}) collective-permute-start(bf16[144,1024]{1,0:T(8,128)(2,1)S(1)} %window_attention.1.refs_0_), channel_id=1, source_target_pairs={{0,1},{1,2},{2,3},{3,0},{4,5},{5,6},{6,7},{7,4},{8,9},{9,10},{10,1... | collective-permute-start | bytes 884744 | tf_op jit(solution)/shard_map/ppermute | solution.py:411
  46.0 7.6 %collective-permute-done.7.refs_3_ = bf16[144,1024]{1,0:T(8,128)(2,1)S(1)} collective-permute-done((bf16[144,1024]{1,0:T(8,128)(2,1)S(1)}, bf16[144,1024]{1,0:T(8,128)(2,1)S(1)}, u32[]{:S(2)}, u32[]{:S(2)}) %collective-permute-start.7) | collective-permute-done | bytes 294944 | tf_op jit(solution)/shard_map/ppermute | solution.py:411
  53.6 17.2 %collective-permute-done.6.refs_2_ = bf16[144,1024]{1,0:T(8,128)(2,1)S(1)} collective-permute-done((bf16[144,1024]{1,0:T(8,128)(2,1)S(1)}, bf16[144,1024]{1,0:T(8,128)(2,1)S(1)}, u32[]{:S(2)}, u32[]{:S(2)}) %collective-permute-start.6) | collective-permute-done | bytes 294944 | tf_op jit(solution)/shard_map/ppermute | solution.py:411
  70.8 2.6 %band_latents.1 = (bf16[576,1024]{1,0:T(8,128)(2,1)S(1)}, bf16[6,24,1024]{2,1,0:T(8,128)(2,1)}) custom-call(s32[2]{0:T(128)S(1)} %pad_add_fusion.place, bf16[576,576]{1,0:T(8,128)(2,1)S(1)} %copy-done.6, bf16[144,1024]{1,0:T(8,128)(2,1)S(1)} %window_attention.1.refs_0_, bf16[144,1024]{1,0:T(8,128)(2,1)S(1)} %collective-permute-done.5.refs_1_, ...), custom_call_target="tpu_custom_call" | custom-call | flops 679477248 | bytes 4000000 | tf_op jit(solution)/shard_map/band_latents/pallas_call | solution.py:238
  73.4 15.5 %slot_group.2 = (bf16[2,2,2,3,320,128]{5,4,3,2,1,0:T(8,128)(2,1)S(1)}, bf16[2,2,2,3,320,128]{5,4,3,2,1,0:T(8,128)(2,1)S(1)}, f32[576,1024]{1,0:T(8,128)}) custom-call(s32[2]{0:T(128)S(1)} %pad_add_fusion.place, s32[4]{0:T(128)S(1)} %copy-done.3, s32[1,4]{1,0:T(1,128)S(1)} %copy-done.4, s32[10]{0:T(128)S(1)} %copy-done.5, s32[576,1]{1,0:T(8,128)S(1)} %copy-done.8, ...), custom_call_target="tpu_custom_call" | custom-call | flops 6794772480 | bytes 15000000 | tf_op jit(solution)/shard_map/slot_group/pallas_call | solution.py:343
  88.9 0.1 collective-permute-start.11
  89.0 10.8 %slot_group.3 = (bf16[2,2,2,2,320,128]{5,4,3,2,1,0:T(8,128)(2,1)S(1)}, bf16[2,2,2,2,320,128]{5,4,3,2,1,0:T(8,128)(2,1)S(1)}, bf16[4,6,24,1024]{3,2,1,0:T(8,128)(2,1)S(1)}) custom-call(s32[2]{0:T(128)S(1)} %pad_add_fusion.place, s32[4]{0:T(128)S(1)} %copy-done.3, s32[1,4]{1,0:T(1,128)S(1)} %copy-done.4, s32[10]{0:T(128)S(1)} %copy-done.5, ...), custom_call_target="tpu_custom_call" | custom-call | flops 4529848320 | bytes 10000000 | tf_op jit(solution)/shard_map/slot_group/pallas_call | solution.py:343
  99.8 0.5 collective-permute-start.16
  100.3 2.7 %collective-permute-done.16 = bf16[2,2,2,2,320,128]{5,4,3,2,1,0:T(8,128)(2,1)S(1)} collective-permute-done((bf16[2,2,2,2,320,128]{5,4,3,2,1,0:T(8,128)(2,1)S(1)}, bf16[2,2,2,2,320,128]{5,4,3,2,1,0:T(8,128)(2,1)S(1)}, u32[]{:S(2)}, u32[]{:S(2)}) %collective-permute-start.16) | collective-permute-done | bytes 1310752 | tf_op jit(solution)/shard_map/ppermute | solution.py:417
  102.9 0.3 add_convert_fusion.5
  103.3 3.1 %collective-permute-start.19 = (bf16[2,2,320,128]{3,2,1,0:T(8,128)(2,1)S(1)}, bf16[2,2,320,128]{3,2,1,0:T(8,128)(2,1)S(1)}, u32[]{:S(2)}, u32[]{:S(2)}) collective-permute-start(bf16[2,2,320,128]{3,2,1,0:T(8,128)(2,1)S(1)} %get-tuple-element.24), channel_id=1, source_target_pairs={{0,16},{4,20},{8,24},{12,28},{16,0},{20,4},{24,8},{28,12},{1,17},{... | collective-permute-start | bytes 983048 | tf_op jit(solution)/shard_map/ppermute | solution.py:417
  106.4 0.6 add_convert_fusion.1
  107.0 1.3 collective-permute-start.14
  108.4 0.7 collective-permute-start.8
  109.1 3.2 %collective-permute-start.10 = (bf16[6,24,1024]{2,1,0:T(8,128)(2,1)S(1)}, bf16[6,24,1024]{2,1,0:T(8,128)(2,1)S(1)}, u32[]{:S(2)}, u32[]{:S(2)}) collective-permute-start(bf16[6,24,1024]{2,1,0:T(8,128)(2,1)S(1)} %get-tuple-element.28), channel_id=1, source_target_pairs={{0,3},{1,0},{2,1},{3,2},{4,7},{5,4},{6,5},{7,6},{8,11},{9,8},{10,9... | collective-permute-start | bytes 884744 | tf_op jit(solution)/shard_map/ppermute | solution.py:434
  112.3 2.6 %collective-permute-done.19 = bf16[2,2,320,128]{3,2,1,0:T(8,128)(2,1)S(1)} collective-permute-done((bf16[2,2,320,128]{3,2,1,0:T(8,128)(2,1)S(1)}, bf16[2,2,320,128]{3,2,1,0:T(8,128)(2,1)S(1)}, u32[]{:S(2)}, u32[]{:S(2)}) %collective-permute-start.19) | collective-permute-done | bytes 327712 | tf_op jit(solution)/shard_map/ppermute | solution.py:417
  114.9 1.3 collective-permute-start.12
  116.2 0.1 fusion.22
  116.3 2.5 %collective-permute-start.9 = (bf16[6,24,1024]{2,1,0:T(8,128)(2,1)S(1)}, bf16[6,24,1024]{2,1,0:T(8,128)(2,1)S(1)}, u32[]{:S(2)}, u32[]{:S(2)}) collective-permute-start(bf16[6,24,1024]{2,1,0:T(8,128)(2,1)S(1)} %get-tuple-element.29), channel_id=1, source_target_pairs={{0,2},{1,3},{2,0},{3,1},{4,6},{5,7},{6,4},{7,5},{8,10},{9,11},{10,... | collective-permute-start | bytes 884744 | tf_op jit(solution)/shard_map/ppermute | solution.py:434
  118.8 0.1 fusion.20
  118.9 6.3 %collective-permute-done.14 = bf16[2,3,320,128]{3,2,1,0:T(8,128)(2,1)S(1)} collective-permute-done((bf16[2,3,320,128]{3,2,1,0:T(8,128)(2,1)S(1)}, bf16[2,3,320,128]{3,2,1,0:T(8,128)(2,1)S(1)}, u32[]{:S(2)}, u32[]{:S(2)}) %collective-permute-start.14) | collective-permute-done | bytes 491552 | tf_op jit(solution)/shard_map/ppermute | solution.py:417
  125.1 0.8 collective-permute-start.20
  125.9 0.1 fusion.18
  126.0 1.5 %collective-permute-done.12 = bf16[2,3,320,128]{3,2,1,0:T(8,128)(2,1)S(1)} collective-permute-done((bf16[2,3,320,128]{3,2,1,0:T(8,128)(2,1)S(1)}, bf16[2,3,320,128]{3,2,1,0:T(8,128)(2,1)S(1)}, u32[]{:S(2)}, u32[]{:S(2)}) %collective-permute-start.12) | collective-permute-done | bytes 491552 | tf_op jit(solution)/shard_map/ppermute | solution.py:417
  127.5 1.5 %collective-permute-start.18 = (bf16[2,320,128]{2,1,0:T(8,128)(2,1)S(1)}, bf16[2,320,128]{2,1,0:T(8,128)(2,1)S(1)}, u32[]{:S(2)}, u32[]{:S(2)}) collective-permute-start(bf16[2,320,128]{2,1,0:T(8,128)(2,1)S(1)} %get-tuple-element.36), channel_id=1, source_target_pairs={{0,16},{4,20},{8,24},{12,28},{16,0},{20,4},{24,8},{28,12},{1,17},{... | collective-permute-start | bytes 491528 | tf_op jit(solution)/shard_map/ppermute | solution.py:417
  129.0 0.1 fusion.16
  129.2 0.3 collective-permute-start.15
  129.5 0.5 collective-permute-start.13
  130.1 7.4 %collective-permute-done.9 = bf16[6,24,1024]{2,1,0:T(8,128)(2,1)S(1)} collective-permute-done((bf16[6,24,1024]{2,1,0:T(8,128)(2,1)S(1)}, bf16[6,24,1024]{2,1,0:T(8,128)(2,1)S(1)}, u32[]{:S(2)}, u32[]{:S(2)}) %collective-permute-start.9) | collective-permute-done | bytes 294944 | tf_op jit(solution)/shard_map/ppermute | solution.py:434
  137.4 0.9 fusion.2
  138.4 1.4 join_heads.1
  (38 shorter events, 0.3 us)
Async XLA Ops:
  7.2 66.2 %all-gather.3.cloned.1.call-start = ((), (), s32[]{:S(2)}) async-start(), calls=%async_computation | async-start | bytes 7372800 | tf_op jit(solution)/shard_map/all_gather | solution.py:394
  8.9 20.8 %collective-permute-start.3 = (bf16[3,24,1024]{2,1,0:T(8,128)(2,1)S(1)}, bf16[3,24,1024]{2,1,0:T(8,128)(2,1)S(1)}, u32[]{:S(2)}, u32[]{:S(2)}) collective-permute-start(bf16[3,24,1024]{2,1,0:T(8,128)(2,1)S(1)} %get-tuple-element.40), channel_id=1, source_target_pairs={{4,0},{8,4},{12,8},{16,12},{20,16},{24,20},{28,24},{5,1},{9,5},{13... | collective-permute-start | bytes 442376 | tf_op jit(solution)/shard_map/ppermute | solution.py:402
  10.2 19.5 %collective-permute-start.1 = (bf16[3,24,1024]{2,1,0:T(8,128)(2,1)S(1)}, bf16[3,24,1024]{2,1,0:T(8,128)(2,1)S(1)}, u32[]{:S(2)}, u32[]{:S(2)}) collective-permute-start(bf16[3,24,1024]{2,1,0:T(8,128)(2,1)S(1)} %get-tuple-element.41), channel_id=1, source_target_pairs={{0,4},{4,8},{8,12},{12,16},{16,20},{20,24},{24,28},{1,5},{5,9},{9,... | collective-permute-start | bytes 442376 | tf_op jit(solution)/shard_map/ppermute | solution.py:401
  14.1 10.8 %collective-permute-start.4 = (bf16[3,6,1024]{2,1,0:T(8,128)(2,1)S(1)}, bf16[3,6,1024]{2,1,0:T(8,128)(2,1)S(1)}, u32[]{:S(2)}, u32[]{:S(2)}) collective-permute-start(bf16[3,6,1024]{2,1,0:T(8,128)(2,1)S(1)} %get-tuple-element.38), channel_id=1, source_target_pairs={{4,1},{5,2},{6,3},{7,0},{8,5},{9,6},{10,7},{11,4},{12,9},{13,10},{... | collective-permute-start | bytes 110600 | tf_op jit(solution)/shard_map/ppermute | solution.py:405
  15.4 9.5 %collective-permute-start.2 = (bf16[3,6,1024]{2,1,0:T(8,128)(2,1)S(1)}, bf16[3,6,1024]{2,1,0:T(8,128)(2,1)S(1)}, u32[]{:S(2)}, u32[]{:S(2)}) collective-permute-start(bf16[3,6,1024]{2,1,0:T(8,128)(2,1)S(1)} %get-tuple-element.39), channel_id=1, source_target_pairs={{0,5},{1,6},{2,7},{3,4},{4,9},{5,10},{6,11},{7,8},{8,13},{9,14},{1... | collective-permute-start | bytes 110600 | tf_op jit(solution)/shard_map/ppermute | solution.py:404
  23.2 6.5 %collective-permute-start = (bf16[6,6,1024]{2,1,0:T(8,128)(2,1)S(1)}, bf16[6,6,1024]{2,1,0:T(8,128)(2,1)S(1)}, u32[]{:S(2)}, u32[]{:S(2)}) collective-permute-start(bf16[6,6,1024]{2,1,0:T(8,128)(2,1)S(1)} %slice.133), channel_id=1, source_target_pairs={{0,1},{1,2},{2,3},{3,0},{4,5},{5,6},{6,7},{7,4},{8,9},{9,10},{10,1... | collective-permute-start | bytes 221192 | tf_op jit(solution)/shard_map/ppermute | solution.py:403
  29.7 1.0 copy-start
  30.6 1.6 %copy-start.1 = (bf16[1024,1024]{1,0:T(8,128)(2,1)S(1)}, bf16[1024,1024]{1,0:T(8,128)(2,1)}, u32[]{:S(2)}) copy-start(bf16[1024,1024]{1,0:T(8,128)(2,1)} %out_hbm.1) | copy-start | bytes 6291460
  32.2 0.7 copy-start.2
  32.9 1.0 copy-start.7
  34.0 12.0 %copy-start.9 = (f32[10,1024]{1,0:T(8,128)S(1)}, f32[10,1024]{1,0:T(8,128)}, u32[]{:S(2)}) copy-start(f32[10,1024]{1,0:T(8,128)} %param.18) | copy-start | bytes 122884
  34.0 12.0 %copy-start.10 = (f32[10,1024]{1,0:T(8,128)S(1)}, f32[10,1024]{1,0:T(8,128)}, u32[]{:S(2)}) copy-start(f32[10,1024]{1,0:T(8,128)} %param.19) | copy-start | bytes 122884
  34.0 36.8 %copy-start.6 = (bf16[576,576]{1,0:T(8,128)(2,1)S(1)}, bf16[576,576]{1,0:T(8,128)(2,1)}, u32[]{:S(2)}) copy-start(bf16[576,576]{1,0:T(8,128)(2,1)} %constant.16.clone.chosen) | copy-start | bytes 1990660
  42.9 30.5 %copy-start.3 = (s32[4]{0:T(128)S(1)}, s32[4]{0:T(128)}, u32[]{:S(2)}) copy-start(s32[4]{0:T(128)} %counts.3) | copy-start | bytes 52
  42.9 30.5 %copy-start.4 = (s32[1,4]{1,0:T(1,128)S(1)}, s32[1,4]{1,0:T(1,128)}, u32[]{:S(2)}) copy-start(s32[1,4]{1,0:T(1,128)} %datasets.3) | copy-start | bytes 52
  42.9 30.5 %copy-start.5 = (s32[10]{0:T(128)S(1)}, s32[10]{0:T(128)}, u32[]{:S(2)}) copy-start(s32[10]{0:T(128)} %levels.3) | copy-start | bytes 124
  42.9 30.4 %copy-start.8 = (s32[576,1]{1,0:T(8,128)S(1)}, s32[576,1]{1,0:T(8,128)}, u32[]{:S(2)}) copy-start(s32[576,1]{1,0:T(8,128)} %constant.17.clone.tile_of) | copy-start | bytes 6916
  42.9 10.7 %collective-permute-start.7 = (bf16[144,1024]{1,0:T(8,128)(2,1)S(1)}, bf16[144,1024]{1,0:T(8,128)(2,1)S(1)}, u32[]{:S(2)}, u32[]{:S(2)}) collective-permute-start(bf16[144,1024]{1,0:T(8,128)(2,1)S(1)} %window_attention.1.refs_0_), channel_id=1, source_target_pairs={{0,3},{1,0},{2,1},{3,2},{4,7},{5,4},{6,5},{7,6},{8,11},{9,8},{10,9... | collective-permute-start | bytes 884744 | tf_op jit(solution)/shard_map/ppermute | solution.py:411
  43.5 27.3 %collective-permute-start.6 = (bf16[144,1024]{1,0:T(8,128)(2,1)S(1)}, bf16[144,1024]{1,0:T(8,128)(2,1)S(1)}, u32[]{:S(2)}, u32[]{:S(2)}) collective-permute-start(bf16[144,1024]{1,0:T(8,128)(2,1)S(1)} %window_attention.1.refs_0_), channel_id=1, source_target_pairs={{0,2},{1,3},{2,0},{3,1},{4,6},{5,7},{6,4},{7,5},{8,10},{9,11},{10,... | collective-permute-start | bytes 884744 | tf_op jit(solution)/shard_map/ppermute | solution.py:411
  44.2 26.5 %collective-permute-start.5 = (bf16[144,1024]{1,0:T(8,128)(2,1)S(1)}, bf16[144,1024]{1,0:T(8,128)(2,1)S(1)}, u32[]{:S(2)}, u32[]{:S(2)}) collective-permute-start(bf16[144,1024]{1,0:T(8,128)(2,1)S(1)} %window_attention.1.refs_0_), channel_id=1, source_target_pairs={{0,1},{1,2},{2,3},{3,0},{4,5},{5,6},{6,7},{7,4},{8,9},{9,10},{10,1... | collective-permute-start | bytes 884744 | tf_op jit(solution)/shard_map/ppermute | solution.py:411
  88.9 17.5 %collective-permute-start.11 = (bf16[2,2,2,3,320,128]{5,4,3,2,1,0:T(8,128)(2,1)S(1)}, bf16[2,2,2,3,320,128]{5,4,3,2,1,0:T(8,128)(2,1)S(1)}, u32[]{:S(2)}, u32[]{:S(2)}) collective-permute-start(bf16[2,2,2,3,320,128]{5,4,3,2,1,0:T(8,128)(2,1)S(1)} %get-tuple-element.16), channel_id=1, source_target_pairs={{0,4},{4,0},{8,12},{12,8},{16,20},{20,16},{24,28},{28,24},{1,5},{5... | collective-permute-start | bytes 5898248 | tf_op jit(solution)/shard_map/ppermute | solution.py:417
  99.8 3.1 %collective-permute-start.16 = (bf16[2,2,2,2,320,128]{5,4,3,2,1,0:T(8,128)(2,1)S(1)}, bf16[2,2,2,2,320,128]{5,4,3,2,1,0:T(8,128)(2,1)S(1)}, u32[]{:S(2)}, u32[]{:S(2)}) collective-permute-start(bf16[2,2,2,2,320,128]{5,4,3,2,1,0:T(8,128)(2,1)S(1)} %get-tuple-element.18), channel_id=1, source_target_pairs={{0,4},{4,0},{8,12},{12,8},{16,20},{20,16},{24,28},{28,24},{1,5},{5... | collective-permute-start | bytes 3932168 | tf_op jit(solution)/shard_map/ppermute | solution.py:417
  103.3 11.6 %collective-permute-start.19 = (bf16[2,2,320,128]{3,2,1,0:T(8,128)(2,1)S(1)}, bf16[2,2,320,128]{3,2,1,0:T(8,128)(2,1)S(1)}, u32[]{:S(2)}, u32[]{:S(2)}) collective-permute-start(bf16[2,2,320,128]{3,2,1,0:T(8,128)(2,1)S(1)} %get-tuple-element.24), channel_id=1, source_target_pairs={{0,16},{4,20},{8,24},{12,28},{16,0},{20,4},{24,8},{28,12},{1,17},{... | collective-permute-start | bytes 983048 | tf_op jit(solution)/shard_map/ppermute | solution.py:417
  106.4 9.9 %collective-permute-start.17 = (bf16[2,2,320,128]{3,2,1,0:T(8,128)(2,1)S(1)}, bf16[2,2,320,128]{3,2,1,0:T(8,128)(2,1)S(1)}, u32[]{:S(2)}, u32[]{:S(2)}) collective-permute-start(bf16[2,2,320,128]{3,2,1,0:T(8,128)(2,1)S(1)} %get-tuple-element.25), channel_id=1, source_target_pairs={{0,8},{4,12},{8,0},{12,4},{16,24},{20,28},{24,16},{28,20},{1,9},{5... | collective-permute-start | bytes 983048 | tf_op jit(solution)/shard_map/ppermute | solution.py:417
  107.0 18.1 %collective-permute-start.14 = (bf16[2,3,320,128]{3,2,1,0:T(8,128)(2,1)S(1)}, bf16[2,3,320,128]{3,2,1,0:T(8,128)(2,1)S(1)}, u32[]{:S(2)}, u32[]{:S(2)}) collective-permute-start(bf16[2,3,320,128]{3,2,1,0:T(8,128)(2,1)S(1)} %get-tuple-element.20), channel_id=1, source_target_pairs={{0,16},{4,20},{8,24},{12,28},{16,0},{20,4},{24,8},{28,12},{1,17},{... | collective-permute-start | bytes 1474568 | tf_op jit(solution)/shard_map/ppermute | solution.py:417
  108.4 20.7 %collective-permute-start.8 = (bf16[6,24,1024]{2,1,0:T(8,128)(2,1)S(1)}, bf16[6,24,1024]{2,1,0:T(8,128)(2,1)S(1)}, u32[]{:S(2)}, u32[]{:S(2)}) collective-permute-start(bf16[6,24,1024]{2,1,0:T(8,128)(2,1)S(1)} %get-tuple-element.27), channel_id=1, source_target_pairs={{0,1},{1,2},{2,3},{3,0},{4,5},{5,6},{6,7},{7,4},{8,9},{9,10},{10,1... | collective-permute-start | bytes 884744 | tf_op jit(solution)/shard_map/ppermute | solution.py:434
  109.1 20.4 %collective-permute-start.10 = (bf16[6,24,1024]{2,1,0:T(8,128)(2,1)S(1)}, bf16[6,24,1024]{2,1,0:T(8,128)(2,1)S(1)}, u32[]{:S(2)}, u32[]{:S(2)}) collective-permute-start(bf16[6,24,1024]{2,1,0:T(8,128)(2,1)S(1)} %get-tuple-element.28), channel_id=1, source_target_pairs={{0,3},{1,0},{2,1},{3,2},{4,7},{5,4},{6,5},{7,6},{8,11},{9,8},{10,9... | collective-permute-start | bytes 884744 | tf_op jit(solution)/shard_map/ppermute | solution.py:434
  114.9 12.6 %collective-permute-start.12 = (bf16[2,3,320,128]{3,2,1,0:T(8,128)(2,1)S(1)}, bf16[2,3,320,128]{3,2,1,0:T(8,128)(2,1)S(1)}, u32[]{:S(2)}, u32[]{:S(2)}) collective-permute-start(bf16[2,3,320,128]{3,2,1,0:T(8,128)(2,1)S(1)} %get-tuple-element.21), channel_id=1, source_target_pairs={{0,8},{4,12},{8,0},{12,4},{16,24},{20,28},{24,16},{28,20},{1,9},{5... | collective-permute-start | bytes 1474568 | tf_op jit(solution)/shard_map/ppermute | solution.py:417
  116.3 21.2 %collective-permute-start.9 = (bf16[6,24,1024]{2,1,0:T(8,128)(2,1)S(1)}, bf16[6,24,1024]{2,1,0:T(8,128)(2,1)S(1)}, u32[]{:S(2)}, u32[]{:S(2)}) collective-permute-start(bf16[6,24,1024]{2,1,0:T(8,128)(2,1)S(1)} %get-tuple-element.29), channel_id=1, source_target_pairs={{0,2},{1,3},{2,0},{3,1},{4,6},{5,7},{6,4},{7,5},{8,10},{9,11},{10,... | collective-permute-start | bytes 884744 | tf_op jit(solution)/shard_map/ppermute | solution.py:434
  125.1 13.2 %collective-permute-start.20 = (bf16[2,320,128]{2,1,0:T(8,128)(2,1)S(1)}, bf16[2,320,128]{2,1,0:T(8,128)(2,1)S(1)}, u32[]{:S(2)}, u32[]{:S(2)}) collective-permute-start(bf16[2,320,128]{2,1,0:T(8,128)(2,1)S(1)} %get-tuple-element.34), channel_id=1, source_target_pairs={{0,8},{4,12},{8,0},{12,4},{16,24},{20,28},{24,16},{28,20},{1,9},{5... | collective-permute-start | bytes 491528 | tf_op jit(solution)/shard_map/ppermute | solution.py:417
  127.5 10.8 %collective-permute-start.18 = (bf16[2,320,128]{2,1,0:T(8,128)(2,1)S(1)}, bf16[2,320,128]{2,1,0:T(8,128)(2,1)S(1)}, u32[]{:S(2)}, u32[]{:S(2)}) collective-permute-start(bf16[2,320,128]{2,1,0:T(8,128)(2,1)S(1)} %get-tuple-element.36), channel_id=1, source_target_pairs={{0,16},{4,20},{8,24},{12,28},{16,0},{20,4},{24,8},{28,12},{1,17},{... | collective-permute-start | bytes 491528 | tf_op jit(solution)/shard_map/ppermute | solution.py:417
  129.2 9.2 %collective-permute-start.15 = (bf16[3,320,128]{2,1,0:T(8,128)(2,1)S(1)}, bf16[3,320,128]{2,1,0:T(8,128)(2,1)S(1)}, u32[]{:S(2)}, u32[]{:S(2)}) collective-permute-start(bf16[3,320,128]{2,1,0:T(8,128)(2,1)S(1)} %get-tuple-element.30), channel_id=1, source_target_pairs={{0,8},{4,12},{8,0},{12,4},{16,24},{20,28},{24,16},{28,20},{1,9},{5... | collective-permute-start | bytes 737288 | tf_op jit(solution)/shard_map/ppermute | solution.py:417
  129.5 8.8 %collective-permute-start.13 = (bf16[3,320,128]{2,1,0:T(8,128)(2,1)S(1)}, bf16[3,320,128]{2,1,0:T(8,128)(2,1)S(1)}, u32[]{:S(2)}, u32[]{:S(2)}) collective-permute-start(bf16[3,320,128]{2,1,0:T(8,128)(2,1)S(1)} %get-tuple-element.32), channel_id=1, source_target_pairs={{0,16},{4,20},{8,24},{12,28},{16,0},{20,4},{24,8},{28,12},{1,17},{... | collective-permute-start | bytes 737288 | tf_op jit(solution)/shard_map/ppermute | solution.py:417
Sparse Core Ops, SparseCore 0:
  9.9 49.9 all-gather.2

commit v4 on v3

--- a/solution.py
+++ b/solution.py
@@ -190,7 +190,7 @@
             pltpu.VMEM(proj_out.shape, BF16),
             pltpu.SemaphoreType.DMA((4,)),
         ],
-        compiler_params=pltpu.CompilerParams(vmem_limit_bytes=VMEM_LIMIT),
+        compiler_params=pltpu.CompilerParams(vmem_limit_bytes=53 * 1024 * 1024),
         cost_estimate=pl.CostEstimate(
             flops=6_000_000_000, bytes_accessed=12_000_000, transcendentals=400_000
         ),
@@ -252,43 +252,38 @@
     )(place, jnp.asarray(band_map(tiles, cols), BF16), *pieces)
 
 
-def slot_kernel(first_slot, lats, tiles, final, place, counts, datasets, levels, tile_of, band, scale, shift, gathered, target, *refs):
-    keep, send, out = refs[-8:-5] if final else refs[-7:-4]
-    rows, errs, turned = refs[-4:-2], refs[-2], refs[-1]
-    total = refs[-5] if final else out
-    step = pl.program_id(0)
-    outs = target.shape[-1]
-    places, width = band.shape
-    piece = width // lats
-
-    @pl.when(step == 0)
-    def _():
-        total[...] = refs[0][...] if final else jnp.zeros_like(total)
-
-    tile = tile_of[...]
+def slot_errors(slot, tiles, counts, datasets, levels, tile, rows, weight, target):
+    predicted = lax.dot_general(
+        rows, weight, (((1,), (1,)), ((), ())), preferred_element_type=F32
+    )
+    live = jnp.zeros(tile.shape, F32)
+    for t in range(tiles):
+        alive = levels[slot] < counts[datasets[0, t]]
+        live = live + jnp.where(jnp.logical_and(tile == t, alive), 1.0, 0.0)
+    diff = predicted - target.astype(F32).reshape(predicted.shape)
+    return (diff * live).astype(BF16)
+
+
+def head_halves(k, lats, lat, errors, rows, turned, keep, send):
+    turned[k] = lax.dot_general(
+        errors, rows, (((0,), (0,)), ((), ())), preferred_element_type=F32
+    ).astype(BF16)
+    piece = turned.shape[-1] // lats
+    for q in range(lats):
+        core, x, y = q & 1, (q >> 1) & 1, (q >> 2) & 1
+        outer, inner = (x, y) if k == 0 else (y, x)
+        start = pl.multiple_of(jnp.bitwise_xor(lat, q) * piece, piece)
+        to = send if core else keep
+        to[k, outer, inner, 0] = turned[k, :, pl.ds(start, piece)]
+
+
+def scaled_rows(band, scale, shift, rows):
     for k in range(2):
         rows[k][...] = (band[...].astype(F32) * scale[k] + shift[k]).astype(BF16)
-    for k in range(2):
-        weight = jnp.concatenate([gathered[l, k] for l in range(lats)], axis=1)
-        predicted = lax.dot_general(
-            rows[k][...], weight, (((1,), (1,)), ((), ())), preferred_element_type=F32
-        )
-        live = jnp.zeros(tile.shape, F32)
-        for t in range(tiles):
-            alive = levels[first_slot + 2 * step + k] < counts[datasets[0, t]]
-            live = live + jnp.where(jnp.logical_and(tile == t, alive), 1.0, 0.0)
-        diff = predicted - target[k].astype(F32).reshape(places, outs)
-        errs[k] = (diff * live).astype(BF16)
-    for k in range(2):
-        turned[k] = lax.dot_general(
-            errs[k], rows[k][...], (((0,), (0,)), ((), ())), preferred_element_type=F32
-        ).astype(BF16)
-        for q in range(lats):
-            core, x, y = q & 1, (q >> 1) & 1, (q >> 2) & 1
-            outer, inner = (x, y) if k == 0 else (y, x)
-            start = pl.multiple_of(jnp.bitwise_xor(place[0], q) * piece, piece)
-            to = send if core else keep
-            to[k, outer, inner, 0] = turned[k, :, pl.ds(start, piece)]
+
+
+def add_back(lats, errs, gathered, scale, total):
+    piece = gathered.shape[-1]
     for l in range(0, lats, 2):
         lanes = slice(l * piece, (l + 2) * piece)
         term = 0.0
@@ -297,62 +292,146 @@
             term = term + jnp.dot(errs[k], weight, preferred_element_type=F32) * scale[k][:, lanes]
         total[:, lanes] += term
 
-    if final:
-
-        @pl.when(step == pl.num_programs(0) - 1)
-        def _():
-            cols = out.shape[2]
-            for s in range(tiles):
-                at = lax.rem(place[1] + s, tiles)
-                for r in range(WH):
-                    start = pl.multiple_of(r * tiles * cols + at * cols, 8)
-                    out[s, r] = total[pl.ds(start, cols), :].astype(BF16)
-
-
-def slot_group(pair, pairs, lats, place, small, tile_of, band, scale, shift, gathered, targets, before):
+
+def first_kernel(lats, tiles, place, counts, datasets, levels, tile_of, band, scale, shift, gathered, target,
+                 keep, send, total, rows0, rows1, errs, turned):
+    rows = (rows0, rows1)
+    step = pl.program_id(0)
+
+    @pl.when(step == 0)
+    def _():
+        total[...] = jnp.zeros_like(total)
+
+    tile = tile_of[...]
+    scaled_rows(band, scale, shift, rows)
+    for k in range(2):
+        weight = jnp.concatenate([gathered[l, k] for l in range(lats)], axis=1)
+        errs[k] = slot_errors(
+            2 * step + k, tiles, counts, datasets, levels, tile, rows[k][...], weight, target[k]
+        )
+    for k in range(2):
+        head_halves(k, lats, place[0], errs[k], rows[k][...], turned, keep, send)
+    add_back(lats, errs, gathered, scale, total)
+
+
+def second_kernel(first_slot, lats, tiles, place, counts, datasets, levels, tile_of, band, scale, shift,
+                  gathered, target, before, errs, out, total, rows0, rows1):
+    rows = (rows0, rows1)
+    step = pl.program_id(0)
+
+    @pl.when(step == 0)
+    def _():
+        total[...] = before[...]
+
+    tile = tile_of[...]
+    scaled_rows(band, scale, shift, rows)
+    for k in range(2):
+        weight = jnp.concatenate([gathered[l, k] for l in range(lats)], axis=1)
+        errs[k] = slot_errors(
+            first_slot + 2 * step + k, tiles, counts, datasets, levels, tile, rows[k][...], weight, target[k]
+        )
+    add_back(lats, errs, gathered, scale, total)
+
+    @pl.when(step == pl.num_programs(0) - 1)
+    def _():
+        cols = out.shape[2]
+        for s in range(tiles):
+            for r in range(WH):
+                start = (r * tiles + s) * cols
+                out[s, r] = total[start : start + cols, :].astype(BF16)
+
+
+def heads_kernel(lats, place, band, scale, shift, errs, *refs):
+    keep, send, rows0, rows1, turned = refs[-5:]
+    rows = (rows0, rows1)
+    scaled_rows(band, scale, shift, rows)
+    for k in range(2):
+        head_halves(k, lats, place[0], errs[k], rows[k][...], turned, keep, send)
+
+
+def slot_specs(pair, lats, band, outs):
+    places, width = band.shape
+    piece = width // lats
+    return dict(
+        smem=pl.BlockSpec(memory_space=pltpu.SMEM),
+        tile_of=pl.BlockSpec((places, 1), lambda i: (0, 0)),
+        band=pl.BlockSpec((places, width), lambda i: (0, 0)),
+        level=pl.BlockSpec((2, 1, width), lambda i: (i + pair, 0, 0)),
+        heads=pl.BlockSpec((lats, 2, outs, piece), lambda i: (0, i + pair, 0, 0)),
+        halves=pl.BlockSpec((2, 2, 2, 1, outs, piece), lambda i: (0, 0, 0, i, 0, 0)),
+        errs=pl.BlockSpec((2, places, outs), lambda i: (i, 0, 0)),
+        rows=pltpu.VMEM((places, width), BF16),
+        turned=pltpu.VMEM((2, outs, width), BF16),
+    )
+
+
+def slot_cost(pairs, products, places, width, outs):
+    return pl.CostEstimate(
+        flops=pairs * 4 * products * places * width * outs, bytes_accessed=pairs * 4_000_000, transcendentals=0
+    )
+
+
+def first_slots(pairs, lats, place, small, tile_of, band, scale, shift, gathered, targets):
+    places, width = band.shape
+    outs = targets.shape[-1]
+    sp = slot_specs(0, lats, band, outs)
+    halves = jax.ShapeDtypeStruct((2, 2, 2, pairs, outs, width // lats), BF16)
+    target = pl.BlockSpec((2,) + targets.shape[1:], lambda i: (i, 0, 0, 0))
+    return pl.pallas_call(
+        functools.partial(first_kernel, lats, small[1].shape[1]),
+        grid=(pairs,),
+        out_shape=(halves, halves, jax.ShapeDtypeStruct((places, width), F32)),
+        in_specs=[sp["smem"]] * 4
+        + [sp["tile_of"], sp["band"], sp["level"], sp["level"], sp["heads"], target],
+        out_specs=(sp["halves"], sp["halves"], sp["band"]),
+        scratch_shapes=[sp["rows"], sp["rows"], pltpu.VMEM((2, places, outs), BF16), sp["turned"]],
+        compiler_params=pltpu.CompilerParams(vmem_limit_bytes=VMEM_LIMIT),
+        cost_estimate=slot_cost(pairs, 3, places, width, outs),
+        name="first_slots",
+    )(place, *small, tile_of, band, scale, shift, gathered, targets)
+
+
+def second_slots(pair, pairs, lats, place, small, tile_of, band, scale, shift, gathered, targets, before):
     places, width = band.shape
     outs = targets.shape[-1]
     tiles = small[1].shape[1]
-    piece = width // lats
-    smem = pl.BlockSpec(memory_space=pltpu.SMEM)
-    halves = jax.ShapeDtypeStruct((2, 2, 2, pairs, outs, piece), BF16)
-    half_spec = pl.BlockSpec((2, 2, 2, 1, outs, piece), lambda i: (0, 0, 0, i, 0, 0))
-    in_specs = [
-        smem, smem, smem, smem,
-        pl.BlockSpec((places, 1), lambda i: (0, 0)),
-        pl.BlockSpec((places, width), lambda i: (0, 0)),
-        pl.BlockSpec((2, 1, width), lambda i: (i + pair, 0, 0)),
-        pl.BlockSpec((2, 1, width), lambda i: (i + pair, 0, 0)),
-        pl.BlockSpec((lats, 2, outs, piece), lambda i: (0, i + pair, 0, 0)),
-        pl.BlockSpec((2,) + targets.shape[1:], lambda i: (i + pair, 0, 0, 0)),
-    ]
-    args = [place, *small, tile_of, band, scale, shift, gathered, targets]
-    final = before is not None
-    scratch = [
-        pltpu.VMEM((places, width), BF16),
-        pltpu.VMEM((places, width), BF16),
-        pltpu.VMEM((2, places, outs), BF16),
-        pltpu.VMEM((2, outs, width), BF16),
-    ]
-    sums = jax.ShapeDtypeStruct((places, width), F32)
-    if final:
-        in_specs.append(pl.BlockSpec((places, width), lambda i: (0, 0)))
-        args.append(before)
-        scratch.insert(0, pltpu.VMEM(sums.shape, F32))
-        sums = jax.ShapeDtypeStruct((tiles, WH, places // (WH * tiles), width), BF16)
+    sp = slot_specs(pair, lats, band, outs)
+    target = pl.BlockSpec((2,) + targets.shape[1:], lambda i: (i + pair, 0, 0, 0))
+    terms = (tiles, WH, places // (WH * tiles), width)
     return pl.pallas_call(
-        functools.partial(slot_kernel, 2 * pair, lats, tiles, final),
+        functools.partial(second_kernel, 2 * pair, lats, tiles),
         grid=(pairs,),
-        out_shape=(halves, halves, sums),
-        in_specs=in_specs,
-        out_specs=(half_spec, half_spec, pl.BlockSpec(sums.shape, lambda i: (0,) * len(sums.shape))),
-        scratch_shapes=scratch,
+        out_shape=(
+            jax.ShapeDtypeStruct((2 * pairs, places, outs), BF16),
+            jax.ShapeDtypeStruct(terms, BF16),
+        ),
+        in_specs=[sp["smem"]] * 4
+        + [sp["tile_of"], sp["band"], sp["level"], sp["level"], sp["heads"], target, sp["band"]],
+        out_specs=(sp["errs"], pl.BlockSpec(terms, lambda i: (0, 0, 0, 0))),
+        scratch_shapes=[pltpu.VMEM((places, width), F32), sp["rows"], sp["rows"]],
         compiler_params=pltpu.CompilerParams(vmem_limit_bytes=VMEM_LIMIT),
-        cost_estimate=pl.CostEstimate(
-            flops=pairs * 12 * places * width * outs, bytes_accessed=pairs * 5_000_000, transcendentals=0
-        ),
-        name="slot_group",
-    )(*args)
+        cost_estimate=slot_cost(pairs, 2, places, width, outs),
+        name="second_slots",
+    )(place, *small, tile_of, band, scale, shift, gathered, targets, before)
+
+
+def second_heads(pair, pairs, lats, place, band, scale, shift, errs, after):
+    places, width = band.shape
+    outs = errs.shape[-1]
+    sp = slot_specs(pair, lats, band, outs)
+    halves = jax.ShapeDtypeStruct((2, 2, 2, pairs, outs, width // lats), BF16)
+    return pl.pallas_call(
+        functools.partial(heads_kernel, lats),
+        grid=(pairs,),
+        out_shape=(halves, halves),
+        in_specs=[sp["smem"], sp["band"], sp["level"], sp["level"], sp["errs"]]
+        + [pl.BlockSpec(memory_space=pl.ANY)] * len(after),
+        out_specs=(sp["halves"], sp["halves"]),
+        scratch_shapes=[sp["rows"], sp["rows"], sp["turned"]],
+        compiler_params=pltpu.CompilerParams(vmem_limit_bytes=VMEM_LIMIT),
+        cost_estimate=slot_cost(pairs, 1, places, width, outs),
+        name="second_heads",
+    )(place, band, scale, shift, errs, *after)
 
 
 def join_kernel(norm, *refs):
@@ -418,22 +497,28 @@
     add = lambda a, b: (a.astype(F32) + b.astype(F32)).astype(BF16)
     common = (lats, place, small, tile_of, band, scale3, shift3, gathered, targets)
     most = slots // 4 + 1
-    keep_a, send_a, so_far = slot_group(0, most, *common, None)
-    keep_b, send_b, terms = slot_group(most, slots // 2 - most, *common, so_far)
+    rest = slots // 2 - most
+    bits = (2, 4)
+
+    def halve(keep, send):
+        came = flip(send, 1)
+        return (
+            [add(keep[k, 0], came[k, 0]) for k in range(2)],
+            [add(keep[k, 1], came[k, 1]) for k in range(2)],
+        )
+
+    keep, send, so_far = first_slots(most, *common)
+    errs, terms = second_slots(most, rest, *common, so_far)
+    kept_a, sent_a = halve(keep, send)
+    keep, send = second_heads(most, rest, lats, place, band, scale3, shift3, errs, sent_a)
+    kept_b, sent_b = halve(keep, send)
+    grad_latent = lax.psum_scatter(terms, "var", scatter_dimension=0, tiled=False)
     pairs = []
-    for keep, send in ((keep_a, send_a), (keep_b, send_b)):
-        came = flip(send, 1)
-        bits = (2, 4)
-        kept = [add(keep[k, 0], came[k, 0]) for k in range(2)]
-        sent = [flip(add(keep[k, 1], came[k, 1]), bits[k]) for k in range(2)]
+    for kept, sent in ((kept_a, sent_a), (kept_b, sent_b)):
+        came = [flip(sent[k], bits[k]) for k in range(2)]
         for k in range(2):
-            last = flip(add(kept[k][1], sent[k][1]), bits[1 - k])
-            pairs.append((add(kept[k][0], sent[k][0]), last))
-    total = terms[0].astype(F32)
-    for s in range(1, tiles):
-        came = lax.ppermute(terms[s], "var", [(i, (i + s) % tiles) for i in range(tiles)])
-        total = total + came.astype(F32)
-    grad_latent = total.astype(BF16)
+            last = flip(add(kept[k][1], came[k][1]), bits[1 - k])
+            pairs.append((add(kept[k][0], came[k][0]), last))
     grad_head = join_heads(pairs, 1.0 / math.sqrt(lats * rows * tiles * cols))
     return (latent, grad_latent, jnp.transpose(grad_head, (0, 2, 1)))
 

time: 147 us -> 146 us (level)
  the two profiles are of different devices: /device:TPU:0 before, /device:TPU:10 now
where the time goes in v4:
time: 146 us; the launch traced here: 145 us
  waiting for transfers between devices  58.6 us (40%)
  Pallas kernels  41.4 us (28%)
  starting transfers between devices  22.3 us (15%)
  between operations  14.3 us (10%)
  local copies, waits for them, and re-layouts  4.8 us (3%)
  other arithmetic  3.82 us (3%)
    ppermute x10, waiting for transfers between devices, fast_local(): lax.ppermute(array, 'lat', [(i, i ^ bit) for i in range(lats)])  29 us
    ppermute x3, waiting for transfers between devices, fast_local(): lax.ppermute(mine, 'var', [(i, (i + s) % tiles) for i in range(tiles)])  24.6 us
    pallas_call x1, Pallas kernels, first_slots(): pl.pallas_call(functools.partial(first_kernel, lats, small[1].shape[1]),...  15.4 us
    pallas_call x1, Pallas kernels, attention(): pl.pallas_call(functools.partial(attention_kernel, bands), out_shape=jax....  8.78 us
    pallas_call x1, Pallas kernels, second_slots(): pl.pallas_call(functools.partial(second_kernel, 2 * pair, lats, tiles), g...  8.09 us
    pallas_call x1, Pallas kernels, second_heads(): pl.pallas_call(functools.partial(heads_kernel, lats), grid=(pairs,), out_...  5.21 us
    ppermute x3, starting transfers between devices, fast_local(): lax.ppermute(mine, 'var', [(i, (i + s) % tiles) for i in range(tiles)])  4.66 us
    ppermute x1, starting transfers between devices, fast_local(): below_left = lax.ppermute(high[:, cols - HC:], ('lat', 'var'), both(down))  4.63 us
  transfers between devices with their start and end apart: 20, of which 11 were waited for; matrix products, arithmetic and copies ran while one was open for 3% of the time, Pallas kernels for 14%

profile of v4, /device:TPU:10, one launch (start us, length us, event | category | flops | bytes accessed | tf_op | source)
XLA Modules:
  0.0 145.2 jit_solution(7606471858432103593)
XLA Ops:
  7.2 0.0 all-gather.3.cloned.1.call-start
  7.2 0.7 all-gather.3.cloned.1.call-update
  7.9 0.0 reduce-scatter.2.cloned.1.call-start
  7.9 1.0 fusion.21
  8.9 1.9 %collective-permute-start.1 = (bf16[3,24,1024]{2,1,0:T(8,128)(2,1)S(1)}, bf16[3,24,1024]{2,1,0:T(8,128)(2,1)S(1)}, u32[]{:S(2)}, u32[]{:S(2)}) collective-permute-start(bf16[3,24,1024]{2,1,0:T(8,128)(2,1)S(1)} %get-tuple-element.40), channel_id=1, source_target_pairs={{0,4},{4,8},{8,12},{12,16},{16,20},{20,24},{24,28},{1,5},{5,9},{9,... | collective-permute-start | bytes 442376 | tf_op jit(solution)/shard_map/ppermute | solution.py:480
  10.9 3.6 %collective-permute-start.3 = (bf16[3,24,1024]{2,1,0:T(8,128)(2,1)S(1)}, bf16[3,24,1024]{2,1,0:T(8,128)(2,1)S(1)}, u32[]{:S(2)}, u32[]{:S(2)}) collective-permute-start(bf16[3,24,1024]{2,1,0:T(8,128)(2,1)S(1)} %get-tuple-element.39), channel_id=1, source_target_pairs={{4,0},{8,4},{12,8},{16,12},{20,16},{24,20},{28,24},{5,1},{9,5},{13... | collective-permute-start | bytes 442376 | tf_op jit(solution)/shard_map/ppermute | solution.py:481
  14.5 0.9 fusion.20
  15.4 3.0 %collective-permute-start.2 = (bf16[3,6,1024]{2,1,0:T(8,128)(2,1)S(1)}, bf16[3,6,1024]{2,1,0:T(8,128)(2,1)S(1)}, u32[]{:S(2)}, u32[]{:S(2)}) collective-permute-start(bf16[3,6,1024]{2,1,0:T(8,128)(2,1)S(1)} %get-tuple-element.38), channel_id=1, source_target_pairs={{0,5},{1,6},{2,7},{3,4},{4,9},{5,10},{6,11},{7,8},{8,13},{9,14},{1... | collective-permute-start | bytes 110600 | tf_op jit(solution)/shard_map/ppermute | solution.py:483
  18.4 4.6 %collective-permute-start.4 = (bf16[3,6,1024]{2,1,0:T(8,128)(2,1)S(1)}, bf16[3,6,1024]{2,1,0:T(8,128)(2,1)S(1)}, u32[]{:S(2)}, u32[]{:S(2)}) collective-permute-start(bf16[3,6,1024]{2,1,0:T(8,128)(2,1)S(1)} %get-tuple-element.37), channel_id=1, source_target_pairs={{4,1},{5,2},{6,3},{7,0},{8,5},{9,6},{10,7},{11,4},{12,9},{13,10},{... | collective-permute-start | bytes 110600 | tf_op jit(solution)/shard_map/ppermute | solution.py:484
  23.0 0.9 slice.121
  23.9 0.3 collective-permute-start
  24.2 0.1 pad_add_fusion.place
  24.3 0.4 collective-permute-done.4.below_left
  24.7 3.9 %collective-permute-done.left = bf16[6,6,1024]{2,1,0:T(8,128)(2,1)S(1)} collective-permute-done((bf16[6,6,1024]{2,1,0:T(8,128)(2,1)S(1)}, bf16[6,6,1024]{2,1,0:T(8,128)(2,1)S(1)}, u32[]{:S(2)}, u32[]{:S(2)}) %collective-permute-start) | collective-permute-done | bytes 73760 | tf_op jit(solution)/shard_map/ppermute | solution.py:482
  28.6 0.7 copy-done.8
  29.3 8.8 %window_attention.1.refs_0_ = bf16[144,1024]{1,0:T(8,128)(2,1)S(1)} custom-call(s32[2]{0:T(128)S(1)} %pad_add_fusion.place, bf16[6,6,1024]{2,1,0:T(8,128)(2,1)S(1)} %collective-permute-done.left, bf16[3,24,1024]{2,1,0:T(8,128)(2,1)S(1)} %collective-permute-done.1.above, bf16[3,6,1024]{2,1,0:T(8,128)(2,1)S(1)} %collective-permute-done.2.above_left, ...), custom_call_target="tpu_custom_call" | custom-call | flops 6000000000 | bytes 12000000 | tf_op jit(solution)/shard_map/window_attention/pallas_call | solution.py:178
  38.1 1.2 collective-permute-start.5
  39.3 3.5 %collective-permute-start.6 = (bf16[144,1024]{1,0:T(8,128)(2,1)S(1)}, bf16[144,1024]{1,0:T(8,128)(2,1)S(1)}, u32[]{:S(2)}, u32[]{:S(2)}) collective-permute-start(bf16[144,1024]{1,0:T(8,128)(2,1)S(1)} %window_attention.1.refs_0_), channel_id=1, source_target_pairs={{0,2},{1,3},{2,0},{3,1},{4,6},{5,7},{6,4},{7,5},{8,10},{9,11},{10,... | collective-permute-start | bytes 884744 | tf_op jit(solution)/shard_map/ppermute | solution.py:490
  42.9 16.3 %collective-permute-done.5.refs_1_ = bf16[144,1024]{1,0:T(8,128)(2,1)S(1)} collective-permute-done((bf16[144,1024]{1,0:T(8,128)(2,1)S(1)}, bf16[144,1024]{1,0:T(8,128)(2,1)S(1)}, u32[]{:S(2)}, u32[]{:S(2)}) %collective-permute-start.5) | collective-permute-done | bytes 294944 | tf_op jit(solution)/shard_map/ppermute | solution.py:490
  59.2 5.9 %collective-permute-done.6.refs_2_ = bf16[144,1024]{1,0:T(8,128)(2,1)S(1)} collective-permute-done((bf16[144,1024]{1,0:T(8,128)(2,1)S(1)}, bf16[144,1024]{1,0:T(8,128)(2,1)S(1)}, u32[]{:S(2)}, u32[]{:S(2)}) %collective-permute-start.6) | collective-permute-done | bytes 294944 | tf_op jit(solution)/shard_map/ppermute | solution.py:490
  65.1 2.4 %collective-permute-done.7.refs_3_ = bf16[144,1024]{1,0:T(8,128)(2,1)S(1)} collective-permute-done((bf16[144,1024]{1,0:T(8,128)(2,1)S(1)}, bf16[144,1024]{1,0:T(8,128)(2,1)S(1)}, u32[]{:S(2)}, u32[]{:S(2)}) %collective-permute-start.7) | collective-permute-done | bytes 294944 | tf_op jit(solution)/shard_map/ppermute | solution.py:490
  67.5 2.6 %band_latents.1 = (bf16[576,1024]{1,0:T(8,128)(2,1)S(1)}, bf16[6,24,1024]{2,1,0:T(8,128)(2,1)}) custom-call(s32[2]{0:T(128)S(1)} %pad_add_fusion.place, bf16[576,576]{1,0:T(8,128)(2,1)S(1)} %copy-done.9, bf16[144,1024]{1,0:T(8,128)(2,1)S(1)} %window_attention.1.refs_0_, bf16[144,1024]{1,0:T(8,128)(2,1)S(1)} %collective-permute-done.5.refs_1_, ...), custom_call_target="tpu_custom_call" | custom-call | flops 679477248 | bytes 4000000 | tf_op jit(solution)/shard_map/band_latents/pallas_call | solution.py:238
  70.1 15.4 %first_slots.1 = (bf16[2,2,2,3,320,128]{5,4,3,2,1,0:T(8,128)(2,1)S(1)}, bf16[2,2,2,3,320,128]{5,4,3,2,1,0:T(8,128)(2,1)S(1)}, f32[576,1024]{1,0:T(8,128)}) custom-call(s32[2]{0:T(128)S(1)} %pad_add_fusion.place, s32[4]{0:T(128)S(1)} %copy-done.2, s32[1,4]{1,0:T(1,128)S(1)} %copy-done.3, s32[10]{0:T(128)S(1)} %copy-done.4, s32[576,1]{1,0:T(8,128)S(1)} %copy-done.1, ...), custom_call_target="tpu_custom_call" | custom-call | flops 6794772480 | bytes 12000000 | tf_op jit(solution)/shard_map/first_slots/pallas_call | solution.py:380
  85.5 8.1 %second_slots.1 = (bf16[4,576,320]{2,1,0:T(8,128)(2,1)S(1)}, bf16[4,6,24,1024]{3,2,1,0:T(8,128)(2,1)S(1)}) custom-call(s32[2]{0:T(128)S(1)} %pad_add_fusion.place, s32[4]{0:T(128)S(1)} %copy-done.2, s32[1,4]{1,0:T(1,128)S(1)} %copy-done.3, s32[10]{0:T(128)S(1)} %copy-done.4, s32[576,1]{1,0:T(8,128)S(1)} %copy-done.1, ...), custom_call_target="tpu_custom_call" | custom-call | flops 3019898880 | bytes 8000000 | tf_op jit(solution)/shard_map/second_slots/pallas_call | solution.py:401
  93.6 1.2 copy-done.7
  94.8 1.6 %add_convert_fusion.1 = (bf16[1,1,2,3,320,128]{5,4,3,2,1,0:T(8,128)(2,1)}, bf16[2,3,320,128]{3,2,1,0:T(8,128)(2,1)S(1)}, bf16[2,3,320,128]{3,2,1,0:T(8,128)(2,1)S(1)}, bf16[1,1,2,3,320,128]{5,4,3,2,1,0:T(8,128)(2,1)}) fusion(bf16[2,2,2,3,320,128]{5,4,3,2,1,0:T(8,128)(2,1)S(1)} %collective-permute-done.8, bf16[2,2,2,3,320,128]{5,4,3,2,1,0:T(8,128)(2,1)S(1)} %get-tuple-element.16), kind=kLoop, calls=%fused_computation.1 | loop fusion | flops 3932160 | bytes 5898240 | tf_op jit(solution)/shard_map/convert_element_type | solution.py:497
  96.4 5.2 %second_heads.1 = (bf16[2,2,2,2,320,128]{5,4,3,2,1,0:T(8,128)(2,1)S(1)}, bf16[2,2,2,2,320,128]{5,4,3,2,1,0:T(8,128)(2,1)}) custom-call(s32[2]{0:T(128)S(1)} %copy-done.6, bf16[576,1024]{1,0:T(8,128)(2,1)S(1)} %get-tuple-element.13.band, f32[10,1,1024]{2,1,0:T(1,128)S(1)} %reshape.104.scale, f32[10,1,1024]{2,1,0:T(1,128)S(1)} %reshape.105.shift, ...), custom_call_target="tpu_custom_call" | custom-call | flops 1509949440 | bytes 8000000 | tf_op jit(solution)/shard_map/second_heads/pallas_call | solution.py:423
  101.6 0.5 collective-permute-start.13
  102.1 0.1 collective-permute-start.11
  102.2 0.6 collective-permute-start.9
  102.8 2.3 %collective-permute-done.13 = bf16[2,2,2,2,320,128]{5,4,3,2,1,0:T(8,128)(2,1)} collective-permute-done((bf16[2,2,2,2,320,128]{5,4,3,2,1,0:T(8,128)(2,1)}, bf16[2,2,2,2,320,128]{5,4,3,2,1,0:T(8,128)(2,1)}, u32[]{:S(2)}, u32[]{:S(2)}) %collective-permute-start.13) | collective-permute-done | bytes 1310752 | tf_op jit(solution)/shard_map/ppermute | solution.py:496
  105.1 1.7 %add_convert_fusion.5 = (bf16[1,1,2,2,320,128]{5,4,3,2,1,0:T(8,128)(2,1)S(1)}, bf16[2,2,320,128]{3,2,1,0:T(8,128)(2,1)S(1)}, bf16[2,2,320,128]{3,2,1,0:T(8,128)(2,1)S(1)}, bf16[1,1,2,2,320,128]{5,4,3,2,1,0:T(8,128)(2,1)S(1)}) fusion(bf16[2,2,2,2,320,128]{5,4,3,2,1,0:T(8,128)(2,1)} %collective-permute-done.13, ...), kind=kLoop, calls=%fused_computation.5 | loop fusion | flops 2621440 | bytes 3932160 | tf_op jit(solution)/shard_map/convert_element_type | solution.py:497
  106.8 0.1 collective-permute-start.16
  106.9 9.4 %collective-permute-done.11 = bf16[2,3,320,128]{3,2,1,0:T(8,128)(2,1)S(1)} collective-permute-done((bf16[2,3,320,128]{3,2,1,0:T(8,128)(2,1)S(1)}, bf16[2,3,320,128]{3,2,1,0:T(8,128)(2,1)S(1)}, u32[]{:S(2)}, u32[]{:S(2)}) %collective-permute-start.11) | collective-permute-done | bytes 491552 | tf_op jit(solution)/shard_map/ppermute | solution.py:496
  116.3 0.1 fusion.15
  116.4 0.1 collective-permute-start.12
  116.5 2.0 %collective-permute-start.14 = (bf16[2,2,320,128]{3,2,1,0:T(8,128)(2,1)S(1)}, bf16[2,2,320,128]{3,2,1,0:T(8,128)(2,1)S(1)}, u32[]{:S(2)}, u32[]{:S(2)}) collective-permute-start(bf16[2,2,320,128]{3,2,1,0:T(8,128)(2,1)S(1)} %get-tuple-element.27), channel_id=1, source_target_pairs={{0,8},{4,12},{8,0},{12,4},{16,24},{20,28},{24,16},{28,20},{1,9},{5... | collective-permute-start | bytes 983048 | tf_op jit(solution)/shard_map/ppermute | solution.py:496
  118.5 0.1 fusion.13
  118.6 0.1 collective-permute-start.10
  118.7 4.6 %collective-permute-done.16 = bf16[2,2,320,128]{3,2,1,0:T(8,128)(2,1)S(1)} collective-permute-done((bf16[2,2,320,128]{3,2,1,0:T(8,128)(2,1)S(1)}, bf16[2,2,320,128]{3,2,1,0:T(8,128)(2,1)S(1)}, u32[]{:S(2)}, u32[]{:S(2)}) %collective-permute-start.16) | collective-permute-done | bytes 327712 | tf_op jit(solution)/shard_map/ppermute | solution.py:496
  123.3 0.1 fusion.19
  123.4 0.1 collective-permute-start.17
  123.4 8.0 %collective-permute-done.14 = bf16[2,2,320,128]{3,2,1,0:T(8,128)(2,1)S(1)} collective-permute-done((bf16[2,2,320,128]{3,2,1,0:T(8,128)(2,1)S(1)}, bf16[2,2,320,128]{3,2,1,0:T(8,128)(2,1)S(1)}, u32[]{:S(2)}, u32[]{:S(2)}) %collective-permute-start.14) | collective-permute-done | bytes 327712 | tf_op jit(solution)/shard_map/ppermute | solution.py:496
  131.5 0.1 fusion.17
  131.6 0.7 collective-permute-start.15
  132.2 1.0 collective-permute-done.17.refs_7_
  133.2 3.7 %collective-permute-done.15.refs_5_ = bf16[2,320,128]{2,1,0:T(8,128)(2,1)S(1)} collective-permute-done((bf16[2,320,128]{2,1,0:T(8,128)(2,1)S(1)}, bf16[2,320,128]{2,1,0:T(8,128)(2,1)S(1)}, u32[]{:S(2)}, u32[]{:S(2)}) %collective-permute-start.15) | collective-permute-done | bytes 163872 | tf_op jit(solution)/shard_map/ppermute | solution.py:496
  136.9 1.4 join_heads.1
  (40 shorter events, 0.2 us)
Async XLA Ops:
  7.2 62.9 %all-gather.3.cloned.1.call-start = ((), (), s32[]{:S(2)}) async-start(), calls=%async_computation.2 | async-start | bytes 7372800 | tf_op jit(solution)/shard_map/all_gather | solution.py:473
  7.9 130.4 %reduce-scatter.2.cloned.1.call-start = ((), (), s32[]{:S(2)}) async-start(), calls=%async_computation.1 | async-start | bytes 1474560 | tf_op jit(solution)/shard_map/reduce_scatter | solution.py:515
  8.9 19.6 %collective-permute-start.1 = (bf16[3,24,1024]{2,1,0:T(8,128)(2,1)S(1)}, bf16[3,24,1024]{2,1,0:T(8,128)(2,1)S(1)}, u32[]{:S(2)}, u32[]{:S(2)}) collective-permute-start(bf16[3,24,1024]{2,1,0:T(8,128)(2,1)S(1)} %get-tuple-element.40), channel_id=1, source_target_pairs={{0,4},{4,8},{8,12},{12,16},{16,20},{20,24},{24,28},{1,5},{5,9},{9,... | collective-permute-start | bytes 442376 | tf_op jit(solution)/shard_map/ppermute | solution.py:480
  10.9 17.7 %collective-permute-start.3 = (bf16[3,24,1024]{2,1,0:T(8,128)(2,1)S(1)}, bf16[3,24,1024]{2,1,0:T(8,128)(2,1)S(1)}, u32[]{:S(2)}, u32[]{:S(2)}) collective-permute-start(bf16[3,24,1024]{2,1,0:T(8,128)(2,1)S(1)} %get-tuple-element.39), channel_id=1, source_target_pairs={{4,0},{8,4},{12,8},{16,12},{20,16},{24,20},{28,24},{5,1},{9,5},{13... | collective-permute-start | bytes 442376 | tf_op jit(solution)/shard_map/ppermute | solution.py:481
  15.4 8.9 %collective-permute-start.2 = (bf16[3,6,1024]{2,1,0:T(8,128)(2,1)S(1)}, bf16[3,6,1024]{2,1,0:T(8,128)(2,1)S(1)}, u32[]{:S(2)}, u32[]{:S(2)}) collective-permute-start(bf16[3,6,1024]{2,1,0:T(8,128)(2,1)S(1)} %get-tuple-element.38), channel_id=1, source_target_pairs={{0,5},{1,6},{2,7},{3,4},{4,9},{5,10},{6,11},{7,8},{8,13},{9,14},{1... | collective-permute-start | bytes 110600 | tf_op jit(solution)/shard_map/ppermute | solution.py:483
  18.4 6.4 %collective-permute-start.4 = (bf16[3,6,1024]{2,1,0:T(8,128)(2,1)S(1)}, bf16[3,6,1024]{2,1,0:T(8,128)(2,1)S(1)}, u32[]{:S(2)}, u32[]{:S(2)}) collective-permute-start(bf16[3,6,1024]{2,1,0:T(8,128)(2,1)S(1)} %get-tuple-element.37), channel_id=1, source_target_pairs={{4,1},{5,2},{6,3},{7,0},{8,5},{9,6},{10,7},{11,4},{12,9},{13,10},{... | collective-permute-start | bytes 110600 | tf_op jit(solution)/shard_map/ppermute | solution.py:484
  23.9 4.7 %collective-permute-start = (bf16[6,6,1024]{2,1,0:T(8,128)(2,1)S(1)}, bf16[6,6,1024]{2,1,0:T(8,128)(2,1)S(1)}, u32[]{:S(2)}, u32[]{:S(2)}) collective-permute-start(bf16[6,6,1024]{2,1,0:T(8,128)(2,1)S(1)} %slice.121), channel_id=1, source_target_pairs={{0,1},{1,2},{2,3},{3,0},{4,5},{5,6},{6,7},{7,4},{8,9},{9,10},{10,1... | collective-permute-start | bytes 221192 | tf_op jit(solution)/shard_map/ppermute | solution.py:482
  24.3 61.2 %copy-start.5 = (s32[2]{0:T(128)}, s32[2]{0:T(128)S(1)}, u32[]{:S(2)}) copy-start(s32[2]{0:T(128)S(1)} %pad_add_fusion.place) | copy-start | bytes 28
  28.6 0.7 copy-start.8
  29.3 13.5 %copy-start.12 = (f32[10,1024]{1,0:T(8,128)S(1)}, f32[10,1024]{1,0:T(8,128)}, u32[]{:S(2)}) copy-start(f32[10,1024]{1,0:T(8,128)} %param.18) | copy-start | bytes 122884
  29.3 13.5 %copy-start.13 = (f32[10,1024]{1,0:T(8,128)S(1)}, f32[10,1024]{1,0:T(8,128)}, u32[]{:S(2)}) copy-start(f32[10,1024]{1,0:T(8,128)} %param.19) | copy-start | bytes 122884
  29.3 38.2 %copy-start.9 = (bf16[576,576]{1,0:T(8,128)(2,1)S(1)}, bf16[576,576]{1,0:T(8,128)(2,1)}, u32[]{:S(2)}) copy-start(bf16[576,576]{1,0:T(8,128)(2,1)} %constant.16.clone.chosen) | copy-start | bytes 1990660
  38.1 32.0 %copy-start.1 = (s32[576,1]{1,0:T(8,128)S(1)}, s32[576,1]{1,0:T(8,128)}, u32[]{:S(2)}) copy-start(s32[576,1]{1,0:T(8,128)} %constant.17.clone.tile_of) | copy-start | bytes 6916
  38.1 32.0 %copy-start.2 = (s32[4]{0:T(128)S(1)}, s32[4]{0:T(128)}, u32[]{:S(2)}) copy-start(s32[4]{0:T(128)} %counts.3) | copy-start | bytes 52
  38.1 32.0 %copy-start.3 = (s32[1,4]{1,0:T(1,128)S(1)}, s32[1,4]{1,0:T(1,128)}, u32[]{:S(2)}) copy-start(s32[1,4]{1,0:T(1,128)} %datasets.3) | copy-start | bytes 52
  38.1 32.0 %copy-start.4 = (s32[10]{0:T(128)S(1)}, s32[10]{0:T(128)}, u32[]{:S(2)}) copy-start(s32[10]{0:T(128)} %levels.3) | copy-start | bytes 124
  38.1 21.0 %collective-permute-start.5 = (bf16[144,1024]{1,0:T(8,128)(2,1)S(1)}, bf16[144,1024]{1,0:T(8,128)(2,1)S(1)}, u32[]{:S(2)}, u32[]{:S(2)}) collective-permute-start(bf16[144,1024]{1,0:T(8,128)(2,1)S(1)} %window_attention.1.refs_0_), channel_id=1, source_target_pairs={{0,1},{1,2},{2,3},{3,0},{4,5},{5,6},{6,7},{7,4},{8,9},{9,10},{10,1... | collective-permute-start | bytes 884744 | tf_op jit(solution)/shard_map/ppermute | solution.py:490
  39.3 25.7 %collective-permute-start.6 = (bf16[144,1024]{1,0:T(8,128)(2,1)S(1)}, bf16[144,1024]{1,0:T(8,128)(2,1)S(1)}, u32[]{:S(2)}, u32[]{:S(2)}) collective-permute-start(bf16[144,1024]{1,0:T(8,128)(2,1)S(1)} %window_attention.1.refs_0_), channel_id=1, source_target_pairs={{0,2},{1,3},{2,0},{3,1},{4,6},{5,7},{6,4},{7,5},{8,10},{9,11},{10,... | collective-permute-start | bytes 884744 | tf_op jit(solution)/shard_map/ppermute | solution.py:490
  42.8 24.7 %collective-permute-start.7 = (bf16[144,1024]{1,0:T(8,128)(2,1)S(1)}, bf16[144,1024]{1,0:T(8,128)(2,1)S(1)}, u32[]{:S(2)}, u32[]{:S(2)}) collective-permute-start(bf16[144,1024]{1,0:T(8,128)(2,1)S(1)} %window_attention.1.refs_0_), channel_id=1, source_target_pairs={{0,3},{1,0},{2,1},{3,2},{4,7},{5,4},{6,5},{7,6},{8,11},{9,8},{10,9... | collective-permute-start | bytes 884744 | tf_op jit(solution)/shard_map/ppermute | solution.py:490
  85.5 9.3 %collective-permute-start.8 = (bf16[2,2,2,3,320,128]{5,4,3,2,1,0:T(8,128)(2,1)S(1)}, bf16[2,2,2,3,320,128]{5,4,3,2,1,0:T(8,128)(2,1)S(1)}, u32[]{:S(2)}, u32[]{:S(2)}) collective-permute-start(bf16[2,2,2,3,320,128]{5,4,3,2,1,0:T(8,128)(2,1)S(1)} %get-tuple-element.17), channel_id=1, source_target_pairs={{0,4},{4,0},{8,12},{12,8},{16,20},{20,16},{24,28},{28,24},{1,5},{5... | collective-permute-start | bytes 5898248 | tf_op jit(solution)/shard_map/ppermute | solution.py:496
  93.6 1.2 copy-start.7
  94.8 1.6 %copy-start = (bf16[4,6,24,1024]{3,2,1,0:T(8,128)(2,1)}, bf16[4,6,24,1024]{3,2,1,0:T(8,128)(2,1)S(1)}, u32[]{:S(2)}) copy-start(bf16[4,6,24,1024]{3,2,1,0:T(8,128)(2,1)S(1)} %get-tuple-element.15) | copy-start | bytes 3538948
  94.8 1.6 %copy-start.6 = (s32[2]{0:T(128)S(1)}, s32[2]{0:T(128)}, u32[]{:S(2)}) copy-start(s32[2]{0:T(128)} %copy-done.5) | copy-start | bytes 28
  101.6 3.5 %collective-permute-start.13 = (bf16[2,2,2,2,320,128]{5,4,3,2,1,0:T(8,128)(2,1)}, bf16[2,2,2,2,320,128]{5,4,3,2,1,0:T(8,128)(2,1)}, u32[]{:S(2)}, u32[]{:S(2)}) collective-permute-start(bf16[2,2,2,2,320,128]{5,4,3,2,1,0:T(8,128)(2,1)} %get-tuple-element.20), channel_id=1, source_target_pairs={{0,4},{4,0},{8,12},{12,8},{16,20},{20,16},{24,28},{28,24},{1,5},{5... | collective-permute-start | bytes 3932168 | tf_op jit(solution)/shard_map/ppermute | solution.py:496
  102.1 14.1 %collective-permute-start.11 = (bf16[2,3,320,128]{3,2,1,0:T(8,128)(2,1)S(1)}, bf16[2,3,320,128]{3,2,1,0:T(8,128)(2,1)S(1)}, u32[]{:S(2)}, u32[]{:S(2)}) collective-permute-start(bf16[2,3,320,128]{3,2,1,0:T(8,128)(2,1)S(1)} %get-tuple-element.22.refs_1_), channel_id=1, source_target_pairs={{0,16},{4,20},{8,24},{12,28},{16,0},{20,4},{24,8},{28,12},{1,17},{... | collective-permute-start | bytes 1474568 | tf_op jit(solution)/shard_map/ppermute | solution.py:496
  102.2 16.3 %collective-permute-start.9 = (bf16[2,3,320,128]{3,2,1,0:T(8,128)(2,1)S(1)}, bf16[2,3,320,128]{3,2,1,0:T(8,128)(2,1)S(1)}, u32[]{:S(2)}, u32[]{:S(2)}) collective-permute-start(bf16[2,3,320,128]{3,2,1,0:T(8,128)(2,1)S(1)} %get-tuple-element.23.refs_0_), channel_id=1, source_target_pairs={{0,8},{4,12},{8,0},{12,4},{16,24},{20,28},{24,16},{28,20},{1,9},{5... | collective-permute-start | bytes 1474568 | tf_op jit(solution)/shard_map/ppermute | solution.py:496
  105.1 11.2 %copy-start.11 = (bf16[1,1,2,3,320,128]{5,4,3,2,1,0:T(8,128)(2,1)S(1)}, bf16[1,1,2,3,320,128]{5,4,3,2,1,0:T(8,128)(2,1)}, u32[]{:S(2)}) copy-start(bf16[1,1,2,3,320,128]{5,4,3,2,1,0:T(8,128)(2,1)} %get-tuple-element.21) | copy-start | bytes 1474564
  105.1 13.4 %copy-start.10 = (bf16[1,1,2,3,320,128]{5,4,3,2,1,0:T(8,128)(2,1)S(1)}, bf16[1,1,2,3,320,128]{5,4,3,2,1,0:T(8,128)(2,1)}, u32[]{:S(2)}) copy-start(bf16[1,1,2,3,320,128]{5,4,3,2,1,0:T(8,128)(2,1)} %get-tuple-element.24) | copy-start | bytes 1474564
  106.8 16.5 %collective-permute-start.16 = (bf16[2,2,320,128]{3,2,1,0:T(8,128)(2,1)S(1)}, bf16[2,2,320,128]{3,2,1,0:T(8,128)(2,1)S(1)}, u32[]{:S(2)}, u32[]{:S(2)}) collective-permute-start(bf16[2,2,320,128]{3,2,1,0:T(8,128)(2,1)S(1)} %get-tuple-element.26), channel_id=1, source_target_pairs={{0,16},{4,20},{8,24},{12,28},{16,0},{20,4},{24,8},{28,12},{1,17},{... | collective-permute-start | bytes 983048 | tf_op jit(solution)/shard_map/ppermute | solution.py:496
  116.4 15.8 %collective-permute-start.12 = (bf16[3,320,128]{2,1,0:T(8,128)(2,1)S(1)}, bf16[3,320,128]{2,1,0:T(8,128)(2,1)S(1)}, u32[]{:S(2)}, u32[]{:S(2)}) collective-permute-start(bf16[3,320,128]{2,1,0:T(8,128)(2,1)S(1)} %get-tuple-element.29), channel_id=1, source_target_pairs={{0,8},{4,12},{8,0},{12,4},{16,24},{20,28},{24,16},{28,20},{1,9},{5... | collective-permute-start | bytes 737288 | tf_op jit(solution)/shard_map/ppermute | solution.py:496
  116.5 15.0 %collective-permute-start.14 = (bf16[2,2,320,128]{3,2,1,0:T(8,128)(2,1)S(1)}, bf16[2,2,320,128]{3,2,1,0:T(8,128)(2,1)S(1)}, u32[]{:S(2)}, u32[]{:S(2)}) collective-permute-start(bf16[2,2,320,128]{3,2,1,0:T(8,128)(2,1)S(1)} %get-tuple-element.27), channel_id=1, source_target_pairs={{0,8},{4,12},{8,0},{12,4},{16,24},{20,28},{24,16},{28,20},{1,9},{5... | collective-permute-start | bytes 983048 | tf_op jit(solution)/shard_map/ppermute | solution.py:496
  118.6 13.6 %collective-permute-start.10 = (bf16[3,320,128]{2,1,0:T(8,128)(2,1)S(1)}, bf16[3,320,128]{2,1,0:T(8,128)(2,1)S(1)}, u32[]{:S(2)}, u32[]{:S(2)}) collective-permute-start(bf16[3,320,128]{2,1,0:T(8,128)(2,1)S(1)} %get-tuple-element.31), channel_id=1, source_target_pairs={{0,16},{4,20},{8,24},{12,28},{16,0},{20,4},{24,8},{28,12},{1,17},{... | collective-permute-start | bytes 737288 | tf_op jit(solution)/shard_map/ppermute | solution.py:496
  123.4 9.8 %collective-permute-start.17 = (bf16[2,320,128]{2,1,0:T(8,128)(2,1)S(1)}, bf16[2,320,128]{2,1,0:T(8,128)(2,1)S(1)}, u32[]{:S(2)}, u32[]{:S(2)}) collective-permute-start(bf16[2,320,128]{2,1,0:T(8,128)(2,1)S(1)} %get-tuple-element.33), channel_id=1, source_target_pairs={{0,8},{4,12},{8,0},{12,4},{16,24},{20,28},{24,16},{28,20},{1,9},{5... | collective-permute-start | bytes 491528 | tf_op jit(solution)/shard_map/ppermute | solution.py:496
  131.6 5.4 %collective-permute-start.15 = (bf16[2,320,128]{2,1,0:T(8,128)(2,1)S(1)}, bf16[2,320,128]{2,1,0:T(8,128)(2,1)S(1)}, u32[]{:S(2)}, u32[]{:S(2)}) collective-permute-start(bf16[2,320,128]{2,1,0:T(8,128)(2,1)S(1)} %get-tuple-element.35), channel_id=1, source_target_pairs={{0,16},{4,20},{8,24},{12,28},{16,0},{20,4},{24,8},{28,12},{1,17},{... | collective-permute-start | bytes 491528 | tf_op jit(solution)/shard_map/ppermute | solution.py:496
Sparse Core Ops, SparseCore 0:
  9.9 48.4 all-gather.2
  102.2 25.7 reduce-scatter.1

commit v5 on v3

--- a/solution.py
+++ b/solution.py
@@ -190,7 +190,7 @@
             pltpu.VMEM(proj_out.shape, BF16),
             pltpu.SemaphoreType.DMA((4,)),
         ],
-        compiler_params=pltpu.CompilerParams(vmem_limit_bytes=VMEM_LIMIT),
+        compiler_params=pltpu.CompilerParams(vmem_limit_bytes=53 * 1024 * 1024),
         cost_estimate=pl.CostEstimate(
             flops=6_000_000_000, bytes_accessed=12_000_000, transcendentals=400_000
         ),
@@ -252,77 +252,114 @@
     )(place, jnp.asarray(band_map(tiles, cols), BF16), *pieces)
 
 
-def slot_kernel(first_slot, lats, tiles, final, place, counts, datasets, levels, tile_of, band, scale, shift, gathered, target, *refs):
-    keep, send, out = refs[-8:-5] if final else refs[-7:-4]
-    rows, errs, turned = refs[-4:-2], refs[-2], refs[-1]
-    total = refs[-5] if final else out
-    step = pl.program_id(0)
-    outs = target.shape[-1]
-    places, width = band.shape
-    piece = width // lats
-
-    @pl.when(step == 0)
-    def _():
-        total[...] = refs[0][...] if final else jnp.zeros_like(total)
-
-    tile = tile_of[...]
+def slot_errors(level, tile_counts, rows, weight, target):
+    predicted = lax.dot_general(
+        rows, weight, (((1,), (1,)), ((), ())), preferred_element_type=F32
+    )
+    live = jnp.where(level < tile_counts, 1.0, 0.0)
+    diff = predicted - target.astype(F32).reshape(predicted.shape)
+    return (diff * live).astype(BF16)
+
+
+def head_halves(k, lats, lat, errors, rows, turned, keep, send):
+    turned[k] = lax.dot_general(
+        errors, rows, (((0,), (0,)), ((), ())), preferred_element_type=F32
+    ).astype(BF16)
+    piece = turned.shape[-1] // lats
+    for q in range(lats):
+        core, x, y = q & 1, (q >> 1) & 1, (q >> 2) & 1
+        outer, inner = (x, y) if k == 0 else (y, x)
+        start = pl.multiple_of(jnp.bitwise_xor(lat, q) * piece, piece)
+        to = send if core else keep
+        to[k, outer, inner, 0] = turned[k, :, pl.ds(start, piece)]
+
+
+def scaled_rows(band, scale, shift, slot, rows):
     for k in range(2):
-        rows[k][...] = (band[...].astype(F32) * scale[k] + shift[k]).astype(BF16)
-    for k in range(2):
-        weight = jnp.concatenate([gathered[l, k] for l in range(lats)], axis=1)
-        predicted = lax.dot_general(
-            rows[k][...], weight, (((1,), (1,)), ((), ())), preferred_element_type=F32
-        )
-        live = jnp.zeros(tile.shape, F32)
-        for t in range(tiles):
-            alive = levels[first_slot + 2 * step + k] < counts[datasets[0, t]]
-            live = live + jnp.where(jnp.logical_and(tile == t, alive), 1.0, 0.0)
-        diff = predicted - target[k].astype(F32).reshape(places, outs)
-        errs[k] = (diff * live).astype(BF16)
-    for k in range(2):
-        turned[k] = lax.dot_general(
-            errs[k], rows[k][...], (((0,), (0,)), ((), ())), preferred_element_type=F32
-        ).astype(BF16)
-        for q in range(lats):
-            core, x, y = q & 1, (q >> 1) & 1, (q >> 2) & 1
-            outer, inner = (x, y) if k == 0 else (y, x)
-            start = pl.multiple_of(jnp.bitwise_xor(place[0], q) * piece, piece)
-            to = send if core else keep
-            to[k, outer, inner, 0] = turned[k, :, pl.ds(start, piece)]
+        rows[k][...] = (band[...].astype(F32) * scale[slot + k] + shift[slot + k]).astype(BF16)
+
+
+def add_back(lats, errs, gathered, scale, slot, total):
+    piece = gathered.shape[-1]
     for l in range(0, lats, 2):
         lanes = slice(l * piece, (l + 2) * piece)
         term = 0.0
         for k in range(2):
             weight = jnp.concatenate([gathered[l, k], gathered[l + 1, k]], axis=1)
-            term = term + jnp.dot(errs[k], weight, preferred_element_type=F32) * scale[k][:, lanes]
+            factor = scale[slot + k][:, lanes]
+            term = term + jnp.dot(errs[k], weight, preferred_element_type=F32) * factor
         total[:, lanes] += term
 
+
+def slot_kernel(
+    first_slot,
+    lats,
+    tiles,
+    final,
+    place,
+    counts,
+    datasets,
+    levels,
+    tile_of,
+    band,
+    scale,
+    shift,
+    gathered,
+    target,
+    *refs,
+):
     if final:
-
-        @pl.when(step == pl.num_programs(0) - 1)
+        before, keep, send, out, total, rows0, rows1, errs, turned, tile_counts = refs
+    else:
+        keep, send, total, rows0, rows1, errs, turned, tile_counts = refs
+    rows = (rows0, rows1)
+    step, steps = pl.program_id(0), pl.num_programs(0)
+    slot = first_slot + 2 * step
+
+    @pl.when(step == 0)
+    def _():
+        total[...] = before[...] if final else jnp.zeros_like(total)
+        tile = tile_of[...]
+        wanted = jnp.zeros_like(tile)
+        for t in range(tiles):
+            wanted = jnp.where(tile == t, counts[datasets[0, t]], wanted)
+        tile_counts[...] = wanted
+        scaled_rows(band, scale, shift, slot, rows)
+
+    for k in range(2):
+        weight = jnp.concatenate([gathered[l, k] for l in range(lats)], axis=1)
+        errs[k] = slot_errors(levels[slot + k], tile_counts[...], rows[k][...], weight, target[k])
+    for k in range(2):
+        head_halves(k, lats, place[0], errs[k], rows[k][...], turned, keep, send)
+    scaled_rows(band, scale, shift, first_slot + 2 * jnp.minimum(step + 1, steps - 1), rows)
+    add_back(lats, errs, gathered, scale, slot, total)
+
+    if final:
+
+        @pl.when(step == steps - 1)
         def _():
             cols = out.shape[2]
             for s in range(tiles):
-                at = lax.rem(place[1] + s, tiles)
                 for r in range(WH):
-                    start = pl.multiple_of(r * tiles * cols + at * cols, 8)
-                    out[s, r] = total[pl.ds(start, cols), :].astype(BF16)
+                    start = (r * tiles + s) * cols
+                    out[s, r] = total[start : start + cols, :].astype(BF16)
 
 
 def slot_group(pair, pairs, lats, place, small, tile_of, band, scale, shift, gathered, targets, before):
     places, width = band.shape
-    outs = targets.shape[-1]
+    slots, outs = targets.shape[0], targets.shape[-1]
     tiles = small[1].shape[1]
     piece = width // lats
     smem = pl.BlockSpec(memory_space=pltpu.SMEM)
     halves = jax.ShapeDtypeStruct((2, 2, 2, pairs, outs, piece), BF16)
     half_spec = pl.BlockSpec((2, 2, 2, 1, outs, piece), lambda i: (0, 0, 0, i, 0, 0))
-    in_specs = [
-        smem, smem, smem, smem,
+    level_spec = pl.BlockSpec((slots, 1, width), lambda i: (0, 0, 0))
+    sum_spec = pl.BlockSpec((places, width), lambda i: (0, 0))
+    in_specs = [smem] * 4 + [
         pl.BlockSpec((places, 1), lambda i: (0, 0)),
-        pl.BlockSpec((places, width), lambda i: (0, 0)),
-        pl.BlockSpec((2, 1, width), lambda i: (i + pair, 0, 0)),
-        pl.BlockSpec((2, 1, width), lambda i: (i + pair, 0, 0)),
+        sum_spec,
+        level_spec,
+        level_spec,
         pl.BlockSpec((lats, 2, outs, piece), lambda i: (0, i + pair, 0, 0)),
         pl.BlockSpec((2,) + targets.shape[1:], lambda i: (i + pair, 0, 0, 0)),
     ]
@@ -333,10 +370,11 @@
         pltpu.VMEM((places, width), BF16),
         pltpu.VMEM((2, places, outs), BF16),
         pltpu.VMEM((2, outs, width), BF16),
+        pltpu.VMEM((places, 1), jnp.int32),
     ]
     sums = jax.ShapeDtypeStruct((places, width), F32)
     if final:
-        in_specs.append(pl.BlockSpec((places, width), lambda i: (0, 0)))
+        in_specs.append(sum_spec)
         args.append(before)
         scratch.insert(0, pltpu.VMEM(sums.shape, F32))
         sums = jax.ShapeDtypeStruct((tiles, WH, places // (WH * tiles), width), BF16)
@@ -418,22 +456,27 @@
     add = lambda a, b: (a.astype(F32) + b.astype(F32)).astype(BF16)
     common = (lats, place, small, tile_of, band, scale3, shift3, gathered, targets)
     most = slots // 4 + 1
+    rest = slots // 2 - most
+    bits = (2, 4)
+
+    def halve(keep, send):
+        came = flip(send, 1)
+        return (
+            [add(keep[k, 0], came[k, 0]) for k in range(2)],
+            [add(keep[k, 1], came[k, 1]) for k in range(2)],
+        )
+
     keep_a, send_a, so_far = slot_group(0, most, *common, None)
-    keep_b, send_b, terms = slot_group(most, slots // 2 - most, *common, so_far)
+    keep_b, send_b, terms = slot_group(most, rest, *common, so_far)
+    kept_a, sent_a = halve(keep_a, send_a)
+    kept_b, sent_b = halve(keep_b, send_b)
+    grad_latent = lax.psum_scatter(terms, "var", scatter_dimension=0, tiled=False)
     pairs = []
-    for keep, send in ((keep_a, send_a), (keep_b, send_b)):
-        came = flip(send, 1)
-        bits = (2, 4)
-        kept = [add(keep[k, 0], came[k, 0]) for k in range(2)]
-        sent = [flip(add(keep[k, 1], came[k, 1]), bits[k]) for k in range(2)]
+    for kept, sent in ((kept_a, sent_a), (kept_b, sent_b)):
+        came = [flip(sent[k], bits[k]) for k in range(2)]
         for k in range(2):
-            last = flip(add(kept[k][1], sent[k][1]), bits[1 - k])
-            pairs.append((add(kept[k][0], sent[k][0]), last))
-    total = terms[0].astype(F32)
-    for s in range(1, tiles):
-        came = lax.ppermute(terms[s], "var", [(i, (i + s) % tiles) for i in range(tiles)])
-        total = total + came.astype(F32)
-    grad_latent = total.astype(BF16)
+            last = flip(add(kept[k][1], came[k][1]), bits[1 - k])
+            pairs.append((add(kept[k][0], came[k][0]), last))
     grad_head = join_heads(pairs, 1.0 / math.sqrt(lats * rows * tiles * cols))
     return (latent, grad_latent, jnp.transpose(grad_head, (0, 2, 1)))
 

time: 147 us -> 150 us (1.020)
  starting transfers between devices: 32.9 us -> 28.2 us
  waiting for transfers between devices: 50.6 us -> 54.5 us
  Pallas kernels: 39.2 us -> 41.2 us
  other arithmetic: 2.39 us -> 4.22 us
    ppermute x10, waiting for transfers between devices: 13 us -> 24.3 us  [fast_local(): lax.ppermute(array, 'lat', [(i, i ^ bit) for i in range(lats)])]
    ppermute x3 -> x0, waiting for transfers between devices: 7.39 us -> none  [fast_local(): lax.ppermute(terms[s], 'var', [(i, (i + s) % tiles) for i in range(tiles)])]
    ppermute x3 -> x0, starting transfers between devices: 6.37 us -> none  [fast_local(): lax.ppermute(terms[s], 'var', [(i, (i + s) % tiles) for i in range(tiles)])]
    convert_element_type x6, other arithmetic: 1.41 us -> 4.14 us  [fast_local(): add = lambda a, b: (a.astype(F32) + b.astype(F32)).astype(BF16)]
    pallas_call x2, Pallas kernels: 26.3 us -> 28.5 us  [slot_group(): pl.pallas_call(functools.partial(slot_kernel, 2 * pair, lats, tiles, fina...]
    ppermute x10, starting transfers between devices: 9.42 us -> 11.1 us  [fast_local(): lax.ppermute(array, 'lat', [(i, i ^ bit) for i in range(lats)])]
    unnamed x22 -> x26, local copies, waits for them, and re-layouts: 4.31 us -> 4.04 us
  transfers between devices with their start and end apart: 22 -> 20, of which waited for: 8 -> 10; matrix products, arithmetic and copies ran while one was open for 4% -> 5% of each run, Pallas kernels for 15% -> 17%
where the time goes in v5:
time: 150 us; the launch traced here: 149 us
  waiting for transfers between devices  54.5 us (36%)
  Pallas kernels  41.2 us (27%)
  starting transfers between devices  28.2 us (19%)
  between operations  14.2 us (9%)
  local copies, waits for them, and re-layouts  6.87 us (5%)
  other arithmetic  4.22 us (3%)
    pallas_call x2, Pallas kernels, slot_group(): pl.pallas_call(functools.partial(slot_kernel, 2 * pair, lats, tiles, fina...  28.5 us
    ppermute x3, waiting for transfers between devices, fast_local(): lax.ppermute(mine, 'var', [(i, (i + s) % tiles) for i in range(tiles)])  24.7 us
    ppermute x10, waiting for transfers between devices, fast_local(): lax.ppermute(array, 'lat', [(i, i ^ bit) for i in range(lats)])  24.3 us
    ppermute x10, starting transfers between devices, fast_local(): lax.ppermute(array, 'lat', [(i, i ^ bit) for i in range(lats)])  11.1 us
    pallas_call x1, Pallas kernels, attention(): pl.pallas_call(functools.partial(attention_kernel, bands), out_shape=jax....  8.78 us
    ppermute x1, starting transfers between devices, fast_local(): above_left = lax.ppermute(low[:, cols - HC:], ('lat', 'var'), both(up))  6.84 us
    ppermute x1, waiting for transfers between devices, fast_local(): left = lax.ppermute(patches[:, cols - HC:], 'var', right)  4.77 us
    convert_element_type x6, other arithmetic, fast_local(): add = lambda a, b: (a.astype(F32) + b.astype(F32)).astype(BF16)  4.14 us
  transfers between devices with their start and end apart: 20, of which 10 were waited for; matrix products, arithmetic and copies ran while one was open for 5% of the time, Pallas kernels for 17%

profile of v5, /device:TPU:0, one launch (start us, length us, event | category | flops | bytes accessed | tf_op | source)
XLA Modules:
  0.0 149.2 jit_solution(7436009764421110689)
XLA Ops:
  7.2 0.7 all-gather.3.cloned.1.call-update
  7.9 1.0 fusion.21
  8.9 1.3 collective-permute-start.3
  10.2 3.0 %collective-permute-start.1 = (bf16[3,24,1024]{2,1,0:T(8,128)(2,1)S(1)}, bf16[3,24,1024]{2,1,0:T(8,128)(2,1)S(1)}, u32[]{:S(2)}, u32[]{:S(2)}) collective-permute-start(bf16[3,24,1024]{2,1,0:T(8,128)(2,1)S(1)} %get-tuple-element.38), channel_id=1, source_target_pairs={{0,4},{4,8},{8,12},{12,16},{16,20},{20,24},{24,28},{1,5},{5,9},{9,... | collective-permute-start | bytes 442376 | tf_op jit(solution)/shard_map/ppermute | solution.py:439
  13.3 0.9 fusion.20
  14.2 1.3 collective-permute-start.4
  15.5 6.8 %collective-permute-start.2 = (bf16[3,6,1024]{2,1,0:T(8,128)(2,1)S(1)}, bf16[3,6,1024]{2,1,0:T(8,128)(2,1)S(1)}, u32[]{:S(2)}, u32[]{:S(2)}) collective-permute-start(bf16[3,6,1024]{2,1,0:T(8,128)(2,1)S(1)} %get-tuple-element.36), channel_id=1, source_target_pairs={{0,5},{1,6},{2,7},{3,4},{4,9},{5,10},{6,11},{7,8},{8,13},{9,14},{1... | collective-permute-start | bytes 110600 | tf_op jit(solution)/shard_map/ppermute | solution.py:442
  22.3 0.9 slice.121
  23.2 1.6 %collective-permute-start = (bf16[6,6,1024]{2,1,0:T(8,128)(2,1)S(1)}, bf16[6,6,1024]{2,1,0:T(8,128)(2,1)S(1)}, u32[]{:S(2)}, u32[]{:S(2)}) collective-permute-start(bf16[6,6,1024]{2,1,0:T(8,128)(2,1)S(1)} %slice.121), channel_id=1, source_target_pairs={{0,1},{1,2},{2,3},{3,0},{4,5},{5,6},{6,7},{7,4},{8,9},{9,10},{10,1... | collective-permute-start | bytes 221192 | tf_op jit(solution)/shard_map/ppermute | solution.py:441
  24.9 0.1 pad_add_fusion.place
  24.9 4.8 %collective-permute-done.left = bf16[6,6,1024]{2,1,0:T(8,128)(2,1)S(1)} collective-permute-done((bf16[6,6,1024]{2,1,0:T(8,128)(2,1)S(1)}, bf16[6,6,1024]{2,1,0:T(8,128)(2,1)S(1)}, u32[]{:S(2)}, u32[]{:S(2)}) %collective-permute-start) | collective-permute-done | bytes 73760 | tf_op jit(solution)/shard_map/ppermute | solution.py:441
  29.7 0.7 copy-done.1
  30.4 8.8 %window_attention.1.refs_0_ = bf16[144,1024]{1,0:T(8,128)(2,1)S(1)} custom-call(s32[2]{0:T(128)S(1)} %pad_add_fusion.place, bf16[6,6,1024]{2,1,0:T(8,128)(2,1)S(1)} %collective-permute-done.left, bf16[3,24,1024]{2,1,0:T(8,128)(2,1)S(1)} %collective-permute-done.1.above, bf16[3,6,1024]{2,1,0:T(8,128)(2,1)S(1)} %collective-permute-done.2.above_left, ...), custom_call_target="tpu_custom_call" | custom-call | flops 6000000000 | bytes 12000000 | tf_op jit(solution)/shard_map/window_attention/pallas_call | solution.py:178
  39.3 0.5 collective-permute-start.7
  39.8 0.8 collective-permute-start.6
  40.5 1.7 %collective-permute-start.5 = (bf16[144,1024]{1,0:T(8,128)(2,1)S(1)}, bf16[144,1024]{1,0:T(8,128)(2,1)S(1)}, u32[]{:S(2)}, u32[]{:S(2)}) collective-permute-start(bf16[144,1024]{1,0:T(8,128)(2,1)S(1)} %window_attention.1.refs_0_), channel_id=1, source_target_pairs={{0,1},{1,2},{2,3},{3,0},{4,5},{5,6},{6,7},{7,4},{8,9},{9,10},{10,1... | collective-permute-start | bytes 884744 | tf_op jit(solution)/shard_map/ppermute | solution.py:449
  42.3 7.6 %collective-permute-done.7.refs_3_ = bf16[144,1024]{1,0:T(8,128)(2,1)S(1)} collective-permute-done((bf16[144,1024]{1,0:T(8,128)(2,1)S(1)}, bf16[144,1024]{1,0:T(8,128)(2,1)S(1)}, u32[]{:S(2)}, u32[]{:S(2)}) %collective-permute-start.7) | collective-permute-done | bytes 294944 | tf_op jit(solution)/shard_map/ppermute | solution.py:449
  49.9 17.2 %collective-permute-done.6.refs_2_ = bf16[144,1024]{1,0:T(8,128)(2,1)S(1)} collective-permute-done((bf16[144,1024]{1,0:T(8,128)(2,1)S(1)}, bf16[144,1024]{1,0:T(8,128)(2,1)S(1)}, u32[]{:S(2)}, u32[]{:S(2)}) %collective-permute-start.6) | collective-permute-done | bytes 294944 | tf_op jit(solution)/shard_map/ppermute | solution.py:449
  67.1 2.6 %band_latents.1 = (bf16[576,1024]{1,0:T(8,128)(2,1)S(1)}, bf16[6,24,1024]{2,1,0:T(8,128)(2,1)}) custom-call(s32[2]{0:T(128)S(1)} %pad_add_fusion.place, bf16[576,576]{1,0:T(8,128)(2,1)S(1)} %copy-done.5, bf16[144,1024]{1,0:T(8,128)(2,1)S(1)} %window_attention.1.refs_0_, bf16[144,1024]{1,0:T(8,128)(2,1)S(1)} %collective-permute-done.5.refs_1_, ...), custom_call_target="tpu_custom_call" | custom-call | flops 679477248 | bytes 4000000 | tf_op jit(solution)/shard_map/band_latents/pallas_call | solution.py:238
  69.7 1.0 copy-done.8
  70.7 1.3 copy-done.9
  72.0 16.4 %slot_group.2 = (bf16[2,2,2,3,320,128]{5,4,3,2,1,0:T(8,128)(2,1)S(1)}, bf16[2,2,2,3,320,128]{5,4,3,2,1,0:T(8,128)(2,1)}, f32[576,1024]{1,0:T(8,128)}) custom-call(s32[2]{0:T(128)S(1)} %pad_add_fusion.place, s32[4]{0:T(128)S(1)} %copy-done.2, s32[1,4]{1,0:T(1,128)S(1)} %copy-done.3, s32[10]{0:T(128)S(1)} %copy-done.4, s32[576,1]{1,0:T(8,128)S(1)} %copy-done.6, ...), custom_call_target="tpu_custom_call" | custom-call | flops 6794772480 | bytes 15000000 | tf_op jit(solution)/shard_map/slot_group/pallas_call | solution.py:381
  88.3 0.1 collective-permute-start.8
  88.5 12.1 %slot_group.3 = (bf16[2,2,2,2,320,128]{5,4,3,2,1,0:T(8,128)(2,1)S(1)}, bf16[2,2,2,2,320,128]{5,4,3,2,1,0:T(8,128)(2,1)}, bf16[4,6,24,1024]{3,2,1,0:T(8,128)(2,1)S(1)}) custom-call(s32[2]{0:T(128)S(1)} %pad_add_fusion.place, s32[4]{0:T(128)S(1)} %copy-done.2, s32[1,4]{1,0:T(1,128)S(1)} %copy-done.3, s32[10]{0:T(128)S(1)} %copy-done.4, ...), custom_call_target="tpu_custom_call" | custom-call | flops 4529848320 | bytes 10000000 | tf_op jit(solution)/shard_map/slot_group/pallas_call | solution.py:381
  100.6 1.0 copy-done
  101.6 0.4 collective-permute-start.13
  102.0 3.0 %collective-permute-done.13 = bf16[2,2,2,2,320,128]{5,4,3,2,1,0:T(8,128)(2,1)} collective-permute-done((bf16[2,2,2,2,320,128]{5,4,3,2,1,0:T(8,128)(2,1)}, bf16[2,2,2,2,320,128]{5,4,3,2,1,0:T(8,128)(2,1)}, u32[]{:S(2)}, u32[]{:S(2)}) %collective-permute-start.13) | collective-permute-done | bytes 1310752 | tf_op jit(solution)/shard_map/ppermute | solution.py:455
  105.0 1.6 %add_convert_fusion.5 = (bf16[1,1,2,2,320,128]{5,4,3,2,1,0:T(8,128)(2,1)S(1)}, bf16[2,2,320,128]{3,2,1,0:T(8,128)(2,1)S(1)}, bf16[2,2,320,128]{3,2,1,0:T(8,128)(2,1)S(1)}, bf16[1,1,2,2,320,128]{5,4,3,2,1,0:T(8,128)(2,1)S(1)}) fusion(bf16[2,2,2,2,320,128]{5,4,3,2,1,0:T(8,128)(2,1)} %collective-permute-done.13, ...), kind=kLoop, calls=%fused_computation.5 | loop fusion | flops 2621440 | bytes 3932160 | tf_op jit(solution)/shard_map/convert_element_type | solution.py:456
  106.7 3.1 %collective-permute-start.16 = (bf16[2,2,320,128]{3,2,1,0:T(8,128)(2,1)S(1)}, bf16[2,2,320,128]{3,2,1,0:T(8,128)(2,1)S(1)}, u32[]{:S(2)}, u32[]{:S(2)}) collective-permute-start(bf16[2,2,320,128]{3,2,1,0:T(8,128)(2,1)S(1)} %get-tuple-element.24), channel_id=1, source_target_pairs={{0,16},{4,20},{8,24},{12,28},{16,0},{20,4},{24,8},{28,12},{1,17},{... | collective-permute-start | bytes 983048 | tf_op jit(solution)/shard_map/ppermute | solution.py:455
  109.8 2.1 %add_convert_fusion.1 = (bf16[1,1,2,3,320,128]{5,4,3,2,1,0:T(8,128)(2,1)S(1)}, bf16[2,3,320,128]{3,2,1,0:T(8,128)(2,1)S(1)}, bf16[2,3,320,128]{3,2,1,0:T(8,128)(2,1)S(1)}, bf16[1,1,2,3,320,128]{5,4,3,2,1,0:T(8,128)(2,1)S(1)}) fusion(bf16[2,2,2,3,320,128]{5,4,3,2,1,0:T(8,128)(2,1)} %collective-permute-done.8, ...), kind=kLoop, calls=%fused_computation.1 | loop fusion | flops 3932160 | bytes 5898240 | tf_op jit(solution)/shard_map/convert_element_type | solution.py:456
  111.9 0.2 collective-permute-start.11
  112.0 1.3 collective-permute-start.9
  113.4 0.7 collective-permute-start.14
  114.1 4.3 %collective-permute-done.16 = bf16[2,2,320,128]{3,2,1,0:T(8,128)(2,1)S(1)} collective-permute-done((bf16[2,2,320,128]{3,2,1,0:T(8,128)(2,1)S(1)}, bf16[2,2,320,128]{3,2,1,0:T(8,128)(2,1)S(1)}, u32[]{:S(2)}, u32[]{:S(2)}) %collective-permute-start.16) | collective-permute-done | bytes 327712 | tf_op jit(solution)/shard_map/ppermute | solution.py:455
  118.3 0.1 fusion.19
  118.4 1.3 collective-permute-start.17
  119.7 8.8 %collective-permute-done.11 = bf16[2,3,320,128]{3,2,1,0:T(8,128)(2,1)S(1)} collective-permute-done((bf16[2,3,320,128]{3,2,1,0:T(8,128)(2,1)S(1)}, bf16[2,3,320,128]{3,2,1,0:T(8,128)(2,1)S(1)}, u32[]{:S(2)}, u32[]{:S(2)}) %collective-permute-start.11) | collective-permute-done | bytes 491552 | tf_op jit(solution)/shard_map/ppermute | solution.py:455
  128.6 0.1 fusion.15
  128.7 0.8 collective-permute-start.12
  129.5 0.1 fusion.13
  129.6 1.1 collective-permute-start.10
  130.7 2.4 %collective-permute-done.14 = bf16[2,2,320,128]{3,2,1,0:T(8,128)(2,1)S(1)} collective-permute-done((bf16[2,2,320,128]{3,2,1,0:T(8,128)(2,1)S(1)}, bf16[2,2,320,128]{3,2,1,0:T(8,128)(2,1)S(1)}, u32[]{:S(2)}, u32[]{:S(2)}) %collective-permute-start.14) | collective-permute-done | bytes 327712 | tf_op jit(solution)/shard_map/ppermute | solution.py:455
  133.1 0.1 fusion.17
  133.2 2.0 %collective-permute-start.15 = (bf16[2,320,128]{2,1,0:T(8,128)(2,1)S(1)}, bf16[2,320,128]{2,1,0:T(8,128)(2,1)S(1)}, u32[]{:S(2)}, u32[]{:S(2)}) collective-permute-start(bf16[2,320,128]{2,1,0:T(8,128)(2,1)S(1)} %get-tuple-element.33), channel_id=1, source_target_pairs={{0,16},{4,20},{8,24},{12,28},{16,0},{20,4},{24,8},{28,12},{1,17},{... | collective-permute-start | bytes 491528 | tf_op jit(solution)/shard_map/ppermute | solution.py:455
  135.2 1.4 collective-permute-done.17.refs_7_
  136.7 3.6 %collective-permute-done.15.refs_5_ = bf16[2,320,128]{2,1,0:T(8,128)(2,1)S(1)} collective-permute-done((bf16[2,320,128]{2,1,0:T(8,128)(2,1)S(1)}, bf16[2,320,128]{2,1,0:T(8,128)(2,1)S(1)}, u32[]{:S(2)}, u32[]{:S(2)}) %collective-permute-start.15) | collective-permute-done | bytes 163872 | tf_op jit(solution)/shard_map/ppermute | solution.py:455
  140.2 0.8 collective-permute-done.12.refs_3_
  141.0 1.4 join_heads.1
  (37 shorter events, 0.2 us)
Async XLA Ops:
  7.2 63.5 %all-gather.3.cloned.1.call-start = ((), (), s32[]{:S(2)}) async-start(), calls=%async_computation.2 | async-start | bytes 7372800 | tf_op jit(solution)/shard_map/all_gather | solution.py:432
  7.9 134.5 %reduce-scatter.2.cloned.1.call-start = ((), (), s32[]{:S(2)}) async-start(), calls=%async_computation.1 | async-start | bytes 1474560 | tf_op jit(solution)/shard_map/reduce_scatter | solution.py:473
  8.9 20.8 %collective-permute-start.3 = (bf16[3,24,1024]{2,1,0:T(8,128)(2,1)S(1)}, bf16[3,24,1024]{2,1,0:T(8,128)(2,1)S(1)}, u32[]{:S(2)}, u32[]{:S(2)}) collective-permute-start(bf16[3,24,1024]{2,1,0:T(8,128)(2,1)S(1)} %get-tuple-element.37), channel_id=1, source_target_pairs={{4,0},{8,4},{12,8},{16,12},{20,16},{24,20},{28,24},{5,1},{9,5},{13... | collective-permute-start | bytes 442376 | tf_op jit(solution)/shard_map/ppermute | solution.py:440
  10.2 19.5 %collective-permute-start.1 = (bf16[3,24,1024]{2,1,0:T(8,128)(2,1)S(1)}, bf16[3,24,1024]{2,1,0:T(8,128)(2,1)S(1)}, u32[]{:S(2)}, u32[]{:S(2)}) collective-permute-start(bf16[3,24,1024]{2,1,0:T(8,128)(2,1)S(1)} %get-tuple-element.38), channel_id=1, source_target_pairs={{0,4},{4,8},{8,12},{12,16},{16,20},{20,24},{24,28},{1,5},{5,9},{9,... | collective-permute-start | bytes 442376 | tf_op jit(solution)/shard_map/ppermute | solution.py:439
  14.2 10.8 %collective-permute-start.4 = (bf16[3,6,1024]{2,1,0:T(8,128)(2,1)S(1)}, bf16[3,6,1024]{2,1,0:T(8,128)(2,1)S(1)}, u32[]{:S(2)}, u32[]{:S(2)}) collective-permute-start(bf16[3,6,1024]{2,1,0:T(8,128)(2,1)S(1)} %get-tuple-element.35), channel_id=1, source_target_pairs={{4,1},{5,2},{6,3},{7,0},{8,5},{9,6},{10,7},{11,4},{12,9},{13,10},{... | collective-permute-start | bytes 110600 | tf_op jit(solution)/shard_map/ppermute | solution.py:443
  15.5 9.5 %collective-permute-start.2 = (bf16[3,6,1024]{2,1,0:T(8,128)(2,1)S(1)}, bf16[3,6,1024]{2,1,0:T(8,128)(2,1)S(1)}, u32[]{:S(2)}, u32[]{:S(2)}) collective-permute-start(bf16[3,6,1024]{2,1,0:T(8,128)(2,1)S(1)} %get-tuple-element.36), channel_id=1, source_target_pairs={{0,5},{1,6},{2,7},{3,4},{4,9},{5,10},{6,11},{7,8},{8,13},{9,14},{1... | collective-permute-start | bytes 110600 | tf_op jit(solution)/shard_map/ppermute | solution.py:442
  23.2 6.5 %collective-permute-start = (bf16[6,6,1024]{2,1,0:T(8,128)(2,1)S(1)}, bf16[6,6,1024]{2,1,0:T(8,128)(2,1)S(1)}, u32[]{:S(2)}, u32[]{:S(2)}) collective-permute-start(bf16[6,6,1024]{2,1,0:T(8,128)(2,1)S(1)} %slice.121), channel_id=1, source_target_pairs={{0,1},{1,2},{2,3},{3,0},{4,5},{5,6},{6,7},{7,4},{8,9},{9,10},{10,1... | collective-permute-start | bytes 221192 | tf_op jit(solution)/shard_map/ppermute | solution.py:441
  29.7 0.7 copy-start.1
  30.4 11.9 %copy-start.11 = (f32[10,1024]{1,0:T(8,128)S(1)}, f32[10,1024]{1,0:T(8,128)}, u32[]{:S(2)}) copy-start(f32[10,1024]{1,0:T(8,128)} %param.18) | copy-start | bytes 122884
  30.4 11.9 %copy-start.12 = (f32[10,1024]{1,0:T(8,128)S(1)}, f32[10,1024]{1,0:T(8,128)}, u32[]{:S(2)}) copy-start(f32[10,1024]{1,0:T(8,128)} %param.19) | copy-start | bytes 122884
  30.4 36.7 %copy-start.5 = (bf16[576,576]{1,0:T(8,128)(2,1)S(1)}, bf16[576,576]{1,0:T(8,128)(2,1)}, u32[]{:S(2)}) copy-start(bf16[576,576]{1,0:T(8,128)(2,1)} %constant.16.clone.chosen) | copy-start | bytes 1990660
  39.2 31.5 %copy-start.2 = (s32[4]{0:T(128)S(1)}, s32[4]{0:T(128)}, u32[]{:S(2)}) copy-start(s32[4]{0:T(128)} %counts.3) | copy-start | bytes 52
  39.2 31.5 %copy-start.3 = (s32[1,4]{1,0:T(1,128)S(1)}, s32[1,4]{1,0:T(1,128)}, u32[]{:S(2)}) copy-start(s32[1,4]{1,0:T(1,128)} %datasets.3) | copy-start | bytes 52
  39.2 31.5 %copy-start.4 = (s32[10]{0:T(128)S(1)}, s32[10]{0:T(128)}, u32[]{:S(2)}) copy-start(s32[10]{0:T(128)} %levels.3) | copy-start | bytes 124
  39.2 31.5 %copy-start.6 = (s32[576,1]{1,0:T(8,128)S(1)}, s32[576,1]{1,0:T(8,128)}, u32[]{:S(2)}) copy-start(s32[576,1]{1,0:T(8,128)} %constant.17.clone.tile_of) | copy-start | bytes 6916
  39.3 10.6 %collective-permute-start.7 = (bf16[144,1024]{1,0:T(8,128)(2,1)S(1)}, bf16[144,1024]{1,0:T(8,128)(2,1)S(1)}, u32[]{:S(2)}, u32[]{:S(2)}) collective-permute-start(bf16[144,1024]{1,0:T(8,128)(2,1)S(1)} %window_attention.1.refs_0_), channel_id=1, source_target_pairs={{0,3},{1,0},{2,1},{3,2},{4,7},{5,4},{6,5},{7,6},{8,11},{9,8},{10,9... | collective-permute-start | bytes 884744 | tf_op jit(solution)/shard_map/ppermute | solution.py:449
  39.8 27.3 %collective-permute-start.6 = (bf16[144,1024]{1,0:T(8,128)(2,1)S(1)}, bf16[144,1024]{1,0:T(8,128)(2,1)S(1)}, u32[]{:S(2)}, u32[]{:S(2)}) collective-permute-start(bf16[144,1024]{1,0:T(8,128)(2,1)S(1)} %window_attention.1.refs_0_), channel_id=1, source_target_pairs={{0,2},{1,3},{2,0},{3,1},{4,6},{5,7},{6,4},{7,5},{8,10},{9,11},{10,... | collective-permute-start | bytes 884744 | tf_op jit(solution)/shard_map/ppermute | solution.py:449
  40.5 26.5 %collective-permute-start.5 = (bf16[144,1024]{1,0:T(8,128)(2,1)S(1)}, bf16[144,1024]{1,0:T(8,128)(2,1)S(1)}, u32[]{:S(2)}, u32[]{:S(2)}) collective-permute-start(bf16[144,1024]{1,0:T(8,128)(2,1)S(1)} %window_attention.1.refs_0_), channel_id=1, source_target_pairs={{0,1},{1,2},{2,3},{3,0},{4,5},{5,6},{6,7},{7,4},{8,9},{9,10},{10,1... | collective-permute-start | bytes 884744 | tf_op jit(solution)/shard_map/ppermute | solution.py:449
  69.7 1.0 copy-start.8
  70.7 1.3 copy-start.9
  72.0 16.5 %copy-start.7 = (s32[576,1]{1,0:T(8,128)S(1)}, s32[576,1]{1,0:T(8,128)}, u32[]{:S(2)}) copy-start(s32[576,1]{1,0:T(8,128)} %constant.17.clone.tile_of) | copy-start | bytes 6916
  72.0 16.5 %copy-start.10 = (bf16[576,1024]{1,0:T(8,128)(2,1)S(1)}, bf16[576,1024]{1,0:T(8,128)(2,1)}, u32[]{:S(2)}) copy-start(bf16[576,1024]{1,0:T(8,128)(2,1)} %copy-done.8) | copy-start | bytes 3538948
  88.3 21.4 %collective-permute-start.8 = (bf16[2,2,2,3,320,128]{5,4,3,2,1,0:T(8,128)(2,1)}, bf16[2,2,2,3,320,128]{5,4,3,2,1,0:T(8,128)(2,1)}, u32[]{:S(2)}, u32[]{:S(2)}) collective-permute-start(bf16[2,2,2,3,320,128]{5,4,3,2,1,0:T(8,128)(2,1)} %get-tuple-element.16), channel_id=1, source_target_pairs={{0,4},{4,0},{8,12},{12,8},{16,20},{20,16},{24,28},{28,24},{1,5},{5... | collective-permute-start | bytes 5898248 | tf_op jit(solution)/shard_map/ppermute | solution.py:455
  100.6 1.0 copy-start
  101.6 3.4 %collective-permute-start.13 = (bf16[2,2,2,2,320,128]{5,4,3,2,1,0:T(8,128)(2,1)}, bf16[2,2,2,2,320,128]{5,4,3,2,1,0:T(8,128)(2,1)}, u32[]{:S(2)}, u32[]{:S(2)}) collective-permute-start(bf16[2,2,2,2,320,128]{5,4,3,2,1,0:T(8,128)(2,1)} %get-tuple-element.18), channel_id=1, source_target_pairs={{0,4},{4,0},{8,12},{12,8},{16,20},{20,16},{24,28},{28,24},{1,5},{5... | collective-permute-start | bytes 3932168 | tf_op jit(solution)/shard_map/ppermute | solution.py:455
  106.7 11.7 %collective-permute-start.16 = (bf16[2,2,320,128]{3,2,1,0:T(8,128)(2,1)S(1)}, bf16[2,2,320,128]{3,2,1,0:T(8,128)(2,1)S(1)}, u32[]{:S(2)}, u32[]{:S(2)}) collective-permute-start(bf16[2,2,320,128]{3,2,1,0:T(8,128)(2,1)S(1)} %get-tuple-element.24), channel_id=1, source_target_pairs={{0,16},{4,20},{8,24},{12,28},{16,0},{20,4},{24,8},{28,12},{1,17},{... | collective-permute-start | bytes 983048 | tf_op jit(solution)/shard_map/ppermute | solution.py:455
  111.9 16.7 %collective-permute-start.11 = (bf16[2,3,320,128]{3,2,1,0:T(8,128)(2,1)S(1)}, bf16[2,3,320,128]{3,2,1,0:T(8,128)(2,1)S(1)}, u32[]{:S(2)}, u32[]{:S(2)}) collective-permute-start(bf16[2,3,320,128]{3,2,1,0:T(8,128)(2,1)S(1)} %get-tuple-element.20), channel_id=1, source_target_pairs={{0,16},{4,20},{8,24},{12,28},{16,0},{20,4},{24,8},{28,12},{1,17},{... | collective-permute-start | bytes 1474568 | tf_op jit(solution)/shard_map/ppermute | solution.py:455
  112.0 17.5 %collective-permute-start.9 = (bf16[2,3,320,128]{3,2,1,0:T(8,128)(2,1)S(1)}, bf16[2,3,320,128]{3,2,1,0:T(8,128)(2,1)S(1)}, u32[]{:S(2)}, u32[]{:S(2)}) collective-permute-start(bf16[2,3,320,128]{3,2,1,0:T(8,128)(2,1)S(1)} %get-tuple-element.21), channel_id=1, source_target_pairs={{0,8},{4,12},{8,0},{12,4},{16,24},{20,28},{24,16},{28,20},{1,9},{5... | collective-permute-start | bytes 1474568 | tf_op jit(solution)/shard_map/ppermute | solution.py:455
  113.4 19.8 %collective-permute-start.14 = (bf16[2,2,320,128]{3,2,1,0:T(8,128)(2,1)S(1)}, bf16[2,2,320,128]{3,2,1,0:T(8,128)(2,1)S(1)}, u32[]{:S(2)}, u32[]{:S(2)}) collective-permute-start(bf16[2,2,320,128]{3,2,1,0:T(8,128)(2,1)S(1)} %get-tuple-element.25), channel_id=1, source_target_pairs={{0,8},{4,12},{8,0},{12,4},{16,24},{20,28},{24,16},{28,20},{1,9},{5... | collective-permute-start | bytes 983048 | tf_op jit(solution)/shard_map/ppermute | solution.py:455
  118.4 18.2 %collective-permute-start.17 = (bf16[2,320,128]{2,1,0:T(8,128)(2,1)S(1)}, bf16[2,320,128]{2,1,0:T(8,128)(2,1)S(1)}, u32[]{:S(2)}, u32[]{:S(2)}) collective-permute-start(bf16[2,320,128]{2,1,0:T(8,128)(2,1)S(1)} %get-tuple-element.31), channel_id=1, source_target_pairs={{0,8},{4,12},{8,0},{12,4},{16,24},{20,28},{24,16},{28,20},{1,9},{5... | collective-permute-start | bytes 491528 | tf_op jit(solution)/shard_map/ppermute | solution.py:455
  128.7 12.3 %collective-permute-start.12 = (bf16[3,320,128]{2,1,0:T(8,128)(2,1)S(1)}, bf16[3,320,128]{2,1,0:T(8,128)(2,1)S(1)}, u32[]{:S(2)}, u32[]{:S(2)}) collective-permute-start(bf16[3,320,128]{2,1,0:T(8,128)(2,1)S(1)} %get-tuple-element.27), channel_id=1, source_target_pairs={{0,8},{4,12},{8,0},{12,4},{16,24},{20,28},{24,16},{28,20},{1,9},{5... | collective-permute-start | bytes 737288 | tf_op jit(solution)/shard_map/ppermute | solution.py:455
  129.6 11.4 %collective-permute-start.10 = (bf16[3,320,128]{2,1,0:T(8,128)(2,1)S(1)}, bf16[3,320,128]{2,1,0:T(8,128)(2,1)S(1)}, u32[]{:S(2)}, u32[]{:S(2)}) collective-permute-start(bf16[3,320,128]{2,1,0:T(8,128)(2,1)S(1)} %get-tuple-element.29), channel_id=1, source_target_pairs={{0,16},{4,20},{8,24},{12,28},{16,0},{20,4},{24,8},{28,12},{1,17},{... | collective-permute-start | bytes 737288 | tf_op jit(solution)/shard_map/ppermute | solution.py:455
  133.2 7.0 %collective-permute-start.15 = (bf16[2,320,128]{2,1,0:T(8,128)(2,1)S(1)}, bf16[2,320,128]{2,1,0:T(8,128)(2,1)S(1)}, u32[]{:S(2)}, u32[]{:S(2)}) collective-permute-start(bf16[2,320,128]{2,1,0:T(8,128)(2,1)S(1)} %get-tuple-element.33), channel_id=1, source_target_pairs={{0,16},{4,20},{8,24},{12,28},{16,0},{20,4},{24,8},{28,12},{1,17},{... | collective-permute-start | bytes 491528 | tf_op jit(solution)/shard_map/ppermute | solution.py:455
Sparse Core Ops, SparseCore 0:
  9.9 49.9 all-gather.2
  102.2 29.5 reduce-scatter.1

commit v6 on v5

--- a/solution.py
+++ b/solution.py
@@ -274,19 +274,14 @@
         to[k, outer, inner, 0] = turned[k, :, pl.ds(start, piece)]
 
 
-def scaled_rows(band, scale, shift, slot, rows):
-    for k in range(2):
-        rows[k][...] = (band[...].astype(F32) * scale[slot + k] + shift[slot + k]).astype(BF16)
-
-
-def add_back(lats, errs, gathered, scale, slot, total):
+def add_back(lats, errs, gathered, scale, total):
     piece = gathered.shape[-1]
     for l in range(0, lats, 2):
         lanes = slice(l * piece, (l + 2) * piece)
         term = 0.0
         for k in range(2):
             weight = jnp.concatenate([gathered[l, k], gathered[l + 1, k]], axis=1)
-            factor = scale[slot + k][:, lanes]
+            factor = scale[k][:, lanes]
             term = term + jnp.dot(errs[k], weight, preferred_element_type=F32) * factor
         total[:, lanes] += term
 
@@ -324,15 +319,15 @@
         for t in range(tiles):
             wanted = jnp.where(tile == t, counts[datasets[0, t]], wanted)
         tile_counts[...] = wanted
-        scaled_rows(band, scale, shift, slot, rows)
-
+
+    for k in range(2):
+        rows[k][...] = (band[...].astype(F32) * scale[k] + shift[k]).astype(BF16)
     for k in range(2):
         weight = jnp.concatenate([gathered[l, k] for l in range(lats)], axis=1)
         errs[k] = slot_errors(levels[slot + k], tile_counts[...], rows[k][...], weight, target[k])
     for k in range(2):
         head_halves(k, lats, place[0], errs[k], rows[k][...], turned, keep, send)
-    scaled_rows(band, scale, shift, first_slot + 2 * jnp.minimum(step + 1, steps - 1), rows)
-    add_back(lats, errs, gathered, scale, slot, total)
+    add_back(lats, errs, gathered, scale, total)
 
     if final:
 
@@ -347,13 +342,13 @@
 
 def slot_group(pair, pairs, lats, place, small, tile_of, band, scale, shift, gathered, targets, before):
     places, width = band.shape
-    slots, outs = targets.shape[0], targets.shape[-1]
+    outs = targets.shape[-1]
     tiles = small[1].shape[1]
     piece = width // lats
     smem = pl.BlockSpec(memory_space=pltpu.SMEM)
     halves = jax.ShapeDtypeStruct((2, 2, 2, pairs, outs, piece), BF16)
     half_spec = pl.BlockSpec((2, 2, 2, 1, outs, piece), lambda i: (0, 0, 0, i, 0, 0))
-    level_spec = pl.BlockSpec((slots, 1, width), lambda i: (0, 0, 0))
+    level_spec = pl.BlockSpec((2, 1, width), lambda i: (i + pair, 0, 0))
     sum_spec = pl.BlockSpec((places, width), lambda i: (0, 0))
     in_specs = [smem] * 4 + [
         pl.BlockSpec((places, 1), lambda i: (0, 0)),
@@ -385,12 +380,35 @@
         in_specs=in_specs,
         out_specs=(half_spec, half_spec, pl.BlockSpec(sums.shape, lambda i: (0,) * len(sums.shape))),
         scratch_shapes=scratch,
-        compiler_params=pltpu.CompilerParams(vmem_limit_bytes=VMEM_LIMIT),
+        compiler_params=pltpu.CompilerParams(vmem_limit_bytes=45 * 1024 * 1024),
         cost_estimate=pl.CostEstimate(
             flops=pairs * 12 * places * width * outs, bytes_accessed=pairs * 5_000_000, transcendentals=0
         ),
         name="slot_group",
     )(*args)
+
+
+def halve_kernel(keep, came, *refs):
+    outs = refs[-4:]
+    for k in range(2):
+        for half in range(2):
+            total = keep[k, half].astype(F32) + came[k, half].astype(F32)
+            outs[2 * half + k][...] = total.astype(BF16)
+
+
+def halve(keep, came, after):
+    part = jax.ShapeDtypeStruct(keep.shape[2:], BF16)
+    vmem = pl.BlockSpec(memory_space=pltpu.VMEM)
+    out = pl.pallas_call(
+        halve_kernel,
+        out_shape=(part,) * 4,
+        in_specs=[vmem, vmem] + [pl.BlockSpec(memory_space=pl.ANY)] * len(after),
+        out_specs=(vmem,) * 4,
+        compiler_params=pltpu.CompilerParams(vmem_limit_bytes=24 * 1024 * 1024),
+        cost_estimate=pl.CostEstimate(flops=2_000_000, bytes_accessed=6_000_000, transcendentals=0),
+        name="halve",
+    )(keep, came, *after)
+    return out[0:2], out[2:4]
 
 
 def join_kernel(norm, *refs):
@@ -455,24 +473,14 @@
     flip = lambda array, bit: lax.ppermute(array, "lat", [(i, i ^ bit) for i in range(lats)])
     add = lambda a, b: (a.astype(F32) + b.astype(F32)).astype(BF16)
     common = (lats, place, small, tile_of, band, scale3, shift3, gathered, targets)
-    most = slots // 4 + 1
-    rest = slots // 2 - most
+    most = slots // 2 - 1
     bits = (2, 4)
-
-    def halve(keep, send):
-        came = flip(send, 1)
-        return (
-            [add(keep[k, 0], came[k, 0]) for k in range(2)],
-            [add(keep[k, 1], came[k, 1]) for k in range(2)],
-        )
-
     keep_a, send_a, so_far = slot_group(0, most, *common, None)
-    keep_b, send_b, terms = slot_group(most, rest, *common, so_far)
-    kept_a, sent_a = halve(keep_a, send_a)
-    kept_b, sent_b = halve(keep_b, send_b)
+    keep_b, send_b, terms = slot_group(most, slots // 2 - most, *common, so_far)
     grad_latent = lax.psum_scatter(terms, "var", scatter_dimension=0, tiled=False)
-    pairs = []
-    for kept, sent in ((kept_a, sent_a), (kept_b, sent_b)):
+    pairs, came = [], [terms]
+    for keep, send in ((keep_a, send_a), (keep_b, send_b)):
+        kept, sent = halve(keep, flip(send, 1), came)
         came = [flip(sent[k], bits[k]) for k in range(2)]
         for k in range(2):
             last = flip(add(kept[k][1], came[k][1]), bits[1 - k])

time: 150 us -> 146 us (0.973)
  other arithmetic: 4.22 us -> 0.52 us
  waiting for transfers between devices: 54.5 us -> 57.3 us
  starting transfers between devices: 28.2 us -> 26.6 us
    convert_element_type x6 -> x4, other arithmetic: 4.14 us -> 0.44 us  [fast_local(): add = lambda a, b: (a.astype(F32) + b.astype(F32)).astype(BF16)]
    pallas_call x2, Pallas kernels: 28.5 us -> 25.4 us  [slot_group(): pl.pallas_call(functools.partial(slot_kernel, 2 * pair, lats, tiles, fina...]
    ppermute x10, waiting for transfers between devices: 24.3 us -> 27 us  [fast_local(): lax.ppermute(array, 'lat', [(i, i ^ bit) for i in range(lats)])]
    pallas_call x0 -> x2, Pallas kernels: none -> 2.55 us  [halve(): pl.pallas_call(halve_kernel, out_shape=(part,) * 4, in_specs=[vmem, vmem]...]
    ppermute x10, starting transfers between devices: 11.1 us -> 9.41 us  [fast_local(): lax.ppermute(array, 'lat', [(i, i ^ bit) for i in range(lats)])]
  transfers between devices with their start and end apart: 20 -> 20, of which waited for: 10 -> 8; matrix products, arithmetic and copies ran while one was open for 5% -> 2% of each run, Pallas kernels for 17% -> 15%
where the time goes in v6:
time: 146 us
  waiting for transfers between devices  57.3 us (39%)
  Pallas kernels  40.7 us (28%)
  starting transfers between devices  26.6 us (18%)
  between operations  14.2 us (10%)
  local copies, waits for them, and re-layouts  6.68 us (5%)
    ppermute x10, waiting for transfers between devices, fast_local(): lax.ppermute(array, 'lat', [(i, i ^ bit) for i in range(lats)])  27 us
    pallas_call x2, Pallas kernels, slot_group(): pl.pallas_call(functools.partial(slot_kernel, 2 * pair, lats, tiles, fina...  25.4 us
    ppermute x3, waiting for transfers between devices, fast_local(): lax.ppermute(mine, 'var', [(i, (i + s) % tiles) for i in range(tiles)])  24.7 us
    ppermute x10, starting transfers between devices, fast_local(): lax.ppermute(array, 'lat', [(i, i ^ bit) for i in range(lats)])  9.41 us
    pallas_call x1, Pallas kernels, attention(): pl.pallas_call(functools.partial(attention_kernel, bands), out_shape=jax....  8.78 us
    ppermute x1, starting transfers between devices, fast_local(): above_left = lax.ppermute(low[:, cols - HC:], ('lat', 'var'), both(up))  6.84 us
    ppermute x1, waiting for transfers between devices, fast_local(): left = lax.ppermute(patches[:, cols - HC:], 'var', right)  4.77 us
    unnamed x26, local copies, waits for them, and re-layouts  3.85 us
  transfers between devices with their start and end apart: 20, of which 8 were waited for; matrix products, arithmetic and copies ran while one was open for 2% of the time, Pallas kernels for 15%

profile of v6, /device:TPU:0, one launch (start us, length us, event | category | flops | bytes accessed | tf_op | source)
XLA Modules:
  0.0 146.0 jit_solution(5855751983335440360)
XLA Ops:
  7.2 0.0 all-gather.3.cloned.1.call-start
  7.2 0.7 all-gather.3.cloned.1.call-update
  7.9 0.0 reduce-scatter.2.cloned.1.call-start
  7.9 1.0 fusion.9
  8.9 1.3 collective-permute-start.3
  10.2 3.0 %collective-permute-start.1 = (bf16[3,24,1024]{2,1,0:T(8,128)(2,1)S(1)}, bf16[3,24,1024]{2,1,0:T(8,128)(2,1)S(1)}, u32[]{:S(2)}, u32[]{:S(2)}) collective-permute-start(bf16[3,24,1024]{2,1,0:T(8,128)(2,1)S(1)} %get-tuple-element.46), channel_id=1, source_target_pairs={{0,4},{4,8},{8,12},{12,16},{16,20},{20,24},{24,28},{1,5},{5,9},{9,... | collective-permute-start | bytes 442376 | tf_op jit(solution)/shard_map/ppermute | solution.py:457
  13.3 0.9 fusion.8
  14.2 1.3 collective-permute-start.4
  15.5 6.8 %collective-permute-start.2 = (bf16[3,6,1024]{2,1,0:T(8,128)(2,1)S(1)}, bf16[3,6,1024]{2,1,0:T(8,128)(2,1)S(1)}, u32[]{:S(2)}, u32[]{:S(2)}) collective-permute-start(bf16[3,6,1024]{2,1,0:T(8,128)(2,1)S(1)} %get-tuple-element.44), channel_id=1, source_target_pairs={{0,5},{1,6},{2,7},{3,4},{4,9},{5,10},{6,11},{7,8},{8,13},{9,14},{1... | collective-permute-start | bytes 110600 | tf_op jit(solution)/shard_map/ppermute | solution.py:460
  22.3 0.9 slice.65
  23.2 1.6 %collective-permute-start = (bf16[6,6,1024]{2,1,0:T(8,128)(2,1)S(1)}, bf16[6,6,1024]{2,1,0:T(8,128)(2,1)S(1)}, u32[]{:S(2)}, u32[]{:S(2)}) collective-permute-start(bf16[6,6,1024]{2,1,0:T(8,128)(2,1)S(1)} %slice.65), channel_id=1, source_target_pairs={{0,1},{1,2},{2,3},{3,0},{4,5},{5,6},{6,7},{7,4},{8,9},{9,10},{10,1... | collective-permute-start | bytes 221192 | tf_op jit(solution)/shard_map/ppermute | solution.py:459
  24.9 0.1 pad_add_fusion.place
  24.9 4.8 %collective-permute-done.left = bf16[6,6,1024]{2,1,0:T(8,128)(2,1)S(1)} collective-permute-done((bf16[6,6,1024]{2,1,0:T(8,128)(2,1)S(1)}, bf16[6,6,1024]{2,1,0:T(8,128)(2,1)S(1)}, u32[]{:S(2)}, u32[]{:S(2)}) %collective-permute-start) | collective-permute-done | bytes 73760 | tf_op jit(solution)/shard_map/ppermute | solution.py:459
  29.7 0.7 copy-done.9
  30.4 8.8 %window_attention.1.refs_0_ = bf16[144,1024]{1,0:T(8,128)(2,1)S(1)} custom-call(s32[2]{0:T(128)S(1)} %pad_add_fusion.place, bf16[6,6,1024]{2,1,0:T(8,128)(2,1)S(1)} %collective-permute-done.left, bf16[3,24,1024]{2,1,0:T(8,128)(2,1)S(1)} %collective-permute-done.1.above, bf16[3,6,1024]{2,1,0:T(8,128)(2,1)S(1)} %collective-permute-done.2.above_left, ...), custom_call_target="tpu_custom_call" | custom-call | flops 6000000000 | bytes 12000000 | tf_op jit(solution)/shard_map/window_attention/pallas_call | solution.py:178
  39.2 0.0 copy-start.2
  39.2 0.0 copy-start.5
  39.3 0.5 collective-permute-start.7
  39.8 0.8 collective-permute-start.6
  40.5 1.7 %collective-permute-start.5 = (bf16[144,1024]{1,0:T(8,128)(2,1)S(1)}, bf16[144,1024]{1,0:T(8,128)(2,1)S(1)}, u32[]{:S(2)}, u32[]{:S(2)}) collective-permute-start(bf16[144,1024]{1,0:T(8,128)(2,1)S(1)} %window_attention.1.refs_0_), channel_id=1, source_target_pairs={{0,1},{1,2},{2,3},{3,0},{4,5},{5,6},{6,7},{7,4},{8,9},{9,10},{10,1... | collective-permute-start | bytes 884744 | tf_op jit(solution)/shard_map/ppermute | solution.py:467
  42.3 7.6 %collective-permute-done.7.refs_3_ = bf16[144,1024]{1,0:T(8,128)(2,1)S(1)} collective-permute-done((bf16[144,1024]{1,0:T(8,128)(2,1)S(1)}, bf16[144,1024]{1,0:T(8,128)(2,1)S(1)}, u32[]{:S(2)}, u32[]{:S(2)}) %collective-permute-start.7) | collective-permute-done | bytes 294944 | tf_op jit(solution)/shard_map/ppermute | solution.py:467
  49.9 17.2 %collective-permute-done.6.refs_2_ = bf16[144,1024]{1,0:T(8,128)(2,1)S(1)} collective-permute-done((bf16[144,1024]{1,0:T(8,128)(2,1)S(1)}, bf16[144,1024]{1,0:T(8,128)(2,1)S(1)}, u32[]{:S(2)}, u32[]{:S(2)}) %collective-permute-start.6) | collective-permute-done | bytes 294944 | tf_op jit(solution)/shard_map/ppermute | solution.py:467
  67.1 2.6 %band_latents.1 = (bf16[576,1024]{1,0:T(8,128)(2,1)S(1)}, bf16[6,24,1024]{2,1,0:T(8,128)(2,1)}) custom-call(s32[2]{0:T(128)S(1)} %pad_add_fusion.place, bf16[576,576]{1,0:T(8,128)(2,1)S(1)} %copy-done.10, bf16[144,1024]{1,0:T(8,128)(2,1)S(1)} %window_attention.1.refs_0_, bf16[144,1024]{1,0:T(8,128)(2,1)S(1)} %collective-permute-done.5.refs_1_, ...), custom_call_target="tpu_custom_call" | custom-call | flops 679477248 | bytes 4000000 | tf_op jit(solution)/shard_map/band_latents/pallas_call | solution.py:238
  69.7 1.0 copy-done
  70.7 1.3 copy-done.1
  72.0 18.8 %slot_group.2 = (bf16[2,2,2,4,320,128]{5,4,3,2,1,0:T(8,128)(2,1)S(1)}, bf16[2,2,2,4,320,128]{5,4,3,2,1,0:T(8,128)(2,1)}, f32[576,1024]{1,0:T(8,128)S(1)}) custom-call(s32[2]{0:T(128)S(1)} %pad_add_fusion.place, s32[4]{0:T(128)S(1)} %copy-done.4, s32[1,4]{1,0:T(1,128)S(1)} %copy-done.5, s32[10]{0:T(128)S(1)} %copy-done.6, s32[576,1]{1,0:T(8,128)S(1)} %copy-done.2, ...), custom_call_target="tpu_custom_call" | custom-call | flops 9059696640 | bytes 20000000 | tf_op jit(solution)/shard_map/slot_group/pallas_call | solution.py:376
  90.7 0.1 collective-permute-start.8
  90.9 6.6 %slot_group.3 = (bf16[2,2,2,1,320,128]{5,4,3,2,1,0:T(8,128)(2,1)S(1)}, bf16[2,2,2,1,320,128]{5,4,3,2,1,0:T(8,128)(2,1)S(1)}, bf16[4,6,24,1024]{3,2,1,0:T(8,128)(2,1)}) custom-call(s32[2]{0:T(128)S(1)} %pad_add_fusion.place, s32[4]{0:T(128)S(1)} %copy-done.4, s32[1,4]{1,0:T(1,128)S(1)} %copy-done.5, s32[10]{0:T(128)S(1)} %copy-done.6, ...), custom_call_target="tpu_custom_call" | custom-call | flops 2264924160 | bytes 5000000 | tf_op jit(solution)/shard_map/slot_group/pallas_call | solution.py:376
  97.5 0.8 copy-done.7
  98.3 0.0 reduce-scatter.2.cloned.1.call-update
  98.4 2.4 %halve.2 = (bf16[2,4,320,128]{3,2,1,0:T(8,128)(2,1)S(1)}, bf16[2,4,320,128]{3,2,1,0:T(8,128)(2,1)S(1)}, bf16[2,4,320,128]{3,2,1,0:T(8,128)(2,1)S(1)}, bf16[2,4,320,128]{3,2,1,0:T(8,128)(2,1)S(1)}) custom-call(bf16[2,2,2,4,320,128]{5,4,3,2,1,0:T(8,128)(2,1)S(1)} %get-tuple-element.23.keep, bf16[2,2,2,4,320,128]{5,4,3,2,1,0:T(8,128)(2,1)} %collective-permute-done.8.came, ...), custom_call_target="tpu_custom_call" | custom-call | flops 2000000 | bytes 6000000 | tf_op jit(solution)/shard_map/halve/pallas_call | solution.py:402
  100.8 2.4 %collective-permute-start.9 = (bf16[2,4,320,128]{3,2,1,0:T(8,128)(2,1)S(1)}, bf16[2,4,320,128]{3,2,1,0:T(8,128)(2,1)S(1)}, u32[]{:S(2)}, u32[]{:S(2)}) collective-permute-start(bf16[2,4,320,128]{3,2,1,0:T(8,128)(2,1)S(1)} %get-tuple-element.26), channel_id=1, source_target_pairs={{0,8},{4,12},{8,0},{12,4},{16,24},{20,28},{24,16},{28,20},{1,9},{5... | collective-permute-start | bytes 1966088 | tf_op jit(solution)/shard_map/ppermute | solution.py:473
  103.2 1.2 collective-permute-start.11
  104.4 13.7 %collective-permute-done.9.refs_0_ = bf16[2,4,320,128]{3,2,1,0:T(8,128)(2,1)S(1)} collective-permute-done((bf16[2,4,320,128]{3,2,1,0:T(8,128)(2,1)S(1)}, bf16[2,4,320,128]{3,2,1,0:T(8,128)(2,1)S(1)}, u32[]{:S(2)}, u32[]{:S(2)}) %collective-permute-start.9) | collective-permute-done | bytes 655392 | tf_op jit(solution)/shard_map/ppermute | solution.py:473
  118.1 0.2 fusion.1
  118.2 2.9 %collective-permute-start.10 = (bf16[4,320,128]{2,1,0:T(8,128)(2,1)S(1)}, bf16[4,320,128]{2,1,0:T(8,128)(2,1)S(1)}, u32[]{:S(2)}, u32[]{:S(2)}) collective-permute-start(bf16[4,320,128]{2,1,0:T(8,128)(2,1)S(1)} %get-tuple-element.37), channel_id=1, source_target_pairs={{0,16},{4,20},{8,24},{12,28},{16,0},{20,4},{24,8},{28,12},{1,17},{... | collective-permute-start | bytes 983048 | tf_op jit(solution)/shard_map/ppermute | solution.py:473
  121.2 0.2 halve.3
  121.3 0.4 collective-permute-start.14
  121.7 1.5 %collective-permute-start.16 = (bf16[2,1,320,128]{3,2,1,0:T(8,128)(2,1)S(1)}, bf16[2,1,320,128]{3,2,1,0:T(8,128)(2,1)S(1)}, u32[]{:S(2)}, u32[]{:S(2)}) collective-permute-start(bf16[2,1,320,128]{3,2,1,0:T(8,128)(2,1)S(1)} %get-tuple-element.34), channel_id=1, source_target_pairs={{0,16},{4,20},{8,24},{12,28},{16,0},{20,4},{24,8},{28,12},{1,17},{... | collective-permute-start | bytes 491528 | tf_op jit(solution)/shard_map/ppermute | solution.py:473
  123.2 0.2 fusion.3
  123.3 0.3 collective-permute-start.12
  123.7 4.8 %collective-permute-done.14 = bf16[2,1,320,128]{3,2,1,0:T(8,128)(2,1)S(1)} collective-permute-done((bf16[2,1,320,128]{3,2,1,0:T(8,128)(2,1)S(1)}, bf16[2,1,320,128]{3,2,1,0:T(8,128)(2,1)S(1)}, u32[]{:S(2)}, u32[]{:S(2)}) %collective-permute-start.14) | collective-permute-done | bytes 163872 | tf_op jit(solution)/shard_map/ppermute | solution.py:473
  128.6 0.1 collective-permute-start.15
  128.6 4.6 %collective-permute-done.16 = bf16[2,1,320,128]{3,2,1,0:T(8,128)(2,1)S(1)} collective-permute-done((bf16[2,1,320,128]{3,2,1,0:T(8,128)(2,1)S(1)}, bf16[2,1,320,128]{3,2,1,0:T(8,128)(2,1)S(1)}, u32[]{:S(2)}, u32[]{:S(2)}) %collective-permute-start.16) | collective-permute-done | bytes 163872 | tf_op jit(solution)/shard_map/ppermute | solution.py:473
  133.2 0.6 collective-permute-start.17
  133.8 0.3 collective-permute-done.15.refs_5_
  134.1 3.7 %collective-permute-done.17.refs_7_ = bf16[1,320,128]{2,1,0:T(8,128)(2,1)S(1)} collective-permute-done((bf16[1,320,128]{2,1,0:T(8,128)(2,1)S(1)}, bf16[1,320,128]{2,1,0:T(8,128)(2,1)S(1)}, u32[]{:S(2)}, u32[]{:S(2)}) %collective-permute-start.17) | collective-permute-done | bytes 81952 | tf_op jit(solution)/shard_map/ppermute | solution.py:473
  137.8 1.4 join_heads.1
  (37 shorter events, 0.2 us)
Async XLA Ops:
  7.2 63.5 %all-gather.3.cloned.1.call-start = ((), (), s32[]{:S(2)}) async-start(), calls=%async_computation.2 | async-start | bytes 7372800 | tf_op jit(solution)/shard_map/all_gather | solution.py:450
  7.9 131.2 %reduce-scatter.2.cloned.1.call-start = ((), (), s32[]{:S(2)}) async-start(), calls=%async_computation.1 | async-start | bytes 1474560 | tf_op jit(solution)/shard_map/reduce_scatter | solution.py:480
  8.9 20.8 %collective-permute-start.3 = (bf16[3,24,1024]{2,1,0:T(8,128)(2,1)S(1)}, bf16[3,24,1024]{2,1,0:T(8,128)(2,1)S(1)}, u32[]{:S(2)}, u32[]{:S(2)}) collective-permute-start(bf16[3,24,1024]{2,1,0:T(8,128)(2,1)S(1)} %get-tuple-element.45), channel_id=1, source_target_pairs={{4,0},{8,4},{12,8},{16,12},{20,16},{24,20},{28,24},{5,1},{9,5},{13... | collective-permute-start | bytes 442376 | tf_op jit(solution)/shard_map/ppermute | solution.py:458
  10.2 19.5 %collective-permute-start.1 = (bf16[3,24,1024]{2,1,0:T(8,128)(2,1)S(1)}, bf16[3,24,1024]{2,1,0:T(8,128)(2,1)S(1)}, u32[]{:S(2)}, u32[]{:S(2)}) collective-permute-start(bf16[3,24,1024]{2,1,0:T(8,128)(2,1)S(1)} %get-tuple-element.46), channel_id=1, source_target_pairs={{0,4},{4,8},{8,12},{12,16},{16,20},{20,24},{24,28},{1,5},{5,9},{9,... | collective-permute-start | bytes 442376 | tf_op jit(solution)/shard_map/ppermute | solution.py:457
  14.2 10.8 %collective-permute-start.4 = (bf16[3,6,1024]{2,1,0:T(8,128)(2,1)S(1)}, bf16[3,6,1024]{2,1,0:T(8,128)(2,1)S(1)}, u32[]{:S(2)}, u32[]{:S(2)}) collective-permute-start(bf16[3,6,1024]{2,1,0:T(8,128)(2,1)S(1)} %get-tuple-element.43), channel_id=1, source_target_pairs={{4,1},{5,2},{6,3},{7,0},{8,5},{9,6},{10,7},{11,4},{12,9},{13,10},{... | collective-permute-start | bytes 110600 | tf_op jit(solution)/shard_map/ppermute | solution.py:461
  15.5 9.5 %collective-permute-start.2 = (bf16[3,6,1024]{2,1,0:T(8,128)(2,1)S(1)}, bf16[3,6,1024]{2,1,0:T(8,128)(2,1)S(1)}, u32[]{:S(2)}, u32[]{:S(2)}) collective-permute-start(bf16[3,6,1024]{2,1,0:T(8,128)(2,1)S(1)} %get-tuple-element.44), channel_id=1, source_target_pairs={{0,5},{1,6},{2,7},{3,4},{4,9},{5,10},{6,11},{7,8},{8,13},{9,14},{1... | collective-permute-start | bytes 110600 | tf_op jit(solution)/shard_map/ppermute | solution.py:460
  23.2 6.5 %collective-permute-start = (bf16[6,6,1024]{2,1,0:T(8,128)(2,1)S(1)}, bf16[6,6,1024]{2,1,0:T(8,128)(2,1)S(1)}, u32[]{:S(2)}, u32[]{:S(2)}) collective-permute-start(bf16[6,6,1024]{2,1,0:T(8,128)(2,1)S(1)} %slice.65), channel_id=1, source_target_pairs={{0,1},{1,2},{2,3},{3,0},{4,5},{5,6},{6,7},{7,4},{8,9},{9,10},{10,1... | collective-permute-start | bytes 221192 | tf_op jit(solution)/shard_map/ppermute | solution.py:459
  29.7 0.7 copy-start.9
  30.4 11.9 %copy-start.11 = (f32[10,1024]{1,0:T(8,128)S(1)}, f32[10,1024]{1,0:T(8,128)}, u32[]{:S(2)}) copy-start(f32[10,1024]{1,0:T(8,128)} %param.18) | copy-start | bytes 122884
  30.4 11.9 %copy-start.12 = (f32[10,1024]{1,0:T(8,128)S(1)}, f32[10,1024]{1,0:T(8,128)}, u32[]{:S(2)}) copy-start(f32[10,1024]{1,0:T(8,128)} %param.19) | copy-start | bytes 122884
  30.4 36.7 %copy-start.10 = (bf16[576,576]{1,0:T(8,128)(2,1)S(1)}, bf16[576,576]{1,0:T(8,128)(2,1)}, u32[]{:S(2)}) copy-start(bf16[576,576]{1,0:T(8,128)(2,1)} %constant.16.clone.chosen) | copy-start | bytes 1990660
  39.2 31.5 %copy-start.2 = (s32[576,1]{1,0:T(8,128)S(1)}, s32[576,1]{1,0:T(8,128)}, u32[]{:S(2)}) copy-start(s32[576,1]{1,0:T(8,128)} %constant.17.clone.tile_of) | copy-start | bytes 6916
  39.2 31.5 %copy-start.4 = (s32[4]{0:T(128)S(1)}, s32[4]{0:T(128)}, u32[]{:S(2)}) copy-start(s32[4]{0:T(128)} %counts.3) | copy-start | bytes 52
  39.2 31.5 %copy-start.5 = (s32[1,4]{1,0:T(1,128)S(1)}, s32[1,4]{1,0:T(1,128)}, u32[]{:S(2)}) copy-start(s32[1,4]{1,0:T(1,128)} %datasets.3) | copy-start | bytes 52
  39.2 31.5 %copy-start.6 = (s32[10]{0:T(128)S(1)}, s32[10]{0:T(128)}, u32[]{:S(2)}) copy-start(s32[10]{0:T(128)} %levels.3) | copy-start | bytes 124
  39.3 10.6 %collective-permute-start.7 = (bf16[144,1024]{1,0:T(8,128)(2,1)S(1)}, bf16[144,1024]{1,0:T(8,128)(2,1)S(1)}, u32[]{:S(2)}, u32[]{:S(2)}) collective-permute-start(bf16[144,1024]{1,0:T(8,128)(2,1)S(1)} %window_attention.1.refs_0_), channel_id=1, source_target_pairs={{0,3},{1,0},{2,1},{3,2},{4,7},{5,4},{6,5},{7,6},{8,11},{9,8},{10,9... | collective-permute-start | bytes 884744 | tf_op jit(solution)/shard_map/ppermute | solution.py:467
  39.8 27.3 %collective-permute-start.6 = (bf16[144,1024]{1,0:T(8,128)(2,1)S(1)}, bf16[144,1024]{1,0:T(8,128)(2,1)S(1)}, u32[]{:S(2)}, u32[]{:S(2)}) collective-permute-start(bf16[144,1024]{1,0:T(8,128)(2,1)S(1)} %window_attention.1.refs_0_), channel_id=1, source_target_pairs={{0,2},{1,3},{2,0},{3,1},{4,6},{5,7},{6,4},{7,5},{8,10},{9,11},{10,... | collective-permute-start | bytes 884744 | tf_op jit(solution)/shard_map/ppermute | solution.py:467
  40.5 26.5 %collective-permute-start.5 = (bf16[144,1024]{1,0:T(8,128)(2,1)S(1)}, bf16[144,1024]{1,0:T(8,128)(2,1)S(1)}, u32[]{:S(2)}, u32[]{:S(2)}) collective-permute-start(bf16[144,1024]{1,0:T(8,128)(2,1)S(1)} %window_attention.1.refs_0_), channel_id=1, source_target_pairs={{0,1},{1,2},{2,3},{3,0},{4,5},{5,6},{6,7},{7,4},{8,9},{9,10},{10,1... | collective-permute-start | bytes 884744 | tf_op jit(solution)/shard_map/ppermute | solution.py:467
  69.7 1.0 copy-start
  70.7 1.3 copy-start.1
  72.0 18.9 %copy-start.3 = (s32[576,1]{1,0:T(8,128)S(1)}, s32[576,1]{1,0:T(8,128)}, u32[]{:S(2)}) copy-start(s32[576,1]{1,0:T(8,128)} %constant.17.clone.tile_of) | copy-start | bytes 6916
  90.7 7.6 %collective-permute-start.8 = (bf16[2,2,2,4,320,128]{5,4,3,2,1,0:T(8,128)(2,1)}, bf16[2,2,2,4,320,128]{5,4,3,2,1,0:T(8,128)(2,1)}, u32[]{:S(2)}, u32[]{:S(2)}) collective-permute-start(bf16[2,2,2,4,320,128]{5,4,3,2,1,0:T(8,128)(2,1)} %get-tuple-element.24), channel_id=1, source_target_pairs={{0,4},{4,0},{8,12},{12,8},{16,20},{20,16},{24,28},{28,24},{1,5},{5... | collective-permute-start | bytes 7864328 | tf_op jit(solution)/shard_map/ppermute | solution.py:473
  97.5 0.8 copy-start.7
  98.4 4.8 %copy-start.8 = (bf16[2,2,2,1,320,128]{5,4,3,2,1,0:T(8,128)(2,1)S(1)}, bf16[2,2,2,1,320,128]{5,4,3,2,1,0:T(8,128)(2,1)}, u32[]{:S(2)}) copy-start(bf16[2,2,2,1,320,128]{5,4,3,2,1,0:T(8,128)(2,1)} %copy-done.7) | copy-start | bytes 1966084
  100.8 17.3 %collective-permute-start.9 = (bf16[2,4,320,128]{3,2,1,0:T(8,128)(2,1)S(1)}, bf16[2,4,320,128]{3,2,1,0:T(8,128)(2,1)S(1)}, u32[]{:S(2)}, u32[]{:S(2)}) collective-permute-start(bf16[2,4,320,128]{3,2,1,0:T(8,128)(2,1)S(1)} %get-tuple-element.26), channel_id=1, source_target_pairs={{0,8},{4,12},{8,0},{12,4},{16,24},{20,28},{24,16},{28,20},{1,9},{5... | collective-permute-start | bytes 1966088 | tf_op jit(solution)/shard_map/ppermute | solution.py:473
  103.2 18.0 %collective-permute-start.13 = (bf16[2,2,2,1,320,128]{5,4,3,2,1,0:T(8,128)(2,1)S(1)}, bf16[2,2,2,1,320,128]{5,4,3,2,1,0:T(8,128)(2,1)S(1)}, u32[]{:S(2)}, u32[]{:S(2)}) collective-permute-start(bf16[2,2,2,1,320,128]{5,4,3,2,1,0:T(8,128)(2,1)S(1)} %copy-done.8), channel_id=1, source_target_pairs={{0,4},{4,0},{8,12},{12,8},{16,20},{20,16},{24,28},{28,24},{1,5},{5... | collective-permute-start | bytes 1966088 | tf_op jit(solution)/shard_map/ppermute | solution.py:473
  103.2 18.0 %collective-permute-start.11 = (bf16[2,4,320,128]{3,2,1,0:T(8,128)(2,1)S(1)}, bf16[2,4,320,128]{3,2,1,0:T(8,128)(2,1)S(1)}, u32[]{:S(2)}, u32[]{:S(2)}) collective-permute-start(bf16[2,4,320,128]{3,2,1,0:T(8,128)(2,1)S(1)} %get-tuple-element.28), channel_id=1, source_target_pairs={{0,16},{4,20},{8,24},{12,28},{16,0},{20,4},{24,8},{28,12},{1,17},{... | collective-permute-start | bytes 1966088 | tf_op jit(solution)/shard_map/ppermute | solution.py:473
  118.2 19.5 %collective-permute-start.10 = (bf16[4,320,128]{2,1,0:T(8,128)(2,1)S(1)}, bf16[4,320,128]{2,1,0:T(8,128)(2,1)S(1)}, u32[]{:S(2)}, u32[]{:S(2)}) collective-permute-start(bf16[4,320,128]{2,1,0:T(8,128)(2,1)S(1)} %get-tuple-element.37), channel_id=1, source_target_pairs={{0,16},{4,20},{8,24},{12,28},{16,0},{20,4},{24,8},{28,12},{1,17},{... | collective-permute-start | bytes 983048 | tf_op jit(solution)/shard_map/ppermute | solution.py:473
  121.3 7.2 %collective-permute-start.14 = (bf16[2,1,320,128]{3,2,1,0:T(8,128)(2,1)S(1)}, bf16[2,1,320,128]{3,2,1,0:T(8,128)(2,1)S(1)}, u32[]{:S(2)}, u32[]{:S(2)}) collective-permute-start(bf16[2,1,320,128]{3,2,1,0:T(8,128)(2,1)S(1)} %get-tuple-element.32), channel_id=1, source_target_pairs={{0,8},{4,12},{8,0},{12,4},{16,24},{20,28},{24,16},{28,20},{1,9},{5... | collective-permute-start | bytes 491528 | tf_op jit(solution)/shard_map/ppermute | solution.py:473
  121.7 11.5 %collective-permute-start.16 = (bf16[2,1,320,128]{3,2,1,0:T(8,128)(2,1)S(1)}, bf16[2,1,320,128]{3,2,1,0:T(8,128)(2,1)S(1)}, u32[]{:S(2)}, u32[]{:S(2)}) collective-permute-start(bf16[2,1,320,128]{3,2,1,0:T(8,128)(2,1)S(1)} %get-tuple-element.34), channel_id=1, source_target_pairs={{0,16},{4,20},{8,24},{12,28},{16,0},{20,4},{24,8},{28,12},{1,17},{... | collective-permute-start | bytes 491528 | tf_op jit(solution)/shard_map/ppermute | solution.py:473
  123.3 14.4 %collective-permute-start.12 = (bf16[4,320,128]{2,1,0:T(8,128)(2,1)S(1)}, bf16[4,320,128]{2,1,0:T(8,128)(2,1)S(1)}, u32[]{:S(2)}, u32[]{:S(2)}) collective-permute-start(bf16[4,320,128]{2,1,0:T(8,128)(2,1)S(1)} %get-tuple-element.35), channel_id=1, source_target_pairs={{0,8},{4,12},{8,0},{12,4},{16,24},{20,28},{24,16},{28,20},{1,9},{5... | collective-permute-start | bytes 983048 | tf_op jit(solution)/shard_map/ppermute | solution.py:473
  128.6 5.5 %collective-permute-start.15 = (bf16[1,320,128]{2,1,0:T(8,128)(2,1)S(1)}, bf16[1,320,128]{2,1,0:T(8,128)(2,1)S(1)}, u32[]{:S(2)}, u32[]{:S(2)}) collective-permute-start(bf16[1,320,128]{2,1,0:T(8,128)(2,1)S(1)} %get-tuple-element.41), channel_id=1, source_target_pairs={{0,16},{4,20},{8,24},{12,28},{16,0},{20,4},{24,8},{28,12},{1,17},{... | collective-permute-start | bytes 245768 | tf_op jit(solution)/shard_map/ppermute | solution.py:473
  133.2 4.5 %collective-permute-start.17 = (bf16[1,320,128]{2,1,0:T(8,128)(2,1)S(1)}, bf16[1,320,128]{2,1,0:T(8,128)(2,1)S(1)}, u32[]{:S(2)}, u32[]{:S(2)}) collective-permute-start(bf16[1,320,128]{2,1,0:T(8,128)(2,1)S(1)} %get-tuple-element.39), channel_id=1, source_target_pairs={{0,8},{4,12},{8,0},{12,4},{16,24},{20,28},{24,16},{28,20},{1,9},{5... | collective-permute-start | bytes 245768 | tf_op jit(solution)/shard_map/ppermute | solution.py:473
Sparse Core Ops, SparseCore 0:
  9.9 49.9 all-gather.2
  98.5 29.5 reduce-scatter.1

commit v7 on v6

--- a/solution.py
+++ b/solution.py
@@ -16,63 +16,34 @@
 HR = WH // 2
 HC = WW // 2
 QP = 48
-LEFT = 8
 VMEM_LIMIT = 48 * 1024 * 1024
 F32 = jnp.float32
 BF16 = jnp.bfloat16
 
 
-def source_base(cols):
-    own = 0
-    left = own + WH * cols
-    above = left + WH * LEFT
-    above_left = above + HR * cols
-    below = above_left + HR * LEFT
-    below_left = below + HR * cols
-    total = below_left + HR * LEFT
-    return own, left, above, above_left, below, below_left, total
-
-
 def gather_maps(cols):
-    own, left, above, above_left, below, below_left, total = source_base(cols)
     win_cols = cols // WW
     windows = 2 * win_cols
-
-    def source(part, win_row, row, col):
-        if part == 0:
-            r = win_row * HR + row
-            return left + r * LEFT + col if col < HC else own + r * cols + col - HC
-        if win_row == 0:
-            return above_left + row * LEFT + col if col < HC else above + row * cols + col - HC
-        return below_left + row * LEFT + col if col < HC else below + row * cols + col - HC
-
-    into = np.zeros((windows * 2 * QP, total), np.float32)
-    keep = np.zeros((WH * cols, total), np.float32)
+    into = np.zeros((windows * 2 * QP, 2 * WH * cols), np.float32)
     back = np.zeros((WH * cols, windows * QP), np.float32)
     for win in range(windows):
         win_row, win_col = divmod(win, win_cols)
-        for part in range(2):
-            for row in range(HR):
-                for c in range(WW):
-                    at = source(part, win_row, row, win_col * WW + c)
-                    slot = row * WW + c
-                    into[win * 2 * QP + part * QP + slot, at] = 1
-                    if part == 0:
-                        natural = (win_row * HR + row) * cols + win_col * WW + c
-                        keep[natural, at] = 1
-                        back[natural, win * QP + slot] = 1
-    return into, keep, back
+        for row in range(HR):
+            for c in range(WW):
+                own = (win_row * HR + row) * cols + win_col * WW + c
+                slot = row * WW + c
+                into[win * 2 * QP + slot, own] = 1
+                into[win * 2 * QP + QP + slot, WH * cols + own] = 1
+                back[own, win * QP + slot] = 1
+    return into, back
 
 
 def attention_kernel(
     bands,
     place,
-    left,
+    own,
     above,
-    above_left,
     below,
-    below_left,
-    own_hbm,
     gain,
     maps_hbm,
     in_hbm,
@@ -81,7 +52,6 @@
     raw,
     qkv,
     attn,
-    own,
     maps,
     proj_in,
     proj_out,
@@ -89,38 +59,30 @@
 ):
     moves = [
         pltpu.make_async_copy(src, dst, sems.at[i])
-        for i, (src, dst) in enumerate(
-            ((own_hbm, own), (maps_hbm, maps), (in_hbm, proj_in), (out_hbm, proj_out))
-        )
+        for i, (src, dst) in enumerate(((maps_hbm, maps), (in_hbm, proj_in), (out_hbm, proj_out)))
     ]
     for move in moves:
         move.start()
     cols, width = own.shape[1], own.shape[2]
-    bases = source_base(cols)
-    total = bases[-1]
     win_cols = cols // WW
     windows = 2 * win_cols
     slots = windows * 2 * QP
     head_size = width // HEADS
     quad = 256 // head_size
-    for base, ref in zip(bases, (own, left, above, above_left, below, below_left)):
-        count = ref.shape[0]
-        if ref is own:
-            moves[0].wait()
-        if ref.shape[1] == cols:
-            raw[base : base + count * cols, :] = ref[...].astype(F32).reshape(count * cols, width)
-        else:
-            for r in range(count):
-                raw[base + r * LEFT : base + (r + 1) * LEFT, :] = jnp.zeros((LEFT, width), F32)
-                raw[base + r * LEFT : base + r * LEFT + HC, :] = ref[r].astype(F32)
+    size = WH * cols
+    start = 0
+    for ref in (own, above, below):
+        count = ref.shape[0] * cols
+        raw[start : start + count, :] = ref[...].astype(F32).reshape(count, width)
+        start += count
     wide = raw[...]
     average = jnp.mean(wide, axis=-1, keepdims=True)
     centred = wide - average
     variance = jnp.mean(centred * centred, axis=-1, keepdims=True)
     normed = (centred * lax.rsqrt(variance + EPS) * gain[...]).astype(BF16)
+    moves[0].wait()
+    win_x = jnp.dot(maps[0:slots, :], normed, preferred_element_type=F32).astype(BF16)
     moves[1].wait()
-    win_x = jnp.dot(maps[0:slots, :], normed, preferred_element_type=F32).astype(BF16)
-    moves[2].wait()
     step = 512
     for j in range(3 * width // step):
         part = slice(j * step, (j + 1) * step)
@@ -156,39 +118,35 @@
             for h in range(1, quad):
                 chosen = chosen + mixed[h * QP : (h + 1) * QP] * heads[h]
             attn[win * QP : (win + 1) * QP, lanes] = chosen.astype(BF16)
-    size = WH * cols
-    keep = maps[slots : slots + size, :]
-    back = maps[slots + size : slots + 2 * size, 0 : windows * QP]
+    back = maps[slots : slots + size, 0 : windows * QP]
     ordered = jnp.dot(back, attn[...], preferred_element_type=F32).astype(BF16)
-    residual = jnp.dot(keep, raw[...].astype(BF16), preferred_element_type=F32)
-    moves[3].wait()
+    moves[2].wait()
     update = jnp.dot(ordered, proj_out[...], preferred_element_type=F32)
-    out[...] = (residual + update).astype(BF16)
-
-
-def attention(place, patches, pieces, gain, proj_in, proj_out, bands):
-    rows, cols, width = patches.shape
-    into, keep, back = gather_maps(cols)
-    total = source_base(cols)[-1]
+    out[...] = (raw[0:size, :] + update).astype(BF16)
+
+
+def attention(place, pieces, gain, proj_in, proj_out, bands):
+    rows, cols, width = pieces[0].shape
+    into, back = gather_maps(cols)
+    total = into.shape[1]
     windows = 2 * (cols // WW)
     back = np.pad(back, ((0, 0), (0, total - back.shape[1])))
-    maps = np.concatenate([into, keep, back])
+    maps = np.concatenate([into, back])
     vmem = pl.BlockSpec(memory_space=pltpu.VMEM)
     hbm = pl.BlockSpec(memory_space=pltpu.HBM)
     return pl.pallas_call(
         functools.partial(attention_kernel, bands),
         out_shape=jax.ShapeDtypeStruct((rows * cols, width), BF16),
-        in_specs=[pl.BlockSpec(memory_space=pltpu.SMEM)] + [vmem] * 5 + [hbm, vmem, hbm, hbm, hbm],
+        in_specs=[pl.BlockSpec(memory_space=pltpu.SMEM)] + [vmem] * 4 + [hbm] * 3,
         out_specs=vmem,
         scratch_shapes=[
             pltpu.VMEM((total, width), F32),
             pltpu.VMEM((windows * 2 * QP, 3 * width), BF16),
             pltpu.VMEM((windows * QP, width), BF16),
-            pltpu.VMEM(patches.shape, BF16),
             pltpu.VMEM(maps.shape, BF16),
             pltpu.VMEM(proj_in.shape, BF16),
             pltpu.VMEM(proj_out.shape, BF16),
-            pltpu.SemaphoreType.DMA((4,)),
+            pltpu.SemaphoreType.DMA((3,)),
         ],
         compiler_params=pltpu.CompilerParams(vmem_limit_bytes=53 * 1024 * 1024),
         cost_estimate=pl.CostEstimate(
@@ -198,7 +156,6 @@
     )(
         place,
         *pieces,
-        patches,
         gain.reshape(1, width),
         jnp.asarray(maps, BF16),
         proj_in,
@@ -216,10 +173,8 @@
     return chosen
 
 
-def band_kernel(tiles, cols, place, chosen, *refs):
-    pieces, (band, latent, laid, wide) = refs[:tiles], refs[tiles:]
+def order_band(tiles, cols, var, chosen, pieces, laid, wide, band, latent):
     size = WH * cols
-    var = place[1]
     for s in range(tiles):
         tile = lax.rem(var + tiles - s, tiles)
         laid[pl.ds(pl.multiple_of(tile * size, 16), size), :] = pieces[s][...]
@@ -228,28 +183,6 @@
     for r in range(WH):
         start = pl.multiple_of(r * tiles * cols + var * cols, 8)
         latent[r] = wide[pl.ds(start, cols), :].astype(BF16)
-
-
-def band_latents(place, pieces, cols):
-    tiles = len(pieces)
-    width = pieces[0].shape[1]
-    total = WH * tiles * cols
-    vmem = pl.BlockSpec(memory_space=pltpu.VMEM)
-    return pl.pallas_call(
-        functools.partial(band_kernel, tiles, cols),
-        out_shape=(
-            jax.ShapeDtypeStruct((total, width), BF16),
-            jax.ShapeDtypeStruct((WH, cols, width), BF16),
-        ),
-        in_specs=[pl.BlockSpec(memory_space=pltpu.SMEM)] + [vmem] * (tiles + 1),
-        out_specs=(vmem, vmem),
-        scratch_shapes=[pltpu.VMEM((total, width), BF16), pltpu.VMEM((total, width), F32)],
-        compiler_params=pltpu.CompilerParams(vmem_limit_bytes=VMEM_LIMIT),
-        cost_estimate=pl.CostEstimate(
-            flops=2 * total * total * width, bytes_accessed=4_000_000, transcendentals=0
-        ),
-        name="band_latents",
-    )(place, jnp.asarray(band_map(tiles, cols), BF16), *pieces)
 
 
 def slot_errors(level, tile_counts, rows, weight, target):
@@ -296,7 +229,6 @@
     datasets,
     levels,
     tile_of,
-    band,
     scale,
     shift,
     gathered,
@@ -304,16 +236,21 @@
     *refs,
 ):
     if final:
-        before, keep, send, out, total, rows0, rows1, errs, turned, tile_counts = refs
+        band, before, keep, send, out, total, rows0, rows1, errs, turned, tile_counts = refs
     else:
-        keep, send, total, rows0, rows1, errs, turned, tile_counts = refs
+        chosen, pieces = refs[0], refs[1 : 1 + tiles]
+        keep, send, total, band, latent, rows0, rows1, errs, turned, tile_counts = refs[1 + tiles :]
     rows = (rows0, rows1)
     step, steps = pl.program_id(0), pl.num_programs(0)
     slot = first_slot + 2 * step
 
     @pl.when(step == 0)
     def _():
-        total[...] = before[...] if final else jnp.zeros_like(total)
+        if final:
+            total[...] = before[...]
+        else:
+            order_band(tiles, latent.shape[1], place[1], chosen, pieces, rows0, total, band, latent)
+            total[...] = jnp.zeros_like(total)
         tile = tile_of[...]
         wanted = jnp.zeros_like(tile)
         for t in range(tiles):
@@ -340,25 +277,25 @@
                     out[s, r] = total[start : start + cols, :].astype(BF16)
 
 
-def slot_group(pair, pairs, lats, place, small, tile_of, band, scale, shift, gathered, targets, before):
-    places, width = band.shape
+def slot_group(pair, pairs, lats, place, small, tile_of, scale, shift, gathered, targets, pieces, before):
+    places, width = tile_of.shape[0], scale.shape[-1]
     outs = targets.shape[-1]
     tiles = small[1].shape[1]
     piece = width // lats
+    cols = places // (WH * tiles)
     smem = pl.BlockSpec(memory_space=pltpu.SMEM)
+    fixed = lambda shape: pl.BlockSpec(shape, lambda i: (0,) * len(shape))
     halves = jax.ShapeDtypeStruct((2, 2, 2, pairs, outs, piece), BF16)
     half_spec = pl.BlockSpec((2, 2, 2, 1, outs, piece), lambda i: (0, 0, 0, i, 0, 0))
     level_spec = pl.BlockSpec((2, 1, width), lambda i: (i + pair, 0, 0))
-    sum_spec = pl.BlockSpec((places, width), lambda i: (0, 0))
     in_specs = [smem] * 4 + [
-        pl.BlockSpec((places, 1), lambda i: (0, 0)),
-        sum_spec,
+        fixed(tile_of.shape),
         level_spec,
         level_spec,
         pl.BlockSpec((lats, 2, outs, piece), lambda i: (0, i + pair, 0, 0)),
         pl.BlockSpec((2,) + targets.shape[1:], lambda i: (i + pair, 0, 0, 0)),
     ]
-    args = [place, *small, tile_of, band, scale, shift, gathered, targets]
+    args = [place, *small, tile_of, scale, shift, gathered, targets]
     final = before is not None
     scratch = [
         pltpu.VMEM((places, width), BF16),
@@ -369,18 +306,26 @@
     ]
     sums = jax.ShapeDtypeStruct((places, width), F32)
     if final:
-        in_specs.append(sum_spec)
-        args.append(before)
+        args.extend(before)
         scratch.insert(0, pltpu.VMEM(sums.shape, F32))
-        sums = jax.ShapeDtypeStruct((tiles, WH, places // (WH * tiles), width), BF16)
+        results = [jax.ShapeDtypeStruct((tiles, WH, cols, width), BF16)]
+    else:
+        args.extend([jnp.asarray(band_map(tiles, cols), BF16), *pieces])
+        results = [
+            sums,
+            jax.ShapeDtypeStruct((places, width), BF16),
+            jax.ShapeDtypeStruct((WH, cols, width), BF16),
+        ]
+    in_specs.extend(fixed(arg.shape) for arg in args[len(in_specs) :])
+    limit = (45 if final else 48) * 1024 * 1024
     return pl.pallas_call(
         functools.partial(slot_kernel, 2 * pair, lats, tiles, final),
         grid=(pairs,),
-        out_shape=(halves, halves, sums),
+        out_shape=(halves, halves, *results),
         in_specs=in_specs,
-        out_specs=(half_spec, half_spec, pl.BlockSpec(sums.shape, lambda i: (0,) * len(sums.shape))),
+        out_specs=(half_spec, half_spec, *(fixed(r.shape) for r in results)),
         scratch_shapes=scratch,
-        compiler_params=pltpu.CompilerParams(vmem_limit_bytes=45 * 1024 * 1024),
+        compiler_params=pltpu.CompilerParams(vmem_limit_bytes=limit),
         cost_estimate=pl.CostEstimate(
             flops=pairs * 12 * places * width * outs, bytes_accessed=pairs * 5_000_000, transcendentals=0
         ),
@@ -452,31 +397,25 @@
     right = [(i, (i + 1) % tiles) for i in range(tiles)]
     up = [(i, i + 1) for i in range(lats - 1)]
     down = [(i + 1, i) for i in range(lats - 1)]
-    both = lambda pairs: [(a * tiles + c, b * tiles + d) for a, b in pairs for c, d in right]
-    low, high = patches[HR:], patches[:HR]
-    above = lax.ppermute(low, "lat", up)
-    below = lax.ppermute(high, "lat", down)
     left = lax.ppermute(patches[:, cols - HC :], "var", right)
-    above_left = lax.ppermute(low[:, cols - HC :], ("lat", "var"), both(up))
-    below_left = lax.ppermute(high[:, cols - HC :], ("lat", "var"), both(down))
-    mine = attention(
-        place, patches, (left, above, above_left, below, below_left), norm_gain, input_proj, output_proj, lats
-    )
+    shifted = jnp.concatenate([left, patches[:, : cols - HC]], axis=1)
+    above = lax.ppermute(shifted[HR:], "lat", up)
+    below = lax.ppermute(shifted[:HR], "lat", down)
+    mine = attention(place, (shifted, above, below), norm_gain, input_proj, output_proj, lats)
     pieces = [mine]
     for s in range(1, tiles):
         pieces.append(lax.ppermute(mine, "var", [(i, (i + s) % tiles) for i in range(tiles)]))
-    band, latent = band_latents(place, pieces, cols)
 
     tile_of = jnp.asarray(np.arange(rows * tiles * cols)[:, None] % (tiles * cols) // cols, jnp.int32)
     scale3, shift3 = level_scale.reshape(slots, 1, width), level_shift.reshape(slots, 1, width)
     small = (level_counts, tile_dataset, slot_level)
     flip = lambda array, bit: lax.ppermute(array, "lat", [(i, i ^ bit) for i in range(lats)])
     add = lambda a, b: (a.astype(F32) + b.astype(F32)).astype(BF16)
-    common = (lats, place, small, tile_of, band, scale3, shift3, gathered, targets)
+    common = (lats, place, small, tile_of, scale3, shift3, gathered, targets)
     most = slots // 2 - 1
     bits = (2, 4)
-    keep_a, send_a, so_far = slot_group(0, most, *common, None)
-    keep_b, send_b, terms = slot_group(most, slots // 2 - most, *common, so_far)
+    keep_a, send_a, so_far, band, latent = slot_group(0, most, *common, pieces, None)
+    keep_b, send_b, terms = slot_group(most, slots // 2 - most, *common, None, (band, so_far))
     grad_latent = lax.psum_scatter(terms, "var", scatter_dimension=0, tiled=False)
     pairs, came = [], [terms]
     for keep, send in ((keep_a, send_a), (keep_b, send_b)):

time: 146 us -> 139 us (0.952)
  local copies, waits for them, and re-layouts: 6.68 us -> 2.55 us
  starting transfers between devices: 26.6 us -> 22.9 us
  other arithmetic: 0.52 us -> 2.66 us
  Pallas kernels: 40.7 us -> 39.1 us
    ppermute x4 -> x2, starting transfers between devices: 12.5 us -> 4.33 us  [the longest x1 3.04 us: fast_local(): above = lax.ppermute(shifted[HR:], 'lat', up)]
    ppermute x10, starting transfers between devices: 9.41 us -> 12.5 us  [fast_local(): lax.ppermute(array, 'lat', [(i, i ^ bit) for i in range(lats)])]
    all_gather x1, waiting for transfers between devices: 0.01 us -> 2.84 us  [fast_local(): lax.all_gather(jnp.transpose(head_weight, (0, 2, 1)), 'lat', axis=0, tile...]
    ppermute x3, waiting for transfers between devices: 24.7 us -> 22.1 us  [fast_local(): lax.ppermute(mine, 'var', [(i, (i + s) % tiles) for i in range(tiles)])]
    pallas_call x1 -> x0, Pallas kernels: 2.59 us -> none  [band_latents(): pl.pallas_call(functools.partial(band_kernel, tiles, cols), out_shape=(ja...]
    unnamed x26 -> x24, local copies, waits for them, and re-layouts: 3.85 us -> 1.57 us
    concatenate x0 -> x2, other arithmetic: none -> 2.14 us  [fast_local(): shifted = jnp.concatenate([left, patches[:, :cols - HC]], axis=1)]
    slice x2 -> x0, local copies, waits for them, and re-layouts: 1.86 us -> none  [the longest x1 1 us: fast_local(): low, high = (patches[HR:], patches[:HR])]
  transfers between devices with their start and end apart: 20 -> 18, of which waited for: 8 -> 8; matrix products, arithmetic and copies ran while one was open for 2% -> 3% of each run, Pallas kernels for 15% -> 14%
where the time goes in v7:
time: 139 us
  waiting for transfers between devices  57.3 us (41%)
  Pallas kernels  39.1 us (28%)
  starting transfers between devices  22.9 us (16%)
  between operations  14.2 us (10%)
  other arithmetic  2.66 us (2%)
  local copies, waits for them, and re-layouts  2.55 us (2%)
    ppermute x10, waiting for transfers between devices, fast_local(): lax.ppermute(array, 'lat', [(i, i ^ bit) for i in range(lats)])  26.8 us
    pallas_call x2, Pallas kernels, slot_group(): pl.pallas_call(functools.partial(slot_kernel, 2 * pair, lats, tiles, fina...  26.8 us
    ppermute x3, waiting for transfers between devices, fast_local(): lax.ppermute(mine, 'var', [(i, (i + s) % tiles) for i in range(tiles)])  22.1 us
    ppermute x10, starting transfers between devices, fast_local(): lax.ppermute(array, 'lat', [(i, i ^ bit) for i in range(lats)])  12.5 us
    pallas_call x1, Pallas kernels, attention(): pl.pallas_call(functools.partial(attention_kernel, bands), out_shape=jax....  8.42 us
    ppermute x1, waiting for transfers between devices, fast_local(): left = lax.ppermute(patches[:, cols - HC:], 'var', right)  4.82 us
    ppermute x1, starting transfers between devices, fast_local(): left = lax.ppermute(patches[:, cols - HC:], 'var', right)  3.08 us
    ppermute x1, starting transfers between devices, fast_local(): above = lax.ppermute(shifted[HR:], 'lat', up)  3.04 us
  transfers between devices with their start and end apart: 18, of which 8 were waited for; matrix products, arithmetic and copies ran while one was open for 3% of the time, Pallas kernels for 14%

profile of v7, /device:TPU:0, one launch (start us, length us, event | category | flops | bytes accessed | tf_op | source)
XLA Modules:
  0.0 138.7 jit_solution(8603650119650753603)
XLA Ops:
  7.2 0.0 all-gather.3.cloned.1.call-start
  7.2 0.7 all-gather.3.cloned.1.call-update
  7.9 0.0 reduce-scatter.2.cloned.1.call-start
  7.9 0.9 slice.60
  8.9 3.1 %collective-permute-start = (bf16[6,6,1024]{2,1,0:T(8,128)(2,1)S(1)}, bf16[6,6,1024]{2,1,0:T(8,128)(2,1)S(1)}, u32[]{:S(2)}, u32[]{:S(2)}) collective-permute-start(bf16[6,6,1024]{2,1,0:T(8,128)(2,1)S(1)} %slice.60), channel_id=1, source_target_pairs={{0,1},{1,2},{2,3},{3,0},{4,5},{5,6},{6,7},{7,4},{8,9},{9,10},{10,1... | collective-permute-start | bytes 221192 | tf_op jit(solution)/shard_map/ppermute | solution.py:400
  11.9 4.8 %collective-permute-done = bf16[6,6,1024]{2,1,0:T(8,128)(2,1)S(1)} collective-permute-done((bf16[6,6,1024]{2,1,0:T(8,128)(2,1)S(1)}, bf16[6,6,1024]{2,1,0:T(8,128)(2,1)S(1)}, u32[]{:S(2)}, u32[]{:S(2)}) %collective-permute-start) | collective-permute-done | bytes 73760 | tf_op jit(solution)/shard_map/ppermute | solution.py:400
  16.8 1.1 fusion.5
  17.8 1.3 collective-permute-start.2
  19.1 3.0 %collective-permute-start.1 = (bf16[3,24,1024]{2,1,0:T(8,128)(2,1)S(1)}, bf16[3,24,1024]{2,1,0:T(8,128)(2,1)S(1)}, u32[]{:S(2)}, u32[]{:S(2)}) collective-permute-start(bf16[3,24,1024]{2,1,0:T(8,128)(2,1)S(1)} %get-tuple-element.40), channel_id=1, source_target_pairs={{0,4},{4,8},{8,12},{12,16},{16,20},{20,24},{24,28},{1,5},{5,9},{9,... | collective-permute-start | bytes 442376 | tf_op jit(solution)/shard_map/ppermute | solution.py:402
  22.2 0.1 pad_add_fusion.place
  22.3 1.1 pad_maximum_fusion.own
  23.3 0.0 collective-permute-done.2.below
  23.4 0.0 copy-start.8
  23.4 0.7 copy-done.8
  24.1 0.0 copy-start.4
  24.1 0.0 copy-start.5
  24.1 0.0 copy-start.9
  24.1 8.4 %window_attention.1.refs_1_ = bf16[144,1024]{1,0:T(8,128)(2,1)S(1)} custom-call(s32[2]{0:T(128)S(1)} %pad_add_fusion.place, bf16[6,24,1024]{2,1,0:T(8,128)(2,1)S(1)} %pad_maximum_fusion.own, bf16[3,24,1024]{2,1,0:T(8,128)(2,1)S(1)} %collective-permute-done.1.above, bf16[3,24,1024]{2,1,0:T(8,128)(2,1)S(1)} %collective-permute-done.2.below, ...), custom_call_target="tpu_custom_call" | custom-call | flops 6000000000 | bytes 12000000 | tf_op jit(solution)/shard_map/window_attention/pallas_call | solution.py:137
  32.5 1.9 %collective-permute-start.5 = (bf16[144,1024]{1,0:T(8,128)(2,1)S(1)}, bf16[144,1024]{1,0:T(8,128)(2,1)S(1)}, u32[]{:S(2)}, u32[]{:S(2)}) collective-permute-start(bf16[144,1024]{1,0:T(8,128)(2,1)S(1)} %window_attention.1.refs_1_), channel_id=1, source_target_pairs={{0,3},{1,0},{2,1},{3,2},{4,7},{5,4},{6,5},{7,6},{8,11},{9,8},{10,9... | collective-permute-start | bytes 884744 | tf_op jit(solution)/shard_map/ppermute | solution.py:407
  34.4 1.0 collective-permute-start.3
  35.5 4.3 %collective-permute-done.5.refs_4_ = bf16[144,1024]{1,0:T(8,128)(2,1)S(1)} collective-permute-done((bf16[144,1024]{1,0:T(8,128)(2,1)S(1)}, bf16[144,1024]{1,0:T(8,128)(2,1)S(1)}, u32[]{:S(2)}, u32[]{:S(2)}) %collective-permute-start.5) | collective-permute-done | bytes 294944 | tf_op jit(solution)/shard_map/ppermute | solution.py:407
  39.8 17.7 %collective-permute-done.4.refs_3_ = bf16[144,1024]{1,0:T(8,128)(2,1)S(1)} collective-permute-done((bf16[144,1024]{1,0:T(8,128)(2,1)S(1)}, bf16[144,1024]{1,0:T(8,128)(2,1)S(1)}, u32[]{:S(2)}, u32[]{:S(2)}) %collective-permute-start.4) | collective-permute-done | bytes 294944 | tf_op jit(solution)/shard_map/ppermute | solution.py:407
  57.6 2.8 %all-gather.3.cloned.1.call-done = bf16[80,320,128]{2,1,0:T(8,128)(2,1)} async-done(((bf16[10,320,128]{2,1,0:T(8,128)(2,1)}), bf16[80,320,128]{2,1,0:T(8,128)(2,1)}) %all-gather.3.cloned.1.call-update) | async-done | bytes 6553616 | tf_op jit(solution)/shard_map/all_gather | solution.py:395
  60.4 0.0 copy-start.2
  60.5 20.1 %slot_group.2 = (bf16[2,2,2,4,320,128]{5,4,3,2,1,0:T(8,128)(2,1)}, bf16[2,2,2,4,320,128]{5,4,3,2,1,0:T(8,128)(2,1)}, f32[576,1024]{1,0:T(8,128)S(1)}, bf16[576,1024]{1,0:T(8,128)(2,1)S(1)}, bf16[6,24,1024]{2,1,0:T(8,128)(2,1)}) custom-call(s32[2]{0:T(128)S(1)} %pad_add_fusion.place, s32[4]{0:T(128)S(1)} %copy-done.3, s32[1,4]{1,0:T(1,128)S(1)} %copy-done.4, ...), custom_call_target="tpu_custom_call" | custom-call | flops 9059696640 | bytes 20000000 | tf_op jit(solution)/shard_map/slot_group/pallas_call | solution.py:321
  80.5 0.5 collective-permute-start.6
  81.0 6.7 %slot_group.3 = (bf16[2,2,2,1,320,128]{5,4,3,2,1,0:T(8,128)(2,1)S(1)}, bf16[2,2,2,1,320,128]{5,4,3,2,1,0:T(8,128)(2,1)S(1)}, bf16[4,6,24,1024]{3,2,1,0:T(8,128)(2,1)}) custom-call(s32[2]{0:T(128)S(1)} %pad_add_fusion.place, s32[4]{0:T(128)S(1)} %copy-done.3, s32[1,4]{1,0:T(1,128)S(1)} %copy-done.4, s32[10]{0:T(128)S(1)} %copy-done.5, ...), custom_call_target="tpu_custom_call" | custom-call | flops 2264924160 | bytes 5000000 | tf_op jit(solution)/shard_map/slot_group/pallas_call | solution.py:321
  87.7 0.8 copy-done.6
  88.6 0.0 reduce-scatter.2.cloned.1.call-update
  88.6 0.0 copy-start.7
  88.6 2.4 %halve.2 = (bf16[2,4,320,128]{3,2,1,0:T(8,128)(2,1)S(1)}, bf16[2,4,320,128]{3,2,1,0:T(8,128)(2,1)S(1)}, bf16[2,4,320,128]{3,2,1,0:T(8,128)(2,1)S(1)}, bf16[2,4,320,128]{3,2,1,0:T(8,128)(2,1)S(1)}) custom-call(bf16[2,2,2,4,320,128]{5,4,3,2,1,0:T(8,128)(2,1)S(1)} %copy-done, bf16[2,2,2,4,320,128]{5,4,3,2,1,0:T(8,128)(2,1)} %collective-permute-done.6.came, ...), custom_call_target="tpu_custom_call" | custom-call | flops 2000000 | bytes 6000000 | tf_op jit(solution)/shard_map/halve/pallas_call | solution.py:347
  91.0 5.3 %collective-permute-start.7 = (bf16[2,4,320,128]{3,2,1,0:T(8,128)(2,1)S(1)}, bf16[2,4,320,128]{3,2,1,0:T(8,128)(2,1)S(1)}, u32[]{:S(2)}, u32[]{:S(2)}) collective-permute-start(bf16[2,4,320,128]{3,2,1,0:T(8,128)(2,1)S(1)} %get-tuple-element.26), channel_id=1, source_target_pairs={{0,8},{4,12},{8,0},{12,4},{16,24},{20,28},{24,16},{28,20},{1,9},{5... | collective-permute-start | bytes 1966088 | tf_op jit(solution)/shard_map/ppermute | solution.py:412
  96.3 0.2 collective-permute-start.11
  96.5 0.4 collective-permute-start.9
  96.9 14.8 %collective-permute-done.7.refs_0_ = bf16[2,4,320,128]{3,2,1,0:T(8,128)(2,1)S(1)} collective-permute-done((bf16[2,4,320,128]{3,2,1,0:T(8,128)(2,1)S(1)}, bf16[2,4,320,128]{3,2,1,0:T(8,128)(2,1)S(1)}, u32[]{:S(2)}, u32[]{:S(2)}) %collective-permute-start.7) | collective-permute-done | bytes 655392 | tf_op jit(solution)/shard_map/ppermute | solution.py:412
  111.7 0.2 fusion.1
  111.9 1.8 %collective-permute-start.8 = (bf16[4,320,128]{2,1,0:T(8,128)(2,1)S(1)}, bf16[4,320,128]{2,1,0:T(8,128)(2,1)S(1)}, u32[]{:S(2)}, u32[]{:S(2)}) collective-permute-start(bf16[4,320,128]{2,1,0:T(8,128)(2,1)S(1)} %get-tuple-element.37), channel_id=1, source_target_pairs={{0,16},{4,20},{8,24},{12,28},{16,0},{20,4},{24,8},{28,12},{1,17},{... | collective-permute-start | bytes 983048 | tf_op jit(solution)/shard_map/ppermute | solution.py:412
  113.7 0.2 halve.3
  113.9 0.4 collective-permute-start.12
  114.2 1.7 %collective-permute-start.14 = (bf16[2,1,320,128]{3,2,1,0:T(8,128)(2,1)S(1)}, bf16[2,1,320,128]{3,2,1,0:T(8,128)(2,1)S(1)}, u32[]{:S(2)}, u32[]{:S(2)}) collective-permute-start(bf16[2,1,320,128]{3,2,1,0:T(8,128)(2,1)S(1)} %get-tuple-element.34), channel_id=1, source_target_pairs={{0,16},{4,20},{8,24},{12,28},{16,0},{20,4},{24,8},{28,12},{1,17},{... | collective-permute-start | bytes 491528 | tf_op jit(solution)/shard_map/ppermute | solution.py:412
  115.9 0.2 fusion.3
  116.1 0.4 collective-permute-start.10
  116.5 4.6 %collective-permute-done.12 = bf16[2,1,320,128]{3,2,1,0:T(8,128)(2,1)S(1)} collective-permute-done((bf16[2,1,320,128]{3,2,1,0:T(8,128)(2,1)S(1)}, bf16[2,1,320,128]{3,2,1,0:T(8,128)(2,1)S(1)}, u32[]{:S(2)}, u32[]{:S(2)}) %collective-permute-start.12) | collective-permute-done | bytes 163872 | tf_op jit(solution)/shard_map/ppermute | solution.py:412
  121.1 0.3 collective-permute-start.13
  121.4 4.5 %collective-permute-done.14 = bf16[2,1,320,128]{3,2,1,0:T(8,128)(2,1)S(1)} collective-permute-done((bf16[2,1,320,128]{3,2,1,0:T(8,128)(2,1)S(1)}, bf16[2,1,320,128]{3,2,1,0:T(8,128)(2,1)S(1)}, u32[]{:S(2)}, u32[]{:S(2)}) %collective-permute-start.14) | collective-permute-done | bytes 163872 | tf_op jit(solution)/shard_map/ppermute | solution.py:412
  126.0 1.6 %collective-permute-start.15 = (bf16[1,320,128]{2,1,0:T(8,128)(2,1)S(1)}, bf16[1,320,128]{2,1,0:T(8,128)(2,1)S(1)}, u32[]{:S(2)}, u32[]{:S(2)}) collective-permute-start(bf16[1,320,128]{2,1,0:T(8,128)(2,1)S(1)} %get-tuple-element.41), channel_id=1, source_target_pairs={{0,8},{4,12},{8,0},{12,4},{16,24},{20,28},{24,16},{28,20},{1,9},{5... | collective-permute-start | bytes 245768 | tf_op jit(solution)/shard_map/ppermute | solution.py:412
  127.6 2.9 %collective-permute-done.15.refs_7_ = bf16[1,320,128]{2,1,0:T(8,128)(2,1)S(1)} collective-permute-done((bf16[1,320,128]{2,1,0:T(8,128)(2,1)S(1)}, bf16[1,320,128]{2,1,0:T(8,128)(2,1)S(1)}, u32[]{:S(2)}, u32[]{:S(2)}) %collective-permute-start.15) | collective-permute-done | bytes 81952 | tf_op jit(solution)/shard_map/ppermute | solution.py:412
  130.5 1.4 join_heads.1
  (30 shorter events, 0.2 us)
Async XLA Ops:
  7.2 53.3 %all-gather.3.cloned.1.call-start = ((), (), s32[]{:S(2)}) async-start(), calls=%async_computation.2 | async-start | bytes 7372800 | tf_op jit(solution)/shard_map/all_gather | solution.py:395
  7.9 124.0 %reduce-scatter.2.cloned.1.call-start = ((), (), s32[]{:S(2)}) async-start(), calls=%async_computation.1 | async-start | bytes 1474560 | tf_op jit(solution)/shard_map/reduce_scatter | solution.py:419
  8.9 7.9 %collective-permute-start = (bf16[6,6,1024]{2,1,0:T(8,128)(2,1)S(1)}, bf16[6,6,1024]{2,1,0:T(8,128)(2,1)S(1)}, u32[]{:S(2)}, u32[]{:S(2)}) collective-permute-start(bf16[6,6,1024]{2,1,0:T(8,128)(2,1)S(1)} %slice.60), channel_id=1, source_target_pairs={{0,1},{1,2},{2,3},{3,0},{4,5},{5,6},{6,7},{7,4},{8,9},{9,10},{10,1... | collective-permute-start | bytes 221192 | tf_op jit(solution)/shard_map/ppermute | solution.py:400
  17.8 5.5 %collective-permute-start.2 = (bf16[3,24,1024]{2,1,0:T(8,128)(2,1)S(1)}, bf16[3,24,1024]{2,1,0:T(8,128)(2,1)S(1)}, u32[]{:S(2)}, u32[]{:S(2)}) collective-permute-start(bf16[3,24,1024]{2,1,0:T(8,128)(2,1)S(1)} %get-tuple-element.39), channel_id=1, source_target_pairs={{4,0},{8,4},{12,8},{16,12},{20,16},{24,20},{28,24},{5,1},{9,5},{13... | collective-permute-start | bytes 442376 | tf_op jit(solution)/shard_map/ppermute | solution.py:403
  19.1 4.2 %collective-permute-start.1 = (bf16[3,24,1024]{2,1,0:T(8,128)(2,1)S(1)}, bf16[3,24,1024]{2,1,0:T(8,128)(2,1)S(1)}, u32[]{:S(2)}, u32[]{:S(2)}) collective-permute-start(bf16[3,24,1024]{2,1,0:T(8,128)(2,1)S(1)} %get-tuple-element.40), channel_id=1, source_target_pairs={{0,4},{4,8},{8,12},{12,16},{16,20},{20,24},{24,28},{1,5},{5,9},{9,... | collective-permute-start | bytes 442376 | tf_op jit(solution)/shard_map/ppermute | solution.py:402
  23.4 0.7 copy-start.8
  24.0 11.4 %copy-start.10 = (f32[10,1024]{1,0:T(8,128)S(1)}, f32[10,1024]{1,0:T(8,128)}, u32[]{:S(2)}) copy-start(f32[10,1024]{1,0:T(8,128)} %param.18) | copy-start | bytes 122884
  24.0 11.4 %copy-start.11 = (f32[10,1024]{1,0:T(8,128)S(1)}, f32[10,1024]{1,0:T(8,128)}, u32[]{:S(2)}) copy-start(f32[10,1024]{1,0:T(8,128)} %param.19) | copy-start | bytes 122884
  24.1 36.4 %copy-start.1 = (s32[576,1]{1,0:T(8,128)S(1)}, s32[576,1]{1,0:T(8,128)}, u32[]{:S(2)}) copy-start(s32[576,1]{1,0:T(8,128)} %constant.16.clone.tile_of) | copy-start | bytes 6916
  24.1 36.4 %copy-start.3 = (s32[4]{0:T(128)S(1)}, s32[4]{0:T(128)}, u32[]{:S(2)}) copy-start(s32[4]{0:T(128)} %counts.3) | copy-start | bytes 52
  24.1 36.4 %copy-start.4 = (s32[1,4]{1,0:T(1,128)S(1)}, s32[1,4]{1,0:T(1,128)}, u32[]{:S(2)}) copy-start(s32[1,4]{1,0:T(1,128)} %datasets.3) | copy-start | bytes 52
  24.1 36.4 %copy-start.5 = (s32[10]{0:T(128)S(1)}, s32[10]{0:T(128)}, u32[]{:S(2)}) copy-start(s32[10]{0:T(128)} %levels.3) | copy-start | bytes 124
  24.1 36.3 %copy-start.9 = (bf16[576,576]{1,0:T(8,128)(2,1)S(1)}, bf16[576,576]{1,0:T(8,128)(2,1)}, u32[]{:S(2)}) copy-start(bf16[576,576]{1,0:T(8,128)(2,1)} %constant.17.clone.refs_0_) | copy-start | bytes 1990660
  32.5 7.3 %collective-permute-start.5 = (bf16[144,1024]{1,0:T(8,128)(2,1)S(1)}, bf16[144,1024]{1,0:T(8,128)(2,1)S(1)}, u32[]{:S(2)}, u32[]{:S(2)}) collective-permute-start(bf16[144,1024]{1,0:T(8,128)(2,1)S(1)} %window_attention.1.refs_1_), channel_id=1, source_target_pairs={{0,3},{1,0},{2,1},{3,2},{4,7},{5,4},{6,5},{7,6},{8,11},{9,8},{10,9... | collective-permute-start | bytes 884744 | tf_op jit(solution)/shard_map/ppermute | solution.py:407
  34.4 23.2 %collective-permute-start.4 = (bf16[144,1024]{1,0:T(8,128)(2,1)S(1)}, bf16[144,1024]{1,0:T(8,128)(2,1)S(1)}, u32[]{:S(2)}, u32[]{:S(2)}) collective-permute-start(bf16[144,1024]{1,0:T(8,128)(2,1)S(1)} %window_attention.1.refs_1_), channel_id=1, source_target_pairs={{0,2},{1,3},{2,0},{3,1},{4,6},{5,7},{6,4},{7,5},{8,10},{9,11},{10,... | collective-permute-start | bytes 884744 | tf_op jit(solution)/shard_map/ppermute | solution.py:407
  34.4 23.2 %collective-permute-start.3 = (bf16[144,1024]{1,0:T(8,128)(2,1)S(1)}, bf16[144,1024]{1,0:T(8,128)(2,1)S(1)}, u32[]{:S(2)}, u32[]{:S(2)}) collective-permute-start(bf16[144,1024]{1,0:T(8,128)(2,1)S(1)} %window_attention.1.refs_1_), channel_id=1, source_target_pairs={{0,1},{1,2},{2,3},{3,0},{4,5},{5,6},{6,7},{7,4},{8,9},{9,10},{10,1... | collective-permute-start | bytes 884744 | tf_op jit(solution)/shard_map/ppermute | solution.py:407
  60.4 20.6 %copy-start.2 = (s32[576,1]{1,0:T(8,128)S(1)}, s32[576,1]{1,0:T(8,128)}, u32[]{:S(2)}) copy-start(s32[576,1]{1,0:T(8,128)} %constant.16.clone.tile_of) | copy-start | bytes 6916
  80.5 8.1 %collective-permute-start.6 = (bf16[2,2,2,4,320,128]{5,4,3,2,1,0:T(8,128)(2,1)}, bf16[2,2,2,4,320,128]{5,4,3,2,1,0:T(8,128)(2,1)}, u32[]{:S(2)}, u32[]{:S(2)}) collective-permute-start(bf16[2,2,2,4,320,128]{5,4,3,2,1,0:T(8,128)(2,1)} %get-tuple-element.24), channel_id=1, source_target_pairs={{0,4},{4,0},{8,12},{12,8},{16,20},{20,16},{24,28},{28,24},{1,5},{5... | collective-permute-start | bytes 7864328 | tf_op jit(solution)/shard_map/ppermute | solution.py:412
  81.0 7.6 %copy-start = (bf16[2,2,2,4,320,128]{5,4,3,2,1,0:T(8,128)(2,1)S(1)}, bf16[2,2,2,4,320,128]{5,4,3,2,1,0:T(8,128)(2,1)}, u32[]{:S(2)}) copy-start(bf16[2,2,2,4,320,128]{5,4,3,2,1,0:T(8,128)(2,1)} %get-tuple-element.23.keep) | copy-start | bytes 7864324
  87.7 0.8 copy-start.6
  88.6 7.7 %copy-start.7 = (bf16[2,2,2,1,320,128]{5,4,3,2,1,0:T(8,128)(2,1)S(1)}, bf16[2,2,2,1,320,128]{5,4,3,2,1,0:T(8,128)(2,1)}, u32[]{:S(2)}) copy-start(bf16[2,2,2,1,320,128]{5,4,3,2,1,0:T(8,128)(2,1)} %copy-done.6) | copy-start | bytes 1966084
  91.0 20.7 %collective-permute-start.7 = (bf16[2,4,320,128]{3,2,1,0:T(8,128)(2,1)S(1)}, bf16[2,4,320,128]{3,2,1,0:T(8,128)(2,1)S(1)}, u32[]{:S(2)}, u32[]{:S(2)}) collective-permute-start(bf16[2,4,320,128]{3,2,1,0:T(8,128)(2,1)S(1)} %get-tuple-element.26), channel_id=1, source_target_pairs={{0,8},{4,12},{8,0},{12,4},{16,24},{20,28},{24,16},{28,20},{1,9},{5... | collective-permute-start | bytes 1966088 | tf_op jit(solution)/shard_map/ppermute | solution.py:412
  96.3 17.4 %collective-permute-start.11 = (bf16[2,2,2,1,320,128]{5,4,3,2,1,0:T(8,128)(2,1)S(1)}, bf16[2,2,2,1,320,128]{5,4,3,2,1,0:T(8,128)(2,1)S(1)}, u32[]{:S(2)}, u32[]{:S(2)}) collective-permute-start(bf16[2,2,2,1,320,128]{5,4,3,2,1,0:T(8,128)(2,1)S(1)} %copy-done.7), channel_id=1, source_target_pairs={{0,4},{4,0},{8,12},{12,8},{16,20},{20,16},{24,28},{28,24},{1,5},{5... | collective-permute-start | bytes 1966088 | tf_op jit(solution)/shard_map/ppermute | solution.py:412
  96.5 17.2 %collective-permute-start.9 = (bf16[2,4,320,128]{3,2,1,0:T(8,128)(2,1)S(1)}, bf16[2,4,320,128]{3,2,1,0:T(8,128)(2,1)S(1)}, u32[]{:S(2)}, u32[]{:S(2)}) collective-permute-start(bf16[2,4,320,128]{3,2,1,0:T(8,128)(2,1)S(1)} %get-tuple-element.28), channel_id=1, source_target_pairs={{0,16},{4,20},{8,24},{12,28},{16,0},{20,4},{24,8},{28,12},{1,17},{... | collective-permute-start | bytes 1966088 | tf_op jit(solution)/shard_map/ppermute | solution.py:412
  111.9 18.6 %collective-permute-start.8 = (bf16[4,320,128]{2,1,0:T(8,128)(2,1)S(1)}, bf16[4,320,128]{2,1,0:T(8,128)(2,1)S(1)}, u32[]{:S(2)}, u32[]{:S(2)}) collective-permute-start(bf16[4,320,128]{2,1,0:T(8,128)(2,1)S(1)} %get-tuple-element.37), channel_id=1, source_target_pairs={{0,16},{4,20},{8,24},{12,28},{16,0},{20,4},{24,8},{28,12},{1,17},{... | collective-permute-start | bytes 983048 | tf_op jit(solution)/shard_map/ppermute | solution.py:412
  113.9 7.2 %collective-permute-start.12 = (bf16[2,1,320,128]{3,2,1,0:T(8,128)(2,1)S(1)}, bf16[2,1,320,128]{3,2,1,0:T(8,128)(2,1)S(1)}, u32[]{:S(2)}, u32[]{:S(2)}) collective-permute-start(bf16[2,1,320,128]{3,2,1,0:T(8,128)(2,1)S(1)} %get-tuple-element.32), channel_id=1, source_target_pairs={{0,8},{4,12},{8,0},{12,4},{16,24},{20,28},{24,16},{28,20},{1,9},{5... | collective-permute-start | bytes 491528 | tf_op jit(solution)/shard_map/ppermute | solution.py:412
  114.2 11.7 %collective-permute-start.14 = (bf16[2,1,320,128]{3,2,1,0:T(8,128)(2,1)S(1)}, bf16[2,1,320,128]{3,2,1,0:T(8,128)(2,1)S(1)}, u32[]{:S(2)}, u32[]{:S(2)}) collective-permute-start(bf16[2,1,320,128]{3,2,1,0:T(8,128)(2,1)S(1)} %get-tuple-element.34), channel_id=1, source_target_pairs={{0,16},{4,20},{8,24},{12,28},{16,0},{20,4},{24,8},{28,12},{1,17},{... | collective-permute-start | bytes 491528 | tf_op jit(solution)/shard_map/ppermute | solution.py:412
  116.1 14.4 %collective-permute-start.10 = (bf16[4,320,128]{2,1,0:T(8,128)(2,1)S(1)}, bf16[4,320,128]{2,1,0:T(8,128)(2,1)S(1)}, u32[]{:S(2)}, u32[]{:S(2)}) collective-permute-start(bf16[4,320,128]{2,1,0:T(8,128)(2,1)S(1)} %get-tuple-element.35), channel_id=1, source_target_pairs={{0,8},{4,12},{8,0},{12,4},{16,24},{20,28},{24,16},{28,20},{1,9},{5... | collective-permute-start | bytes 983048 | tf_op jit(solution)/shard_map/ppermute | solution.py:412
  121.1 6.5 %collective-permute-start.13 = (bf16[1,320,128]{2,1,0:T(8,128)(2,1)S(1)}, bf16[1,320,128]{2,1,0:T(8,128)(2,1)S(1)}, u32[]{:S(2)}, u32[]{:S(2)}) collective-permute-start(bf16[1,320,128]{2,1,0:T(8,128)(2,1)S(1)} %get-tuple-element.43), channel_id=1, source_target_pairs={{0,16},{4,20},{8,24},{12,28},{16,0},{20,4},{24,8},{28,12},{1,17},{... | collective-permute-start | bytes 245768 | tf_op jit(solution)/shard_map/ppermute | solution.py:412
  126.0 4.5 %collective-permute-start.15 = (bf16[1,320,128]{2,1,0:T(8,128)(2,1)S(1)}, bf16[1,320,128]{2,1,0:T(8,128)(2,1)S(1)}, u32[]{:S(2)}, u32[]{:S(2)}) collective-permute-start(bf16[1,320,128]{2,1,0:T(8,128)(2,1)S(1)} %get-tuple-element.41), channel_id=1, source_target_pairs={{0,8},{4,12},{8,0},{12,4},{16,24},{20,28},{24,16},{28,20},{1,9},{5... | collective-permute-start | bytes 245768 | tf_op jit(solution)/shard_map/ppermute | solution.py:412
Sparse Core Ops, SparseCore 0:
  9.9 50.4 all-gather.2
  88.7 32.8 reduce-scatter.1

commit v8 on v7

--- a/solution.py
+++ b/solution.py
@@ -44,7 +44,7 @@
     own,
     above,
     below,
-    gain,
+    gain_hbm,
     maps_hbm,
     in_hbm,
     out_hbm,
@@ -52,6 +52,7 @@
     raw,
     qkv,
     attn,
+    gain,
     maps,
     proj_in,
     proj_out,
@@ -59,7 +60,9 @@
 ):
     moves = [
         pltpu.make_async_copy(src, dst, sems.at[i])
-        for i, (src, dst) in enumerate(((maps_hbm, maps), (in_hbm, proj_in), (out_hbm, proj_out)))
+        for i, (src, dst) in enumerate(
+            ((gain_hbm, gain), (maps_hbm, maps), (in_hbm, proj_in), (out_hbm, proj_out))
+        )
     ]
     for move in moves:
         move.start()
@@ -75,14 +78,15 @@
         count = ref.shape[0] * cols
         raw[start : start + count, :] = ref[...].astype(F32).reshape(count, width)
         start += count
+    moves[0].wait()
     wide = raw[...]
     average = jnp.mean(wide, axis=-1, keepdims=True)
     centred = wide - average
     variance = jnp.mean(centred * centred, axis=-1, keepdims=True)
     normed = (centred * lax.rsqrt(variance + EPS) * gain[...]).astype(BF16)
-    moves[0].wait()
+    moves[1].wait()
     win_x = jnp.dot(maps[0:slots, :], normed, preferred_element_type=F32).astype(BF16)
-    moves[1].wait()
+    moves[2].wait()
     step = 512
     for j in range(3 * width // step):
         part = slice(j * step, (j + 1) * step)
@@ -120,7 +124,7 @@
             attn[win * QP : (win + 1) * QP, lanes] = chosen.astype(BF16)
     back = maps[slots : slots + size, 0 : windows * QP]
     ordered = jnp.dot(back, attn[...], preferred_element_type=F32).astype(BF16)
-    moves[2].wait()
+    moves[3].wait()
     update = jnp.dot(ordered, proj_out[...], preferred_element_type=F32)
     out[...] = (raw[0:size, :] + update).astype(BF16)
 
@@ -137,16 +141,17 @@
     return pl.pallas_call(
         functools.partial(attention_kernel, bands),
         out_shape=jax.ShapeDtypeStruct((rows * cols, width), BF16),
-        in_specs=[pl.BlockSpec(memory_space=pltpu.SMEM)] + [vmem] * 4 + [hbm] * 3,
+        in_specs=[pl.BlockSpec(memory_space=pltpu.SMEM)] + [vmem] * 3 + [hbm] * 4,
         out_specs=vmem,
         scratch_shapes=[
             pltpu.VMEM((total, width), F32),
             pltpu.VMEM((windows * 2 * QP, 3 * width), BF16),
             pltpu.VMEM((windows * QP, width), BF16),
+            pltpu.VMEM((1, width), F32),
             pltpu.VMEM(maps.shape, BF16),
             pltpu.VMEM(proj_in.shape, BF16),
             pltpu.VMEM(proj_out.shape, BF16),
-            pltpu.SemaphoreType.DMA((3,)),
+            pltpu.SemaphoreType.DMA((4,)),
         ],
         compiler_params=pltpu.CompilerParams(vmem_limit_bytes=53 * 1024 * 1024),
         cost_estimate=pl.CostEstimate(
@@ -173,8 +178,10 @@
     return chosen
 
 
-def order_band(tiles, cols, var, chosen, pieces, laid, wide, band, latent):
+def band_kernel(tiles, cols, place, chosen, *refs):
+    pieces, (band, latent, laid, wide) = refs[:tiles], refs[tiles:]
     size = WH * cols
+    var = place[1]
     for s in range(tiles):
         tile = lax.rem(var + tiles - s, tiles)
         laid[pl.ds(pl.multiple_of(tile * size, 16), size), :] = pieces[s][...]
@@ -183,6 +190,28 @@
     for r in range(WH):
         start = pl.multiple_of(r * tiles * cols + var * cols, 8)
         latent[r] = wide[pl.ds(start, cols), :].astype(BF16)
+
+
+def band_latents(place, pieces, cols):
+    tiles = len(pieces)
+    width = pieces[0].shape[1]
+    total = WH * tiles * cols
+    vmem = pl.BlockSpec(memory_space=pltpu.VMEM)
+    return pl.pallas_call(
+        functools.partial(band_kernel, tiles, cols),
+        out_shape=(
+            jax.ShapeDtypeStruct((total, width), BF16),
+            jax.ShapeDtypeStruct((WH, cols, width), BF16),
+        ),
+        in_specs=[pl.BlockSpec(memory_space=pltpu.SMEM)] + [vmem] * (tiles + 1),
+        out_specs=(vmem, vmem),
+        scratch_shapes=[pltpu.VMEM((total, width), BF16), pltpu.VMEM((total, width), F32)],
+        compiler_params=pltpu.CompilerParams(vmem_limit_bytes=VMEM_LIMIT),
+        cost_estimate=pl.CostEstimate(
+            flops=2 * total * total * width, bytes_accessed=4_000_000, transcendentals=0
+        ),
+        name="band_latents",
+    )(place, jnp.asarray(band_map(tiles, cols), BF16), *pieces)
 
 
 def slot_errors(level, tile_counts, rows, weight, target):
@@ -238,19 +267,14 @@
     if final:
         band, before, keep, send, out, total, rows0, rows1, errs, turned, tile_counts = refs
     else:
-        chosen, pieces = refs[0], refs[1 : 1 + tiles]
-        keep, send, total, band, latent, rows0, rows1, errs, turned, tile_counts = refs[1 + tiles :]
+        band, keep, send, total, rows0, rows1, errs, turned, tile_counts = refs
     rows = (rows0, rows1)
     step, steps = pl.program_id(0), pl.num_programs(0)
     slot = first_slot + 2 * step
 
     @pl.when(step == 0)
     def _():
-        if final:
-            total[...] = before[...]
-        else:
-            order_band(tiles, latent.shape[1], place[1], chosen, pieces, rows0, total, band, latent)
-            total[...] = jnp.zeros_like(total)
+        total[...] = before[...] if final else jnp.zeros_like(total)
         tile = tile_of[...]
         wanted = jnp.zeros_like(tile)
         for t in range(tiles):
@@ -277,7 +301,7 @@
                     out[s, r] = total[start : start + cols, :].astype(BF16)
 
 
-def slot_group(pair, pairs, lats, place, small, tile_of, scale, shift, gathered, targets, pieces, before):
+def slot_group(pair, pairs, lats, place, small, tile_of, scale, shift, gathered, targets, band, before):
     places, width = tile_of.shape[0], scale.shape[-1]
     outs = targets.shape[-1]
     tiles = small[1].shape[1]
@@ -295,7 +319,7 @@
         pl.BlockSpec((lats, 2, outs, piece), lambda i: (0, i + pair, 0, 0)),
         pl.BlockSpec((2,) + targets.shape[1:], lambda i: (i + pair, 0, 0, 0)),
     ]
-    args = [place, *small, tile_of, scale, shift, gathered, targets]
+    args = [place, *small, tile_of, scale, shift, gathered, targets, band]
     final = before is not None
     scratch = [
         pltpu.VMEM((places, width), BF16),
@@ -306,18 +330,13 @@
     ]
     sums = jax.ShapeDtypeStruct((places, width), F32)
     if final:
-        args.extend(before)
+        args.append(before)
         scratch.insert(0, pltpu.VMEM(sums.shape, F32))
         results = [jax.ShapeDtypeStruct((tiles, WH, cols, width), BF16)]
     else:
-        args.extend([jnp.asarray(band_map(tiles, cols), BF16), *pieces])
-        results = [
-            sums,
-            jax.ShapeDtypeStruct((places, width), BF16),
-            jax.ShapeDtypeStruct((WH, cols, width), BF16),
-        ]
+        results = [sums]
     in_specs.extend(fixed(arg.shape) for arg in args[len(in_specs) :])
-    limit = (45 if final else 48) * 1024 * 1024
+    limit = (45 if final else 46) * 1024 * 1024
     return pl.pallas_call(
         functools.partial(slot_kernel, 2 * pair, lats, tiles, final),
         grid=(pairs,),
@@ -325,7 +344,9 @@
         in_specs=in_specs,
         out_specs=(half_spec, half_spec, *(fixed(r.shape) for r in results)),
         scratch_shapes=scratch,
-        compiler_params=pltpu.CompilerParams(vmem_limit_bytes=limit),
+        compiler_params=pltpu.CompilerParams(
+            vmem_limit_bytes=limit, fuse_transposed_lhs_in_matmul=True
+        ),
         cost_estimate=pl.CostEstimate(
             flops=pairs * 12 * places * width * outs, bytes_accessed=pairs * 5_000_000, transcendentals=0
         ),
@@ -406,16 +427,17 @@
     for s in range(1, tiles):
         pieces.append(lax.ppermute(mine, "var", [(i, (i + s) % tiles) for i in range(tiles)]))
 
+    band, latent = band_latents(place, pieces, cols)
     tile_of = jnp.asarray(np.arange(rows * tiles * cols)[:, None] % (tiles * cols) // cols, jnp.int32)
     scale3, shift3 = level_scale.reshape(slots, 1, width), level_shift.reshape(slots, 1, width)
     small = (level_counts, tile_dataset, slot_level)
     flip = lambda array, bit: lax.ppermute(array, "lat", [(i, i ^ bit) for i in range(lats)])
     add = lambda a, b: (a.astype(F32) + b.astype(F32)).astype(BF16)
-    common = (lats, place, small, tile_of, scale3, shift3, gathered, targets)
+    common = (lats, place, small, tile_of, scale3, shift3, gathered, targets, band)
     most = slots // 2 - 1
     bits = (2, 4)
-    keep_a, send_a, so_far, band, latent = slot_group(0, most, *common, pieces, None)
-    keep_b, send_b, terms = slot_group(most, slots // 2 - most, *common, None, (band, so_far))
+    keep_a, send_a, so_far = slot_group(0, most, *common, None)
+    keep_b, send_b, terms = slot_group(most, slots // 2 - most, *common, so_far)
     grad_latent = lax.psum_scatter(terms, "var", scatter_dimension=0, tiled=False)
     pairs, came = [], [terms]
     for keep, send in ((keep_a, send_a), (keep_b, send_b)):

time: 139 us -> 145 us (1.043)
  Pallas kernels: 39.1 us -> 42.6 us
  waiting for transfers between devices: 57.3 us -> 54.4 us
  starting transfers between devices: 22.9 us -> 25.7 us
  local copies, waits for them, and re-layouts: 2.55 us -> 4.83 us
    all_gather x1, waiting for transfers between devices: 2.84 us -> 0.01 us  [fast_local(): lax.all_gather(jnp.transpose(head_weight, (0, 2, 1)), 'lat', axis=0, tile...]
    ppermute x10, starting transfers between devices: 12.5 us -> 15.3 us  [fast_local(): lax.ppermute(array, 'lat', [(i, i ^ bit) for i in range(lats)])]
    pallas_call x0 -> x1, Pallas kernels: none -> 2.59 us  [band_latents(): pl.pallas_call(functools.partial(band_kernel, tiles, cols), out_shape=(ja...]
    unnamed x24 -> x28, local copies, waits for them, and re-layouts: 1.57 us -> 3.85 us
  transfers between devices with their start and end apart: 18 -> 18, of which waited for: 8 -> 7; matrix products, arithmetic and copies ran while one was open for 3% -> 3% of each run, Pallas kernels for 14% -> 15%
where the time goes in v8:
time: 145 us; the launch traced here: 144 us
  waiting for transfers between devices  54.4 us (38%)
  Pallas kernels  42.6 us (29%)
  starting transfers between devices  25.7 us (18%)
  between operations  14.2 us (10%)
  local copies, waits for them, and re-layouts  4.83 us (3%)
  other arithmetic  2.66 us (2%)
    pallas_call x2, Pallas kernels, slot_group(): pl.pallas_call(functools.partial(slot_kernel, 2 * pair, lats, tiles, fina...  27.6 us
    ppermute x10, waiting for transfers between devices, fast_local(): lax.ppermute(array, 'lat', [(i, i ^ bit) for i in range(lats)])  26.9 us
    ppermute x3, waiting for transfers between devices, fast_local(): lax.ppermute(mine, 'var', [(i, (i + s) % tiles) for i in range(tiles)])  22.1 us
    ppermute x10, starting transfers between devices, fast_local(): lax.ppermute(array, 'lat', [(i, i ^ bit) for i in range(lats)])  15.3 us
    pallas_call x1, Pallas kernels, attention(): pl.pallas_call(functools.partial(attention_kernel, bands), out_shape=jax....  8.43 us
    ppermute x1, waiting for transfers between devices, fast_local(): left = lax.ppermute(patches[:, cols - HC:], 'var', right)  4.82 us
    unnamed x28, local copies, waits for them, and re-layouts  3.85 us
    ppermute x1, starting transfers between devices, fast_local(): left = lax.ppermute(patches[:, cols - HC:], 'var', right)  3.08 us
  transfers between devices with their start and end apart: 18, of which 7 were waited for; matrix products, arithmetic and copies ran while one was open for 3% of the time, Pallas kernels for 15%

profile of v8, /device:TPU:0, one launch (start us, length us, event | category | flops | bytes accessed | tf_op | source)
XLA Modules:
  0.0 144.4 jit_solution(5611483802236258359)
XLA Ops:
  7.2 0.0 all-gather.3.cloned.1.call-start
  7.2 0.7 all-gather.3.cloned.1.call-update
  7.9 0.0 reduce-scatter.2.cloned.1.call-start
  7.9 0.9 slice.60
  8.9 3.1 %collective-permute-start = (bf16[6,6,1024]{2,1,0:T(8,128)(2,1)S(1)}, bf16[6,6,1024]{2,1,0:T(8,128)(2,1)S(1)}, u32[]{:S(2)}, u32[]{:S(2)}) collective-permute-start(bf16[6,6,1024]{2,1,0:T(8,128)(2,1)S(1)} %slice.60), channel_id=1, source_target_pairs={{0,1},{1,2},{2,3},{3,0},{4,5},{5,6},{6,7},{7,4},{8,9},{9,10},{10,1... | collective-permute-start | bytes 221192 | tf_op jit(solution)/shard_map/ppermute | solution.py:421
  11.9 4.8 %collective-permute-done = bf16[6,6,1024]{2,1,0:T(8,128)(2,1)S(1)} collective-permute-done((bf16[6,6,1024]{2,1,0:T(8,128)(2,1)S(1)}, bf16[6,6,1024]{2,1,0:T(8,128)(2,1)S(1)}, u32[]{:S(2)}, u32[]{:S(2)}) %collective-permute-start) | collective-permute-done | bytes 73760 | tf_op jit(solution)/shard_map/ppermute | solution.py:421
  16.8 1.1 fusion.5
  17.8 1.3 collective-permute-start.2
  19.1 3.0 %collective-permute-start.1 = (bf16[3,24,1024]{2,1,0:T(8,128)(2,1)S(1)}, bf16[3,24,1024]{2,1,0:T(8,128)(2,1)S(1)}, u32[]{:S(2)}, u32[]{:S(2)}) collective-permute-start(bf16[3,24,1024]{2,1,0:T(8,128)(2,1)S(1)} %get-tuple-element.40), channel_id=1, source_target_pairs={{0,4},{4,8},{8,12},{12,16},{16,20},{20,24},{24,28},{1,5},{5,9},{9,... | collective-permute-start | bytes 442376 | tf_op jit(solution)/shard_map/ppermute | solution.py:423
  22.2 0.1 pad_add_fusion.place
  22.3 1.1 pad_maximum_fusion.own
  23.4 0.0 copy-start.10
  23.4 0.7 copy-done.10
  24.1 8.4 %window_attention.1.refs_0_ = bf16[144,1024]{1,0:T(8,128)(2,1)S(1)} custom-call(s32[2]{0:T(128)S(1)} %pad_add_fusion.place, bf16[6,24,1024]{2,1,0:T(8,128)(2,1)S(1)} %pad_maximum_fusion.own, bf16[3,24,1024]{2,1,0:T(8,128)(2,1)S(1)} %collective-permute-done.1.above, bf16[3,24,1024]{2,1,0:T(8,128)(2,1)S(1)} %collective-permute-done.2.below, ...), custom_call_target="tpu_custom_call" | custom-call | flops 6000000000 | bytes 12000000 | tf_op jit(solution)/shard_map/window_attention/pallas_call | solution.py:141
  32.5 0.0 copy-start.3
  32.5 0.0 copy-start.5
  32.5 0.0 copy-start.7
  32.5 1.9 %collective-permute-start.5 = (bf16[144,1024]{1,0:T(8,128)(2,1)S(1)}, bf16[144,1024]{1,0:T(8,128)(2,1)S(1)}, u32[]{:S(2)}, u32[]{:S(2)}) collective-permute-start(bf16[144,1024]{1,0:T(8,128)(2,1)S(1)} %window_attention.1.refs_0_), channel_id=1, source_target_pairs={{0,3},{1,0},{2,1},{3,2},{4,7},{5,4},{6,5},{7,6},{8,11},{9,8},{10,9... | collective-permute-start | bytes 884744 | tf_op jit(solution)/shard_map/ppermute | solution.py:428
  34.4 1.0 collective-permute-start.3
  35.5 4.3 %collective-permute-done.5.refs_3_ = bf16[144,1024]{1,0:T(8,128)(2,1)S(1)} collective-permute-done((bf16[144,1024]{1,0:T(8,128)(2,1)S(1)}, bf16[144,1024]{1,0:T(8,128)(2,1)S(1)}, u32[]{:S(2)}, u32[]{:S(2)}) %collective-permute-start.5) | collective-permute-done | bytes 294944 | tf_op jit(solution)/shard_map/ppermute | solution.py:428
  39.8 17.7 %collective-permute-done.4.refs_2_ = bf16[144,1024]{1,0:T(8,128)(2,1)S(1)} collective-permute-done((bf16[144,1024]{1,0:T(8,128)(2,1)S(1)}, bf16[144,1024]{1,0:T(8,128)(2,1)S(1)}, u32[]{:S(2)}, u32[]{:S(2)}) %collective-permute-start.4) | collective-permute-done | bytes 294944 | tf_op jit(solution)/shard_map/ppermute | solution.py:428
  57.6 2.6 %band_latents.1 = (bf16[576,1024]{1,0:T(8,128)(2,1)S(1)}, bf16[6,24,1024]{2,1,0:T(8,128)(2,1)}) custom-call(s32[2]{0:T(128)S(1)} %pad_add_fusion.place, bf16[576,576]{1,0:T(8,128)(2,1)S(1)} %copy-done.11, bf16[144,1024]{1,0:T(8,128)(2,1)S(1)} %window_attention.1.refs_0_, bf16[144,1024]{1,0:T(8,128)(2,1)S(1)} %collective-permute-done.3.refs_1_, ...), custom_call_target="tpu_custom_call" | custom-call | flops 679477248 | bytes 4000000 | tf_op jit(solution)/shard_map/band_latents/pallas_call | solution.py:200
  60.2 1.0 copy-done
  61.2 0.0 copy-start.1
  61.2 1.3 copy-done.1
  62.5 20.6 %slot_group.2 = (bf16[2,2,2,4,320,128]{5,4,3,2,1,0:T(8,128)(2,1)S(1)}, bf16[2,2,2,4,320,128]{5,4,3,2,1,0:T(8,128)(2,1)}, f32[576,1024]{1,0:T(8,128)S(1)}) custom-call(s32[2]{0:T(128)S(1)} %pad_add_fusion.place, s32[4]{0:T(128)S(1)} %copy-done.5, s32[1,4]{1,0:T(1,128)S(1)} %copy-done.6, s32[10]{0:T(128)S(1)} %copy-done.7, s32[576,1]{1,0:T(8,128)S(1)} %copy-done.3, ...), custom_call_target="tpu_custom_call" | custom-call | flops 9059696640 | bytes 20000000 | tf_op jit(solution)/shard_map/slot_group/pallas_call | solution.py:340
  83.0 3.2 %collective-permute-start.6 = (bf16[2,2,2,4,320,128]{5,4,3,2,1,0:T(8,128)(2,1)}, bf16[2,2,2,4,320,128]{5,4,3,2,1,0:T(8,128)(2,1)}, u32[]{:S(2)}, u32[]{:S(2)}) collective-permute-start(bf16[2,2,2,4,320,128]{5,4,3,2,1,0:T(8,128)(2,1)} %get-tuple-element.24), channel_id=1, source_target_pairs={{0,4},{4,0},{8,12},{12,8},{16,20},{20,16},{24,28},{28,24},{1,5},{5... | collective-permute-start | bytes 7864328 | tf_op jit(solution)/shard_map/ppermute | solution.py:434
  86.3 7.1 %slot_group.3 = (bf16[2,2,2,1,320,128]{5,4,3,2,1,0:T(8,128)(2,1)S(1)}, bf16[2,2,2,1,320,128]{5,4,3,2,1,0:T(8,128)(2,1)S(1)}, bf16[4,6,24,1024]{3,2,1,0:T(8,128)(2,1)}) custom-call(s32[2]{0:T(128)S(1)} %pad_add_fusion.place, s32[4]{0:T(128)S(1)} %copy-done.5, s32[1,4]{1,0:T(1,128)S(1)} %copy-done.6, s32[10]{0:T(128)S(1)} %copy-done.7, ...), custom_call_target="tpu_custom_call" | custom-call | flops 2264924160 | bytes 5000000 | tf_op jit(solution)/shard_map/slot_group/pallas_call | solution.py:340
  93.4 0.8 copy-done.8
  94.2 0.0 reduce-scatter.2.cloned.1.call-update
  94.2 2.4 %halve.2 = (bf16[2,4,320,128]{3,2,1,0:T(8,128)(2,1)S(1)}, bf16[2,4,320,128]{3,2,1,0:T(8,128)(2,1)S(1)}, bf16[2,4,320,128]{3,2,1,0:T(8,128)(2,1)S(1)}, bf16[2,4,320,128]{3,2,1,0:T(8,128)(2,1)S(1)}) custom-call(bf16[2,2,2,4,320,128]{5,4,3,2,1,0:T(8,128)(2,1)S(1)} %get-tuple-element.23.keep, bf16[2,2,2,4,320,128]{5,4,3,2,1,0:T(8,128)(2,1)} %collective-permute-done.6.came, ...), custom_call_target="tpu_custom_call" | custom-call | flops 2000000 | bytes 6000000 | tf_op jit(solution)/shard_map/halve/pallas_call | solution.py:368
  96.6 5.3 %collective-permute-start.7 = (bf16[2,4,320,128]{3,2,1,0:T(8,128)(2,1)S(1)}, bf16[2,4,320,128]{3,2,1,0:T(8,128)(2,1)S(1)}, u32[]{:S(2)}, u32[]{:S(2)}) collective-permute-start(bf16[2,4,320,128]{3,2,1,0:T(8,128)(2,1)S(1)} %get-tuple-element.26), channel_id=1, source_target_pairs={{0,8},{4,12},{8,0},{12,4},{16,24},{20,28},{24,16},{28,20},{1,9},{5... | collective-permute-start | bytes 1966088 | tf_op jit(solution)/shard_map/ppermute | solution.py:434
  101.9 0.2 collective-permute-start.11
  102.1 0.4 collective-permute-start.9
  102.5 14.8 %collective-permute-done.7.refs_0_ = bf16[2,4,320,128]{3,2,1,0:T(8,128)(2,1)S(1)} collective-permute-done((bf16[2,4,320,128]{3,2,1,0:T(8,128)(2,1)S(1)}, bf16[2,4,320,128]{3,2,1,0:T(8,128)(2,1)S(1)}, u32[]{:S(2)}, u32[]{:S(2)}) %collective-permute-start.7) | collective-permute-done | bytes 655392 | tf_op jit(solution)/shard_map/ppermute | solution.py:434
  117.3 0.2 fusion.1
  117.5 1.8 %collective-permute-start.8 = (bf16[4,320,128]{2,1,0:T(8,128)(2,1)S(1)}, bf16[4,320,128]{2,1,0:T(8,128)(2,1)S(1)}, u32[]{:S(2)}, u32[]{:S(2)}) collective-permute-start(bf16[4,320,128]{2,1,0:T(8,128)(2,1)S(1)} %get-tuple-element.37), channel_id=1, source_target_pairs={{0,16},{4,20},{8,24},{12,28},{16,0},{20,4},{24,8},{28,12},{1,17},{... | collective-permute-start | bytes 983048 | tf_op jit(solution)/shard_map/ppermute | solution.py:434
  119.3 0.2 halve.3
  119.5 0.4 collective-permute-start.12
  119.8 1.7 %collective-permute-start.14 = (bf16[2,1,320,128]{3,2,1,0:T(8,128)(2,1)S(1)}, bf16[2,1,320,128]{3,2,1,0:T(8,128)(2,1)S(1)}, u32[]{:S(2)}, u32[]{:S(2)}) collective-permute-start(bf16[2,1,320,128]{3,2,1,0:T(8,128)(2,1)S(1)} %get-tuple-element.34), channel_id=1, source_target_pairs={{0,16},{4,20},{8,24},{12,28},{16,0},{20,4},{24,8},{28,12},{1,17},{... | collective-permute-start | bytes 491528 | tf_op jit(solution)/shard_map/ppermute | solution.py:434
  121.5 0.2 fusion.3
  121.7 0.4 collective-permute-start.10
  122.1 4.6 %collective-permute-done.12 = bf16[2,1,320,128]{3,2,1,0:T(8,128)(2,1)S(1)} collective-permute-done((bf16[2,1,320,128]{3,2,1,0:T(8,128)(2,1)S(1)}, bf16[2,1,320,128]{3,2,1,0:T(8,128)(2,1)S(1)}, u32[]{:S(2)}, u32[]{:S(2)}) %collective-permute-start.12) | collective-permute-done | bytes 163872 | tf_op jit(solution)/shard_map/ppermute | solution.py:434
  126.7 0.3 collective-permute-start.13
  127.0 4.6 %collective-permute-done.14 = bf16[2,1,320,128]{3,2,1,0:T(8,128)(2,1)S(1)} collective-permute-done((bf16[2,1,320,128]{3,2,1,0:T(8,128)(2,1)S(1)}, bf16[2,1,320,128]{3,2,1,0:T(8,128)(2,1)S(1)}, u32[]{:S(2)}, u32[]{:S(2)}) %collective-permute-start.14) | collective-permute-done | bytes 163872 | tf_op jit(solution)/shard_map/ppermute | solution.py:434
  131.6 1.6 %collective-permute-start.15 = (bf16[1,320,128]{2,1,0:T(8,128)(2,1)S(1)}, bf16[1,320,128]{2,1,0:T(8,128)(2,1)S(1)}, u32[]{:S(2)}, u32[]{:S(2)}) collective-permute-start(bf16[1,320,128]{2,1,0:T(8,128)(2,1)S(1)} %get-tuple-element.41), channel_id=1, source_target_pairs={{0,8},{4,12},{8,0},{12,4},{16,24},{20,28},{24,16},{28,20},{1,9},{5... | collective-permute-start | bytes 245768 | tf_op jit(solution)/shard_map/ppermute | solution.py:434
  133.2 2.9 %collective-permute-done.15.refs_7_ = bf16[1,320,128]{2,1,0:T(8,128)(2,1)S(1)} collective-permute-done((bf16[1,320,128]{2,1,0:T(8,128)(2,1)S(1)}, bf16[1,320,128]{2,1,0:T(8,128)(2,1)S(1)}, u32[]{:S(2)}, u32[]{:S(2)}) %collective-permute-start.15) | collective-permute-done | bytes 81952 | tf_op jit(solution)/shard_map/ppermute | solution.py:434
  136.1 1.4 join_heads.1
  (35 shorter events, 0.2 us)
Async XLA Ops:
  7.2 54.0 %all-gather.3.cloned.1.call-start = ((), (), s32[]{:S(2)}) async-start(), calls=%async_computation.2 | async-start | bytes 7372800 | tf_op jit(solution)/shard_map/all_gather | solution.py:416
  7.9 129.6 %reduce-scatter.2.cloned.1.call-start = ((), (), s32[]{:S(2)}) async-start(), calls=%async_computation.1 | async-start | bytes 1474560 | tf_op jit(solution)/shard_map/reduce_scatter | solution.py:441
  8.9 7.9 %collective-permute-start = (bf16[6,6,1024]{2,1,0:T(8,128)(2,1)S(1)}, bf16[6,6,1024]{2,1,0:T(8,128)(2,1)S(1)}, u32[]{:S(2)}, u32[]{:S(2)}) collective-permute-start(bf16[6,6,1024]{2,1,0:T(8,128)(2,1)S(1)} %slice.60), channel_id=1, source_target_pairs={{0,1},{1,2},{2,3},{3,0},{4,5},{5,6},{6,7},{7,4},{8,9},{9,10},{10,1... | collective-permute-start | bytes 221192 | tf_op jit(solution)/shard_map/ppermute | solution.py:421
  17.8 5.5 %collective-permute-start.2 = (bf16[3,24,1024]{2,1,0:T(8,128)(2,1)S(1)}, bf16[3,24,1024]{2,1,0:T(8,128)(2,1)S(1)}, u32[]{:S(2)}, u32[]{:S(2)}) collective-permute-start(bf16[3,24,1024]{2,1,0:T(8,128)(2,1)S(1)} %get-tuple-element.39), channel_id=1, source_target_pairs={{4,0},{8,4},{12,8},{16,12},{20,16},{24,20},{28,24},{5,1},{9,5},{13... | collective-permute-start | bytes 442376 | tf_op jit(solution)/shard_map/ppermute | solution.py:424
  19.1 4.2 %collective-permute-start.1 = (bf16[3,24,1024]{2,1,0:T(8,128)(2,1)S(1)}, bf16[3,24,1024]{2,1,0:T(8,128)(2,1)S(1)}, u32[]{:S(2)}, u32[]{:S(2)}) collective-permute-start(bf16[3,24,1024]{2,1,0:T(8,128)(2,1)S(1)} %get-tuple-element.40), channel_id=1, source_target_pairs={{0,4},{4,8},{8,12},{12,16},{16,20},{20,24},{24,28},{1,5},{5,9},{9,... | collective-permute-start | bytes 442376 | tf_op jit(solution)/shard_map/ppermute | solution.py:423
  23.4 0.7 copy-start.10
  24.0 11.4 %copy-start.12 = (f32[10,1024]{1,0:T(8,128)S(1)}, f32[10,1024]{1,0:T(8,128)}, u32[]{:S(2)}) copy-start(f32[10,1024]{1,0:T(8,128)} %param.18) | copy-start | bytes 122884
  24.0 11.4 %copy-start.13 = (f32[10,1024]{1,0:T(8,128)S(1)}, f32[10,1024]{1,0:T(8,128)}, u32[]{:S(2)}) copy-start(f32[10,1024]{1,0:T(8,128)} %param.19) | copy-start | bytes 122884
  24.1 33.5 %copy-start.11 = (bf16[576,576]{1,0:T(8,128)(2,1)S(1)}, bf16[576,576]{1,0:T(8,128)(2,1)}, u32[]{:S(2)}) copy-start(bf16[576,576]{1,0:T(8,128)(2,1)} %constant.16.clone.chosen) | copy-start | bytes 1990660
  32.5 28.7 %copy-start.3 = (s32[576,1]{1,0:T(8,128)S(1)}, s32[576,1]{1,0:T(8,128)}, u32[]{:S(2)}) copy-start(s32[576,1]{1,0:T(8,128)} %constant.17.clone.tile_of) | copy-start | bytes 6916
  32.5 28.7 %copy-start.5 = (s32[4]{0:T(128)S(1)}, s32[4]{0:T(128)}, u32[]{:S(2)}) copy-start(s32[4]{0:T(128)} %counts.3) | copy-start | bytes 52
  32.5 28.7 %copy-start.6 = (s32[1,4]{1,0:T(1,128)S(1)}, s32[1,4]{1,0:T(1,128)}, u32[]{:S(2)}) copy-start(s32[1,4]{1,0:T(1,128)} %datasets.3) | copy-start | bytes 52
  32.5 28.7 %copy-start.7 = (s32[10]{0:T(128)S(1)}, s32[10]{0:T(128)}, u32[]{:S(2)}) copy-start(s32[10]{0:T(128)} %levels.3) | copy-start | bytes 124
  32.5 7.3 %collective-permute-start.5 = (bf16[144,1024]{1,0:T(8,128)(2,1)S(1)}, bf16[144,1024]{1,0:T(8,128)(2,1)S(1)}, u32[]{:S(2)}, u32[]{:S(2)}) collective-permute-start(bf16[144,1024]{1,0:T(8,128)(2,1)S(1)} %window_attention.1.refs_0_), channel_id=1, source_target_pairs={{0,3},{1,0},{2,1},{3,2},{4,7},{5,4},{6,5},{7,6},{8,11},{9,8},{10,9... | collective-permute-start | bytes 884744 | tf_op jit(solution)/shard_map/ppermute | solution.py:428
  34.4 23.2 %collective-permute-start.4 = (bf16[144,1024]{1,0:T(8,128)(2,1)S(1)}, bf16[144,1024]{1,0:T(8,128)(2,1)S(1)}, u32[]{:S(2)}, u32[]{:S(2)}) collective-permute-start(bf16[144,1024]{1,0:T(8,128)(2,1)S(1)} %window_attention.1.refs_0_), channel_id=1, source_target_pairs={{0,2},{1,3},{2,0},{3,1},{4,6},{5,7},{6,4},{7,5},{8,10},{9,11},{10,... | collective-permute-start | bytes 884744 | tf_op jit(solution)/shard_map/ppermute | solution.py:428
  34.4 23.2 %collective-permute-start.3 = (bf16[144,1024]{1,0:T(8,128)(2,1)S(1)}, bf16[144,1024]{1,0:T(8,128)(2,1)S(1)}, u32[]{:S(2)}, u32[]{:S(2)}) collective-permute-start(bf16[144,1024]{1,0:T(8,128)(2,1)S(1)} %window_attention.1.refs_0_), channel_id=1, source_target_pairs={{0,1},{1,2},{2,3},{3,0},{4,5},{5,6},{6,7},{7,4},{8,9},{9,10},{10,1... | collective-permute-start | bytes 884744 | tf_op jit(solution)/shard_map/ppermute | solution.py:428
  60.2 1.0 copy-start
  61.2 1.3 copy-start.1
  62.5 23.8 %copy-start.2 = (bf16[576,1024]{1,0:T(8,128)(2,1)S(1)}, bf16[576,1024]{1,0:T(8,128)(2,1)}, u32[]{:S(2)}) copy-start(bf16[576,1024]{1,0:T(8,128)(2,1)} %copy-done) | copy-start | bytes 3538948
  62.5 23.8 %copy-start.4 = (s32[576,1]{1,0:T(8,128)S(1)}, s32[576,1]{1,0:T(8,128)}, u32[]{:S(2)}) copy-start(s32[576,1]{1,0:T(8,128)} %constant.17.clone.tile_of) | copy-start | bytes 6916
  83.0 11.2 %collective-permute-start.6 = (bf16[2,2,2,4,320,128]{5,4,3,2,1,0:T(8,128)(2,1)}, bf16[2,2,2,4,320,128]{5,4,3,2,1,0:T(8,128)(2,1)}, u32[]{:S(2)}, u32[]{:S(2)}) collective-permute-start(bf16[2,2,2,4,320,128]{5,4,3,2,1,0:T(8,128)(2,1)} %get-tuple-element.24), channel_id=1, source_target_pairs={{0,4},{4,0},{8,12},{12,8},{16,20},{20,16},{24,28},{28,24},{1,5},{5... | collective-permute-start | bytes 7864328 | tf_op jit(solution)/shard_map/ppermute | solution.py:434
  93.4 0.8 copy-start.8
  94.2 7.7 %copy-start.9 = (bf16[2,2,2,1,320,128]{5,4,3,2,1,0:T(8,128)(2,1)S(1)}, bf16[2,2,2,1,320,128]{5,4,3,2,1,0:T(8,128)(2,1)}, u32[]{:S(2)}) copy-start(bf16[2,2,2,1,320,128]{5,4,3,2,1,0:T(8,128)(2,1)} %copy-done.8) | copy-start | bytes 1966084
  96.6 20.7 %collective-permute-start.7 = (bf16[2,4,320,128]{3,2,1,0:T(8,128)(2,1)S(1)}, bf16[2,4,320,128]{3,2,1,0:T(8,128)(2,1)S(1)}, u32[]{:S(2)}, u32[]{:S(2)}) collective-permute-start(bf16[2,4,320,128]{3,2,1,0:T(8,128)(2,1)S(1)} %get-tuple-element.26), channel_id=1, source_target_pairs={{0,8},{4,12},{8,0},{12,4},{16,24},{20,28},{24,16},{28,20},{1,9},{5... | collective-permute-start | bytes 1966088 | tf_op jit(solution)/shard_map/ppermute | solution.py:434
  101.9 17.4 %collective-permute-start.11 = (bf16[2,2,2,1,320,128]{5,4,3,2,1,0:T(8,128)(2,1)S(1)}, bf16[2,2,2,1,320,128]{5,4,3,2,1,0:T(8,128)(2,1)S(1)}, u32[]{:S(2)}, u32[]{:S(2)}) collective-permute-start(bf16[2,2,2,1,320,128]{5,4,3,2,1,0:T(8,128)(2,1)S(1)} %copy-done.9), channel_id=1, source_target_pairs={{0,4},{4,0},{8,12},{12,8},{16,20},{20,16},{24,28},{28,24},{1,5},{5... | collective-permute-start | bytes 1966088 | tf_op jit(solution)/shard_map/ppermute | solution.py:434
  102.1 17.2 %collective-permute-start.9 = (bf16[2,4,320,128]{3,2,1,0:T(8,128)(2,1)S(1)}, bf16[2,4,320,128]{3,2,1,0:T(8,128)(2,1)S(1)}, u32[]{:S(2)}, u32[]{:S(2)}) collective-permute-start(bf16[2,4,320,128]{3,2,1,0:T(8,128)(2,1)S(1)} %get-tuple-element.28), channel_id=1, source_target_pairs={{0,16},{4,20},{8,24},{12,28},{16,0},{20,4},{24,8},{28,12},{1,17},{... | collective-permute-start | bytes 1966088 | tf_op jit(solution)/shard_map/ppermute | solution.py:434
  117.5 18.7 %collective-permute-start.8 = (bf16[4,320,128]{2,1,0:T(8,128)(2,1)S(1)}, bf16[4,320,128]{2,1,0:T(8,128)(2,1)S(1)}, u32[]{:S(2)}, u32[]{:S(2)}) collective-permute-start(bf16[4,320,128]{2,1,0:T(8,128)(2,1)S(1)} %get-tuple-element.37), channel_id=1, source_target_pairs={{0,16},{4,20},{8,24},{12,28},{16,0},{20,4},{24,8},{28,12},{1,17},{... | collective-permute-start | bytes 983048 | tf_op jit(solution)/shard_map/ppermute | solution.py:434
  119.5 7.2 %collective-permute-start.12 = (bf16[2,1,320,128]{3,2,1,0:T(8,128)(2,1)S(1)}, bf16[2,1,320,128]{3,2,1,0:T(8,128)(2,1)S(1)}, u32[]{:S(2)}, u32[]{:S(2)}) collective-permute-start(bf16[2,1,320,128]{3,2,1,0:T(8,128)(2,1)S(1)} %get-tuple-element.32), channel_id=1, source_target_pairs={{0,8},{4,12},{8,0},{12,4},{16,24},{20,28},{24,16},{28,20},{1,9},{5... | collective-permute-start | bytes 491528 | tf_op jit(solution)/shard_map/ppermute | solution.py:434
  119.8 11.8 %collective-permute-start.14 = (bf16[2,1,320,128]{3,2,1,0:T(8,128)(2,1)S(1)}, bf16[2,1,320,128]{3,2,1,0:T(8,128)(2,1)S(1)}, u32[]{:S(2)}, u32[]{:S(2)}) collective-permute-start(bf16[2,1,320,128]{3,2,1,0:T(8,128)(2,1)S(1)} %get-tuple-element.34), channel_id=1, source_target_pairs={{0,16},{4,20},{8,24},{12,28},{16,0},{20,4},{24,8},{28,12},{1,17},{... | collective-permute-start | bytes 491528 | tf_op jit(solution)/shard_map/ppermute | solution.py:434
  121.7 14.4 %collective-permute-start.10 = (bf16[4,320,128]{2,1,0:T(8,128)(2,1)S(1)}, bf16[4,320,128]{2,1,0:T(8,128)(2,1)S(1)}, u32[]{:S(2)}, u32[]{:S(2)}) collective-permute-start(bf16[4,320,128]{2,1,0:T(8,128)(2,1)S(1)} %get-tuple-element.35), channel_id=1, source_target_pairs={{0,8},{4,12},{8,0},{12,4},{16,24},{20,28},{24,16},{28,20},{1,9},{5... | collective-permute-start | bytes 983048 | tf_op jit(solution)/shard_map/ppermute | solution.py:434
  126.7 6.5 %collective-permute-start.13 = (bf16[1,320,128]{2,1,0:T(8,128)(2,1)S(1)}, bf16[1,320,128]{2,1,0:T(8,128)(2,1)S(1)}, u32[]{:S(2)}, u32[]{:S(2)}) collective-permute-start(bf16[1,320,128]{2,1,0:T(8,128)(2,1)S(1)} %get-tuple-element.43), channel_id=1, source_target_pairs={{0,16},{4,20},{8,24},{12,28},{16,0},{20,4},{24,8},{28,12},{1,17},{... | collective-permute-start | bytes 245768 | tf_op jit(solution)/shard_map/ppermute | solution.py:434
  131.6 4.5 %collective-permute-start.15 = (bf16[1,320,128]{2,1,0:T(8,128)(2,1)S(1)}, bf16[1,320,128]{2,1,0:T(8,128)(2,1)S(1)}, u32[]{:S(2)}, u32[]{:S(2)}) collective-permute-start(bf16[1,320,128]{2,1,0:T(8,128)(2,1)S(1)} %get-tuple-element.41), channel_id=1, source_target_pairs={{0,8},{4,12},{8,0},{12,4},{16,24},{20,28},{24,16},{28,20},{1,9},{5... | collective-permute-start | bytes 245768 | tf_op jit(solution)/shard_map/ppermute | solution.py:434
Sparse Core Ops, SparseCore 0:
  9.9 50.4 all-gather.2
  94.3 32.8 reduce-scatter.1

commit v9 on v7

--- a/solution.py
+++ b/solution.py
@@ -44,7 +44,7 @@
     own,
     above,
     below,
-    gain,
+    gain_hbm,
     maps_hbm,
     in_hbm,
     out_hbm,
@@ -52,6 +52,7 @@
     raw,
     qkv,
     attn,
+    gain,
     maps,
     proj_in,
     proj_out,
@@ -59,7 +60,9 @@
 ):
     moves = [
         pltpu.make_async_copy(src, dst, sems.at[i])
-        for i, (src, dst) in enumerate(((maps_hbm, maps), (in_hbm, proj_in), (out_hbm, proj_out)))
+        for i, (src, dst) in enumerate(
+            ((gain_hbm, gain), (maps_hbm, maps), (in_hbm, proj_in), (out_hbm, proj_out))
+        )
     ]
     for move in moves:
         move.start()
@@ -75,14 +78,15 @@
         count = ref.shape[0] * cols
         raw[start : start + count, :] = ref[...].astype(F32).reshape(count, width)
         start += count
+    moves[0].wait()
     wide = raw[...]
     average = jnp.mean(wide, axis=-1, keepdims=True)
     centred = wide - average
     variance = jnp.mean(centred * centred, axis=-1, keepdims=True)
     normed = (centred * lax.rsqrt(variance + EPS) * gain[...]).astype(BF16)
-    moves[0].wait()
+    moves[1].wait()
     win_x = jnp.dot(maps[0:slots, :], normed, preferred_element_type=F32).astype(BF16)
-    moves[1].wait()
+    moves[2].wait()
     step = 512
     for j in range(3 * width // step):
         part = slice(j * step, (j + 1) * step)
@@ -120,7 +124,7 @@
             attn[win * QP : (win + 1) * QP, lanes] = chosen.astype(BF16)
     back = maps[slots : slots + size, 0 : windows * QP]
     ordered = jnp.dot(back, attn[...], preferred_element_type=F32).astype(BF16)
-    moves[2].wait()
+    moves[3].wait()
     update = jnp.dot(ordered, proj_out[...], preferred_element_type=F32)
     out[...] = (raw[0:size, :] + update).astype(BF16)
 
@@ -137,16 +141,17 @@
     return pl.pallas_call(
         functools.partial(attention_kernel, bands),
         out_shape=jax.ShapeDtypeStruct((rows * cols, width), BF16),
-        in_specs=[pl.BlockSpec(memory_space=pltpu.SMEM)] + [vmem] * 4 + [hbm] * 3,
+        in_specs=[pl.BlockSpec(memory_space=pltpu.SMEM)] + [vmem] * 3 + [hbm] * 4,
         out_specs=vmem,
         scratch_shapes=[
             pltpu.VMEM((total, width), F32),
             pltpu.VMEM((windows * 2 * QP, 3 * width), BF16),
             pltpu.VMEM((windows * QP, width), BF16),
+            pltpu.VMEM((1, width), F32),
             pltpu.VMEM(maps.shape, BF16),
             pltpu.VMEM(proj_in.shape, BF16),
             pltpu.VMEM(proj_out.shape, BF16),
-            pltpu.SemaphoreType.DMA((3,)),
+            pltpu.SemaphoreType.DMA((4,)),
         ],
         compiler_params=pltpu.CompilerParams(vmem_limit_bytes=53 * 1024 * 1024),
         cost_estimate=pl.CostEstimate(
@@ -207,13 +212,13 @@
         to[k, outer, inner, 0] = turned[k, :, pl.ds(start, piece)]
 
 
-def add_back(lats, errs, gathered, scale, total):
+def add_back(lats, at, errs, gathered, scale, total):
     piece = gathered.shape[-1]
     for l in range(0, lats, 2):
         lanes = slice(l * piece, (l + 2) * piece)
         term = 0.0
         for k in range(2):
-            weight = jnp.concatenate([gathered[l, k], gathered[l + 1, k]], axis=1)
+            weight = jnp.concatenate([gathered[at[l], k], gathered[at[l + 1], k]], axis=1)
             factor = scale[k][:, lanes]
             term = term + jnp.dot(errs[k], weight, preferred_element_type=F32) * factor
         total[:, lanes] += term
@@ -239,10 +244,15 @@
         band, before, keep, send, out, total, rows0, rows1, errs, turned, tile_counts = refs
     else:
         chosen, pieces = refs[0], refs[1 : 1 + tiles]
+        refs = refs[1:]
         keep, send, total, band, latent, rows0, rows1, errs, turned, tile_counts = refs[1 + tiles :]
     rows = (rows0, rows1)
     step, steps = pl.program_id(0), pl.num_programs(0)
     slot = first_slot + 2 * step
+    at = range(lats)
+    if final:
+        flips = [jnp.bitwise_xor(place[0], l) for l in range(lats)]
+        at = [(q % 2) * 4 + q // 2 % 2 * 2 + q // 4 for q in flips]
 
     @pl.when(step == 0)
     def _():
@@ -260,11 +270,11 @@
     for k in range(2):
         rows[k][...] = (band[...].astype(F32) * scale[k] + shift[k]).astype(BF16)
     for k in range(2):
-        weight = jnp.concatenate([gathered[l, k] for l in range(lats)], axis=1)
+        weight = jnp.concatenate([gathered[at[l], k] for l in range(lats)], axis=1)
         errs[k] = slot_errors(levels[slot + k], tile_counts[...], rows[k][...], weight, target[k])
     for k in range(2):
         head_halves(k, lats, place[0], errs[k], rows[k][...], turned, keep, send)
-    add_back(lats, errs, gathered, scale, total)
+    add_back(lats, at, errs, gathered, scale, total)
 
     if final:
 
@@ -277,7 +287,7 @@
                     out[s, r] = total[start : start + cols, :].astype(BF16)
 
 
-def slot_group(pair, pairs, lats, place, small, tile_of, scale, shift, gathered, targets, pieces, before):
+def slot_group(pair, pairs, lats, place, small, tile_of, scale, shift, gathered, targets, pieces, before, after=None):
     places, width = tile_of.shape[0], scale.shape[-1]
     outs = targets.shape[-1]
     tiles = small[1].shape[1]
@@ -292,7 +302,7 @@
         fixed(tile_of.shape),
         level_spec,
         level_spec,
-        pl.BlockSpec((lats, 2, outs, piece), lambda i: (0, i + pair, 0, 0)),
+        pl.BlockSpec((lats, 2, outs, piece), lambda i: (0, i, 0, 0)),
         pl.BlockSpec((2,) + targets.shape[1:], lambda i: (i + pair, 0, 0, 0)),
     ]
     args = [place, *small, tile_of, scale, shift, gathered, targets]
@@ -317,6 +327,9 @@
             jax.ShapeDtypeStruct((WH, cols, width), BF16),
         ]
     in_specs.extend(fixed(arg.shape) for arg in args[len(in_specs) :])
+    if after is not None:
+        args.append(after)
+        in_specs.append(pl.BlockSpec(memory_space=pl.ANY))
     limit = (45 if final else 48) * 1024 * 1024
     return pl.pallas_call(
         functools.partial(slot_kernel, 2 * pair, lats, tiles, final),
@@ -392,7 +405,13 @@
     slots = head_weight.shape[0]
     lat, var = lax.axis_index("lat"), lax.axis_index("var")
     place = jnp.stack([lat, var]).astype(jnp.int32)
-    gathered = lax.all_gather(jnp.transpose(head_weight, (0, 2, 1)), "lat", axis=0, tiled=False)
+    most = slots // 2 - 1
+    flip = lambda array, bit: lax.ppermute(array, "lat", [(i, i ^ bit) for i in range(lats)])
+    turned = jnp.transpose(head_weight, (0, 2, 1))
+    gathered_a = lax.all_gather(turned[: 2 * most], "lat", axis=0, tiled=False)
+    gathered_b = turned[None, 2 * most :]
+    for bit in (4, 2, 1):
+        gathered_b = jnp.concatenate([gathered_b, flip(gathered_b, bit)], axis=0)
 
     right = [(i, (i + 1) % tiles) for i in range(tiles)]
     up = [(i, i + 1) for i in range(lats - 1)]
@@ -409,13 +428,15 @@
     tile_of = jnp.asarray(np.arange(rows * tiles * cols)[:, None] % (tiles * cols) // cols, jnp.int32)
     scale3, shift3 = level_scale.reshape(slots, 1, width), level_shift.reshape(slots, 1, width)
     small = (level_counts, tile_dataset, slot_level)
-    flip = lambda array, bit: lax.ppermute(array, "lat", [(i, i ^ bit) for i in range(lats)])
     add = lambda a, b: (a.astype(F32) + b.astype(F32)).astype(BF16)
-    common = (lats, place, small, tile_of, scale3, shift3, gathered, targets)
-    most = slots // 2 - 1
+    common = (lats, place, small, tile_of, scale3, shift3)
     bits = (2, 4)
-    keep_a, send_a, so_far, band, latent = slot_group(0, most, *common, pieces, None)
-    keep_b, send_b, terms = slot_group(most, slots // 2 - most, *common, None, (band, so_far))
+    keep_a, send_a, so_far, band, latent = slot_group(
+        0, most, *common, gathered_a, targets, pieces, None, gathered_b
+    )
+    keep_b, send_b, terms = slot_group(
+        most, slots // 2 - most, *common, gathered_b, targets, None, (band, so_far)
+    )
     grad_latent = lax.psum_scatter(terms, "var", scatter_dimension=0, tiled=False)
     pairs, came = [], [terms]
     for keep, send in ((keep_a, send_a), (keep_b, send_b)):

time: 139 us -> 150 us (1.079)
  starting transfers between devices: 22.9 us -> 28.8 us
  local copies, waits for them, and re-layouts: 2.55 us -> 7.58 us
  waiting for transfers between devices: 57.3 us -> 59.2 us
  other arithmetic: 2.66 us -> 0.94 us
    ppermute x10 -> x13, waiting for transfers between devices: 26.8 us -> 36.2 us  [fast_local(): lax.ppermute(array, 'lat', [(i, i ^ bit) for i in range(lats)])]
    ppermute x10 -> x13, starting transfers between devices: 12.5 us -> 18.1 us  [fast_local(): lax.ppermute(array, 'lat', [(i, i ^ bit) for i in range(lats)])]
    ppermute x1, waiting for transfers between devices: 4.82 us -> 0.41 us  [fast_local(): left = lax.ppermute(patches[:, cols - HC:], 'var', right)]
    unnamed x24 -> x22, local copies, waits for them, and re-layouts: 1.57 us -> 4.56 us
    all_gather x1, waiting for transfers between devices: 2.84 us -> 0.01 us  [fast_local(): gathered_a = lax.all_gather(turned[:2 * most], 'lat', axis=0, tiled=False)]
    slice x0 -> x1, local copies, waits for them, and re-layouts: none -> 2.01 us  [fast_local(): gathered_a = lax.all_gather(turned[:2 * most], 'lat', axis=0, tiled=False)]
    concatenate x2, other arithmetic: 2.14 us -> 0.2 us  [fast_local(): shifted = jnp.concatenate([left, patches[:, :cols - HC]], axis=1)]
    ppermute x3, starting transfers between devices: 2.91 us -> 4.6 us  [fast_local(): lax.ppermute(mine, 'var', [(i, (i + s) % tiles) for i in range(tiles)])]
  transfers between devices with their start and end apart: 18 -> 21, of which waited for: 8 -> 10; matrix products, arithmetic and copies ran while one was open for 3% -> 1% of each run, Pallas kernels for 14% -> 12%
where the time goes in v9:
time: 150 us
  waiting for transfers between devices  59.2 us (39%)
  Pallas kernels  39.3 us (26%)
  starting transfers between devices  28.8 us (19%)
  between operations  14.3 us (10%)
  local copies, waits for them, and re-layouts  7.58 us (5%)
    ppermute x13, waiting for transfers between devices, fast_local(): lax.ppermute(array, 'lat', [(i, i ^ bit) for i in range(lats)])  36.2 us
    pallas_call x2, Pallas kernels, slot_group(): pl.pallas_call(functools.partial(slot_kernel, 2 * pair, lats, tiles, fina...  27 us
    ppermute x3, waiting for transfers between devices, fast_local(): lax.ppermute(mine, 'var', [(i, (i + s) % tiles) for i in range(tiles)])  22.5 us
    ppermute x13, starting transfers between devices, fast_local(): lax.ppermute(array, 'lat', [(i, i ^ bit) for i in range(lats)])  18.1 us
    pallas_call x1, Pallas kernels, attention(): pl.pallas_call(functools.partial(attention_kernel, bands), out_shape=jax....  8.43 us
    ppermute x3, starting transfers between devices, fast_local(): lax.ppermute(mine, 'var', [(i, (i + s) % tiles) for i in range(tiles)])  4.6 us
    unnamed x22, local copies, waits for them, and re-layouts  4.56 us
    ppermute x1, starting transfers between devices, fast_local(): above = lax.ppermute(shifted[HR:], 'lat', up)  3.04 us
  transfers between devices with their start and end apart: 21, of which 10 were waited for; matrix products, arithmetic and copies ran while one was open for 1% of the time, Pallas kernels for 12%

profile of v9, /device:TPU:0, one launch (start us, length us, event | category | flops | bytes accessed | tf_op | source)
XLA Modules:
  0.0 150.0 jit_solution(16748962194797052362)
XLA Ops:
  7.2 0.0 all-gather.3.cloned.1.call-start
  7.2 2.0 %slice.88 = bf16[8,320,128]{2,1,0:T(8,128)(2,1)} slice(bf16[10,320,128]{2,1,0:T(8,128)(2,1)} %bitcast.30), slice={[0:8], [0:320], [0:128]} | slice | bytes 1310720 | tf_op jit(solution)/shard_map/slice | solution.py:411
  9.2 0.0 all-gather.3.cloned.1.call-update
  9.2 0.0 reduce-scatter.2.cloned.1.call-start
  9.3 0.9 slice_bitcast_fusion
  10.2 3.0 %collective-permute-start.6 = (bf16[1,2,320,128]{3,2,1,0:T(8,128)(2,1)S(1)}, bf16[1,2,320,128]{3,2,1,0:T(8,128)(2,1)S(1)}, u32[]{:S(2)}, u32[]{:S(2)}) collective-permute-start(bf16[1,2,320,128]{3,2,1,0:T(8,128)(2,1)S(1)} %slice_bitcast_fusion), channel_id=1, source_target_pairs={{0,16},{4,20},{8,24},{12,28},{16,0},{20,4},{24,8},{28,12},{1,17},{... | collective-permute-start | bytes 491528 | tf_op jit(solution)/shard_map/ppermute | solution.py:409
  13.3 1.6 %collective-permute-start = (bf16[6,6,1024]{2,1,0:T(8,128)(2,1)S(1)}, bf16[6,6,1024]{2,1,0:T(8,128)(2,1)S(1)}, u32[]{:S(2)}, u32[]{:S(2)}) collective-permute-start(bf16[6,6,1024]{2,1,0:T(8,128)(2,1)S(1)} %slice.67), channel_id=1, source_target_pairs={{0,1},{1,2},{2,3},{3,0},{4,5},{5,6},{6,7},{7,4},{8,9},{9,10},{10,1... | collective-permute-start | bytes 221192 | tf_op jit(solution)/shard_map/ppermute | solution.py:419
  14.9 2.5 %collective-permute-done.6 = bf16[1,2,320,128]{3,2,1,0:T(8,128)(2,1)S(1)} collective-permute-done((bf16[1,2,320,128]{3,2,1,0:T(8,128)(2,1)S(1)}, bf16[1,2,320,128]{3,2,1,0:T(8,128)(2,1)S(1)}, u32[]{:S(2)}, u32[]{:S(2)}) %collective-permute-start.6) | collective-permute-done | bytes 163872 | tf_op jit(solution)/shard_map/ppermute | solution.py:409
  17.5 1.8 %collective-permute-start.7 = (bf16[2,2,320,128]{3,2,1,0:T(8,128)(2,1)S(1)}, bf16[2,2,320,128]{3,2,1,0:T(8,128)(2,1)S(1)}, u32[]{:S(2)}, u32[]{:S(2)}) collective-permute-start(bf16[2,2,320,128]{3,2,1,0:T(8,128)(2,1)S(1)} %pad_maximum_fusion.3), channel_id=1, source_target_pairs={{0,8},{4,12},{8,0},{12,4},{16,24},{20,28},{24,16},{28,20},{1,9},{5... | collective-permute-start | bytes 983048 | tf_op jit(solution)/shard_map/ppermute | solution.py:409
  19.3 0.1 pad_add_fusion.place
  19.4 0.4 collective-permute-done
  19.8 0.1 fusion.5
  19.9 1.3 collective-permute-start.2
  21.2 3.0 %collective-permute-start.1 = (bf16[3,24,1024]{2,1,0:T(8,128)(2,1)S(1)}, bf16[3,24,1024]{2,1,0:T(8,128)(2,1)S(1)}, u32[]{:S(2)}, u32[]{:S(2)}) collective-permute-start(bf16[3,24,1024]{2,1,0:T(8,128)(2,1)S(1)} %get-tuple-element.40), channel_id=1, source_target_pairs={{0,4},{4,8},{8,12},{12,16},{16,20},{20,24},{24,28},{1,5},{5,9},{9,... | collective-permute-start | bytes 442376 | tf_op jit(solution)/shard_map/ppermute | solution.py:421
  24.2 0.1 pad_maximum_fusion.2.own
  24.3 8.8 %collective-permute-done.7 = bf16[2,2,320,128]{3,2,1,0:T(8,128)(2,1)S(1)} collective-permute-done((bf16[2,2,320,128]{3,2,1,0:T(8,128)(2,1)S(1)}, bf16[2,2,320,128]{3,2,1,0:T(8,128)(2,1)S(1)}, u32[]{:S(2)}, u32[]{:S(2)}) %collective-permute-start.7) | collective-permute-done | bytes 327712 | tf_op jit(solution)/shard_map/ppermute | solution.py:409
  33.1 0.1 pad_maximum_fusion.1
  33.2 0.1 collective-permute-start.8
  33.3 8.4 %window_attention.1.refs_1_ = bf16[144,1024]{1,0:T(8,128)(2,1)S(1)} custom-call(s32[2]{0:T(128)S(1)} %pad_add_fusion.place, bf16[6,24,1024]{2,1,0:T(8,128)(2,1)S(1)} %pad_maximum_fusion.2.own, bf16[3,24,1024]{2,1,0:T(8,128)(2,1)S(1)} %collective-permute-done.1.above, bf16[3,24,1024]{2,1,0:T(8,128)(2,1)S(1)} %collective-permute-done.2.below, ...), custom_call_target="tpu_custom_call" | custom-call | flops 6000000000 | bytes 12000000 | tf_op jit(solution)/shard_map/window_attention/pallas_call | solution.py:141
  41.8 3.7 %collective-permute-start.5 = (bf16[144,1024]{1,0:T(8,128)(2,1)S(1)}, bf16[144,1024]{1,0:T(8,128)(2,1)S(1)}, u32[]{:S(2)}, u32[]{:S(2)}) collective-permute-start(bf16[144,1024]{1,0:T(8,128)(2,1)S(1)} %window_attention.1.refs_1_), channel_id=1, source_target_pairs={{0,3},{1,0},{2,1},{3,2},{4,7},{5,4},{6,5},{7,6},{8,11},{9,8},{10,9... | collective-permute-start | bytes 884744 | tf_op jit(solution)/shard_map/ppermute | solution.py:426
  45.5 0.9 collective-permute-start.3
  46.5 0.1 pad_maximum_fusion.refs_5_.gathered
  46.7 4.2 %collective-permute-done.5.refs_4_ = bf16[144,1024]{1,0:T(8,128)(2,1)S(1)} collective-permute-done((bf16[144,1024]{1,0:T(8,128)(2,1)S(1)}, bf16[144,1024]{1,0:T(8,128)(2,1)S(1)}, u32[]{:S(2)}, u32[]{:S(2)}) %collective-permute-start.5) | collective-permute-done | bytes 294944 | tf_op jit(solution)/shard_map/ppermute | solution.py:426
  50.9 18.3 %collective-permute-done.4.refs_3_ = bf16[144,1024]{1,0:T(8,128)(2,1)S(1)} collective-permute-done((bf16[144,1024]{1,0:T(8,128)(2,1)S(1)}, bf16[144,1024]{1,0:T(8,128)(2,1)S(1)}, u32[]{:S(2)}, u32[]{:S(2)}) %collective-permute-start.4) | collective-permute-done | bytes 294944 | tf_op jit(solution)/shard_map/ppermute | solution.py:426
  69.2 1.1 copy-done.7
  70.3 20.8 %slot_group.2 = (bf16[2,2,2,4,320,128]{5,4,3,2,1,0:T(8,128)(2,1)}, bf16[2,2,2,4,320,128]{5,4,3,2,1,0:T(8,128)(2,1)}, f32[576,1024]{1,0:T(8,128)}, bf16[576,1024]{1,0:T(8,128)(2,1)S(1)}, bf16[6,24,1024]{2,1,0:T(8,128)(2,1)}) custom-call(s32[2]{0:T(128)S(1)} %pad_add_fusion.place, s32[4]{0:T(128)S(1)} %copy-done.3, s32[1,4]{1,0:T(1,128)S(1)} %copy-done.4, ...), custom_call_target="tpu_custom_call" | custom-call | flops 9059696640 | bytes 20000000 | tf_op jit(solution)/shard_map/slot_group/pallas_call | solution.py:334
  91.1 2.2 %collective-permute-start.9 = (bf16[2,2,2,4,320,128]{5,4,3,2,1,0:T(8,128)(2,1)}, bf16[2,2,2,4,320,128]{5,4,3,2,1,0:T(8,128)(2,1)}, u32[]{:S(2)}, u32[]{:S(2)}) collective-permute-start(bf16[2,2,2,4,320,128]{5,4,3,2,1,0:T(8,128)(2,1)} %get-tuple-element.24), channel_id=1, source_target_pairs={{0,4},{4,0},{8,12},{12,8},{16,20},{20,16},{24,28},{28,24},{1,5},{5... | collective-permute-start | bytes 7864328 | tf_op jit(solution)/shard_map/ppermute | solution.py:409
  93.3 1.7 %copy-done.1 = f32[576,1024]{1,0:T(8,128)S(1)} copy-done((f32[576,1024]{1,0:T(8,128)S(1)}, f32[576,1024]{1,0:T(8,128)}, u32[]{:S(2)}) %copy-start.1) | copy-done | bytes 2359320
  95.0 6.2 %slot_group.3 = (bf16[2,2,2,1,320,128]{5,4,3,2,1,0:T(8,128)(2,1)S(1)}, bf16[2,2,2,1,320,128]{5,4,3,2,1,0:T(8,128)(2,1)S(1)}, bf16[4,6,24,1024]{3,2,1,0:T(8,128)(2,1)}) custom-call(s32[2]{0:T(128)S(1)} %pad_add_fusion.place, s32[4]{0:T(128)S(1)} %copy-done.3, s32[1,4]{1,0:T(1,128)S(1)} %copy-done.4, s32[10]{0:T(128)S(1)} %copy-done.5, ...), custom_call_target="tpu_custom_call" | custom-call | flops 2264924160 | bytes 5000000 | tf_op jit(solution)/shard_map/slot_group/pallas_call | solution.py:334
  101.2 1.7 %copy-done = bf16[2,2,2,4,320,128]{5,4,3,2,1,0:T(8,128)(2,1)S(1)} copy-done((bf16[2,2,2,4,320,128]{5,4,3,2,1,0:T(8,128)(2,1)S(1)}, bf16[2,2,2,4,320,128]{5,4,3,2,1,0:T(8,128)(2,1)}, u32[]{:S(2)}) %copy-start) | copy-done | bytes 2621464
  103.0 2.3 %halve.2 = (bf16[2,4,320,128]{3,2,1,0:T(8,128)(2,1)S(1)}, bf16[2,4,320,128]{3,2,1,0:T(8,128)(2,1)S(1)}, bf16[2,4,320,128]{3,2,1,0:T(8,128)(2,1)S(1)}, bf16[2,4,320,128]{3,2,1,0:T(8,128)(2,1)S(1)}) custom-call(bf16[2,2,2,4,320,128]{5,4,3,2,1,0:T(8,128)(2,1)S(1)} %copy-done, bf16[2,2,2,4,320,128]{5,4,3,2,1,0:T(8,128)(2,1)} %collective-permute-done.9.came, ...), custom_call_target="tpu_custom_call" | custom-call | flops 2000000 | bytes 6000000 | tf_op jit(solution)/shard_map/halve/pallas_call | solution.py:360
  105.3 3.0 %collective-permute-start.10 = (bf16[2,4,320,128]{3,2,1,0:T(8,128)(2,1)S(1)}, bf16[2,4,320,128]{3,2,1,0:T(8,128)(2,1)S(1)}, u32[]{:S(2)}, u32[]{:S(2)}) collective-permute-start(bf16[2,4,320,128]{3,2,1,0:T(8,128)(2,1)S(1)} %get-tuple-element.26), channel_id=1, source_target_pairs={{0,8},{4,12},{8,0},{12,4},{16,24},{20,28},{24,16},{28,20},{1,9},{5... | collective-permute-start | bytes 1966088 | tf_op jit(solution)/shard_map/ppermute | solution.py:409
  108.3 1.0 collective-permute-start.12
  109.3 13.9 %collective-permute-done.10.refs_0_ = bf16[2,4,320,128]{3,2,1,0:T(8,128)(2,1)S(1)} collective-permute-done((bf16[2,4,320,128]{3,2,1,0:T(8,128)(2,1)S(1)}, bf16[2,4,320,128]{3,2,1,0:T(8,128)(2,1)S(1)}, u32[]{:S(2)}, u32[]{:S(2)}) %collective-permute-start.10) | collective-permute-done | bytes 655392 | tf_op jit(solution)/shard_map/ppermute | solution.py:409
  123.3 0.2 fusion.1
  123.4 1.7 %collective-permute-start.11 = (bf16[4,320,128]{2,1,0:T(8,128)(2,1)S(1)}, bf16[4,320,128]{2,1,0:T(8,128)(2,1)S(1)}, u32[]{:S(2)}, u32[]{:S(2)}) collective-permute-start(bf16[4,320,128]{2,1,0:T(8,128)(2,1)S(1)} %get-tuple-element.37), channel_id=1, source_target_pairs={{0,16},{4,20},{8,24},{12,28},{16,0},{20,4},{24,8},{28,12},{1,17},{... | collective-permute-start | bytes 983048 | tf_op jit(solution)/shard_map/ppermute | solution.py:409
  125.2 0.3 collective-permute-done.12.refs_1_
  125.5 0.2 halve.3
  125.6 1.1 collective-permute-start.15
  126.7 0.8 collective-permute-start.17
  127.5 0.2 fusion.3
  127.7 1.1 collective-permute-start.13
  128.8 4.0 %collective-permute-done.15 = bf16[2,1,320,128]{3,2,1,0:T(8,128)(2,1)S(1)} collective-permute-done((bf16[2,1,320,128]{3,2,1,0:T(8,128)(2,1)S(1)}, bf16[2,1,320,128]{3,2,1,0:T(8,128)(2,1)S(1)}, u32[]{:S(2)}, u32[]{:S(2)}) %collective-permute-start.15) | collective-permute-done | bytes 163872 | tf_op jit(solution)/shard_map/ppermute | solution.py:409
  132.8 0.9 collective-permute-start.16
  133.7 3.5 %collective-permute-done.17 = bf16[2,1,320,128]{3,2,1,0:T(8,128)(2,1)S(1)} collective-permute-done((bf16[2,1,320,128]{3,2,1,0:T(8,128)(2,1)S(1)}, bf16[2,1,320,128]{3,2,1,0:T(8,128)(2,1)S(1)}, u32[]{:S(2)}, u32[]{:S(2)}) %collective-permute-start.17) | collective-permute-done | bytes 163872 | tf_op jit(solution)/shard_map/ppermute | solution.py:409
  137.3 1.4 collective-permute-start.18
  138.7 3.1 %collective-permute-done.18.refs_7_ = bf16[1,320,128]{2,1,0:T(8,128)(2,1)S(1)} collective-permute-done((bf16[1,320,128]{2,1,0:T(8,128)(2,1)S(1)}, bf16[1,320,128]{2,1,0:T(8,128)(2,1)S(1)}, u32[]{:S(2)}, u32[]{:S(2)}) %collective-permute-start.18) | collective-permute-done | bytes 81952 | tf_op jit(solution)/shard_map/ppermute | solution.py:409
  141.8 1.4 join_heads.1
  (39 shorter events, 0.3 us)
Async XLA Ops:
  7.2 6.1 %copy-start.8 = (bf16[6,24,1024]{2,1,0:T(8,128)(2,1)S(1)}, bf16[6,24,1024]{2,1,0:T(8,128)(2,1)}, u32[]{:S(2)}) copy-start(bf16[6,24,1024]{2,1,0:T(8,128)(2,1)} %param.14) | copy-start | bytes 884740
  7.2 62.0 %all-gather.3.cloned.1.call-start = ((), (), s32[]{:S(2)}) async-start(), calls=%async_computation.2 | async-start | bytes 5898240 | tf_op jit(solution)/shard_map/all_gather | solution.py:411
  9.2 133.9 %reduce-scatter.2.cloned.1.call-start = ((), (), s32[]{:S(2)}) async-start(), calls=%async_computation.1 | async-start | bytes 1474560 | tf_op jit(solution)/shard_map/reduce_scatter | solution.py:440
  10.2 7.2 %collective-permute-start.6 = (bf16[1,2,320,128]{3,2,1,0:T(8,128)(2,1)S(1)}, bf16[1,2,320,128]{3,2,1,0:T(8,128)(2,1)S(1)}, u32[]{:S(2)}, u32[]{:S(2)}) collective-permute-start(bf16[1,2,320,128]{3,2,1,0:T(8,128)(2,1)S(1)} %slice_bitcast_fusion), channel_id=1, source_target_pairs={{0,16},{4,20},{8,24},{12,28},{16,0},{20,4},{24,8},{28,12},{1,17},{... | collective-permute-start | bytes 491528 | tf_op jit(solution)/shard_map/ppermute | solution.py:409
  13.3 6.5 %collective-permute-start = (bf16[6,6,1024]{2,1,0:T(8,128)(2,1)S(1)}, bf16[6,6,1024]{2,1,0:T(8,128)(2,1)S(1)}, u32[]{:S(2)}, u32[]{:S(2)}) collective-permute-start(bf16[6,6,1024]{2,1,0:T(8,128)(2,1)S(1)} %slice.67), channel_id=1, source_target_pairs={{0,1},{1,2},{2,3},{3,0},{4,5},{5,6},{6,7},{7,4},{8,9},{9,10},{10,1... | collective-permute-start | bytes 221192 | tf_op jit(solution)/shard_map/ppermute | solution.py:419
  17.5 15.6 %collective-permute-start.7 = (bf16[2,2,320,128]{3,2,1,0:T(8,128)(2,1)S(1)}, bf16[2,2,320,128]{3,2,1,0:T(8,128)(2,1)S(1)}, u32[]{:S(2)}, u32[]{:S(2)}) collective-permute-start(bf16[2,2,320,128]{3,2,1,0:T(8,128)(2,1)S(1)} %pad_maximum_fusion.3), channel_id=1, source_target_pairs={{0,8},{4,12},{8,0},{12,4},{16,24},{20,28},{24,16},{28,20},{1,9},{5... | collective-permute-start | bytes 983048 | tf_op jit(solution)/shard_map/ppermute | solution.py:409
  19.8 13.5 %copy-start.6 = (f32[1024]{0:T(1024)S(1)}, f32[1024]{0:T(1024)}, u32[]{:S(2)}) copy-start(f32[1024]{0:T(1024)} %param.15) | copy-start | bytes 12292
  19.9 13.4 %collective-permute-start.2 = (bf16[3,24,1024]{2,1,0:T(8,128)(2,1)S(1)}, bf16[3,24,1024]{2,1,0:T(8,128)(2,1)S(1)}, u32[]{:S(2)}, u32[]{:S(2)}) collective-permute-start(bf16[3,24,1024]{2,1,0:T(8,128)(2,1)S(1)} %get-tuple-element.39), channel_id=1, source_target_pairs={{4,0},{8,4},{12,8},{16,12},{20,16},{24,20},{28,24},{5,1},{9,5},{13... | collective-permute-start | bytes 442376 | tf_op jit(solution)/shard_map/ppermute | solution.py:422
  21.2 12.1 %collective-permute-start.1 = (bf16[3,24,1024]{2,1,0:T(8,128)(2,1)S(1)}, bf16[3,24,1024]{2,1,0:T(8,128)(2,1)S(1)}, u32[]{:S(2)}, u32[]{:S(2)}) collective-permute-start(bf16[3,24,1024]{2,1,0:T(8,128)(2,1)S(1)} %get-tuple-element.40), channel_id=1, source_target_pairs={{0,4},{4,8},{8,12},{12,16},{16,20},{20,24},{24,28},{1,5},{5,9},{9,... | collective-permute-start | bytes 442376 | tf_op jit(solution)/shard_map/ppermute | solution.py:421
  33.2 13.3 %collective-permute-start.8 = (bf16[4,2,320,128]{3,2,1,0:T(8,128)(2,1)S(1)}, bf16[4,2,320,128]{3,2,1,0:T(8,128)(2,1)S(1)}, u32[]{:S(2)}, u32[]{:S(2)}) collective-permute-start(bf16[4,2,320,128]{3,2,1,0:T(8,128)(2,1)S(1)} %pad_maximum_fusion.1), channel_id=1, source_target_pairs={{0,4},{4,0},{8,12},{12,8},{16,20},{20,16},{24,28},{28,24},{1,5},{5... | collective-permute-start | bytes 1966088 | tf_op jit(solution)/shard_map/ppermute | solution.py:409
  33.3 13.1 %copy-start.9 = (f32[10,1024]{1,0:T(8,128)S(1)}, f32[10,1024]{1,0:T(8,128)}, u32[]{:S(2)}) copy-start(f32[10,1024]{1,0:T(8,128)} %param.18) | copy-start | bytes 122884
  33.3 13.1 %copy-start.10 = (f32[10,1024]{1,0:T(8,128)S(1)}, f32[10,1024]{1,0:T(8,128)}, u32[]{:S(2)}) copy-start(f32[10,1024]{1,0:T(8,128)} %param.19) | copy-start | bytes 122884
  41.8 9.1 %collective-permute-start.5 = (bf16[144,1024]{1,0:T(8,128)(2,1)S(1)}, bf16[144,1024]{1,0:T(8,128)(2,1)S(1)}, u32[]{:S(2)}, u32[]{:S(2)}) collective-permute-start(bf16[144,1024]{1,0:T(8,128)(2,1)S(1)} %window_attention.1.refs_1_), channel_id=1, source_target_pairs={{0,3},{1,0},{2,1},{3,2},{4,7},{5,4},{6,5},{7,6},{8,11},{9,8},{10,9... | collective-permute-start | bytes 884744 | tf_op jit(solution)/shard_map/ppermute | solution.py:426
  45.5 23.7 %collective-permute-start.4 = (bf16[144,1024]{1,0:T(8,128)(2,1)S(1)}, bf16[144,1024]{1,0:T(8,128)(2,1)S(1)}, u32[]{:S(2)}, u32[]{:S(2)}) collective-permute-start(bf16[144,1024]{1,0:T(8,128)(2,1)S(1)} %window_attention.1.refs_1_), channel_id=1, source_target_pairs={{0,2},{1,3},{2,0},{3,1},{4,6},{5,7},{6,4},{7,5},{8,10},{9,11},{10,... | collective-permute-start | bytes 884744 | tf_op jit(solution)/shard_map/ppermute | solution.py:426
  45.5 23.7 %collective-permute-start.3 = (bf16[144,1024]{1,0:T(8,128)(2,1)S(1)}, bf16[144,1024]{1,0:T(8,128)(2,1)S(1)}, u32[]{:S(2)}, u32[]{:S(2)}) collective-permute-start(bf16[144,1024]{1,0:T(8,128)(2,1)S(1)} %window_attention.1.refs_1_), channel_id=1, source_target_pairs={{0,1},{1,2},{2,3},{3,0},{4,5},{5,6},{6,7},{7,4},{8,9},{9,10},{10,1... | collective-permute-start | bytes 884744 | tf_op jit(solution)/shard_map/ppermute | solution.py:426
  46.5 22.7 %copy-start.2 = (s32[576,1]{1,0:T(8,128)S(1)}, s32[576,1]{1,0:T(8,128)}, u32[]{:S(2)}) copy-start(s32[576,1]{1,0:T(8,128)} %constant.16.clone.tile_of) | copy-start | bytes 6916
  46.5 22.7 %copy-start.3 = (s32[4]{0:T(128)S(1)}, s32[4]{0:T(128)}, u32[]{:S(2)}) copy-start(s32[4]{0:T(128)} %counts.3) | copy-start | bytes 52
  46.5 22.7 %copy-start.4 = (s32[1,4]{1,0:T(1,128)S(1)}, s32[1,4]{1,0:T(1,128)}, u32[]{:S(2)}) copy-start(s32[1,4]{1,0:T(1,128)} %datasets.3) | copy-start | bytes 52
  46.5 22.7 %copy-start.5 = (s32[10]{0:T(128)S(1)}, s32[10]{0:T(128)}, u32[]{:S(2)}) copy-start(s32[10]{0:T(128)} %levels.3) | copy-start | bytes 124
  69.2 1.1 copy-start.7
  91.1 10.1 %collective-permute-start.9 = (bf16[2,2,2,4,320,128]{5,4,3,2,1,0:T(8,128)(2,1)}, bf16[2,2,2,4,320,128]{5,4,3,2,1,0:T(8,128)(2,1)}, u32[]{:S(2)}, u32[]{:S(2)}) collective-permute-start(bf16[2,2,2,4,320,128]{5,4,3,2,1,0:T(8,128)(2,1)} %get-tuple-element.24), channel_id=1, source_target_pairs={{0,4},{4,0},{8,12},{12,8},{16,20},{20,16},{24,28},{28,24},{1,5},{5... | collective-permute-start | bytes 7864328 | tf_op jit(solution)/shard_map/ppermute | solution.py:409
  93.3 1.7 %copy-start.1 = (f32[576,1024]{1,0:T(8,128)S(1)}, f32[576,1024]{1,0:T(8,128)}, u32[]{:S(2)}) copy-start(f32[576,1024]{1,0:T(8,128)} %get-tuple-element.21.refs_1_) | copy-start | bytes 7077892
  101.2 1.7 %copy-start = (bf16[2,2,2,4,320,128]{5,4,3,2,1,0:T(8,128)(2,1)S(1)}, bf16[2,2,2,4,320,128]{5,4,3,2,1,0:T(8,128)(2,1)}, u32[]{:S(2)}) copy-start(bf16[2,2,2,4,320,128]{5,4,3,2,1,0:T(8,128)(2,1)} %get-tuple-element.23.keep) | copy-start | bytes 7864324
  105.3 18.0 %collective-permute-start.10 = (bf16[2,4,320,128]{3,2,1,0:T(8,128)(2,1)S(1)}, bf16[2,4,320,128]{3,2,1,0:T(8,128)(2,1)S(1)}, u32[]{:S(2)}, u32[]{:S(2)}) collective-permute-start(bf16[2,4,320,128]{3,2,1,0:T(8,128)(2,1)S(1)} %get-tuple-element.26), channel_id=1, source_target_pairs={{0,8},{4,12},{8,0},{12,4},{16,24},{20,28},{24,16},{28,20},{1,9},{5... | collective-permute-start | bytes 1966088 | tf_op jit(solution)/shard_map/ppermute | solution.py:409
  108.3 16.8 %collective-permute-start.14 = (bf16[2,2,2,1,320,128]{5,4,3,2,1,0:T(8,128)(2,1)S(1)}, bf16[2,2,2,1,320,128]{5,4,3,2,1,0:T(8,128)(2,1)S(1)}, u32[]{:S(2)}, u32[]{:S(2)}) collective-permute-start(bf16[2,2,2,1,320,128]{5,4,3,2,1,0:T(8,128)(2,1)S(1)} %get-tuple-element.30), channel_id=1, source_target_pairs={{0,4},{4,0},{8,12},{12,8},{16,20},{20,16},{24,28},{28,24},{1,5},{5... | collective-permute-start | bytes 1966088 | tf_op jit(solution)/shard_map/ppermute | solution.py:409
  108.3 17.1 %collective-permute-start.12 = (bf16[2,4,320,128]{3,2,1,0:T(8,128)(2,1)S(1)}, bf16[2,4,320,128]{3,2,1,0:T(8,128)(2,1)S(1)}, u32[]{:S(2)}, u32[]{:S(2)}) collective-permute-start(bf16[2,4,320,128]{3,2,1,0:T(8,128)(2,1)S(1)} %get-tuple-element.28), channel_id=1, source_target_pairs={{0,16},{4,20},{8,24},{12,28},{16,0},{20,4},{24,8},{28,12},{1,17},{... | collective-permute-start | bytes 1966088 | tf_op jit(solution)/shard_map/ppermute | solution.py:409
  123.4 18.4 %collective-permute-start.11 = (bf16[4,320,128]{2,1,0:T(8,128)(2,1)S(1)}, bf16[4,320,128]{2,1,0:T(8,128)(2,1)S(1)}, u32[]{:S(2)}, u32[]{:S(2)}) collective-permute-start(bf16[4,320,128]{2,1,0:T(8,128)(2,1)S(1)} %get-tuple-element.37), channel_id=1, source_target_pairs={{0,16},{4,20},{8,24},{12,28},{16,0},{20,4},{24,8},{28,12},{1,17},{... | collective-permute-start | bytes 983048 | tf_op jit(solution)/shard_map/ppermute | solution.py:409
  125.6 7.2 %collective-permute-start.15 = (bf16[2,1,320,128]{3,2,1,0:T(8,128)(2,1)S(1)}, bf16[2,1,320,128]{3,2,1,0:T(8,128)(2,1)S(1)}, u32[]{:S(2)}, u32[]{:S(2)}) collective-permute-start(bf16[2,1,320,128]{3,2,1,0:T(8,128)(2,1)S(1)} %get-tuple-element.32), channel_id=1, source_target_pairs={{0,8},{4,12},{8,0},{12,4},{16,24},{20,28},{24,16},{28,20},{1,9},{5... | collective-permute-start | bytes 491528 | tf_op jit(solution)/shard_map/ppermute | solution.py:409
  126.7 10.5 %collective-permute-start.17 = (bf16[2,1,320,128]{3,2,1,0:T(8,128)(2,1)S(1)}, bf16[2,1,320,128]{3,2,1,0:T(8,128)(2,1)S(1)}, u32[]{:S(2)}, u32[]{:S(2)}) collective-permute-start(bf16[2,1,320,128]{3,2,1,0:T(8,128)(2,1)S(1)} %get-tuple-element.34), channel_id=1, source_target_pairs={{0,16},{4,20},{8,24},{12,28},{16,0},{20,4},{24,8},{28,12},{1,17},{... | collective-permute-start | bytes 491528 | tf_op jit(solution)/shard_map/ppermute | solution.py:409
  127.7 14.1 %collective-permute-start.13 = (bf16[4,320,128]{2,1,0:T(8,128)(2,1)S(1)}, bf16[4,320,128]{2,1,0:T(8,128)(2,1)S(1)}, u32[]{:S(2)}, u32[]{:S(2)}) collective-permute-start(bf16[4,320,128]{2,1,0:T(8,128)(2,1)S(1)} %get-tuple-element.35), channel_id=1, source_target_pairs={{0,8},{4,12},{8,0},{12,4},{16,24},{20,28},{24,16},{28,20},{1,9},{5... | collective-permute-start | bytes 983048 | tf_op jit(solution)/shard_map/ppermute | solution.py:409
  132.8 5.9 %collective-permute-start.16 = (bf16[1,320,128]{2,1,0:T(8,128)(2,1)S(1)}, bf16[1,320,128]{2,1,0:T(8,128)(2,1)S(1)}, u32[]{:S(2)}, u32[]{:S(2)}) collective-permute-start(bf16[1,320,128]{2,1,0:T(8,128)(2,1)S(1)} %get-tuple-element.43), channel_id=1, source_target_pairs={{0,16},{4,20},{8,24},{12,28},{16,0},{20,4},{24,8},{28,12},{1,17},{... | collective-permute-start | bytes 245768 | tf_op jit(solution)/shard_map/ppermute | solution.py:409
  137.3 4.5 %collective-permute-start.18 = (bf16[1,320,128]{2,1,0:T(8,128)(2,1)S(1)}, bf16[1,320,128]{2,1,0:T(8,128)(2,1)S(1)}, u32[]{:S(2)}, u32[]{:S(2)}) collective-permute-start(bf16[1,320,128]{2,1,0:T(8,128)(2,1)S(1)} %get-tuple-element.41), channel_id=1, source_target_pairs={{0,8},{4,12},{8,0},{12,4},{16,24},{20,28},{24,16},{28,20},{1,9},{5... | collective-permute-start | bytes 245768 | tf_op jit(solution)/shard_map/ppermute | solution.py:409
Sparse Core Ops, SparseCore 0:
  10.5 49.6 all-gather.2
  101.3 30.6 reduce-scatter.1

commit v10 on v8

--- a/solution.py
+++ b/solution.py
@@ -336,7 +336,7 @@
     else:
         results = [sums]
     in_specs.extend(fixed(arg.shape) for arg in args[len(in_specs) :])
-    limit = (45 if final else 46) * 1024 * 1024
+    limit = (45 if final else 48) * 1024 * 1024
     return pl.pallas_call(
         functools.partial(slot_kernel, 2 * pair, lats, tiles, final),
         grid=(pairs,),
@@ -344,9 +344,7 @@
         in_specs=in_specs,
         out_specs=(half_spec, half_spec, *(fixed(r.shape) for r in results)),
         scratch_shapes=scratch,
-        compiler_params=pltpu.CompilerParams(
-            vmem_limit_bytes=limit, fuse_transposed_lhs_in_matmul=True
-        ),
+        compiler_params=pltpu.CompilerParams(vmem_limit_bytes=limit),
         cost_estimate=pl.CostEstimate(
             flops=pairs * 12 * places * width * outs, bytes_accessed=pairs * 5_000_000, transcendentals=0
         ),
@@ -354,26 +352,33 @@
     )(*args)
 
 
-def halve_kernel(keep, came, *refs):
-    outs = refs[-4:]
-    for k in range(2):
-        for half in range(2):
-            total = keep[k, half].astype(F32) + came[k, half].astype(F32)
-            outs[2 * half + k][...] = total.astype(BF16)
-
-
-def halve(keep, came, after):
-    part = jax.ShapeDtypeStruct(keep.shape[2:], BF16)
+def halve_kernel(*refs):
+    groups, outs = refs[:-4], refs[-4:]
+    start = 0
+    for keep, came in zip(groups[0::2], groups[1::2]):
+        pairs = keep.shape[3]
+        for k in range(2):
+            for half in range(2):
+                total = keep[k, half].astype(F32) + came[k, half].astype(F32)
+                outs[2 * half + k][:, start : start + pairs] = total.astype(BF16)
+        start += pairs
+
+
+def halve(groups):
+    flat = [array for group in groups for array in group]
+    pairs = sum(keep.shape[3] for keep, _ in groups)
+    shape = flat[0].shape
+    part = jax.ShapeDtypeStruct((2, pairs) + shape[4:], BF16)
     vmem = pl.BlockSpec(memory_space=pltpu.VMEM)
     out = pl.pallas_call(
         halve_kernel,
         out_shape=(part,) * 4,
-        in_specs=[vmem, vmem] + [pl.BlockSpec(memory_space=pl.ANY)] * len(after),
+        in_specs=[vmem] * len(flat),
         out_specs=(vmem,) * 4,
         compiler_params=pltpu.CompilerParams(vmem_limit_bytes=24 * 1024 * 1024),
         cost_estimate=pl.CostEstimate(flops=2_000_000, bytes_accessed=6_000_000, transcendentals=0),
         name="halve",
-    )(keep, came, *after)
+    )(*flat)
     return out[0:2], out[2:4]
 
 
@@ -439,13 +444,12 @@
     keep_a, send_a, so_far = slot_group(0, most, *common, None)
     keep_b, send_b, terms = slot_group(most, slots // 2 - most, *common, so_far)
     grad_latent = lax.psum_scatter(terms, "var", scatter_dimension=0, tiled=False)
-    pairs, came = [], [terms]
-    for keep, send in ((keep_a, send_a), (keep_b, send_b)):
-        kept, sent = halve(keep, flip(send, 1), came)
-        came = [flip(sent[k], bits[k]) for k in range(2)]
-        for k in range(2):
-            last = flip(add(kept[k][1], came[k][1]), bits[1 - k])
-            pairs.append((add(kept[k][0], came[k][0]), last))
+    kept, sent = halve([(keep_a, flip(send_a, 1)), (keep_b, flip(send_b, 1))])
+    came = [flip(sent[k], bits[k]) for k in range(2)]
+    pairs = []
+    for k in range(2):
+        last = flip(add(kept[k][1], came[k][1]), bits[1 - k])
+        pairs.append((add(kept[k][0], came[k][0]), last))
     grad_head = join_heads(pairs, 1.0 / math.sqrt(lats * rows * tiles * cols))
     return (latent, grad_latent, jnp.transpose(grad_head, (0, 2, 1)))
 

time: 145 us -> 142 us (0.979)
  waiting for transfers between devices: 54.4 us -> 59.3 us
  starting transfers between devices: 25.7 us -> 21.5 us
  Pallas kernels: 42.6 us -> 39.6 us
    ppermute x10 -> x6, waiting for transfers between devices: 26.9 us -> 31.5 us  [fast_local(): lax.ppermute(array, 'lat', [(i, i ^ bit) for i in range(lats)])]
    ppermute x10 -> x6, starting transfers between devices: 15.3 us -> 11.1 us  [fast_local(): lax.ppermute(array, 'lat', [(i, i ^ bit) for i in range(lats)])]
    pallas_call x2, Pallas kernels: 27.6 us -> 24.6 us  [slot_group(): pl.pallas_call(functools.partial(slot_kernel, 2 * pair, lats, tiles, fina...]
    unnamed x28 -> x26, local copies, waits for them, and re-layouts: 3.85 us -> 3.03 us
  transfers between devices with their start and end apart: 18 -> 14, of which waited for: 7 -> 8; matrix products, arithmetic and copies ran while one was open for 3% -> 3% of each run, Pallas kernels for 15% -> 15%
where the time goes in v10:
time: 142 us; the launch traced here: 141 us
  waiting for transfers between devices  59.3 us (42%)
  Pallas kernels  39.6 us (28%)
  starting transfers between devices  21.5 us (15%)
  between operations  14.2 us (10%)
  local copies, waits for them, and re-layouts  4.01 us (3%)
  other arithmetic  2.68 us (2%)
    ppermute x6, waiting for transfers between devices, fast_local(): lax.ppermute(array, 'lat', [(i, i ^ bit) for i in range(lats)])  31.5 us
    pallas_call x2, Pallas kernels, slot_group(): pl.pallas_call(functools.partial(slot_kernel, 2 * pair, lats, tiles, fina...  24.6 us
    ppermute x3, waiting for transfers between devices, fast_local(): lax.ppermute(mine, 'var', [(i, (i + s) % tiles) for i in range(tiles)])  22.1 us
    ppermute x6, starting transfers between devices, fast_local(): lax.ppermute(array, 'lat', [(i, i ^ bit) for i in range(lats)])  11.1 us
    pallas_call x1, Pallas kernels, attention(): pl.pallas_call(functools.partial(attention_kernel, bands), out_shape=jax....  8.42 us
    ppermute x1, waiting for transfers between devices, fast_local(): left = lax.ppermute(patches[:, cols - HC:], 'var', right)  4.82 us
    ppermute x1, starting transfers between devices, fast_local(): left = lax.ppermute(patches[:, cols - HC:], 'var', right)  3.08 us
    ppermute x1, starting transfers between devices, fast_local(): above = lax.ppermute(shifted[HR:], 'lat', up)  3.04 us
  transfers between devices with their start and end apart: 14, of which 8 were waited for; matrix products, arithmetic and copies ran while one was open for 3% of the time, Pallas kernels for 15%

profile of v10, /device:TPU:0, one launch (start us, length us, event | category | flops | bytes accessed | tf_op | source)
XLA Modules:
  0.0 141.3 jit_solution(9600778650505136084)
XLA Ops:
  7.2 0.0 all-gather.3.cloned.1.call-start
  7.2 0.7 all-gather.3.cloned.1.call-update
  7.9 0.0 reduce-scatter.2.cloned.1.call-start
  7.9 0.9 slice.36
  8.9 3.1 %collective-permute-start = (bf16[6,6,1024]{2,1,0:T(8,128)(2,1)S(1)}, bf16[6,6,1024]{2,1,0:T(8,128)(2,1)S(1)}, u32[]{:S(2)}, u32[]{:S(2)}) collective-permute-start(bf16[6,6,1024]{2,1,0:T(8,128)(2,1)S(1)} %slice.36), channel_id=1, source_target_pairs={{0,1},{1,2},{2,3},{3,0},{4,5},{5,6},{6,7},{7,4},{8,9},{9,10},{10,1... | collective-permute-start | bytes 221192 | tf_op jit(solution)/shard_map/ppermute | solution.py:426
  11.9 4.8 %collective-permute-done = bf16[6,6,1024]{2,1,0:T(8,128)(2,1)S(1)} collective-permute-done((bf16[6,6,1024]{2,1,0:T(8,128)(2,1)S(1)}, bf16[6,6,1024]{2,1,0:T(8,128)(2,1)S(1)}, u32[]{:S(2)}, u32[]{:S(2)}) %collective-permute-start) | collective-permute-done | bytes 73760 | tf_op jit(solution)/shard_map/ppermute | solution.py:426
  16.8 1.1 fusion.5
  17.8 1.3 collective-permute-start.2
  19.1 3.0 %collective-permute-start.1 = (bf16[3,24,1024]{2,1,0:T(8,128)(2,1)S(1)}, bf16[3,24,1024]{2,1,0:T(8,128)(2,1)S(1)}, u32[]{:S(2)}, u32[]{:S(2)}) collective-permute-start(bf16[3,24,1024]{2,1,0:T(8,128)(2,1)S(1)} %get-tuple-element.32), channel_id=1, source_target_pairs={{0,4},{4,8},{8,12},{12,16},{16,20},{20,24},{24,28},{1,5},{5,9},{9,... | collective-permute-start | bytes 442376 | tf_op jit(solution)/shard_map/ppermute | solution.py:428
  22.2 0.1 pad_add_fusion.place
  22.3 1.1 pad_maximum_fusion.own
  23.3 0.0 collective-permute-done.2.below
  23.3 0.0 collective-permute-done.1.above
  23.4 0.0 copy-start.9
  23.4 0.7 copy-done.9
  24.1 8.4 %window_attention.1.refs_0_ = bf16[144,1024]{1,0:T(8,128)(2,1)S(1)} custom-call(s32[2]{0:T(128)S(1)} %pad_add_fusion.place, bf16[6,24,1024]{2,1,0:T(8,128)(2,1)S(1)} %pad_maximum_fusion.own, bf16[3,24,1024]{2,1,0:T(8,128)(2,1)S(1)} %collective-permute-done.1.above, bf16[3,24,1024]{2,1,0:T(8,128)(2,1)S(1)} %collective-permute-done.2.below, ...), custom_call_target="tpu_custom_call" | custom-call | flops 6000000000 | bytes 12000000 | tf_op jit(solution)/shard_map/window_attention/pallas_call | solution.py:141
  32.5 0.0 copy-start.4
  32.5 0.0 copy-start.6
  32.5 0.0 copy-start.7
  32.5 0.0 copy-start.8
  32.5 1.9 %collective-permute-start.5 = (bf16[144,1024]{1,0:T(8,128)(2,1)S(1)}, bf16[144,1024]{1,0:T(8,128)(2,1)S(1)}, u32[]{:S(2)}, u32[]{:S(2)}) collective-permute-start(bf16[144,1024]{1,0:T(8,128)(2,1)S(1)} %window_attention.1.refs_0_), channel_id=1, source_target_pairs={{0,3},{1,0},{2,1},{3,2},{4,7},{5,4},{6,5},{7,6},{8,11},{9,8},{10,9... | collective-permute-start | bytes 884744 | tf_op jit(solution)/shard_map/ppermute | solution.py:433
  34.4 0.0 collective-permute-start.4
  34.4 1.0 collective-permute-start.3
  35.5 4.3 %collective-permute-done.5.refs_3_ = bf16[144,1024]{1,0:T(8,128)(2,1)S(1)} collective-permute-done((bf16[144,1024]{1,0:T(8,128)(2,1)S(1)}, bf16[144,1024]{1,0:T(8,128)(2,1)S(1)}, u32[]{:S(2)}, u32[]{:S(2)}) %collective-permute-start.5) | collective-permute-done | bytes 294944 | tf_op jit(solution)/shard_map/ppermute | solution.py:433
  39.8 17.7 %collective-permute-done.4.refs_2_ = bf16[144,1024]{1,0:T(8,128)(2,1)S(1)} collective-permute-done((bf16[144,1024]{1,0:T(8,128)(2,1)S(1)}, bf16[144,1024]{1,0:T(8,128)(2,1)S(1)}, u32[]{:S(2)}, u32[]{:S(2)}) %collective-permute-start.4) | collective-permute-done | bytes 294944 | tf_op jit(solution)/shard_map/ppermute | solution.py:433
  57.6 0.0 collective-permute-done.3.refs_1_
  57.6 2.6 %band_latents.1 = (bf16[576,1024]{1,0:T(8,128)(2,1)S(1)}, bf16[6,24,1024]{2,1,0:T(8,128)(2,1)}) custom-call(s32[2]{0:T(128)S(1)} %pad_add_fusion.place, bf16[576,576]{1,0:T(8,128)(2,1)S(1)} %copy-done.10, bf16[144,1024]{1,0:T(8,128)(2,1)S(1)} %window_attention.1.refs_0_, bf16[144,1024]{1,0:T(8,128)(2,1)S(1)} %collective-permute-done.3.refs_1_, ...), custom_call_target="tpu_custom_call" | custom-call | flops 679477248 | bytes 4000000 | tf_op jit(solution)/shard_map/band_latents/pallas_call | solution.py:200
  60.2 0.2 all-gather.3.cloned.1.call-done
  60.4 0.0 copy-start.5
  60.4 18.9 %slot_group.2 = (bf16[2,2,2,4,320,128]{5,4,3,2,1,0:T(8,128)(2,1)}, bf16[2,2,2,4,320,128]{5,4,3,2,1,0:T(8,128)(2,1)}, f32[576,1024]{1,0:T(8,128)S(1)}) custom-call(s32[2]{0:T(128)S(1)} %pad_add_fusion.place, s32[4]{0:T(128)S(1)} %copy-done.6, s32[1,4]{1,0:T(1,128)S(1)} %copy-done.7, s32[10]{0:T(128)S(1)} %copy-done.8, s32[576,1]{1,0:T(8,128)S(1)} %copy-done.4, ...), custom_call_target="tpu_custom_call" | custom-call | flops 9059696640 | bytes 20000000 | tf_op jit(solution)/shard_map/slot_group/pallas_call | solution.py:340
  79.4 3.3 %collective-permute-start.6 = (bf16[2,2,2,4,320,128]{5,4,3,2,1,0:T(8,128)(2,1)}, bf16[2,2,2,4,320,128]{5,4,3,2,1,0:T(8,128)(2,1)}, u32[]{:S(2)}, u32[]{:S(2)}) collective-permute-start(bf16[2,2,2,4,320,128]{5,4,3,2,1,0:T(8,128)(2,1)} %get-tuple-element.20), channel_id=1, source_target_pairs={{0,4},{4,0},{8,12},{12,8},{16,20},{20,16},{24,28},{28,24},{1,5},{5... | collective-permute-start | bytes 7864328 | tf_op jit(solution)/shard_map/ppermute | solution.py:439
  82.7 1.3 copy-done.2
  84.0 5.7 %slot_group.3 = (bf16[2,2,2,1,320,128]{5,4,3,2,1,0:T(8,128)(2,1)S(1)}, bf16[2,2,2,1,320,128]{5,4,3,2,1,0:T(8,128)(2,1)}, bf16[4,6,24,1024]{3,2,1,0:T(8,128)(2,1)S(1)}) custom-call(s32[2]{0:T(128)S(1)} %pad_add_fusion.place, s32[4]{0:T(128)S(1)} %copy-done.6, s32[1,4]{1,0:T(1,128)S(1)} %copy-done.7, s32[10]{0:T(128)S(1)} %copy-done.8, ...), custom_call_target="tpu_custom_call" | custom-call | flops 2264924160 | bytes 5000000 | tf_op jit(solution)/shard_map/slot_group/pallas_call | solution.py:340
  89.7 1.0 copy-done.3
  90.7 0.0 collective-permute-start.7
  90.8 0.0 reduce-scatter.2.cloned.1.call-update
  90.8 2.4 %collective-permute-done.7.refs_3_ = bf16[2,2,2,1,320,128]{5,4,3,2,1,0:T(8,128)(2,1)} collective-permute-done((bf16[2,2,2,1,320,128]{5,4,3,2,1,0:T(8,128)(2,1)}, bf16[2,2,2,1,320,128]{5,4,3,2,1,0:T(8,128)(2,1)}, u32[]{:S(2)}, u32[]{:S(2)}) %collective-permute-start.7) | collective-permute-done | bytes 655392 | tf_op jit(solution)/shard_map/ppermute | solution.py:439
  93.2 2.6 %halve.1 = (bf16[2,5,320,128]{3,2,1,0:T(8,128)(2,1)S(1)}, bf16[2,5,320,128]{3,2,1,0:T(8,128)(2,1)S(1)}, bf16[2,5,320,128]{3,2,1,0:T(8,128)(2,1)S(1)}, bf16[2,5,320,128]{3,2,1,0:T(8,128)(2,1)S(1)}) custom-call(bf16[2,2,2,4,320,128]{5,4,3,2,1,0:T(8,128)(2,1)S(1)} %copy-done, bf16[2,2,2,4,320,128]{5,4,3,2,1,0:T(8,128)(2,1)} %collective-permute-done.6.refs_1_, ...), custom_call_target="tpu_custom_call" | custom-call | flops 2000000 | bytes 6000000 | tf_op jit(solution)/shard_map/halve/pallas_call | solution.py:373
  95.8 5.4 %collective-permute-start.8 = (bf16[2,5,320,128]{3,2,1,0:T(8,128)(2,1)S(1)}, bf16[2,5,320,128]{3,2,1,0:T(8,128)(2,1)S(1)}, u32[]{:S(2)}, u32[]{:S(2)}) collective-permute-start(bf16[2,5,320,128]{3,2,1,0:T(8,128)(2,1)S(1)} %get-tuple-element.24), channel_id=1, source_target_pairs={{0,8},{4,12},{8,0},{12,4},{16,24},{20,28},{24,16},{28,20},{1,9},{5... | collective-permute-start | bytes 2457608 | tf_op jit(solution)/shard_map/ppermute | solution.py:439
  101.2 0.1 collective-permute-start.10
  101.3 18.6 %collective-permute-done.8 = bf16[2,5,320,128]{3,2,1,0:T(8,128)(2,1)S(1)} collective-permute-done((bf16[2,5,320,128]{3,2,1,0:T(8,128)(2,1)S(1)}, bf16[2,5,320,128]{3,2,1,0:T(8,128)(2,1)S(1)}, u32[]{:S(2)}, u32[]{:S(2)}) %collective-permute-start.8) | collective-permute-done | bytes 819232 | tf_op jit(solution)/shard_map/ppermute | solution.py:439
  120.0 0.2 fusion.1
  120.2 1.8 %collective-permute-start.9 = (bf16[5,320,128]{2,1,0:T(8,128)(2,1)S(1)}, bf16[5,320,128]{2,1,0:T(8,128)(2,1)S(1)}, u32[]{:S(2)}, u32[]{:S(2)}) collective-permute-start(bf16[5,320,128]{2,1,0:T(8,128)(2,1)S(1)} %get-tuple-element.29), channel_id=1, source_target_pairs={{0,16},{4,20},{8,24},{12,28},{16,0},{20,4},{24,8},{28,12},{1,17},{... | collective-permute-start | bytes 1228808 | tf_op jit(solution)/shard_map/ppermute | solution.py:439
  122.1 0.2 fusion.3
  122.3 0.4 collective-permute-start.11
  122.7 8.9 %collective-permute-done.9.refs_1_ = bf16[5,320,128]{2,1,0:T(8,128)(2,1)S(1)} collective-permute-done((bf16[5,320,128]{2,1,0:T(8,128)(2,1)S(1)}, bf16[5,320,128]{2,1,0:T(8,128)(2,1)S(1)}, u32[]{:S(2)}, u32[]{:S(2)}) %collective-permute-start.9) | collective-permute-done | bytes 409632 | tf_op jit(solution)/shard_map/ppermute | solution.py:439
  131.6 1.6 %collective-permute-done.11.refs_3_ = bf16[5,320,128]{2,1,0:T(8,128)(2,1)S(1)} collective-permute-done((bf16[5,320,128]{2,1,0:T(8,128)(2,1)S(1)}, bf16[5,320,128]{2,1,0:T(8,128)(2,1)S(1)}, u32[]{:S(2)}, u32[]{:S(2)}) %collective-permute-start.11) | collective-permute-done | bytes 409632 | tf_op jit(solution)/shard_map/ppermute | solution.py:439
  133.1 1.4 join_heads.1
  (22 shorter events, 0.1 us)
Async XLA Ops:
  7.2 53.3 %all-gather.3.cloned.1.call-start = ((), (), s32[]{:S(2)}) async-start(), calls=%async_computation.2 | async-start | bytes 7372800 | tf_op jit(solution)/shard_map/all_gather | solution.py:421
  7.9 126.6 %reduce-scatter.2.cloned.1.call-start = ((), (), s32[]{:S(2)}) async-start(), calls=%async_computation.1 | async-start | bytes 1474560 | tf_op jit(solution)/shard_map/reduce_scatter | solution.py:446
  8.9 7.9 %collective-permute-start = (bf16[6,6,1024]{2,1,0:T(8,128)(2,1)S(1)}, bf16[6,6,1024]{2,1,0:T(8,128)(2,1)S(1)}, u32[]{:S(2)}, u32[]{:S(2)}) collective-permute-start(bf16[6,6,1024]{2,1,0:T(8,128)(2,1)S(1)} %slice.36), channel_id=1, source_target_pairs={{0,1},{1,2},{2,3},{3,0},{4,5},{5,6},{6,7},{7,4},{8,9},{9,10},{10,1... | collective-permute-start | bytes 221192 | tf_op jit(solution)/shard_map/ppermute | solution.py:426
  17.8 5.5 %collective-permute-start.2 = (bf16[3,24,1024]{2,1,0:T(8,128)(2,1)S(1)}, bf16[3,24,1024]{2,1,0:T(8,128)(2,1)S(1)}, u32[]{:S(2)}, u32[]{:S(2)}) collective-permute-start(bf16[3,24,1024]{2,1,0:T(8,128)(2,1)S(1)} %get-tuple-element.31), channel_id=1, source_target_pairs={{4,0},{8,4},{12,8},{16,12},{20,16},{24,20},{28,24},{5,1},{9,5},{13... | collective-permute-start | bytes 442376 | tf_op jit(solution)/shard_map/ppermute | solution.py:429
  19.1 4.2 %collective-permute-start.1 = (bf16[3,24,1024]{2,1,0:T(8,128)(2,1)S(1)}, bf16[3,24,1024]{2,1,0:T(8,128)(2,1)S(1)}, u32[]{:S(2)}, u32[]{:S(2)}) collective-permute-start(bf16[3,24,1024]{2,1,0:T(8,128)(2,1)S(1)} %get-tuple-element.32), channel_id=1, source_target_pairs={{0,4},{4,8},{8,12},{12,16},{16,20},{20,24},{24,28},{1,5},{5,9},{9,... | collective-permute-start | bytes 442376 | tf_op jit(solution)/shard_map/ppermute | solution.py:428
  23.4 0.7 copy-start.9
  24.0 11.4 %copy-start.11 = (f32[10,1024]{1,0:T(8,128)S(1)}, f32[10,1024]{1,0:T(8,128)}, u32[]{:S(2)}) copy-start(f32[10,1024]{1,0:T(8,128)} %param.18) | copy-start | bytes 122884
  24.0 11.4 %copy-start.12 = (f32[10,1024]{1,0:T(8,128)S(1)}, f32[10,1024]{1,0:T(8,128)}, u32[]{:S(2)}) copy-start(f32[10,1024]{1,0:T(8,128)} %param.19) | copy-start | bytes 122884
  24.1 33.5 %copy-start.10 = (bf16[576,576]{1,0:T(8,128)(2,1)S(1)}, bf16[576,576]{1,0:T(8,128)(2,1)}, u32[]{:S(2)}) copy-start(bf16[576,576]{1,0:T(8,128)(2,1)} %constant.16.clone.chosen) | copy-start | bytes 1990660
  32.5 27.9 %copy-start.4 = (s32[576,1]{1,0:T(8,128)S(1)}, s32[576,1]{1,0:T(8,128)}, u32[]{:S(2)}) copy-start(s32[576,1]{1,0:T(8,128)} %constant.17.clone.tile_of) | copy-start | bytes 6916
  32.5 27.9 %copy-start.6 = (s32[4]{0:T(128)S(1)}, s32[4]{0:T(128)}, u32[]{:S(2)}) copy-start(s32[4]{0:T(128)} %counts.3) | copy-start | bytes 52
  32.5 27.9 %copy-start.7 = (s32[1,4]{1,0:T(1,128)S(1)}, s32[1,4]{1,0:T(1,128)}, u32[]{:S(2)}) copy-start(s32[1,4]{1,0:T(1,128)} %datasets.3) | copy-start | bytes 52
  32.5 27.9 %copy-start.8 = (s32[10]{0:T(128)S(1)}, s32[10]{0:T(128)}, u32[]{:S(2)}) copy-start(s32[10]{0:T(128)} %levels.3) | copy-start | bytes 124
  32.5 7.3 %collective-permute-start.5 = (bf16[144,1024]{1,0:T(8,128)(2,1)S(1)}, bf16[144,1024]{1,0:T(8,128)(2,1)S(1)}, u32[]{:S(2)}, u32[]{:S(2)}) collective-permute-start(bf16[144,1024]{1,0:T(8,128)(2,1)S(1)} %window_attention.1.refs_0_), channel_id=1, source_target_pairs={{0,3},{1,0},{2,1},{3,2},{4,7},{5,4},{6,5},{7,6},{8,11},{9,8},{10,9... | collective-permute-start | bytes 884744 | tf_op jit(solution)/shard_map/ppermute | solution.py:433
  34.4 23.2 %collective-permute-start.4 = (bf16[144,1024]{1,0:T(8,128)(2,1)S(1)}, bf16[144,1024]{1,0:T(8,128)(2,1)S(1)}, u32[]{:S(2)}, u32[]{:S(2)}) collective-permute-start(bf16[144,1024]{1,0:T(8,128)(2,1)S(1)} %window_attention.1.refs_0_), channel_id=1, source_target_pairs={{0,2},{1,3},{2,0},{3,1},{4,6},{5,7},{6,4},{7,5},{8,10},{9,11},{10,... | collective-permute-start | bytes 884744 | tf_op jit(solution)/shard_map/ppermute | solution.py:433
  34.4 23.2 %collective-permute-start.3 = (bf16[144,1024]{1,0:T(8,128)(2,1)S(1)}, bf16[144,1024]{1,0:T(8,128)(2,1)S(1)}, u32[]{:S(2)}, u32[]{:S(2)}) collective-permute-start(bf16[144,1024]{1,0:T(8,128)(2,1)S(1)} %window_attention.1.refs_0_), channel_id=1, source_target_pairs={{0,1},{1,2},{2,3},{3,0},{4,5},{5,6},{6,7},{7,4},{8,9},{9,10},{10,1... | collective-permute-start | bytes 884744 | tf_op jit(solution)/shard_map/ppermute | solution.py:433
  60.2 19.2 %copy-start.1 = (bf16[576,1024]{1,0:T(8,128)(2,1)}, bf16[576,1024]{1,0:T(8,128)(2,1)S(1)}, u32[]{:S(2)}) copy-start(bf16[576,1024]{1,0:T(8,128)(2,1)S(1)} %get-tuple-element.16.refs_0_) | copy-start | bytes 3538948
  60.4 22.3 %copy-start.5 = (s32[576,1]{1,0:T(8,128)S(1)}, s32[576,1]{1,0:T(8,128)}, u32[]{:S(2)}) copy-start(s32[576,1]{1,0:T(8,128)} %constant.17.clone.tile_of) | copy-start | bytes 6916
  79.4 13.8 %collective-permute-start.6 = (bf16[2,2,2,4,320,128]{5,4,3,2,1,0:T(8,128)(2,1)}, bf16[2,2,2,4,320,128]{5,4,3,2,1,0:T(8,128)(2,1)}, u32[]{:S(2)}, u32[]{:S(2)}) collective-permute-start(bf16[2,2,2,4,320,128]{5,4,3,2,1,0:T(8,128)(2,1)} %get-tuple-element.20), channel_id=1, source_target_pairs={{0,4},{4,0},{8,12},{12,8},{16,20},{20,16},{24,28},{28,24},{1,5},{5... | collective-permute-start | bytes 7864328 | tf_op jit(solution)/shard_map/ppermute | solution.py:439
  82.7 1.3 copy-start.2
  84.0 9.2 %copy-start = (bf16[2,2,2,4,320,128]{5,4,3,2,1,0:T(8,128)(2,1)S(1)}, bf16[2,2,2,4,320,128]{5,4,3,2,1,0:T(8,128)(2,1)}, u32[]{:S(2)}) copy-start(bf16[2,2,2,4,320,128]{5,4,3,2,1,0:T(8,128)(2,1)} %get-tuple-element.19.refs_0_) | copy-start | bytes 7864324
  89.7 1.0 copy-start.3
  90.7 2.4 %collective-permute-start.7 = (bf16[2,2,2,1,320,128]{5,4,3,2,1,0:T(8,128)(2,1)}, bf16[2,2,2,1,320,128]{5,4,3,2,1,0:T(8,128)(2,1)}, u32[]{:S(2)}, u32[]{:S(2)}) collective-permute-start(bf16[2,2,2,1,320,128]{5,4,3,2,1,0:T(8,128)(2,1)} %get-tuple-element.22), channel_id=1, source_target_pairs={{0,4},{4,0},{8,12},{12,8},{16,20},{20,16},{24,28},{28,24},{1,5},{5... | collective-permute-start | bytes 1966088 | tf_op jit(solution)/shard_map/ppermute | solution.py:439
  95.8 24.2 %collective-permute-start.8 = (bf16[2,5,320,128]{3,2,1,0:T(8,128)(2,1)S(1)}, bf16[2,5,320,128]{3,2,1,0:T(8,128)(2,1)S(1)}, u32[]{:S(2)}, u32[]{:S(2)}) collective-permute-start(bf16[2,5,320,128]{3,2,1,0:T(8,128)(2,1)S(1)} %get-tuple-element.24), channel_id=1, source_target_pairs={{0,8},{4,12},{8,0},{12,4},{16,24},{20,28},{24,16},{28,20},{1,9},{5... | collective-permute-start | bytes 2457608 | tf_op jit(solution)/shard_map/ppermute | solution.py:439
  101.2 20.9 %collective-permute-start.10 = (bf16[2,5,320,128]{3,2,1,0:T(8,128)(2,1)S(1)}, bf16[2,5,320,128]{3,2,1,0:T(8,128)(2,1)S(1)}, u32[]{:S(2)}, u32[]{:S(2)}) collective-permute-start(bf16[2,5,320,128]{3,2,1,0:T(8,128)(2,1)S(1)} %get-tuple-element.26), channel_id=1, source_target_pairs={{0,16},{4,20},{8,24},{12,28},{16,0},{20,4},{24,8},{28,12},{1,17},{... | collective-permute-start | bytes 2457608 | tf_op jit(solution)/shard_map/ppermute | solution.py:439
  120.2 11.3 %collective-permute-start.9 = (bf16[5,320,128]{2,1,0:T(8,128)(2,1)S(1)}, bf16[5,320,128]{2,1,0:T(8,128)(2,1)S(1)}, u32[]{:S(2)}, u32[]{:S(2)}) collective-permute-start(bf16[5,320,128]{2,1,0:T(8,128)(2,1)S(1)} %get-tuple-element.29), channel_id=1, source_target_pairs={{0,16},{4,20},{8,24},{12,28},{16,0},{20,4},{24,8},{28,12},{1,17},{... | collective-permute-start | bytes 1228808 | tf_op jit(solution)/shard_map/ppermute | solution.py:439
  122.3 10.8 %collective-permute-start.11 = (bf16[5,320,128]{2,1,0:T(8,128)(2,1)S(1)}, bf16[5,320,128]{2,1,0:T(8,128)(2,1)S(1)}, u32[]{:S(2)}, u32[]{:S(2)}) collective-permute-start(bf16[5,320,128]{2,1,0:T(8,128)(2,1)S(1)} %get-tuple-element.27), channel_id=1, source_target_pairs={{0,8},{4,12},{8,0},{12,4},{16,24},{20,28},{24,16},{28,20},{1,9},{5... | collective-permute-start | bytes 1228808 | tf_op jit(solution)/shard_map/ppermute | solution.py:439
Sparse Core Ops, SparseCore 0:
  9.9 50.4 all-gather.2
  90.9 33.2 reduce-scatter.1

commit v11 on v8

--- a/solution.py
+++ b/solution.py
@@ -336,7 +336,7 @@
     else:
         results = [sums]
     in_specs.extend(fixed(arg.shape) for arg in args[len(in_specs) :])
-    limit = (45 if final else 46) * 1024 * 1024
+    limit = (45 if final else 48) * 1024 * 1024
     return pl.pallas_call(
         functools.partial(slot_kernel, 2 * pair, lats, tiles, final),
         grid=(pairs,),
@@ -344,9 +344,7 @@
         in_specs=in_specs,
         out_specs=(half_spec, half_spec, *(fixed(r.shape) for r in results)),
         scratch_shapes=scratch,
-        compiler_params=pltpu.CompilerParams(
-            vmem_limit_bytes=limit, fuse_transposed_lhs_in_matmul=True
-        ),
+        compiler_params=pltpu.CompilerParams(vmem_limit_bytes=limit),
         cost_estimate=pl.CostEstimate(
             flops=pairs * 12 * places * width * outs, bytes_accessed=pairs * 5_000_000, transcendentals=0
         ),

time: 145 us -> 142 us (0.979)
  Pallas kernels: 42.6 us -> 40.6 us
    pallas_call x2, Pallas kernels: 27.6 us -> 25.6 us  [slot_group(): pl.pallas_call(functools.partial(slot_kernel, 2 * pair, lats, tiles, fina...]
  transfers between devices with their start and end apart: 18 -> 18, of which waited for: 7 -> 8; matrix products, arithmetic and copies ran while one was open for 3% -> 3% of each run, Pallas kernels for 15% -> 15%
where the time goes in v11:
time: 142 us
  waiting for transfers between devices  54.7 us (39%)
  Pallas kernels  40.6 us (29%)
  starting transfers between devices  25.8 us (18%)
  between operations  14.2 us (10%)
  local copies, waits for them, and re-layouts  3.83 us (3%)
  other arithmetic  2.66 us (2%)
    ppermute x10, waiting for transfers between devices, fast_local(): lax.ppermute(array, 'lat', [(i, i ^ bit) for i in range(lats)])  26.8 us
    pallas_call x2, Pallas kernels, slot_group(): pl.pallas_call(functools.partial(slot_kernel, 2 * pair, lats, tiles, fina...  25.6 us
    ppermute x3, waiting for transfers between devices, fast_local(): lax.ppermute(mine, 'var', [(i, (i + s) % tiles) for i in range(tiles)])  22.1 us
    ppermute x10, starting transfers between devices, fast_local(): lax.ppermute(array, 'lat', [(i, i ^ bit) for i in range(lats)])  15.4 us
    pallas_call x1, Pallas kernels, attention(): pl.pallas_call(functools.partial(attention_kernel, bands), out_shape=jax....  8.43 us
    ppermute x1, waiting for transfers between devices, fast_local(): left = lax.ppermute(patches[:, cols - HC:], 'var', right)  4.82 us
    ppermute x1, starting transfers between devices, fast_local(): left = lax.ppermute(patches[:, cols - HC:], 'var', right)  3.08 us
    ppermute x1, starting transfers between devices, fast_local(): above = lax.ppermute(shifted[HR:], 'lat', up)  3.04 us
  transfers between devices with their start and end apart: 18, of which 8 were waited for; matrix products, arithmetic and copies ran while one was open for 3% of the time, Pallas kernels for 15%

profile of v11, /device:TPU:0, one launch (start us, length us, event | category | flops | bytes accessed | tf_op | source)
XLA Modules:
  0.0 141.7 jit_solution(9995291054545010818)
XLA Ops:
  7.2 0.0 all-gather.3.cloned.1.call-start
  7.2 0.7 all-gather.3.cloned.1.call-update
  7.9 0.0 reduce-scatter.2.cloned.1.call-start
  7.9 0.9 slice.60
  8.9 3.1 %collective-permute-start = (bf16[6,6,1024]{2,1,0:T(8,128)(2,1)S(1)}, bf16[6,6,1024]{2,1,0:T(8,128)(2,1)S(1)}, u32[]{:S(2)}, u32[]{:S(2)}) collective-permute-start(bf16[6,6,1024]{2,1,0:T(8,128)(2,1)S(1)} %slice.60), channel_id=1, source_target_pairs={{0,1},{1,2},{2,3},{3,0},{4,5},{5,6},{6,7},{7,4},{8,9},{9,10},{10,1... | collective-permute-start | bytes 221192 | tf_op jit(solution)/shard_map/ppermute | solution.py:419
  11.9 4.8 %collective-permute-done = bf16[6,6,1024]{2,1,0:T(8,128)(2,1)S(1)} collective-permute-done((bf16[6,6,1024]{2,1,0:T(8,128)(2,1)S(1)}, bf16[6,6,1024]{2,1,0:T(8,128)(2,1)S(1)}, u32[]{:S(2)}, u32[]{:S(2)}) %collective-permute-start) | collective-permute-done | bytes 73760 | tf_op jit(solution)/shard_map/ppermute | solution.py:419
  16.8 1.1 fusion.5
  17.8 1.3 collective-permute-start.2
  19.1 3.0 %collective-permute-start.1 = (bf16[3,24,1024]{2,1,0:T(8,128)(2,1)S(1)}, bf16[3,24,1024]{2,1,0:T(8,128)(2,1)S(1)}, u32[]{:S(2)}, u32[]{:S(2)}) collective-permute-start(bf16[3,24,1024]{2,1,0:T(8,128)(2,1)S(1)} %get-tuple-element.40), channel_id=1, source_target_pairs={{0,4},{4,8},{8,12},{12,16},{16,20},{20,24},{24,28},{1,5},{5,9},{9,... | collective-permute-start | bytes 442376 | tf_op jit(solution)/shard_map/ppermute | solution.py:421
  22.2 0.1 pad_add_fusion.place
  22.3 1.1 pad_maximum_fusion.own
  23.4 0.0 copy-start.10
  23.4 0.7 copy-done.10
  24.1 8.4 %window_attention.1.refs_0_ = bf16[144,1024]{1,0:T(8,128)(2,1)S(1)} custom-call(s32[2]{0:T(128)S(1)} %pad_add_fusion.place, bf16[6,24,1024]{2,1,0:T(8,128)(2,1)S(1)} %pad_maximum_fusion.own, bf16[3,24,1024]{2,1,0:T(8,128)(2,1)S(1)} %collective-permute-done.1.above, bf16[3,24,1024]{2,1,0:T(8,128)(2,1)S(1)} %collective-permute-done.2.below, ...), custom_call_target="tpu_custom_call" | custom-call | flops 6000000000 | bytes 12000000 | tf_op jit(solution)/shard_map/window_attention/pallas_call | solution.py:141
  32.5 0.0 copy-start.3
  32.5 0.0 copy-start.5
  32.5 0.0 copy-start.7
  32.5 1.9 %collective-permute-start.5 = (bf16[144,1024]{1,0:T(8,128)(2,1)S(1)}, bf16[144,1024]{1,0:T(8,128)(2,1)S(1)}, u32[]{:S(2)}, u32[]{:S(2)}) collective-permute-start(bf16[144,1024]{1,0:T(8,128)(2,1)S(1)} %window_attention.1.refs_0_), channel_id=1, source_target_pairs={{0,3},{1,0},{2,1},{3,2},{4,7},{5,4},{6,5},{7,6},{8,11},{9,8},{10,9... | collective-permute-start | bytes 884744 | tf_op jit(solution)/shard_map/ppermute | solution.py:426
  34.4 1.0 collective-permute-start.3
  35.5 4.3 %collective-permute-done.5.refs_3_ = bf16[144,1024]{1,0:T(8,128)(2,1)S(1)} collective-permute-done((bf16[144,1024]{1,0:T(8,128)(2,1)S(1)}, bf16[144,1024]{1,0:T(8,128)(2,1)S(1)}, u32[]{:S(2)}, u32[]{:S(2)}) %collective-permute-start.5) | collective-permute-done | bytes 294944 | tf_op jit(solution)/shard_map/ppermute | solution.py:426
  39.8 17.7 %collective-permute-done.4.refs_2_ = bf16[144,1024]{1,0:T(8,128)(2,1)S(1)} collective-permute-done((bf16[144,1024]{1,0:T(8,128)(2,1)S(1)}, bf16[144,1024]{1,0:T(8,128)(2,1)S(1)}, u32[]{:S(2)}, u32[]{:S(2)}) %collective-permute-start.4) | collective-permute-done | bytes 294944 | tf_op jit(solution)/shard_map/ppermute | solution.py:426
  57.6 2.6 %band_latents.1 = (bf16[576,1024]{1,0:T(8,128)(2,1)S(1)}, bf16[6,24,1024]{2,1,0:T(8,128)(2,1)}) custom-call(s32[2]{0:T(128)S(1)} %pad_add_fusion.place, bf16[576,576]{1,0:T(8,128)(2,1)S(1)} %copy-done.11, bf16[144,1024]{1,0:T(8,128)(2,1)S(1)} %window_attention.1.refs_0_, bf16[144,1024]{1,0:T(8,128)(2,1)S(1)} %collective-permute-done.3.refs_1_, ...), custom_call_target="tpu_custom_call" | custom-call | flops 679477248 | bytes 4000000 | tf_op jit(solution)/shard_map/band_latents/pallas_call | solution.py:200
  60.2 0.2 all-gather.3.cloned.1.call-done
  60.4 0.0 copy-start.4
  60.4 18.9 %slot_group.2 = (bf16[2,2,2,4,320,128]{5,4,3,2,1,0:T(8,128)(2,1)}, bf16[2,2,2,4,320,128]{5,4,3,2,1,0:T(8,128)(2,1)}, f32[576,1024]{1,0:T(8,128)S(1)}) custom-call(s32[2]{0:T(128)S(1)} %pad_add_fusion.place, s32[4]{0:T(128)S(1)} %copy-done.5, s32[1,4]{1,0:T(1,128)S(1)} %copy-done.6, s32[10]{0:T(128)S(1)} %copy-done.7, s32[576,1]{1,0:T(8,128)S(1)} %copy-done.3, ...), custom_call_target="tpu_custom_call" | custom-call | flops 9059696640 | bytes 20000000 | tf_op jit(solution)/shard_map/slot_group/pallas_call | solution.py:340
  79.3 3.3 %collective-permute-start.6 = (bf16[2,2,2,4,320,128]{5,4,3,2,1,0:T(8,128)(2,1)}, bf16[2,2,2,4,320,128]{5,4,3,2,1,0:T(8,128)(2,1)}, u32[]{:S(2)}, u32[]{:S(2)}) collective-permute-start(bf16[2,2,2,4,320,128]{5,4,3,2,1,0:T(8,128)(2,1)} %get-tuple-element.24), channel_id=1, source_target_pairs={{0,4},{4,0},{8,12},{12,8},{16,20},{20,16},{24,28},{28,24},{1,5},{5... | collective-permute-start | bytes 7864328 | tf_op jit(solution)/shard_map/ppermute | solution.py:432
  82.7 1.3 copy-done.2
  84.0 6.7 %slot_group.3 = (bf16[2,2,2,1,320,128]{5,4,3,2,1,0:T(8,128)(2,1)S(1)}, bf16[2,2,2,1,320,128]{5,4,3,2,1,0:T(8,128)(2,1)S(1)}, bf16[4,6,24,1024]{3,2,1,0:T(8,128)(2,1)}) custom-call(s32[2]{0:T(128)S(1)} %pad_add_fusion.place, s32[4]{0:T(128)S(1)} %copy-done.5, s32[1,4]{1,0:T(1,128)S(1)} %copy-done.6, s32[10]{0:T(128)S(1)} %copy-done.7, ...), custom_call_target="tpu_custom_call" | custom-call | flops 2264924160 | bytes 5000000 | tf_op jit(solution)/shard_map/slot_group/pallas_call | solution.py:340
  90.7 0.8 copy-done.8
  91.5 0.0 reduce-scatter.2.cloned.1.call-update
  91.6 2.4 %halve.2 = (bf16[2,4,320,128]{3,2,1,0:T(8,128)(2,1)S(1)}, bf16[2,4,320,128]{3,2,1,0:T(8,128)(2,1)S(1)}, bf16[2,4,320,128]{3,2,1,0:T(8,128)(2,1)S(1)}, bf16[2,4,320,128]{3,2,1,0:T(8,128)(2,1)S(1)}) custom-call(bf16[2,2,2,4,320,128]{5,4,3,2,1,0:T(8,128)(2,1)S(1)} %copy-done, bf16[2,2,2,4,320,128]{5,4,3,2,1,0:T(8,128)(2,1)} %collective-permute-done.6.came, ...), custom_call_target="tpu_custom_call" | custom-call | flops 2000000 | bytes 6000000 | tf_op jit(solution)/shard_map/halve/pallas_call | solution.py:366
  94.0 5.3 %collective-permute-start.7 = (bf16[2,4,320,128]{3,2,1,0:T(8,128)(2,1)S(1)}, bf16[2,4,320,128]{3,2,1,0:T(8,128)(2,1)S(1)}, u32[]{:S(2)}, u32[]{:S(2)}) collective-permute-start(bf16[2,4,320,128]{3,2,1,0:T(8,128)(2,1)S(1)} %get-tuple-element.26), channel_id=1, source_target_pairs={{0,8},{4,12},{8,0},{12,4},{16,24},{20,28},{24,16},{28,20},{1,9},{5... | collective-permute-start | bytes 1966088 | tf_op jit(solution)/shard_map/ppermute | solution.py:432
  99.3 0.2 collective-permute-start.11
  99.5 0.4 collective-permute-start.9
  99.9 14.8 %collective-permute-done.7.refs_0_ = bf16[2,4,320,128]{3,2,1,0:T(8,128)(2,1)S(1)} collective-permute-done((bf16[2,4,320,128]{3,2,1,0:T(8,128)(2,1)S(1)}, bf16[2,4,320,128]{3,2,1,0:T(8,128)(2,1)S(1)}, u32[]{:S(2)}, u32[]{:S(2)}) %collective-permute-start.7) | collective-permute-done | bytes 655392 | tf_op jit(solution)/shard_map/ppermute | solution.py:432
  114.7 0.2 fusion.1
  114.9 1.8 %collective-permute-start.8 = (bf16[4,320,128]{2,1,0:T(8,128)(2,1)S(1)}, bf16[4,320,128]{2,1,0:T(8,128)(2,1)S(1)}, u32[]{:S(2)}, u32[]{:S(2)}) collective-permute-start(bf16[4,320,128]{2,1,0:T(8,128)(2,1)S(1)} %get-tuple-element.37), channel_id=1, source_target_pairs={{0,16},{4,20},{8,24},{12,28},{16,0},{20,4},{24,8},{28,12},{1,17},{... | collective-permute-start | bytes 983048 | tf_op jit(solution)/shard_map/ppermute | solution.py:432
  116.7 0.2 halve.3
  116.8 0.4 collective-permute-start.12
  117.2 1.7 %collective-permute-start.14 = (bf16[2,1,320,128]{3,2,1,0:T(8,128)(2,1)S(1)}, bf16[2,1,320,128]{3,2,1,0:T(8,128)(2,1)S(1)}, u32[]{:S(2)}, u32[]{:S(2)}) collective-permute-start(bf16[2,1,320,128]{3,2,1,0:T(8,128)(2,1)S(1)} %get-tuple-element.34), channel_id=1, source_target_pairs={{0,16},{4,20},{8,24},{12,28},{16,0},{20,4},{24,8},{28,12},{1,17},{... | collective-permute-start | bytes 491528 | tf_op jit(solution)/shard_map/ppermute | solution.py:432
  118.9 0.2 fusion.3
  119.1 0.4 collective-permute-start.10
  119.4 4.6 %collective-permute-done.12 = bf16[2,1,320,128]{3,2,1,0:T(8,128)(2,1)S(1)} collective-permute-done((bf16[2,1,320,128]{3,2,1,0:T(8,128)(2,1)S(1)}, bf16[2,1,320,128]{3,2,1,0:T(8,128)(2,1)S(1)}, u32[]{:S(2)}, u32[]{:S(2)}) %collective-permute-start.12) | collective-permute-done | bytes 163872 | tf_op jit(solution)/shard_map/ppermute | solution.py:432
  124.1 0.3 collective-permute-start.13
  124.4 4.5 %collective-permute-done.14 = bf16[2,1,320,128]{3,2,1,0:T(8,128)(2,1)S(1)} collective-permute-done((bf16[2,1,320,128]{3,2,1,0:T(8,128)(2,1)S(1)}, bf16[2,1,320,128]{3,2,1,0:T(8,128)(2,1)S(1)}, u32[]{:S(2)}, u32[]{:S(2)}) %collective-permute-start.14) | collective-permute-done | bytes 163872 | tf_op jit(solution)/shard_map/ppermute | solution.py:432
  129.0 1.6 %collective-permute-start.15 = (bf16[1,320,128]{2,1,0:T(8,128)(2,1)S(1)}, bf16[1,320,128]{2,1,0:T(8,128)(2,1)S(1)}, u32[]{:S(2)}, u32[]{:S(2)}) collective-permute-start(bf16[1,320,128]{2,1,0:T(8,128)(2,1)S(1)} %get-tuple-element.41), channel_id=1, source_target_pairs={{0,8},{4,12},{8,0},{12,4},{16,24},{20,28},{24,16},{28,20},{1,9},{5... | collective-permute-start | bytes 245768 | tf_op jit(solution)/shard_map/ppermute | solution.py:432
  130.6 2.9 %collective-permute-done.15.refs_7_ = bf16[1,320,128]{2,1,0:T(8,128)(2,1)S(1)} collective-permute-done((bf16[1,320,128]{2,1,0:T(8,128)(2,1)S(1)}, bf16[1,320,128]{2,1,0:T(8,128)(2,1)S(1)}, u32[]{:S(2)}, u32[]{:S(2)}) %collective-permute-start.15) | collective-permute-done | bytes 81952 | tf_op jit(solution)/shard_map/ppermute | solution.py:432
  133.5 1.4 join_heads.1
  (35 shorter events, 0.2 us)
Async XLA Ops:
  7.2 53.3 %all-gather.3.cloned.1.call-start = ((), (), s32[]{:S(2)}) async-start(), calls=%async_computation.2 | async-start | bytes 7372800 | tf_op jit(solution)/shard_map/all_gather | solution.py:414
  7.9 127.0 %reduce-scatter.2.cloned.1.call-start = ((), (), s32[]{:S(2)}) async-start(), calls=%async_computation.1 | async-start | bytes 1474560 | tf_op jit(solution)/shard_map/reduce_scatter | solution.py:439
  8.9 7.9 %collective-permute-start = (bf16[6,6,1024]{2,1,0:T(8,128)(2,1)S(1)}, bf16[6,6,1024]{2,1,0:T(8,128)(2,1)S(1)}, u32[]{:S(2)}, u32[]{:S(2)}) collective-permute-start(bf16[6,6,1024]{2,1,0:T(8,128)(2,1)S(1)} %slice.60), channel_id=1, source_target_pairs={{0,1},{1,2},{2,3},{3,0},{4,5},{5,6},{6,7},{7,4},{8,9},{9,10},{10,1... | collective-permute-start | bytes 221192 | tf_op jit(solution)/shard_map/ppermute | solution.py:419
  17.8 5.5 %collective-permute-start.2 = (bf16[3,24,1024]{2,1,0:T(8,128)(2,1)S(1)}, bf16[3,24,1024]{2,1,0:T(8,128)(2,1)S(1)}, u32[]{:S(2)}, u32[]{:S(2)}) collective-permute-start(bf16[3,24,1024]{2,1,0:T(8,128)(2,1)S(1)} %get-tuple-element.39), channel_id=1, source_target_pairs={{4,0},{8,4},{12,8},{16,12},{20,16},{24,20},{28,24},{5,1},{9,5},{13... | collective-permute-start | bytes 442376 | tf_op jit(solution)/shard_map/ppermute | solution.py:422
  19.1 4.2 %collective-permute-start.1 = (bf16[3,24,1024]{2,1,0:T(8,128)(2,1)S(1)}, bf16[3,24,1024]{2,1,0:T(8,128)(2,1)S(1)}, u32[]{:S(2)}, u32[]{:S(2)}) collective-permute-start(bf16[3,24,1024]{2,1,0:T(8,128)(2,1)S(1)} %get-tuple-element.40), channel_id=1, source_target_pairs={{0,4},{4,8},{8,12},{12,16},{16,20},{20,24},{24,28},{1,5},{5,9},{9,... | collective-permute-start | bytes 442376 | tf_op jit(solution)/shard_map/ppermute | solution.py:421
  23.4 0.7 copy-start.10
  24.0 11.4 %copy-start.12 = (f32[10,1024]{1,0:T(8,128)S(1)}, f32[10,1024]{1,0:T(8,128)}, u32[]{:S(2)}) copy-start(f32[10,1024]{1,0:T(8,128)} %param.18) | copy-start | bytes 122884
  24.1 11.4 %copy-start.13 = (f32[10,1024]{1,0:T(8,128)S(1)}, f32[10,1024]{1,0:T(8,128)}, u32[]{:S(2)}) copy-start(f32[10,1024]{1,0:T(8,128)} %param.19) | copy-start | bytes 122884
  24.1 33.5 %copy-start.11 = (bf16[576,576]{1,0:T(8,128)(2,1)S(1)}, bf16[576,576]{1,0:T(8,128)(2,1)}, u32[]{:S(2)}) copy-start(bf16[576,576]{1,0:T(8,128)(2,1)} %constant.16.clone.chosen) | copy-start | bytes 1990660
  32.5 27.9 %copy-start.3 = (s32[576,1]{1,0:T(8,128)S(1)}, s32[576,1]{1,0:T(8,128)}, u32[]{:S(2)}) copy-start(s32[576,1]{1,0:T(8,128)} %constant.17.clone.tile_of) | copy-start | bytes 6916
  32.5 27.9 %copy-start.5 = (s32[4]{0:T(128)S(1)}, s32[4]{0:T(128)}, u32[]{:S(2)}) copy-start(s32[4]{0:T(128)} %counts.3) | copy-start | bytes 52
  32.5 27.9 %copy-start.6 = (s32[1,4]{1,0:T(1,128)S(1)}, s32[1,4]{1,0:T(1,128)}, u32[]{:S(2)}) copy-start(s32[1,4]{1,0:T(1,128)} %datasets.3) | copy-start | bytes 52
  32.5 27.9 %copy-start.7 = (s32[10]{0:T(128)S(1)}, s32[10]{0:T(128)}, u32[]{:S(2)}) copy-start(s32[10]{0:T(128)} %levels.3) | copy-start | bytes 124
  32.5 7.3 %collective-permute-start.5 = (bf16[144,1024]{1,0:T(8,128)(2,1)S(1)}, bf16[144,1024]{1,0:T(8,128)(2,1)S(1)}, u32[]{:S(2)}, u32[]{:S(2)}) collective-permute-start(bf16[144,1024]{1,0:T(8,128)(2,1)S(1)} %window_attention.1.refs_0_), channel_id=1, source_target_pairs={{0,3},{1,0},{2,1},{3,2},{4,7},{5,4},{6,5},{7,6},{8,11},{9,8},{10,9... | collective-permute-start | bytes 884744 | tf_op jit(solution)/shard_map/ppermute | solution.py:426
  34.4 23.2 %collective-permute-start.4 = (bf16[144,1024]{1,0:T(8,128)(2,1)S(1)}, bf16[144,1024]{1,0:T(8,128)(2,1)S(1)}, u32[]{:S(2)}, u32[]{:S(2)}) collective-permute-start(bf16[144,1024]{1,0:T(8,128)(2,1)S(1)} %window_attention.1.refs_0_), channel_id=1, source_target_pairs={{0,2},{1,3},{2,0},{3,1},{4,6},{5,7},{6,4},{7,5},{8,10},{9,11},{10,... | collective-permute-start | bytes 884744 | tf_op jit(solution)/shard_map/ppermute | solution.py:426
  34.4 23.2 %collective-permute-start.3 = (bf16[144,1024]{1,0:T(8,128)(2,1)S(1)}, bf16[144,1024]{1,0:T(8,128)(2,1)S(1)}, u32[]{:S(2)}, u32[]{:S(2)}) collective-permute-start(bf16[144,1024]{1,0:T(8,128)(2,1)S(1)} %window_attention.1.refs_0_), channel_id=1, source_target_pairs={{0,1},{1,2},{2,3},{3,0},{4,5},{5,6},{6,7},{7,4},{8,9},{9,10},{10,1... | collective-permute-start | bytes 884744 | tf_op jit(solution)/shard_map/ppermute | solution.py:426
  60.2 19.2 %copy-start.1 = (bf16[576,1024]{1,0:T(8,128)(2,1)}, bf16[576,1024]{1,0:T(8,128)(2,1)S(1)}, u32[]{:S(2)}) copy-start(bf16[576,1024]{1,0:T(8,128)(2,1)S(1)} %get-tuple-element.20.refs_0_) | copy-start | bytes 3538948
  60.4 22.3 %copy-start.4 = (s32[576,1]{1,0:T(8,128)S(1)}, s32[576,1]{1,0:T(8,128)}, u32[]{:S(2)}) copy-start(s32[576,1]{1,0:T(8,128)} %constant.17.clone.tile_of) | copy-start | bytes 6916
  79.3 12.2 %collective-permute-start.6 = (bf16[2,2,2,4,320,128]{5,4,3,2,1,0:T(8,128)(2,1)}, bf16[2,2,2,4,320,128]{5,4,3,2,1,0:T(8,128)(2,1)}, u32[]{:S(2)}, u32[]{:S(2)}) collective-permute-start(bf16[2,2,2,4,320,128]{5,4,3,2,1,0:T(8,128)(2,1)} %get-tuple-element.24), channel_id=1, source_target_pairs={{0,4},{4,0},{8,12},{12,8},{16,20},{20,16},{24,28},{28,24},{1,5},{5... | collective-permute-start | bytes 7864328 | tf_op jit(solution)/shard_map/ppermute | solution.py:432
  82.7 1.3 copy-start.2
  84.0 7.6 %copy-start = (bf16[2,2,2,4,320,128]{5,4,3,2,1,0:T(8,128)(2,1)S(1)}, bf16[2,2,2,4,320,128]{5,4,3,2,1,0:T(8,128)(2,1)}, u32[]{:S(2)}) copy-start(bf16[2,2,2,4,320,128]{5,4,3,2,1,0:T(8,128)(2,1)} %get-tuple-element.23.keep) | copy-start | bytes 7864324
  90.7 0.8 copy-start.8
  91.6 7.7 %copy-start.9 = (bf16[2,2,2,1,320,128]{5,4,3,2,1,0:T(8,128)(2,1)S(1)}, bf16[2,2,2,1,320,128]{5,4,3,2,1,0:T(8,128)(2,1)}, u32[]{:S(2)}) copy-start(bf16[2,2,2,1,320,128]{5,4,3,2,1,0:T(8,128)(2,1)} %copy-done.8) | copy-start | bytes 1966084
  94.0 20.7 %collective-permute-start.7 = (bf16[2,4,320,128]{3,2,1,0:T(8,128)(2,1)S(1)}, bf16[2,4,320,128]{3,2,1,0:T(8,128)(2,1)S(1)}, u32[]{:S(2)}, u32[]{:S(2)}) collective-permute-start(bf16[2,4,320,128]{3,2,1,0:T(8,128)(2,1)S(1)} %get-tuple-element.26), channel_id=1, source_target_pairs={{0,8},{4,12},{8,0},{12,4},{16,24},{20,28},{24,16},{28,20},{1,9},{5... | collective-permute-start | bytes 1966088 | tf_op jit(solution)/shard_map/ppermute | solution.py:432
  99.3 17.4 %collective-permute-start.11 = (bf16[2,2,2,1,320,128]{5,4,3,2,1,0:T(8,128)(2,1)S(1)}, bf16[2,2,2,1,320,128]{5,4,3,2,1,0:T(8,128)(2,1)S(1)}, u32[]{:S(2)}, u32[]{:S(2)}) collective-permute-start(bf16[2,2,2,1,320,128]{5,4,3,2,1,0:T(8,128)(2,1)S(1)} %copy-done.9), channel_id=1, source_target_pairs={{0,4},{4,0},{8,12},{12,8},{16,20},{20,16},{24,28},{28,24},{1,5},{5... | collective-permute-start | bytes 1966088 | tf_op jit(solution)/shard_map/ppermute | solution.py:432
  99.5 17.2 %collective-permute-start.9 = (bf16[2,4,320,128]{3,2,1,0:T(8,128)(2,1)S(1)}, bf16[2,4,320,128]{3,2,1,0:T(8,128)(2,1)S(1)}, u32[]{:S(2)}, u32[]{:S(2)}) collective-permute-start(bf16[2,4,320,128]{3,2,1,0:T(8,128)(2,1)S(1)} %get-tuple-element.28), channel_id=1, source_target_pairs={{0,16},{4,20},{8,24},{12,28},{16,0},{20,4},{24,8},{28,12},{1,17},{... | collective-permute-start | bytes 1966088 | tf_op jit(solution)/shard_map/ppermute | solution.py:432
  114.9 18.6 %collective-permute-start.8 = (bf16[4,320,128]{2,1,0:T(8,128)(2,1)S(1)}, bf16[4,320,128]{2,1,0:T(8,128)(2,1)S(1)}, u32[]{:S(2)}, u32[]{:S(2)}) collective-permute-start(bf16[4,320,128]{2,1,0:T(8,128)(2,1)S(1)} %get-tuple-element.37), channel_id=1, source_target_pairs={{0,16},{4,20},{8,24},{12,28},{16,0},{20,4},{24,8},{28,12},{1,17},{... | collective-permute-start | bytes 983048 | tf_op jit(solution)/shard_map/ppermute | solution.py:432
  116.8 7.2 %collective-permute-start.12 = (bf16[2,1,320,128]{3,2,1,0:T(8,128)(2,1)S(1)}, bf16[2,1,320,128]{3,2,1,0:T(8,128)(2,1)S(1)}, u32[]{:S(2)}, u32[]{:S(2)}) collective-permute-start(bf16[2,1,320,128]{3,2,1,0:T(8,128)(2,1)S(1)} %get-tuple-element.32), channel_id=1, source_target_pairs={{0,8},{4,12},{8,0},{12,4},{16,24},{20,28},{24,16},{28,20},{1,9},{5... | collective-permute-start | bytes 491528 | tf_op jit(solution)/shard_map/ppermute | solution.py:432
  117.2 11.7 %collective-permute-start.14 = (bf16[2,1,320,128]{3,2,1,0:T(8,128)(2,1)S(1)}, bf16[2,1,320,128]{3,2,1,0:T(8,128)(2,1)S(1)}, u32[]{:S(2)}, u32[]{:S(2)}) collective-permute-start(bf16[2,1,320,128]{3,2,1,0:T(8,128)(2,1)S(1)} %get-tuple-element.34), channel_id=1, source_target_pairs={{0,16},{4,20},{8,24},{12,28},{16,0},{20,4},{24,8},{28,12},{1,17},{... | collective-permute-start | bytes 491528 | tf_op jit(solution)/shard_map/ppermute | solution.py:432
  119.1 14.4 %collective-permute-start.10 = (bf16[4,320,128]{2,1,0:T(8,128)(2,1)S(1)}, bf16[4,320,128]{2,1,0:T(8,128)(2,1)S(1)}, u32[]{:S(2)}, u32[]{:S(2)}) collective-permute-start(bf16[4,320,128]{2,1,0:T(8,128)(2,1)S(1)} %get-tuple-element.35), channel_id=1, source_target_pairs={{0,8},{4,12},{8,0},{12,4},{16,24},{20,28},{24,16},{28,20},{1,9},{5... | collective-permute-start | bytes 983048 | tf_op jit(solution)/shard_map/ppermute | solution.py:432
  124.1 6.5 %collective-permute-start.13 = (bf16[1,320,128]{2,1,0:T(8,128)(2,1)S(1)}, bf16[1,320,128]{2,1,0:T(8,128)(2,1)S(1)}, u32[]{:S(2)}, u32[]{:S(2)}) collective-permute-start(bf16[1,320,128]{2,1,0:T(8,128)(2,1)S(1)} %get-tuple-element.43), channel_id=1, source_target_pairs={{0,16},{4,20},{8,24},{12,28},{16,0},{20,4},{24,8},{28,12},{1,17},{... | collective-permute-start | bytes 245768 | tf_op jit(solution)/shard_map/ppermute | solution.py:432
  129.0 4.5 %collective-permute-start.15 = (bf16[1,320,128]{2,1,0:T(8,128)(2,1)S(1)}, bf16[1,320,128]{2,1,0:T(8,128)(2,1)S(1)}, u32[]{:S(2)}, u32[]{:S(2)}) collective-permute-start(bf16[1,320,128]{2,1,0:T(8,128)(2,1)S(1)} %get-tuple-element.41), channel_id=1, source_target_pairs={{0,8},{4,12},{8,0},{12,4},{16,24},{20,28},{24,16},{28,20},{1,9},{5... | collective-permute-start | bytes 245768 | tf_op jit(solution)/shard_map/ppermute | solution.py:432
Sparse Core Ops, SparseCore 0:
  9.9 50.4 all-gather.2
  91.7 32.8 reduce-scatter.1

commit v12 on v7

--- a/solution.py
+++ b/solution.py
@@ -417,9 +417,10 @@
     keep_a, send_a, so_far, band, latent = slot_group(0, most, *common, pieces, None)
     keep_b, send_b, terms = slot_group(most, slots // 2 - most, *common, None, (band, so_far))
     grad_latent = lax.psum_scatter(terms, "var", scatter_dimension=0, tiled=False)
-    pairs, came = [], [terms]
+    pairs, after = [], [terms]
     for keep, send in ((keep_a, send_a), (keep_b, send_b)):
-        kept, sent = halve(keep, flip(send, 1), came)
+        kept, sent = halve(keep, flip(send, 1), after)
+        after = list(sent)
         came = [flip(sent[k], bits[k]) for k in range(2)]
         for k in range(2):
             last = flip(add(kept[k][1], came[k][1]), bits[1 - k])

time: 139 us -> 134 us (0.964)
  waiting for transfers between devices: 57.3 us -> 51.3 us
    ppermute x10, waiting for transfers between devices: 26.8 us -> 20.9 us  [fast_local(): lax.ppermute(array, 'lat', [(i, i ^ bit) for i in range(lats)])]
  transfers between devices with their start and end apart: 18 -> 18, of which waited for: 8 -> 7; matrix products, arithmetic and copies ran while one was open for 3% -> 3% of each run, Pallas kernels for 14% -> 14%
where the time goes in v12:
time: 134 us
  waiting for transfers between devices  51.3 us (38%)
  Pallas kernels  39.1 us (29%)
  starting transfers between devices  23.9 us (18%)
  between operations  14.2 us (11%)
  other arithmetic  2.66 us (2%)
  local copies, waits for them, and re-layouts  2.54 us (2%)
    pallas_call x2, Pallas kernels, slot_group(): pl.pallas_call(functools.partial(slot_kernel, 2 * pair, lats, tiles, fina...  26.8 us
    ppermute x3, waiting for transfers between devices, fast_local(): lax.ppermute(mine, 'var', [(i, (i + s) % tiles) for i in range(tiles)])  22.1 us
    ppermute x10, waiting for transfers between devices, fast_local(): lax.ppermute(array, 'lat', [(i, i ^ bit) for i in range(lats)])  20.9 us
    ppermute x10, starting transfers between devices, fast_local(): lax.ppermute(array, 'lat', [(i, i ^ bit) for i in range(lats)])  13.5 us
    pallas_call x1, Pallas kernels, attention(): pl.pallas_call(functools.partial(attention_kernel, bands), out_shape=jax....  8.42 us
    ppermute x1, waiting for transfers between devices, fast_local(): left = lax.ppermute(patches[:, cols - HC:], 'var', right)  4.82 us
    ppermute x1, starting transfers between devices, fast_local(): left = lax.ppermute(patches[:, cols - HC:], 'var', right)  3.08 us
    ppermute x1, starting transfers between devices, fast_local(): above = lax.ppermute(shifted[HR:], 'lat', up)  3.04 us
  transfers between devices with their start and end apart: 18, of which 7 were waited for; matrix products, arithmetic and copies ran while one was open for 3% of the time, Pallas kernels for 14%

profile of v12, /device:TPU:0, one launch (start us, length us, event | category | flops | bytes accessed | tf_op | source)
XLA Modules:
  0.0 133.7 jit_solution(10648488073778004449)
XLA Ops:
  7.2 0.0 all-gather.3.cloned.1.call-start
  7.2 0.7 all-gather.3.cloned.1.call-update
  7.9 0.0 reduce-scatter.2.cloned.1.call-start
  7.9 0.9 slice.60
  8.9 3.1 %collective-permute-start = (bf16[6,6,1024]{2,1,0:T(8,128)(2,1)S(1)}, bf16[6,6,1024]{2,1,0:T(8,128)(2,1)S(1)}, u32[]{:S(2)}, u32[]{:S(2)}) collective-permute-start(bf16[6,6,1024]{2,1,0:T(8,128)(2,1)S(1)} %slice.60), channel_id=1, source_target_pairs={{0,1},{1,2},{2,3},{3,0},{4,5},{5,6},{6,7},{7,4},{8,9},{9,10},{10,1... | collective-permute-start | bytes 221192 | tf_op jit(solution)/shard_map/ppermute | solution.py:400
  11.9 4.8 %collective-permute-done = bf16[6,6,1024]{2,1,0:T(8,128)(2,1)S(1)} collective-permute-done((bf16[6,6,1024]{2,1,0:T(8,128)(2,1)S(1)}, bf16[6,6,1024]{2,1,0:T(8,128)(2,1)S(1)}, u32[]{:S(2)}, u32[]{:S(2)}) %collective-permute-start) | collective-permute-done | bytes 73760 | tf_op jit(solution)/shard_map/ppermute | solution.py:400
  16.8 1.1 fusion.5
  17.8 1.3 collective-permute-start.2
  19.1 3.0 %collective-permute-start.1 = (bf16[3,24,1024]{2,1,0:T(8,128)(2,1)S(1)}, bf16[3,24,1024]{2,1,0:T(8,128)(2,1)S(1)}, u32[]{:S(2)}, u32[]{:S(2)}) collective-permute-start(bf16[3,24,1024]{2,1,0:T(8,128)(2,1)S(1)} %get-tuple-element.40), channel_id=1, source_target_pairs={{0,4},{4,8},{8,12},{12,16},{16,20},{20,24},{24,28},{1,5},{5,9},{9,... | collective-permute-start | bytes 442376 | tf_op jit(solution)/shard_map/ppermute | solution.py:402
  22.2 0.1 pad_add_fusion.place
  22.3 1.1 pad_maximum_fusion.own
  23.3 0.0 collective-permute-done.1.above
  23.4 0.0 copy-start.7
  23.4 0.7 copy-done.7
  24.1 0.0 copy-start.4
  24.1 0.0 copy-start.5
  24.1 0.0 copy-start.8
  24.1 8.4 %window_attention.1.refs_1_ = bf16[144,1024]{1,0:T(8,128)(2,1)S(1)} custom-call(s32[2]{0:T(128)S(1)} %pad_add_fusion.place, bf16[6,24,1024]{2,1,0:T(8,128)(2,1)S(1)} %pad_maximum_fusion.own, bf16[3,24,1024]{2,1,0:T(8,128)(2,1)S(1)} %collective-permute-done.1.above, bf16[3,24,1024]{2,1,0:T(8,128)(2,1)S(1)} %collective-permute-done.2.below, ...), custom_call_target="tpu_custom_call" | custom-call | flops 6000000000 | bytes 12000000 | tf_op jit(solution)/shard_map/window_attention/pallas_call | solution.py:137
  32.5 1.9 %collective-permute-start.5 = (bf16[144,1024]{1,0:T(8,128)(2,1)S(1)}, bf16[144,1024]{1,0:T(8,128)(2,1)S(1)}, u32[]{:S(2)}, u32[]{:S(2)}) collective-permute-start(bf16[144,1024]{1,0:T(8,128)(2,1)S(1)} %window_attention.1.refs_1_), channel_id=1, source_target_pairs={{0,3},{1,0},{2,1},{3,2},{4,7},{5,4},{6,5},{7,6},{8,11},{9,8},{10,9... | collective-permute-start | bytes 884744 | tf_op jit(solution)/shard_map/ppermute | solution.py:407
  34.4 1.0 collective-permute-start.3
  35.5 4.3 %collective-permute-done.5.refs_4_ = bf16[144,1024]{1,0:T(8,128)(2,1)S(1)} collective-permute-done((bf16[144,1024]{1,0:T(8,128)(2,1)S(1)}, bf16[144,1024]{1,0:T(8,128)(2,1)S(1)}, u32[]{:S(2)}, u32[]{:S(2)}) %collective-permute-start.5) | collective-permute-done | bytes 294944 | tf_op jit(solution)/shard_map/ppermute | solution.py:407
  39.8 17.7 %collective-permute-done.4.refs_3_ = bf16[144,1024]{1,0:T(8,128)(2,1)S(1)} collective-permute-done((bf16[144,1024]{1,0:T(8,128)(2,1)S(1)}, bf16[144,1024]{1,0:T(8,128)(2,1)S(1)}, u32[]{:S(2)}, u32[]{:S(2)}) %collective-permute-start.4) | collective-permute-done | bytes 294944 | tf_op jit(solution)/shard_map/ppermute | solution.py:407
  57.6 2.8 %all-gather.3.cloned.1.call-done = bf16[80,320,128]{2,1,0:T(8,128)(2,1)} async-done(((bf16[10,320,128]{2,1,0:T(8,128)(2,1)}), bf16[80,320,128]{2,1,0:T(8,128)(2,1)}) %all-gather.3.cloned.1.call-update) | async-done | bytes 6553616 | tf_op jit(solution)/shard_map/all_gather | solution.py:395
  60.4 0.0 copy-start.2
  60.5 20.1 %slot_group.2 = (bf16[2,2,2,4,320,128]{5,4,3,2,1,0:T(8,128)(2,1)}, bf16[2,2,2,4,320,128]{5,4,3,2,1,0:T(8,128)(2,1)}, f32[576,1024]{1,0:T(8,128)S(1)}, bf16[576,1024]{1,0:T(8,128)(2,1)S(1)}, bf16[6,24,1024]{2,1,0:T(8,128)(2,1)}) custom-call(s32[2]{0:T(128)S(1)} %pad_add_fusion.place, s32[4]{0:T(128)S(1)} %copy-done.3, s32[1,4]{1,0:T(1,128)S(1)} %copy-done.4, ...), custom_call_target="tpu_custom_call" | custom-call | flops 9059696640 | bytes 20000000 | tf_op jit(solution)/shard_map/slot_group/pallas_call | solution.py:321
  80.5 0.5 collective-permute-start.6
  81.0 6.7 %slot_group.3 = (bf16[2,2,2,1,320,128]{5,4,3,2,1,0:T(8,128)(2,1)S(1)}, bf16[2,2,2,1,320,128]{5,4,3,2,1,0:T(8,128)(2,1)S(1)}, bf16[4,6,24,1024]{3,2,1,0:T(8,128)(2,1)}) custom-call(s32[2]{0:T(128)S(1)} %pad_add_fusion.place, s32[4]{0:T(128)S(1)} %copy-done.3, s32[1,4]{1,0:T(1,128)S(1)} %copy-done.4, s32[10]{0:T(128)S(1)} %copy-done.5, ...), custom_call_target="tpu_custom_call" | custom-call | flops 2264924160 | bytes 5000000 | tf_op jit(solution)/shard_map/slot_group/pallas_call | solution.py:321
  87.7 0.8 copy-done.6
  88.6 0.0 reduce-scatter.2.cloned.1.call-update
  88.6 0.1 collective-permute-start.11
  88.8 2.3 %halve.2 = (bf16[2,4,320,128]{3,2,1,0:T(8,128)(2,1)S(1)}, bf16[2,4,320,128]{3,2,1,0:T(8,128)(2,1)S(1)}, bf16[2,4,320,128]{3,2,1,0:T(8,128)(2,1)S(1)}, bf16[2,4,320,128]{3,2,1,0:T(8,128)(2,1)S(1)}) custom-call(bf16[2,2,2,4,320,128]{5,4,3,2,1,0:T(8,128)(2,1)S(1)} %copy-done, bf16[2,2,2,4,320,128]{5,4,3,2,1,0:T(8,128)(2,1)} %collective-permute-done.6.came, ...), custom_call_target="tpu_custom_call" | custom-call | flops 2000000 | bytes 6000000 | tf_op jit(solution)/shard_map/halve/pallas_call | solution.py:347
  91.1 5.7 %collective-permute-start.7 = (bf16[2,4,320,128]{3,2,1,0:T(8,128)(2,1)S(1)}, bf16[2,4,320,128]{3,2,1,0:T(8,128)(2,1)S(1)}, u32[]{:S(2)}, u32[]{:S(2)}) collective-permute-start(bf16[2,4,320,128]{3,2,1,0:T(8,128)(2,1)S(1)} %get-tuple-element.26.refs_0_), channel_id=1, source_target_pairs={{0,8},{4,12},{8,0},{12,4},{16,24},{20,28},{24,16},{28,20},{1,9},{5... | collective-permute-start | bytes 1966088 | tf_op jit(solution)/shard_map/ppermute | solution.py:412
  96.8 0.1 collective-permute-start.9
  96.9 0.0 collective-permute-done.11.came
  96.9 0.2 halve.3
  97.1 2.0 %collective-permute-start.12 = (bf16[2,1,320,128]{3,2,1,0:T(8,128)(2,1)S(1)}, bf16[2,1,320,128]{3,2,1,0:T(8,128)(2,1)S(1)}, u32[]{:S(2)}, u32[]{:S(2)}) collective-permute-start(bf16[2,1,320,128]{3,2,1,0:T(8,128)(2,1)S(1)} %get-tuple-element.32), channel_id=1, source_target_pairs={{0,8},{4,12},{8,0},{12,4},{16,24},{20,28},{24,16},{28,20},{1,9},{5... | collective-permute-start | bytes 491528 | tf_op jit(solution)/shard_map/ppermute | solution.py:412
  99.1 0.0 collective-permute-start.14
  99.1 13.2 %collective-permute-done.7 = bf16[2,4,320,128]{3,2,1,0:T(8,128)(2,1)S(1)} collective-permute-done((bf16[2,4,320,128]{3,2,1,0:T(8,128)(2,1)S(1)}, bf16[2,4,320,128]{3,2,1,0:T(8,128)(2,1)S(1)}, u32[]{:S(2)}, u32[]{:S(2)}) %collective-permute-start.7) | collective-permute-done | bytes 655392 | tf_op jit(solution)/shard_map/ppermute | solution.py:412
  112.3 0.2 fusion.1
  112.5 2.2 %collective-permute-start.8 = (bf16[4,320,128]{2,1,0:T(8,128)(2,1)S(1)}, bf16[4,320,128]{2,1,0:T(8,128)(2,1)S(1)}, u32[]{:S(2)}, u32[]{:S(2)}) collective-permute-start(bf16[4,320,128]{2,1,0:T(8,128)(2,1)S(1)} %get-tuple-element.37), channel_id=1, source_target_pairs={{0,16},{4,20},{8,24},{12,28},{16,0},{20,4},{24,8},{28,12},{1,17},{... | collective-permute-start | bytes 983048 | tf_op jit(solution)/shard_map/ppermute | solution.py:412
  114.7 0.2 fusion.3
  114.9 0.1 collective-permute-start.10
  114.9 0.3 collective-permute-done.12
  115.3 2.6 %collective-permute-start.13 = (bf16[1,320,128]{2,1,0:T(8,128)(2,1)S(1)}, bf16[1,320,128]{2,1,0:T(8,128)(2,1)S(1)}, u32[]{:S(2)}, u32[]{:S(2)}) collective-permute-start(bf16[1,320,128]{2,1,0:T(8,128)(2,1)S(1)} %get-tuple-element.43), channel_id=1, source_target_pairs={{0,16},{4,20},{8,24},{12,28},{16,0},{20,4},{24,8},{28,12},{1,17},{... | collective-permute-start | bytes 245768 | tf_op jit(solution)/shard_map/ppermute | solution.py:412
  117.9 0.0 collective-permute-done.14
  118.0 0.1 collective-permute-start.15
  118.1 7.4 %collective-permute-done.13.refs_5_ = bf16[1,320,128]{2,1,0:T(8,128)(2,1)S(1)} collective-permute-done((bf16[1,320,128]{2,1,0:T(8,128)(2,1)S(1)}, bf16[1,320,128]{2,1,0:T(8,128)(2,1)S(1)}, u32[]{:S(2)}, u32[]{:S(2)}) %collective-permute-start.13) | collective-permute-done | bytes 81952 | tf_op jit(solution)/shard_map/ppermute | solution.py:412
  125.5 1.4 %join_heads.1 = f32[10,320,128]{2,1,0:T(8,128)} custom-call(bf16[4,320,128]{2,1,0:T(8,128)(2,1)S(1)} %get-tuple-element.38.refs_0_, bf16[4,320,128]{2,1,0:T(8,128)(2,1)S(1)} %collective-permute-done.8.refs_1_, bf16[4,320,128]{2,1,0:T(8,128)(2,1)S(1)} %get-tuple-element.36.refs_2_, bf16[4,320,128]{2,1,0:T(8,128)(2,1)S(1)} %collective-permute-done.10.refs_3_, ...), custom_call_target="tpu_custom_call" | custom-call | flops 1000000 | bytes 4000000 | tf_op jit(solution)/shard_map/join_heads/pallas_call | solution.py:375
  (28 shorter events, 0.2 us)
Async XLA Ops:
  7.2 53.3 %all-gather.3.cloned.1.call-start = ((), (), s32[]{:S(2)}) async-start(), calls=%async_computation.2 | async-start | bytes 7372800 | tf_op jit(solution)/shard_map/all_gather | solution.py:395
  7.9 119.0 %reduce-scatter.2.cloned.1.call-start = ((), (), s32[]{:S(2)}) async-start(), calls=%async_computation.1 | async-start | bytes 1474560 | tf_op jit(solution)/shard_map/reduce_scatter | solution.py:419
  8.9 7.9 %collective-permute-start = (bf16[6,6,1024]{2,1,0:T(8,128)(2,1)S(1)}, bf16[6,6,1024]{2,1,0:T(8,128)(2,1)S(1)}, u32[]{:S(2)}, u32[]{:S(2)}) collective-permute-start(bf16[6,6,1024]{2,1,0:T(8,128)(2,1)S(1)} %slice.60), channel_id=1, source_target_pairs={{0,1},{1,2},{2,3},{3,0},{4,5},{5,6},{6,7},{7,4},{8,9},{9,10},{10,1... | collective-permute-start | bytes 221192 | tf_op jit(solution)/shard_map/ppermute | solution.py:400
  17.8 5.5 %collective-permute-start.2 = (bf16[3,24,1024]{2,1,0:T(8,128)(2,1)S(1)}, bf16[3,24,1024]{2,1,0:T(8,128)(2,1)S(1)}, u32[]{:S(2)}, u32[]{:S(2)}) collective-permute-start(bf16[3,24,1024]{2,1,0:T(8,128)(2,1)S(1)} %get-tuple-element.39), channel_id=1, source_target_pairs={{4,0},{8,4},{12,8},{16,12},{20,16},{24,20},{28,24},{5,1},{9,5},{13... | collective-permute-start | bytes 442376 | tf_op jit(solution)/shard_map/ppermute | solution.py:403
  19.1 4.2 %collective-permute-start.1 = (bf16[3,24,1024]{2,1,0:T(8,128)(2,1)S(1)}, bf16[3,24,1024]{2,1,0:T(8,128)(2,1)S(1)}, u32[]{:S(2)}, u32[]{:S(2)}) collective-permute-start(bf16[3,24,1024]{2,1,0:T(8,128)(2,1)S(1)} %get-tuple-element.40), channel_id=1, source_target_pairs={{0,4},{4,8},{8,12},{12,16},{16,20},{20,24},{24,28},{1,5},{5,9},{9,... | collective-permute-start | bytes 442376 | tf_op jit(solution)/shard_map/ppermute | solution.py:402
  23.4 0.7 copy-start.7
  24.0 11.4 %copy-start.9 = (f32[10,1024]{1,0:T(8,128)S(1)}, f32[10,1024]{1,0:T(8,128)}, u32[]{:S(2)}) copy-start(f32[10,1024]{1,0:T(8,128)} %param.18) | copy-start | bytes 122884
  24.0 11.4 %copy-start.10 = (f32[10,1024]{1,0:T(8,128)S(1)}, f32[10,1024]{1,0:T(8,128)}, u32[]{:S(2)}) copy-start(f32[10,1024]{1,0:T(8,128)} %param.19) | copy-start | bytes 122884
  24.1 36.4 %copy-start.1 = (s32[576,1]{1,0:T(8,128)S(1)}, s32[576,1]{1,0:T(8,128)}, u32[]{:S(2)}) copy-start(s32[576,1]{1,0:T(8,128)} %constant.16.clone.tile_of) | copy-start | bytes 6916
  24.1 36.4 %copy-start.3 = (s32[4]{0:T(128)S(1)}, s32[4]{0:T(128)}, u32[]{:S(2)}) copy-start(s32[4]{0:T(128)} %counts.3) | copy-start | bytes 52
  24.1 36.4 %copy-start.4 = (s32[1,4]{1,0:T(1,128)S(1)}, s32[1,4]{1,0:T(1,128)}, u32[]{:S(2)}) copy-start(s32[1,4]{1,0:T(1,128)} %datasets.3) | copy-start | bytes 52
  24.1 36.4 %copy-start.5 = (s32[10]{0:T(128)S(1)}, s32[10]{0:T(128)}, u32[]{:S(2)}) copy-start(s32[10]{0:T(128)} %levels.3) | copy-start | bytes 124
  24.1 36.3 %copy-start.8 = (bf16[576,576]{1,0:T(8,128)(2,1)S(1)}, bf16[576,576]{1,0:T(8,128)(2,1)}, u32[]{:S(2)}) copy-start(bf16[576,576]{1,0:T(8,128)(2,1)} %constant.17.clone.refs_0_) | copy-start | bytes 1990660
  32.5 7.3 %collective-permute-start.5 = (bf16[144,1024]{1,0:T(8,128)(2,1)S(1)}, bf16[144,1024]{1,0:T(8,128)(2,1)S(1)}, u32[]{:S(2)}, u32[]{:S(2)}) collective-permute-start(bf16[144,1024]{1,0:T(8,128)(2,1)S(1)} %window_attention.1.refs_1_), channel_id=1, source_target_pairs={{0,3},{1,0},{2,1},{3,2},{4,7},{5,4},{6,5},{7,6},{8,11},{9,8},{10,9... | collective-permute-start | bytes 884744 | tf_op jit(solution)/shard_map/ppermute | solution.py:407
  34.4 23.2 %collective-permute-start.4 = (bf16[144,1024]{1,0:T(8,128)(2,1)S(1)}, bf16[144,1024]{1,0:T(8,128)(2,1)S(1)}, u32[]{:S(2)}, u32[]{:S(2)}) collective-permute-start(bf16[144,1024]{1,0:T(8,128)(2,1)S(1)} %window_attention.1.refs_1_), channel_id=1, source_target_pairs={{0,2},{1,3},{2,0},{3,1},{4,6},{5,7},{6,4},{7,5},{8,10},{9,11},{10,... | collective-permute-start | bytes 884744 | tf_op jit(solution)/shard_map/ppermute | solution.py:407
  34.4 23.2 %collective-permute-start.3 = (bf16[144,1024]{1,0:T(8,128)(2,1)S(1)}, bf16[144,1024]{1,0:T(8,128)(2,1)S(1)}, u32[]{:S(2)}, u32[]{:S(2)}) collective-permute-start(bf16[144,1024]{1,0:T(8,128)(2,1)S(1)} %window_attention.1.refs_1_), channel_id=1, source_target_pairs={{0,1},{1,2},{2,3},{3,0},{4,5},{5,6},{6,7},{7,4},{8,9},{9,10},{10,1... | collective-permute-start | bytes 884744 | tf_op jit(solution)/shard_map/ppermute | solution.py:407
  60.4 20.6 %copy-start.2 = (s32[576,1]{1,0:T(8,128)S(1)}, s32[576,1]{1,0:T(8,128)}, u32[]{:S(2)}) copy-start(s32[576,1]{1,0:T(8,128)} %constant.16.clone.tile_of) | copy-start | bytes 6916
  80.5 8.2 %collective-permute-start.6 = (bf16[2,2,2,4,320,128]{5,4,3,2,1,0:T(8,128)(2,1)}, bf16[2,2,2,4,320,128]{5,4,3,2,1,0:T(8,128)(2,1)}, u32[]{:S(2)}, u32[]{:S(2)}) collective-permute-start(bf16[2,2,2,4,320,128]{5,4,3,2,1,0:T(8,128)(2,1)} %get-tuple-element.24), channel_id=1, source_target_pairs={{0,4},{4,0},{8,12},{12,8},{16,20},{20,16},{24,28},{28,24},{1,5},{5... | collective-permute-start | bytes 7864328 | tf_op jit(solution)/shard_map/ppermute | solution.py:412
  81.0 7.7 %copy-start = (bf16[2,2,2,4,320,128]{5,4,3,2,1,0:T(8,128)(2,1)S(1)}, bf16[2,2,2,4,320,128]{5,4,3,2,1,0:T(8,128)(2,1)}, u32[]{:S(2)}) copy-start(bf16[2,2,2,4,320,128]{5,4,3,2,1,0:T(8,128)(2,1)} %get-tuple-element.23.keep) | copy-start | bytes 7864324
  87.7 0.8 copy-start.6
  88.6 8.3 %collective-permute-start.11 = (bf16[2,2,2,1,320,128]{5,4,3,2,1,0:T(8,128)(2,1)}, bf16[2,2,2,1,320,128]{5,4,3,2,1,0:T(8,128)(2,1)S(1)}, u32[]{:S(2)}, u32[]{:S(2)}) collective-permute-start(bf16[2,2,2,1,320,128]{5,4,3,2,1,0:T(8,128)(2,1)} %copy-done.6), channel_id=1, source_target_pairs={{0,4},{4,0},{8,12},{12,8},{16,20},{20,16},{24,28},{28,24},{1,5},{5... | collective-permute-start | bytes 1966088 | tf_op jit(solution)/shard_map/ppermute | solution.py:412
  91.1 21.2 %collective-permute-start.7 = (bf16[2,4,320,128]{3,2,1,0:T(8,128)(2,1)S(1)}, bf16[2,4,320,128]{3,2,1,0:T(8,128)(2,1)S(1)}, u32[]{:S(2)}, u32[]{:S(2)}) collective-permute-start(bf16[2,4,320,128]{3,2,1,0:T(8,128)(2,1)S(1)} %get-tuple-element.26.refs_0_), channel_id=1, source_target_pairs={{0,8},{4,12},{8,0},{12,4},{16,24},{20,28},{24,16},{28,20},{1,9},{5... | collective-permute-start | bytes 1966088 | tf_op jit(solution)/shard_map/ppermute | solution.py:412
  96.8 17.9 %collective-permute-start.9 = (bf16[2,4,320,128]{3,2,1,0:T(8,128)(2,1)S(1)}, bf16[2,4,320,128]{3,2,1,0:T(8,128)(2,1)S(1)}, u32[]{:S(2)}, u32[]{:S(2)}) collective-permute-start(bf16[2,4,320,128]{3,2,1,0:T(8,128)(2,1)S(1)} %get-tuple-element.28.refs_1_), channel_id=1, source_target_pairs={{0,16},{4,20},{8,24},{12,28},{16,0},{20,4},{24,8},{28,12},{1,17},{... | collective-permute-start | bytes 1966088 | tf_op jit(solution)/shard_map/ppermute | solution.py:412
  97.1 18.2 %collective-permute-start.12 = (bf16[2,1,320,128]{3,2,1,0:T(8,128)(2,1)S(1)}, bf16[2,1,320,128]{3,2,1,0:T(8,128)(2,1)S(1)}, u32[]{:S(2)}, u32[]{:S(2)}) collective-permute-start(bf16[2,1,320,128]{3,2,1,0:T(8,128)(2,1)S(1)} %get-tuple-element.32), channel_id=1, source_target_pairs={{0,8},{4,12},{8,0},{12,4},{16,24},{20,28},{24,16},{28,20},{1,9},{5... | collective-permute-start | bytes 491528 | tf_op jit(solution)/shard_map/ppermute | solution.py:412
  99.1 18.9 %collective-permute-start.14 = (bf16[2,1,320,128]{3,2,1,0:T(8,128)(2,1)S(1)}, bf16[2,1,320,128]{3,2,1,0:T(8,128)(2,1)S(1)}, u32[]{:S(2)}, u32[]{:S(2)}) collective-permute-start(bf16[2,1,320,128]{3,2,1,0:T(8,128)(2,1)S(1)} %get-tuple-element.34), channel_id=1, source_target_pairs={{0,16},{4,20},{8,24},{12,28},{16,0},{20,4},{24,8},{28,12},{1,17},{... | collective-permute-start | bytes 491528 | tf_op jit(solution)/shard_map/ppermute | solution.py:412
  112.5 13.0 %collective-permute-start.8 = (bf16[4,320,128]{2,1,0:T(8,128)(2,1)S(1)}, bf16[4,320,128]{2,1,0:T(8,128)(2,1)S(1)}, u32[]{:S(2)}, u32[]{:S(2)}) collective-permute-start(bf16[4,320,128]{2,1,0:T(8,128)(2,1)S(1)} %get-tuple-element.37), channel_id=1, source_target_pairs={{0,16},{4,20},{8,24},{12,28},{16,0},{20,4},{24,8},{28,12},{1,17},{... | collective-permute-start | bytes 983048 | tf_op jit(solution)/shard_map/ppermute | solution.py:412
  114.9 10.6 %collective-permute-start.10 = (bf16[4,320,128]{2,1,0:T(8,128)(2,1)S(1)}, bf16[4,320,128]{2,1,0:T(8,128)(2,1)S(1)}, u32[]{:S(2)}, u32[]{:S(2)}) collective-permute-start(bf16[4,320,128]{2,1,0:T(8,128)(2,1)S(1)} %get-tuple-element.35), channel_id=1, source_target_pairs={{0,8},{4,12},{8,0},{12,4},{16,24},{20,28},{24,16},{28,20},{1,9},{5... | collective-permute-start | bytes 983048 | tf_op jit(solution)/shard_map/ppermute | solution.py:412
  115.3 10.2 %collective-permute-start.13 = (bf16[1,320,128]{2,1,0:T(8,128)(2,1)S(1)}, bf16[1,320,128]{2,1,0:T(8,128)(2,1)S(1)}, u32[]{:S(2)}, u32[]{:S(2)}) collective-permute-start(bf16[1,320,128]{2,1,0:T(8,128)(2,1)S(1)} %get-tuple-element.43), channel_id=1, source_target_pairs={{0,16},{4,20},{8,24},{12,28},{16,0},{20,4},{24,8},{28,12},{1,17},{... | collective-permute-start | bytes 245768 | tf_op jit(solution)/shard_map/ppermute | solution.py:412
  118.0 7.5 %collective-permute-start.15 = (bf16[1,320,128]{2,1,0:T(8,128)(2,1)S(1)}, bf16[1,320,128]{2,1,0:T(8,128)(2,1)S(1)}, u32[]{:S(2)}, u32[]{:S(2)}) collective-permute-start(bf16[1,320,128]{2,1,0:T(8,128)(2,1)S(1)} %get-tuple-element.41), channel_id=1, source_target_pairs={{0,8},{4,12},{8,0},{12,4},{16,24},{20,28},{24,16},{28,20},{1,9},{5... | collective-permute-start | bytes 245768 | tf_op jit(solution)/shard_map/ppermute | solution.py:412
Sparse Core Ops, SparseCore 0:
  9.9 50.4 all-gather.2
  88.7 32.8 reduce-scatter.1

commit v13 on v12

--- a/solution.py
+++ b/solution.py
@@ -258,7 +258,7 @@
         tile_counts[...] = wanted
 
     for k in range(2):
-        rows[k][...] = (band[...].astype(F32) * scale[k] + shift[k]).astype(BF16)
+        rows[k][...] = band[...] * scale[k].astype(BF16) + shift[k].astype(BF16)
     for k in range(2):
         weight = jnp.concatenate([gathered[l, k] for l in range(lats)], axis=1)
         errs[k] = slot_errors(levels[slot + k], tile_counts[...], rows[k][...], weight, target[k])

time: 134 us -> 134 us (level)
  no operation moved by 1% of the time
where the time goes in v13:
time: 134 us
  waiting for transfers between devices  51.3 us (38%)
  Pallas kernels  39 us (29%)
  starting transfers between devices  23.9 us (18%)
  between operations  14.2 us (11%)
  other arithmetic  2.66 us (2%)
  local copies, waits for them, and re-layouts  2.54 us (2%)
    pallas_call x2, Pallas kernels, slot_group(): pl.pallas_call(functools.partial(slot_kernel, 2 * pair, lats, tiles, fina...  26.7 us
    ppermute x3, waiting for transfers between devices, fast_local(): lax.ppermute(mine, 'var', [(i, (i + s) % tiles) for i in range(tiles)])  22.1 us
    ppermute x10, waiting for transfers between devices, fast_local(): lax.ppermute(array, 'lat', [(i, i ^ bit) for i in range(lats)])  20.9 us
    ppermute x10, starting transfers between devices, fast_local(): lax.ppermute(array, 'lat', [(i, i ^ bit) for i in range(lats)])  13.5 us
    pallas_call x1, Pallas kernels, attention(): pl.pallas_call(functools.partial(attention_kernel, bands), out_shape=jax....  8.42 us
    ppermute x1, waiting for transfers between devices, fast_local(): left = lax.ppermute(patches[:, cols - HC:], 'var', right)  4.82 us
    ppermute x1, starting transfers between devices, fast_local(): left = lax.ppermute(patches[:, cols - HC:], 'var', right)  3.08 us
    ppermute x1, starting transfers between devices, fast_local(): above = lax.ppermute(shifted[HR:], 'lat', up)  3.04 us
  transfers between devices with their start and end apart: 18, of which 7 were waited for; matrix products, arithmetic and copies ran while one was open for 3% of the time, Pallas kernels for 14%

profile of v13, /device:TPU:0, one launch (start us, length us, event | category | flops | bytes accessed | tf_op | source)
XLA Modules:
  0.0 133.7 jit_solution(8072393784973072456)
XLA Ops:
  7.2 0.0 all-gather.3.cloned.1.call-start
  7.2 0.7 all-gather.3.cloned.1.call-update
  7.9 0.0 reduce-scatter.2.cloned.1.call-start
  7.9 0.9 slice.60
  8.9 3.1 %collective-permute-start = (bf16[6,6,1024]{2,1,0:T(8,128)(2,1)S(1)}, bf16[6,6,1024]{2,1,0:T(8,128)(2,1)S(1)}, u32[]{:S(2)}, u32[]{:S(2)}) collective-permute-start(bf16[6,6,1024]{2,1,0:T(8,128)(2,1)S(1)} %slice.60), channel_id=1, source_target_pairs={{0,1},{1,2},{2,3},{3,0},{4,5},{5,6},{6,7},{7,4},{8,9},{9,10},{10,1... | collective-permute-start | bytes 221192 | tf_op jit(solution)/shard_map/ppermute | solution.py:400
  11.9 4.8 %collective-permute-done = bf16[6,6,1024]{2,1,0:T(8,128)(2,1)S(1)} collective-permute-done((bf16[6,6,1024]{2,1,0:T(8,128)(2,1)S(1)}, bf16[6,6,1024]{2,1,0:T(8,128)(2,1)S(1)}, u32[]{:S(2)}, u32[]{:S(2)}) %collective-permute-start) | collective-permute-done | bytes 73760 | tf_op jit(solution)/shard_map/ppermute | solution.py:400
  16.8 1.1 fusion.5
  17.8 1.3 collective-permute-start.2
  19.1 3.0 %collective-permute-start.1 = (bf16[3,24,1024]{2,1,0:T(8,128)(2,1)S(1)}, bf16[3,24,1024]{2,1,0:T(8,128)(2,1)S(1)}, u32[]{:S(2)}, u32[]{:S(2)}) collective-permute-start(bf16[3,24,1024]{2,1,0:T(8,128)(2,1)S(1)} %get-tuple-element.40), channel_id=1, source_target_pairs={{0,4},{4,8},{8,12},{12,16},{16,20},{20,24},{24,28},{1,5},{5,9},{9,... | collective-permute-start | bytes 442376 | tf_op jit(solution)/shard_map/ppermute | solution.py:402
  22.2 0.1 pad_add_fusion.place
  22.3 1.1 pad_maximum_fusion.own
  23.3 0.0 collective-permute-done.1.above
  23.4 0.0 copy-start.7
  23.4 0.7 copy-done.7
  24.1 0.0 copy-start.4
  24.1 0.0 copy-start.5
  24.1 0.0 copy-start.8
  24.1 8.4 %window_attention.1.refs_1_ = bf16[144,1024]{1,0:T(8,128)(2,1)S(1)} custom-call(s32[2]{0:T(128)S(1)} %pad_add_fusion.place, bf16[6,24,1024]{2,1,0:T(8,128)(2,1)S(1)} %pad_maximum_fusion.own, bf16[3,24,1024]{2,1,0:T(8,128)(2,1)S(1)} %collective-permute-done.1.above, bf16[3,24,1024]{2,1,0:T(8,128)(2,1)S(1)} %collective-permute-done.2.below, ...), custom_call_target="tpu_custom_call" | custom-call | flops 6000000000 | bytes 12000000 | tf_op jit(solution)/shard_map/window_attention/pallas_call | solution.py:137
  32.5 1.9 %collective-permute-start.5 = (bf16[144,1024]{1,0:T(8,128)(2,1)S(1)}, bf16[144,1024]{1,0:T(8,128)(2,1)S(1)}, u32[]{:S(2)}, u32[]{:S(2)}) collective-permute-start(bf16[144,1024]{1,0:T(8,128)(2,1)S(1)} %window_attention.1.refs_1_), channel_id=1, source_target_pairs={{0,3},{1,0},{2,1},{3,2},{4,7},{5,4},{6,5},{7,6},{8,11},{9,8},{10,9... | collective-permute-start | bytes 884744 | tf_op jit(solution)/shard_map/ppermute | solution.py:407
  34.4 0.0 collective-permute-start.4
  34.4 1.0 collective-permute-start.3
  35.5 4.3 %collective-permute-done.5.refs_4_ = bf16[144,1024]{1,0:T(8,128)(2,1)S(1)} collective-permute-done((bf16[144,1024]{1,0:T(8,128)(2,1)S(1)}, bf16[144,1024]{1,0:T(8,128)(2,1)S(1)}, u32[]{:S(2)}, u32[]{:S(2)}) %collective-permute-start.5) | collective-permute-done | bytes 294944 | tf_op jit(solution)/shard_map/ppermute | solution.py:407
  39.8 17.7 %collective-permute-done.4.refs_3_ = bf16[144,1024]{1,0:T(8,128)(2,1)S(1)} collective-permute-done((bf16[144,1024]{1,0:T(8,128)(2,1)S(1)}, bf16[144,1024]{1,0:T(8,128)(2,1)S(1)}, u32[]{:S(2)}, u32[]{:S(2)}) %collective-permute-start.4) | collective-permute-done | bytes 294944 | tf_op jit(solution)/shard_map/ppermute | solution.py:407
  57.6 2.8 %all-gather.3.cloned.1.call-done = bf16[80,320,128]{2,1,0:T(8,128)(2,1)} async-done(((bf16[10,320,128]{2,1,0:T(8,128)(2,1)}), bf16[80,320,128]{2,1,0:T(8,128)(2,1)}) %all-gather.3.cloned.1.call-update) | async-done | bytes 6553616 | tf_op jit(solution)/shard_map/all_gather | solution.py:395
  60.4 0.0 copy-start.2
  60.5 20.0 %slot_group.2 = (bf16[2,2,2,4,320,128]{5,4,3,2,1,0:T(8,128)(2,1)}, bf16[2,2,2,4,320,128]{5,4,3,2,1,0:T(8,128)(2,1)}, f32[576,1024]{1,0:T(8,128)S(1)}, bf16[576,1024]{1,0:T(8,128)(2,1)S(1)}, bf16[6,24,1024]{2,1,0:T(8,128)(2,1)}) custom-call(s32[2]{0:T(128)S(1)} %pad_add_fusion.place, s32[4]{0:T(128)S(1)} %copy-done.3, s32[1,4]{1,0:T(1,128)S(1)} %copy-done.4, ...), custom_call_target="tpu_custom_call" | custom-call | flops 9059696640 | bytes 20000000 | tf_op jit(solution)/shard_map/slot_group/pallas_call | solution.py:321
  80.5 0.5 collective-permute-start.6
  81.0 6.7 %slot_group.3 = (bf16[2,2,2,1,320,128]{5,4,3,2,1,0:T(8,128)(2,1)S(1)}, bf16[2,2,2,1,320,128]{5,4,3,2,1,0:T(8,128)(2,1)S(1)}, bf16[4,6,24,1024]{3,2,1,0:T(8,128)(2,1)}) custom-call(s32[2]{0:T(128)S(1)} %pad_add_fusion.place, s32[4]{0:T(128)S(1)} %copy-done.3, s32[1,4]{1,0:T(1,128)S(1)} %copy-done.4, s32[10]{0:T(128)S(1)} %copy-done.5, ...), custom_call_target="tpu_custom_call" | custom-call | flops 2264924160 | bytes 5000000 | tf_op jit(solution)/shard_map/slot_group/pallas_call | solution.py:321
  87.7 0.8 copy-done.6
  88.5 0.0 reduce-scatter.2.cloned.1.call-update
  88.5 0.1 collective-permute-start.11
  88.7 2.3 %halve.2 = (bf16[2,4,320,128]{3,2,1,0:T(8,128)(2,1)S(1)}, bf16[2,4,320,128]{3,2,1,0:T(8,128)(2,1)S(1)}, bf16[2,4,320,128]{3,2,1,0:T(8,128)(2,1)S(1)}, bf16[2,4,320,128]{3,2,1,0:T(8,128)(2,1)S(1)}) custom-call(bf16[2,2,2,4,320,128]{5,4,3,2,1,0:T(8,128)(2,1)S(1)} %copy-done, bf16[2,2,2,4,320,128]{5,4,3,2,1,0:T(8,128)(2,1)} %collective-permute-done.6.came, ...), custom_call_target="tpu_custom_call" | custom-call | flops 2000000 | bytes 6000000 | tf_op jit(solution)/shard_map/halve/pallas_call | solution.py:347
  91.0 5.7 %collective-permute-start.7 = (bf16[2,4,320,128]{3,2,1,0:T(8,128)(2,1)S(1)}, bf16[2,4,320,128]{3,2,1,0:T(8,128)(2,1)S(1)}, u32[]{:S(2)}, u32[]{:S(2)}) collective-permute-start(bf16[2,4,320,128]{3,2,1,0:T(8,128)(2,1)S(1)} %get-tuple-element.26.refs_0_), channel_id=1, source_target_pairs={{0,8},{4,12},{8,0},{12,4},{16,24},{20,28},{24,16},{28,20},{1,9},{5... | collective-permute-start | bytes 1966088 | tf_op jit(solution)/shard_map/ppermute | solution.py:412
  96.7 0.1 collective-permute-start.9
  96.9 0.2 halve.3
  97.0 2.0 %collective-permute-start.12 = (bf16[2,1,320,128]{3,2,1,0:T(8,128)(2,1)S(1)}, bf16[2,1,320,128]{3,2,1,0:T(8,128)(2,1)S(1)}, u32[]{:S(2)}, u32[]{:S(2)}) collective-permute-start(bf16[2,1,320,128]{3,2,1,0:T(8,128)(2,1)S(1)} %get-tuple-element.32), channel_id=1, source_target_pairs={{0,8},{4,12},{8,0},{12,4},{16,24},{20,28},{24,16},{28,20},{1,9},{5... | collective-permute-start | bytes 491528 | tf_op jit(solution)/shard_map/ppermute | solution.py:412
  99.0 0.0 collective-permute-start.14
  99.1 13.2 %collective-permute-done.7 = bf16[2,4,320,128]{3,2,1,0:T(8,128)(2,1)S(1)} collective-permute-done((bf16[2,4,320,128]{3,2,1,0:T(8,128)(2,1)S(1)}, bf16[2,4,320,128]{3,2,1,0:T(8,128)(2,1)S(1)}, u32[]{:S(2)}, u32[]{:S(2)}) %collective-permute-start.7) | collective-permute-done | bytes 655392 | tf_op jit(solution)/shard_map/ppermute | solution.py:412
  112.3 0.2 fusion.1
  112.5 2.2 %collective-permute-start.8 = (bf16[4,320,128]{2,1,0:T(8,128)(2,1)S(1)}, bf16[4,320,128]{2,1,0:T(8,128)(2,1)S(1)}, u32[]{:S(2)}, u32[]{:S(2)}) collective-permute-start(bf16[4,320,128]{2,1,0:T(8,128)(2,1)S(1)} %get-tuple-element.37), channel_id=1, source_target_pairs={{0,16},{4,20},{8,24},{12,28},{16,0},{20,4},{24,8},{28,12},{1,17},{... | collective-permute-start | bytes 983048 | tf_op jit(solution)/shard_map/ppermute | solution.py:412
  114.6 0.2 fusion.3
  114.8 0.1 collective-permute-start.10
  114.9 0.3 collective-permute-done.12
  115.2 2.7 %collective-permute-start.13 = (bf16[1,320,128]{2,1,0:T(8,128)(2,1)S(1)}, bf16[1,320,128]{2,1,0:T(8,128)(2,1)S(1)}, u32[]{:S(2)}, u32[]{:S(2)}) collective-permute-start(bf16[1,320,128]{2,1,0:T(8,128)(2,1)S(1)} %get-tuple-element.43), channel_id=1, source_target_pairs={{0,16},{4,20},{8,24},{12,28},{16,0},{20,4},{24,8},{28,12},{1,17},{... | collective-permute-start | bytes 245768 | tf_op jit(solution)/shard_map/ppermute | solution.py:412
  117.9 0.1 collective-permute-start.15
  118.0 7.4 %collective-permute-done.13.refs_5_ = bf16[1,320,128]{2,1,0:T(8,128)(2,1)S(1)} collective-permute-done((bf16[1,320,128]{2,1,0:T(8,128)(2,1)S(1)}, bf16[1,320,128]{2,1,0:T(8,128)(2,1)S(1)}, u32[]{:S(2)}, u32[]{:S(2)}) %collective-permute-start.13) | collective-permute-done | bytes 81952 | tf_op jit(solution)/shard_map/ppermute | solution.py:412
  125.4 0.0 collective-permute-done.10.refs_3_
  125.4 1.4 %join_heads.1 = f32[10,320,128]{2,1,0:T(8,128)} custom-call(bf16[4,320,128]{2,1,0:T(8,128)(2,1)S(1)} %get-tuple-element.38.refs_0_, bf16[4,320,128]{2,1,0:T(8,128)(2,1)S(1)} %collective-permute-done.8.refs_1_, bf16[4,320,128]{2,1,0:T(8,128)(2,1)S(1)} %get-tuple-element.36.refs_2_, bf16[4,320,128]{2,1,0:T(8,128)(2,1)S(1)} %collective-permute-done.10.refs_3_, ...), custom_call_target="tpu_custom_call" | custom-call | flops 1000000 | bytes 4000000 | tf_op jit(solution)/shard_map/join_heads/pallas_call | solution.py:375
  (28 shorter events, 0.2 us)
Async XLA Ops:
  7.2 53.3 %all-gather.3.cloned.1.call-start = ((), (), s32[]{:S(2)}) async-start(), calls=%async_computation.2 | async-start | bytes 7372800 | tf_op jit(solution)/shard_map/all_gather | solution.py:395
  7.9 118.9 %reduce-scatter.2.cloned.1.call-start = ((), (), s32[]{:S(2)}) async-start(), calls=%async_computation.1 | async-start | bytes 1474560 | tf_op jit(solution)/shard_map/reduce_scatter | solution.py:419
  8.9 7.9 %collective-permute-start = (bf16[6,6,1024]{2,1,0:T(8,128)(2,1)S(1)}, bf16[6,6,1024]{2,1,0:T(8,128)(2,1)S(1)}, u32[]{:S(2)}, u32[]{:S(2)}) collective-permute-start(bf16[6,6,1024]{2,1,0:T(8,128)(2,1)S(1)} %slice.60), channel_id=1, source_target_pairs={{0,1},{1,2},{2,3},{3,0},{4,5},{5,6},{6,7},{7,4},{8,9},{9,10},{10,1... | collective-permute-start | bytes 221192 | tf_op jit(solution)/shard_map/ppermute | solution.py:400
  17.8 5.5 %collective-permute-start.2 = (bf16[3,24,1024]{2,1,0:T(8,128)(2,1)S(1)}, bf16[3,24,1024]{2,1,0:T(8,128)(2,1)S(1)}, u32[]{:S(2)}, u32[]{:S(2)}) collective-permute-start(bf16[3,24,1024]{2,1,0:T(8,128)(2,1)S(1)} %get-tuple-element.39), channel_id=1, source_target_pairs={{4,0},{8,4},{12,8},{16,12},{20,16},{24,20},{28,24},{5,1},{9,5},{13... | collective-permute-start | bytes 442376 | tf_op jit(solution)/shard_map/ppermute | solution.py:403
  19.1 4.2 %collective-permute-start.1 = (bf16[3,24,1024]{2,1,0:T(8,128)(2,1)S(1)}, bf16[3,24,1024]{2,1,0:T(8,128)(2,1)S(1)}, u32[]{:S(2)}, u32[]{:S(2)}) collective-permute-start(bf16[3,24,1024]{2,1,0:T(8,128)(2,1)S(1)} %get-tuple-element.40), channel_id=1, source_target_pairs={{0,4},{4,8},{8,12},{12,16},{16,20},{20,24},{24,28},{1,5},{5,9},{9,... | collective-permute-start | bytes 442376 | tf_op jit(solution)/shard_map/ppermute | solution.py:402
  23.4 0.7 copy-start.7
  24.0 11.4 %copy-start.9 = (f32[10,1024]{1,0:T(8,128)S(1)}, f32[10,1024]{1,0:T(8,128)}, u32[]{:S(2)}) copy-start(f32[10,1024]{1,0:T(8,128)} %param.18) | copy-start | bytes 122884
  24.0 11.4 %copy-start.10 = (f32[10,1024]{1,0:T(8,128)S(1)}, f32[10,1024]{1,0:T(8,128)}, u32[]{:S(2)}) copy-start(f32[10,1024]{1,0:T(8,128)} %param.19) | copy-start | bytes 122884
  24.1 36.4 %copy-start.1 = (s32[576,1]{1,0:T(8,128)S(1)}, s32[576,1]{1,0:T(8,128)}, u32[]{:S(2)}) copy-start(s32[576,1]{1,0:T(8,128)} %constant.16.clone.tile_of) | copy-start | bytes 6916
  24.1 36.4 %copy-start.3 = (s32[4]{0:T(128)S(1)}, s32[4]{0:T(128)}, u32[]{:S(2)}) copy-start(s32[4]{0:T(128)} %counts.3) | copy-start | bytes 52
  24.1 36.4 %copy-start.4 = (s32[1,4]{1,0:T(1,128)S(1)}, s32[1,4]{1,0:T(1,128)}, u32[]{:S(2)}) copy-start(s32[1,4]{1,0:T(1,128)} %datasets.3) | copy-start | bytes 52
  24.1 36.4 %copy-start.5 = (s32[10]{0:T(128)S(1)}, s32[10]{0:T(128)}, u32[]{:S(2)}) copy-start(s32[10]{0:T(128)} %levels.3) | copy-start | bytes 124
  24.1 36.3 %copy-start.8 = (bf16[576,576]{1,0:T(8,128)(2,1)S(1)}, bf16[576,576]{1,0:T(8,128)(2,1)}, u32[]{:S(2)}) copy-start(bf16[576,576]{1,0:T(8,128)(2,1)} %constant.17.clone.refs_0_) | copy-start | bytes 1990660
  32.5 7.3 %collective-permute-start.5 = (bf16[144,1024]{1,0:T(8,128)(2,1)S(1)}, bf16[144,1024]{1,0:T(8,128)(2,1)S(1)}, u32[]{:S(2)}, u32[]{:S(2)}) collective-permute-start(bf16[144,1024]{1,0:T(8,128)(2,1)S(1)} %window_attention.1.refs_1_), channel_id=1, source_target_pairs={{0,3},{1,0},{2,1},{3,2},{4,7},{5,4},{6,5},{7,6},{8,11},{9,8},{10,9... | collective-permute-start | bytes 884744 | tf_op jit(solution)/shard_map/ppermute | solution.py:407
  34.4 23.2 %collective-permute-start.4 = (bf16[144,1024]{1,0:T(8,128)(2,1)S(1)}, bf16[144,1024]{1,0:T(8,128)(2,1)S(1)}, u32[]{:S(2)}, u32[]{:S(2)}) collective-permute-start(bf16[144,1024]{1,0:T(8,128)(2,1)S(1)} %window_attention.1.refs_1_), channel_id=1, source_target_pairs={{0,2},{1,3},{2,0},{3,1},{4,6},{5,7},{6,4},{7,5},{8,10},{9,11},{10,... | collective-permute-start | bytes 884744 | tf_op jit(solution)/shard_map/ppermute | solution.py:407
  34.4 23.2 %collective-permute-start.3 = (bf16[144,1024]{1,0:T(8,128)(2,1)S(1)}, bf16[144,1024]{1,0:T(8,128)(2,1)S(1)}, u32[]{:S(2)}, u32[]{:S(2)}) collective-permute-start(bf16[144,1024]{1,0:T(8,128)(2,1)S(1)} %window_attention.1.refs_1_), channel_id=1, source_target_pairs={{0,1},{1,2},{2,3},{3,0},{4,5},{5,6},{6,7},{7,4},{8,9},{9,10},{10,1... | collective-permute-start | bytes 884744 | tf_op jit(solution)/shard_map/ppermute | solution.py:407
  60.4 20.5 %copy-start.2 = (s32[576,1]{1,0:T(8,128)S(1)}, s32[576,1]{1,0:T(8,128)}, u32[]{:S(2)}) copy-start(s32[576,1]{1,0:T(8,128)} %constant.16.clone.tile_of) | copy-start | bytes 6916
  80.5 8.2 %collective-permute-start.6 = (bf16[2,2,2,4,320,128]{5,4,3,2,1,0:T(8,128)(2,1)}, bf16[2,2,2,4,320,128]{5,4,3,2,1,0:T(8,128)(2,1)}, u32[]{:S(2)}, u32[]{:S(2)}) collective-permute-start(bf16[2,2,2,4,320,128]{5,4,3,2,1,0:T(8,128)(2,1)} %get-tuple-element.24), channel_id=1, source_target_pairs={{0,4},{4,0},{8,12},{12,8},{16,20},{20,16},{24,28},{28,24},{1,5},{5... | collective-permute-start | bytes 7864328 | tf_op jit(solution)/shard_map/ppermute | solution.py:412
  81.0 7.7 %copy-start = (bf16[2,2,2,4,320,128]{5,4,3,2,1,0:T(8,128)(2,1)S(1)}, bf16[2,2,2,4,320,128]{5,4,3,2,1,0:T(8,128)(2,1)}, u32[]{:S(2)}) copy-start(bf16[2,2,2,4,320,128]{5,4,3,2,1,0:T(8,128)(2,1)} %get-tuple-element.23.keep) | copy-start | bytes 7864324
  87.7 0.8 copy-start.6
  88.5 8.3 %collective-permute-start.11 = (bf16[2,2,2,1,320,128]{5,4,3,2,1,0:T(8,128)(2,1)}, bf16[2,2,2,1,320,128]{5,4,3,2,1,0:T(8,128)(2,1)S(1)}, u32[]{:S(2)}, u32[]{:S(2)}) collective-permute-start(bf16[2,2,2,1,320,128]{5,4,3,2,1,0:T(8,128)(2,1)} %copy-done.6), channel_id=1, source_target_pairs={{0,4},{4,0},{8,12},{12,8},{16,20},{20,16},{24,28},{28,24},{1,5},{5... | collective-permute-start | bytes 1966088 | tf_op jit(solution)/shard_map/ppermute | solution.py:412
  91.0 21.2 %collective-permute-start.7 = (bf16[2,4,320,128]{3,2,1,0:T(8,128)(2,1)S(1)}, bf16[2,4,320,128]{3,2,1,0:T(8,128)(2,1)S(1)}, u32[]{:S(2)}, u32[]{:S(2)}) collective-permute-start(bf16[2,4,320,128]{3,2,1,0:T(8,128)(2,1)S(1)} %get-tuple-element.26.refs_0_), channel_id=1, source_target_pairs={{0,8},{4,12},{8,0},{12,4},{16,24},{20,28},{24,16},{28,20},{1,9},{5... | collective-permute-start | bytes 1966088 | tf_op jit(solution)/shard_map/ppermute | solution.py:412
  96.7 17.9 %collective-permute-start.9 = (bf16[2,4,320,128]{3,2,1,0:T(8,128)(2,1)S(1)}, bf16[2,4,320,128]{3,2,1,0:T(8,128)(2,1)S(1)}, u32[]{:S(2)}, u32[]{:S(2)}) collective-permute-start(bf16[2,4,320,128]{3,2,1,0:T(8,128)(2,1)S(1)} %get-tuple-element.28.refs_1_), channel_id=1, source_target_pairs={{0,16},{4,20},{8,24},{12,28},{16,0},{20,4},{24,8},{28,12},{1,17},{... | collective-permute-start | bytes 1966088 | tf_op jit(solution)/shard_map/ppermute | solution.py:412
  97.0 18.2 %collective-permute-start.12 = (bf16[2,1,320,128]{3,2,1,0:T(8,128)(2,1)S(1)}, bf16[2,1,320,128]{3,2,1,0:T(8,128)(2,1)S(1)}, u32[]{:S(2)}, u32[]{:S(2)}) collective-permute-start(bf16[2,1,320,128]{3,2,1,0:T(8,128)(2,1)S(1)} %get-tuple-element.32), channel_id=1, source_target_pairs={{0,8},{4,12},{8,0},{12,4},{16,24},{20,28},{24,16},{28,20},{1,9},{5... | collective-permute-start | bytes 491528 | tf_op jit(solution)/shard_map/ppermute | solution.py:412
  99.0 18.8 %collective-permute-start.14 = (bf16[2,1,320,128]{3,2,1,0:T(8,128)(2,1)S(1)}, bf16[2,1,320,128]{3,2,1,0:T(8,128)(2,1)S(1)}, u32[]{:S(2)}, u32[]{:S(2)}) collective-permute-start(bf16[2,1,320,128]{3,2,1,0:T(8,128)(2,1)S(1)} %get-tuple-element.34), channel_id=1, source_target_pairs={{0,16},{4,20},{8,24},{12,28},{16,0},{20,4},{24,8},{28,12},{1,17},{... | collective-permute-start | bytes 491528 | tf_op jit(solution)/shard_map/ppermute | solution.py:412
  112.5 13.0 %collective-permute-start.8 = (bf16[4,320,128]{2,1,0:T(8,128)(2,1)S(1)}, bf16[4,320,128]{2,1,0:T(8,128)(2,1)S(1)}, u32[]{:S(2)}, u32[]{:S(2)}) collective-permute-start(bf16[4,320,128]{2,1,0:T(8,128)(2,1)S(1)} %get-tuple-element.37), channel_id=1, source_target_pairs={{0,16},{4,20},{8,24},{12,28},{16,0},{20,4},{24,8},{28,12},{1,17},{... | collective-permute-start | bytes 983048 | tf_op jit(solution)/shard_map/ppermute | solution.py:412
  114.8 10.6 %collective-permute-start.10 = (bf16[4,320,128]{2,1,0:T(8,128)(2,1)S(1)}, bf16[4,320,128]{2,1,0:T(8,128)(2,1)S(1)}, u32[]{:S(2)}, u32[]{:S(2)}) collective-permute-start(bf16[4,320,128]{2,1,0:T(8,128)(2,1)S(1)} %get-tuple-element.35), channel_id=1, source_target_pairs={{0,8},{4,12},{8,0},{12,4},{16,24},{20,28},{24,16},{28,20},{1,9},{5... | collective-permute-start | bytes 983048 | tf_op jit(solution)/shard_map/ppermute | solution.py:412
  115.2 10.2 %collective-permute-start.13 = (bf16[1,320,128]{2,1,0:T(8,128)(2,1)S(1)}, bf16[1,320,128]{2,1,0:T(8,128)(2,1)S(1)}, u32[]{:S(2)}, u32[]{:S(2)}) collective-permute-start(bf16[1,320,128]{2,1,0:T(8,128)(2,1)S(1)} %get-tuple-element.43), channel_id=1, source_target_pairs={{0,16},{4,20},{8,24},{12,28},{16,0},{20,4},{24,8},{28,12},{1,17},{... | collective-permute-start | bytes 245768 | tf_op jit(solution)/shard_map/ppermute | solution.py:412
  117.9 7.5 %collective-permute-start.15 = (bf16[1,320,128]{2,1,0:T(8,128)(2,1)S(1)}, bf16[1,320,128]{2,1,0:T(8,128)(2,1)S(1)}, u32[]{:S(2)}, u32[]{:S(2)}) collective-permute-start(bf16[1,320,128]{2,1,0:T(8,128)(2,1)S(1)} %get-tuple-element.41), channel_id=1, source_target_pairs={{0,8},{4,12},{8,0},{12,4},{16,24},{20,28},{24,16},{28,20},{1,9},{5... | collective-permute-start | bytes 245768 | tf_op jit(solution)/shard_map/ppermute | solution.py:412
Sparse Core Ops, SparseCore 0:
  9.9 50.4 all-gather.2
  88.7 32.9 reduce-scatter.1

commit v14 on v12

--- a/solution.py
+++ b/solution.py
@@ -412,7 +412,7 @@
     flip = lambda array, bit: lax.ppermute(array, "lat", [(i, i ^ bit) for i in range(lats)])
     add = lambda a, b: (a.astype(F32) + b.astype(F32)).astype(BF16)
     common = (lats, place, small, tile_of, scale3, shift3, gathered, targets)
-    most = slots // 2 - 1
+    most = slots // 4 + 1
     bits = (2, 4)
     keep_a, send_a, so_far, band, latent = slot_group(0, most, *common, pieces, None)
     keep_b, send_b, terms = slot_group(most, slots // 2 - most, *common, None, (band, so_far))

time: 134 us -> 143 us (1.067)
  waiting for transfers between devices: 51.3 us -> 55.1 us
  local copies, waits for them, and re-layouts: 2.54 us -> 4.76 us
  Pallas kernels: 39.1 us -> 41.2 us
    ppermute x10, waiting for transfers between devices: 20.9 us -> 24 us  [fast_local(): lax.ppermute(array, 'lat', [(i, i ^ bit) for i in range(lats)])]
    unnamed x22 -> x20, local copies, waits for them, and re-layouts: 1.56 us -> 3.78 us
  transfers between devices with their start and end apart: 18 -> 18, of which waited for: 7 -> 9; matrix products, arithmetic and copies ran while one was open for 3% -> 3% of each run, Pallas kernels for 14% -> 17%
where the time goes in v14:
time: 143 us; the launch traced here: 142 us
  waiting for transfers between devices  55.1 us (39%)
  Pallas kernels  41.2 us (29%)
  starting transfers between devices  24.2 us (17%)
  between operations  14.2 us (10%)
  local copies, waits for them, and re-layouts  4.76 us (3%)
  other arithmetic  2.65 us (2%)
    pallas_call x2, Pallas kernels, slot_group(): pl.pallas_call(functools.partial(slot_kernel, 2 * pair, lats, tiles, fina...  27.8 us
    ppermute x10, waiting for transfers between devices, fast_local(): lax.ppermute(array, 'lat', [(i, i ^ bit) for i in range(lats)])  24 us
    ppermute x3, waiting for transfers between devices, fast_local(): lax.ppermute(mine, 'var', [(i, (i + s) % tiles) for i in range(tiles)])  22 us
    ppermute x10, starting transfers between devices, fast_local(): lax.ppermute(array, 'lat', [(i, i ^ bit) for i in range(lats)])  13.8 us
    pallas_call x1, Pallas kernels, attention(): pl.pallas_call(functools.partial(attention_kernel, bands), out_shape=jax....  8.42 us
    ppermute x1, waiting for transfers between devices, fast_local(): left = lax.ppermute(patches[:, cols - HC:], 'var', right)  4.82 us
    unnamed x20, local copies, waits for them, and re-layouts  3.78 us
    pallas_call x2, Pallas kernels, halve(): pl.pallas_call(halve_kernel, out_shape=(part,) * 4, in_specs=[vmem, vmem]...  3.61 us
  transfers between devices with their start and end apart: 18, of which 9 were waited for; matrix products, arithmetic and copies ran while one was open for 3% of the time, Pallas kernels for 17%

profile of v14, /device:TPU:0, one launch (start us, length us, event | category | flops | bytes accessed | tf_op | source)
XLA Modules:
  0.0 142.2 jit_solution(15069188326057567621)
XLA Ops:
  7.2 0.0 all-gather.3.cloned.1.call-start
  7.2 0.7 all-gather.3.cloned.1.call-update
  7.9 0.0 reduce-scatter.2.cloned.1.call-start
  8.0 0.9 slice.60
  8.9 3.1 %collective-permute-start = (bf16[6,6,1024]{2,1,0:T(8,128)(2,1)S(1)}, bf16[6,6,1024]{2,1,0:T(8,128)(2,1)S(1)}, u32[]{:S(2)}, u32[]{:S(2)}) collective-permute-start(bf16[6,6,1024]{2,1,0:T(8,128)(2,1)S(1)} %slice.60), channel_id=1, source_target_pairs={{0,1},{1,2},{2,3},{3,0},{4,5},{5,6},{6,7},{7,4},{8,9},{9,10},{10,1... | collective-permute-start | bytes 221192 | tf_op jit(solution)/shard_map/ppermute | solution.py:400
  12.0 4.8 %collective-permute-done = bf16[6,6,1024]{2,1,0:T(8,128)(2,1)S(1)} collective-permute-done((bf16[6,6,1024]{2,1,0:T(8,128)(2,1)S(1)}, bf16[6,6,1024]{2,1,0:T(8,128)(2,1)S(1)}, u32[]{:S(2)}, u32[]{:S(2)}) %collective-permute-start) | collective-permute-done | bytes 73760 | tf_op jit(solution)/shard_map/ppermute | solution.py:400
  16.8 1.1 fusion.9
  17.9 1.3 collective-permute-start.2
  19.2 3.0 %collective-permute-start.1 = (bf16[3,24,1024]{2,1,0:T(8,128)(2,1)S(1)}, bf16[3,24,1024]{2,1,0:T(8,128)(2,1)S(1)}, u32[]{:S(2)}, u32[]{:S(2)}) collective-permute-start(bf16[3,24,1024]{2,1,0:T(8,128)(2,1)S(1)} %get-tuple-element.44), channel_id=1, source_target_pairs={{0,4},{4,8},{8,12},{12,16},{16,20},{20,24},{24,28},{1,5},{5,9},{9,... | collective-permute-start | bytes 442376 | tf_op jit(solution)/shard_map/ppermute | solution.py:402
  22.2 0.1 pad_add_fusion.place
  22.3 1.1 pad_maximum_fusion.own
  23.4 0.0 copy-start.8
  23.4 0.0 copy-start.9
  23.4 0.0 copy-start.1
  23.4 8.4 %window_attention.1.refs_1_ = bf16[144,1024]{1,0:T(8,128)(2,1)S(1)} custom-call(s32[2]{0:T(128)S(1)} %pad_add_fusion.place, bf16[6,24,1024]{2,1,0:T(8,128)(2,1)S(1)} %pad_maximum_fusion.own, bf16[3,24,1024]{2,1,0:T(8,128)(2,1)S(1)} %collective-permute-done.1.above, bf16[3,24,1024]{2,1,0:T(8,128)(2,1)S(1)} %collective-permute-done.2.below, ...), custom_call_target="tpu_custom_call" | custom-call | flops 6000000000 | bytes 12000000 | tf_op jit(solution)/shard_map/window_attention/pallas_call | solution.py:137
  31.9 1.9 %collective-permute-start.5 = (bf16[144,1024]{1,0:T(8,128)(2,1)S(1)}, bf16[144,1024]{1,0:T(8,128)(2,1)S(1)}, u32[]{:S(2)}, u32[]{:S(2)}) collective-permute-start(bf16[144,1024]{1,0:T(8,128)(2,1)S(1)} %window_attention.1.refs_1_), channel_id=1, source_target_pairs={{0,3},{1,0},{2,1},{3,2},{4,7},{5,4},{6,5},{7,6},{8,11},{9,8},{10,9... | collective-permute-start | bytes 884744 | tf_op jit(solution)/shard_map/ppermute | solution.py:407
  33.8 1.0 collective-permute-start.3
  34.9 4.4 %collective-permute-done.5.refs_4_ = bf16[144,1024]{1,0:T(8,128)(2,1)S(1)} collective-permute-done((bf16[144,1024]{1,0:T(8,128)(2,1)S(1)}, bf16[144,1024]{1,0:T(8,128)(2,1)S(1)}, u32[]{:S(2)}, u32[]{:S(2)}) %collective-permute-start.5) | collective-permute-done | bytes 294944 | tf_op jit(solution)/shard_map/ppermute | solution.py:407
  39.2 17.6 %collective-permute-done.4.refs_3_ = bf16[144,1024]{1,0:T(8,128)(2,1)S(1)} collective-permute-done((bf16[144,1024]{1,0:T(8,128)(2,1)S(1)}, bf16[144,1024]{1,0:T(8,128)(2,1)S(1)}, u32[]{:S(2)}, u32[]{:S(2)}) %collective-permute-start.4) | collective-permute-done | bytes 294944 | tf_op jit(solution)/shard_map/ppermute | solution.py:407
  56.8 3.6 %all-gather.3.cloned.1.call-done = bf16[80,320,128]{2,1,0:T(8,128)(2,1)} async-done(((bf16[10,320,128]{2,1,0:T(8,128)(2,1)}), bf16[80,320,128]{2,1,0:T(8,128)(2,1)}) %all-gather.3.cloned.1.call-update) | async-done | bytes 6553616 | tf_op jit(solution)/shard_map/all_gather | solution.py:395
  60.4 1.1 copy-done.4
  61.6 1.0 copy-done.5
  62.5 16.7 %slot_group.2 = (bf16[2,2,2,3,320,128]{5,4,3,2,1,0:T(8,128)(2,1)S(1)}, bf16[2,2,2,3,320,128]{5,4,3,2,1,0:T(8,128)(2,1)}, f32[576,1024]{1,0:T(8,128)}, bf16[576,1024]{1,0:T(8,128)(2,1)S(1)}, bf16[6,24,1024]{2,1,0:T(8,128)(2,1)}) custom-call(s32[2]{0:T(128)S(1)} %pad_add_fusion.place, s32[4]{0:T(128)S(1)} %copy-done.1, s32[1,4]{1,0:T(1,128)S(1)} %copy-done.2, ...), custom_call_target="tpu_custom_call" | custom-call | flops 6794772480 | bytes 15000000 | tf_op jit(solution)/shard_map/slot_group/pallas_call | solution.py:321
  79.2 0.3 collective-permute-start.6
  79.6 1.7 %copy-done.7 = f32[576,1024]{1,0:T(8,128)S(1)} copy-done((f32[576,1024]{1,0:T(8,128)S(1)}, f32[576,1024]{1,0:T(8,128)}, u32[]{:S(2)}) %copy-start.7) | copy-done | bytes 2359320
  81.2 11.1 %slot_group.3 = (bf16[2,2,2,2,320,128]{5,4,3,2,1,0:T(8,128)(2,1)S(1)}, bf16[2,2,2,2,320,128]{5,4,3,2,1,0:T(8,128)(2,1)}, bf16[4,6,24,1024]{3,2,1,0:T(8,128)(2,1)}) custom-call(s32[2]{0:T(128)S(1)} %pad_add_fusion.place, s32[4]{0:T(128)S(1)} %copy-done.1, s32[1,4]{1,0:T(1,128)S(1)} %copy-done.2, s32[10]{0:T(128)S(1)} %copy-done.3, s32[576,1]{1,0:T(8,128)S(1)} %copy-done.6, ...), custom_call_target="tpu_custom_call" | custom-call | flops 4529848320 | bytes 10000000 | tf_op jit(solution)/shard_map/slot_group/pallas_call | solution.py:321
  92.3 0.2 collective-permute-start.11
  92.6 0.0 reduce-scatter.2.cloned.1.call-update
  92.6 2.0 %halve.2 = (bf16[2,3,320,128]{3,2,1,0:T(8,128)(2,1)S(1)}, bf16[2,3,320,128]{3,2,1,0:T(8,128)(2,1)S(1)}, bf16[2,3,320,128]{3,2,1,0:T(8,128)(2,1)S(1)}, bf16[2,3,320,128]{3,2,1,0:T(8,128)(2,1)S(1)}) custom-call(bf16[2,2,2,3,320,128]{5,4,3,2,1,0:T(8,128)(2,1)S(1)} %get-tuple-element.23.keep, bf16[2,2,2,3,320,128]{5,4,3,2,1,0:T(8,128)(2,1)} %collective-permute-done.6.came, ...), custom_call_target="tpu_custom_call" | custom-call | flops 2000000 | bytes 6000000 | tf_op jit(solution)/shard_map/halve/pallas_call | solution.py:347
  94.6 1.1 collective-permute-done.11.came
  95.7 1.6 %halve.3 = (bf16[2,2,320,128]{3,2,1,0:T(8,128)(2,1)S(1)}, bf16[2,2,320,128]{3,2,1,0:T(8,128)(2,1)S(1)}, bf16[2,2,320,128]{3,2,1,0:T(8,128)(2,1)S(1)}, bf16[2,2,320,128]{3,2,1,0:T(8,128)(2,1)S(1)}) custom-call(bf16[2,2,2,2,320,128]{5,4,3,2,1,0:T(8,128)(2,1)S(1)} %get-tuple-element.29.keep, bf16[2,2,2,2,320,128]{5,4,3,2,1,0:T(8,128)(2,1)} %collective-permute-done.11.came, ...), custom_call_target="tpu_custom_call" | custom-call | flops 2000000 | bytes 6000000 | tf_op jit(solution)/shard_map/halve/pallas_call | solution.py:347
  97.3 4.9 %collective-permute-start.12 = (bf16[2,2,320,128]{3,2,1,0:T(8,128)(2,1)S(1)}, bf16[2,2,320,128]{3,2,1,0:T(8,128)(2,1)S(1)}, u32[]{:S(2)}, u32[]{:S(2)}) collective-permute-start(bf16[2,2,320,128]{3,2,1,0:T(8,128)(2,1)S(1)} %get-tuple-element.32), channel_id=1, source_target_pairs={{0,8},{4,12},{8,0},{12,4},{16,24},{20,28},{24,16},{28,20},{1,9},{5... | collective-permute-start | bytes 983048 | tf_op jit(solution)/shard_map/ppermute | solution.py:412
  102.2 0.1 collective-permute-start.7
  102.3 2.0 %collective-permute-start.9 = (bf16[2,3,320,128]{3,2,1,0:T(8,128)(2,1)S(1)}, bf16[2,3,320,128]{3,2,1,0:T(8,128)(2,1)S(1)}, u32[]{:S(2)}, u32[]{:S(2)}) collective-permute-start(bf16[2,3,320,128]{3,2,1,0:T(8,128)(2,1)S(1)} %get-tuple-element.28.refs_1_), channel_id=1, source_target_pairs={{0,16},{4,20},{8,24},{12,28},{16,0},{20,4},{24,8},{28,12},{1,17},{... | collective-permute-start | bytes 1474568 | tf_op jit(solution)/shard_map/ppermute | solution.py:412
  104.3 0.0 collective-permute-start.14
  104.3 6.4 %collective-permute-done.12 = bf16[2,2,320,128]{3,2,1,0:T(8,128)(2,1)S(1)} collective-permute-done((bf16[2,2,320,128]{3,2,1,0:T(8,128)(2,1)S(1)}, bf16[2,2,320,128]{3,2,1,0:T(8,128)(2,1)S(1)}, u32[]{:S(2)}, u32[]{:S(2)}) %collective-permute-start.12) | collective-permute-done | bytes 327712 | tf_op jit(solution)/shard_map/ppermute | solution.py:412
  110.8 0.1 fusion.5
  110.9 2.1 %collective-permute-start.13 = (bf16[2,320,128]{2,1,0:T(8,128)(2,1)S(1)}, bf16[2,320,128]{2,1,0:T(8,128)(2,1)S(1)}, u32[]{:S(2)}, u32[]{:S(2)}) collective-permute-start(bf16[2,320,128]{2,1,0:T(8,128)(2,1)S(1)} %get-tuple-element.41), channel_id=1, source_target_pairs={{0,16},{4,20},{8,24},{12,28},{16,0},{20,4},{24,8},{28,12},{1,17},{... | collective-permute-start | bytes 491528 | tf_op jit(solution)/shard_map/ppermute | solution.py:412
  113.0 8.1 %collective-permute-done.7 = bf16[2,3,320,128]{3,2,1,0:T(8,128)(2,1)S(1)} collective-permute-done((bf16[2,3,320,128]{3,2,1,0:T(8,128)(2,1)S(1)}, bf16[2,3,320,128]{3,2,1,0:T(8,128)(2,1)S(1)}, u32[]{:S(2)}, u32[]{:S(2)}) %collective-permute-start.7) | collective-permute-done | bytes 491552 | tf_op jit(solution)/shard_map/ppermute | solution.py:412
  121.0 0.1 fusion.1
  121.1 1.8 %collective-permute-start.8 = (bf16[3,320,128]{2,1,0:T(8,128)(2,1)S(1)}, bf16[3,320,128]{2,1,0:T(8,128)(2,1)S(1)}, u32[]{:S(2)}, u32[]{:S(2)}) collective-permute-start(bf16[3,320,128]{2,1,0:T(8,128)(2,1)S(1)} %get-tuple-element.37), channel_id=1, source_target_pairs={{0,16},{4,20},{8,24},{12,28},{16,0},{20,4},{24,8},{28,12},{1,17},{... | collective-permute-start | bytes 737288 | tf_op jit(solution)/shard_map/ppermute | solution.py:412
  123.0 0.1 fusion.3
  123.1 0.4 collective-permute-start.10
  123.5 0.1 fusion.7
  123.6 2.0 %collective-permute-start.15 = (bf16[2,320,128]{2,1,0:T(8,128)(2,1)S(1)}, bf16[2,320,128]{2,1,0:T(8,128)(2,1)S(1)}, u32[]{:S(2)}, u32[]{:S(2)}) collective-permute-start(bf16[2,320,128]{2,1,0:T(8,128)(2,1)S(1)} %get-tuple-element.39), channel_id=1, source_target_pairs={{0,8},{4,12},{8,0},{12,4},{16,24},{20,28},{24,16},{28,20},{1,9},{5... | collective-permute-start | bytes 491528 | tf_op jit(solution)/shard_map/ppermute | solution.py:412
  125.6 1.4 collective-permute-done.13.refs_5_
  126.9 7.0 %collective-permute-done.15.refs_7_ = bf16[2,320,128]{2,1,0:T(8,128)(2,1)S(1)} collective-permute-done((bf16[2,320,128]{2,1,0:T(8,128)(2,1)S(1)}, bf16[2,320,128]{2,1,0:T(8,128)(2,1)S(1)}, u32[]{:S(2)}, u32[]{:S(2)}) %collective-permute-start.15) | collective-permute-done | bytes 163872 | tf_op jit(solution)/shard_map/ppermute | solution.py:412
  133.9 1.4 join_heads.1
  (26 shorter events, 0.1 us)
Async XLA Ops:
  7.2 16.2 %copy-start = (f32[1024]{0:T(1024)S(1)}, f32[1024]{0:T(1024)}, u32[]{:S(2)}) copy-start(f32[1024]{0:T(1024)} %param.15) | copy-start | bytes 12292
  7.2 53.3 %all-gather.3.cloned.1.call-start = ((), (), s32[]{:S(2)}) async-start(), calls=%async_computation.2 | async-start | bytes 7372800 | tf_op jit(solution)/shard_map/all_gather | solution.py:395
  7.9 127.4 %reduce-scatter.2.cloned.1.call-start = ((), (), s32[]{:S(2)}) async-start(), calls=%async_computation.1 | async-start | bytes 1474560 | tf_op jit(solution)/shard_map/reduce_scatter | solution.py:419
  8.9 7.9 %collective-permute-start = (bf16[6,6,1024]{2,1,0:T(8,128)(2,1)S(1)}, bf16[6,6,1024]{2,1,0:T(8,128)(2,1)S(1)}, u32[]{:S(2)}, u32[]{:S(2)}) collective-permute-start(bf16[6,6,1024]{2,1,0:T(8,128)(2,1)S(1)} %slice.60), channel_id=1, source_target_pairs={{0,1},{1,2},{2,3},{3,0},{4,5},{5,6},{6,7},{7,4},{8,9},{9,10},{10,1... | collective-permute-start | bytes 221192 | tf_op jit(solution)/shard_map/ppermute | solution.py:400
  17.9 5.5 %collective-permute-start.2 = (bf16[3,24,1024]{2,1,0:T(8,128)(2,1)S(1)}, bf16[3,24,1024]{2,1,0:T(8,128)(2,1)S(1)}, u32[]{:S(2)}, u32[]{:S(2)}) collective-permute-start(bf16[3,24,1024]{2,1,0:T(8,128)(2,1)S(1)} %get-tuple-element.43), channel_id=1, source_target_pairs={{4,0},{8,4},{12,8},{16,12},{20,16},{24,20},{28,24},{5,1},{9,5},{13... | collective-permute-start | bytes 442376 | tf_op jit(solution)/shard_map/ppermute | solution.py:403
  19.2 4.2 %collective-permute-start.1 = (bf16[3,24,1024]{2,1,0:T(8,128)(2,1)S(1)}, bf16[3,24,1024]{2,1,0:T(8,128)(2,1)S(1)}, u32[]{:S(2)}, u32[]{:S(2)}) collective-permute-start(bf16[3,24,1024]{2,1,0:T(8,128)(2,1)S(1)} %get-tuple-element.44), channel_id=1, source_target_pairs={{0,4},{4,8},{8,12},{12,16},{16,20},{20,24},{24,28},{1,5},{5,9},{9,... | collective-permute-start | bytes 442376 | tf_op jit(solution)/shard_map/ppermute | solution.py:402
  23.4 11.4 %copy-start.8 = (f32[10,1024]{1,0:T(8,128)S(1)}, f32[10,1024]{1,0:T(8,128)}, u32[]{:S(2)}) copy-start(f32[10,1024]{1,0:T(8,128)} %param.18) | copy-start | bytes 122884
  23.4 11.4 %copy-start.9 = (f32[10,1024]{1,0:T(8,128)S(1)}, f32[10,1024]{1,0:T(8,128)}, u32[]{:S(2)}) copy-start(f32[10,1024]{1,0:T(8,128)} %param.19) | copy-start | bytes 122884
  23.4 37.0 %copy-start.1 = (s32[4]{0:T(128)S(1)}, s32[4]{0:T(128)}, u32[]{:S(2)}) copy-start(s32[4]{0:T(128)} %counts.3) | copy-start | bytes 52
  23.4 37.0 %copy-start.2 = (s32[1,4]{1,0:T(1,128)S(1)}, s32[1,4]{1,0:T(1,128)}, u32[]{:S(2)}) copy-start(s32[1,4]{1,0:T(1,128)} %datasets.3) | copy-start | bytes 52
  23.4 37.0 %copy-start.3 = (s32[10]{0:T(128)S(1)}, s32[10]{0:T(128)}, u32[]{:S(2)}) copy-start(s32[10]{0:T(128)} %levels.3) | copy-start | bytes 124
  31.9 7.3 %collective-permute-start.5 = (bf16[144,1024]{1,0:T(8,128)(2,1)S(1)}, bf16[144,1024]{1,0:T(8,128)(2,1)S(1)}, u32[]{:S(2)}, u32[]{:S(2)}) collective-permute-start(bf16[144,1024]{1,0:T(8,128)(2,1)S(1)} %window_attention.1.refs_1_), channel_id=1, source_target_pairs={{0,3},{1,0},{2,1},{3,2},{4,7},{5,4},{6,5},{7,6},{8,11},{9,8},{10,9... | collective-permute-start | bytes 884744 | tf_op jit(solution)/shard_map/ppermute | solution.py:407
  33.8 23.1 %collective-permute-start.4 = (bf16[144,1024]{1,0:T(8,128)(2,1)S(1)}, bf16[144,1024]{1,0:T(8,128)(2,1)S(1)}, u32[]{:S(2)}, u32[]{:S(2)}) collective-permute-start(bf16[144,1024]{1,0:T(8,128)(2,1)S(1)} %window_attention.1.refs_1_), channel_id=1, source_target_pairs={{0,2},{1,3},{2,0},{3,1},{4,6},{5,7},{6,4},{7,5},{8,10},{9,11},{10,... | collective-permute-start | bytes 884744 | tf_op jit(solution)/shard_map/ppermute | solution.py:407
  33.8 23.1 %collective-permute-start.3 = (bf16[144,1024]{1,0:T(8,128)(2,1)S(1)}, bf16[144,1024]{1,0:T(8,128)(2,1)S(1)}, u32[]{:S(2)}, u32[]{:S(2)}) collective-permute-start(bf16[144,1024]{1,0:T(8,128)(2,1)S(1)} %window_attention.1.refs_1_), channel_id=1, source_target_pairs={{0,1},{1,2},{2,3},{3,0},{4,5},{5,6},{6,7},{7,4},{8,9},{9,10},{10,1... | collective-permute-start | bytes 884744 | tf_op jit(solution)/shard_map/ppermute | solution.py:407
  60.4 1.1 copy-start.4
  61.6 1.0 copy-start.5
  62.5 17.0 %copy-start.6 = (s32[576,1]{1,0:T(8,128)S(1)}, s32[576,1]{1,0:T(8,128)}, u32[]{:S(2)}) copy-start(s32[576,1]{1,0:T(8,128)} %constant.16.clone.tile_of) | copy-start | bytes 6916
  79.2 13.4 %collective-permute-start.6 = (bf16[2,2,2,3,320,128]{5,4,3,2,1,0:T(8,128)(2,1)}, bf16[2,2,2,3,320,128]{5,4,3,2,1,0:T(8,128)(2,1)}, u32[]{:S(2)}, u32[]{:S(2)}) collective-permute-start(bf16[2,2,2,3,320,128]{5,4,3,2,1,0:T(8,128)(2,1)} %get-tuple-element.24), channel_id=1, source_target_pairs={{0,4},{4,0},{8,12},{12,8},{16,20},{20,16},{24,28},{28,24},{1,5},{5... | collective-permute-start | bytes 5898248 | tf_op jit(solution)/shard_map/ppermute | solution.py:412
  79.6 1.7 %copy-start.7 = (f32[576,1024]{1,0:T(8,128)S(1)}, f32[576,1024]{1,0:T(8,128)}, u32[]{:S(2)}) copy-start(f32[576,1024]{1,0:T(8,128)} %get-tuple-element.21.refs_1_) | copy-start | bytes 7077892
  92.3 3.4 %collective-permute-start.11 = (bf16[2,2,2,2,320,128]{5,4,3,2,1,0:T(8,128)(2,1)}, bf16[2,2,2,2,320,128]{5,4,3,2,1,0:T(8,128)(2,1)}, u32[]{:S(2)}, u32[]{:S(2)}) collective-permute-start(bf16[2,2,2,2,320,128]{5,4,3,2,1,0:T(8,128)(2,1)} %get-tuple-element.30), channel_id=1, source_target_pairs={{0,4},{4,0},{8,12},{12,8},{16,20},{20,16},{24,28},{28,24},{1,5},{5... | collective-permute-start | bytes 3932168 | tf_op jit(solution)/shard_map/ppermute | solution.py:412
  97.3 13.4 %collective-permute-start.12 = (bf16[2,2,320,128]{3,2,1,0:T(8,128)(2,1)S(1)}, bf16[2,2,320,128]{3,2,1,0:T(8,128)(2,1)S(1)}, u32[]{:S(2)}, u32[]{:S(2)}) collective-permute-start(bf16[2,2,320,128]{3,2,1,0:T(8,128)(2,1)S(1)} %get-tuple-element.32), channel_id=1, source_target_pairs={{0,8},{4,12},{8,0},{12,4},{16,24},{20,28},{24,16},{28,20},{1,9},{5... | collective-permute-start | bytes 983048 | tf_op jit(solution)/shard_map/ppermute | solution.py:412
  102.2 18.8 %collective-permute-start.7 = (bf16[2,3,320,128]{3,2,1,0:T(8,128)(2,1)S(1)}, bf16[2,3,320,128]{3,2,1,0:T(8,128)(2,1)S(1)}, u32[]{:S(2)}, u32[]{:S(2)}) collective-permute-start(bf16[2,3,320,128]{3,2,1,0:T(8,128)(2,1)S(1)} %get-tuple-element.26.refs_0_), channel_id=1, source_target_pairs={{0,8},{4,12},{8,0},{12,4},{16,24},{20,28},{24,16},{28,20},{1,9},{5... | collective-permute-start | bytes 1474568 | tf_op jit(solution)/shard_map/ppermute | solution.py:412
  102.3 20.7 %collective-permute-start.9 = (bf16[2,3,320,128]{3,2,1,0:T(8,128)(2,1)S(1)}, bf16[2,3,320,128]{3,2,1,0:T(8,128)(2,1)S(1)}, u32[]{:S(2)}, u32[]{:S(2)}) collective-permute-start(bf16[2,3,320,128]{3,2,1,0:T(8,128)(2,1)S(1)} %get-tuple-element.28.refs_1_), channel_id=1, source_target_pairs={{0,16},{4,20},{8,24},{12,28},{16,0},{20,4},{24,8},{28,12},{1,17},{... | collective-permute-start | bytes 1474568 | tf_op jit(solution)/shard_map/ppermute | solution.py:412
  104.3 19.2 %collective-permute-start.14 = (bf16[2,2,320,128]{3,2,1,0:T(8,128)(2,1)S(1)}, bf16[2,2,320,128]{3,2,1,0:T(8,128)(2,1)S(1)}, u32[]{:S(2)}, u32[]{:S(2)}) collective-permute-start(bf16[2,2,320,128]{3,2,1,0:T(8,128)(2,1)S(1)} %get-tuple-element.34), channel_id=1, source_target_pairs={{0,16},{4,20},{8,24},{12,28},{16,0},{20,4},{24,8},{28,12},{1,17},{... | collective-permute-start | bytes 983048 | tf_op jit(solution)/shard_map/ppermute | solution.py:412
  110.9 16.1 %collective-permute-start.13 = (bf16[2,320,128]{2,1,0:T(8,128)(2,1)S(1)}, bf16[2,320,128]{2,1,0:T(8,128)(2,1)S(1)}, u32[]{:S(2)}, u32[]{:S(2)}) collective-permute-start(bf16[2,320,128]{2,1,0:T(8,128)(2,1)S(1)} %get-tuple-element.41), channel_id=1, source_target_pairs={{0,16},{4,20},{8,24},{12,28},{16,0},{20,4},{24,8},{28,12},{1,17},{... | collective-permute-start | bytes 491528 | tf_op jit(solution)/shard_map/ppermute | solution.py:412
  121.1 12.8 %collective-permute-start.8 = (bf16[3,320,128]{2,1,0:T(8,128)(2,1)S(1)}, bf16[3,320,128]{2,1,0:T(8,128)(2,1)S(1)}, u32[]{:S(2)}, u32[]{:S(2)}) collective-permute-start(bf16[3,320,128]{2,1,0:T(8,128)(2,1)S(1)} %get-tuple-element.37), channel_id=1, source_target_pairs={{0,16},{4,20},{8,24},{12,28},{16,0},{20,4},{24,8},{28,12},{1,17},{... | collective-permute-start | bytes 737288 | tf_op jit(solution)/shard_map/ppermute | solution.py:412
  123.1 10.8 %collective-permute-start.10 = (bf16[3,320,128]{2,1,0:T(8,128)(2,1)S(1)}, bf16[3,320,128]{2,1,0:T(8,128)(2,1)S(1)}, u32[]{:S(2)}, u32[]{:S(2)}) collective-permute-start(bf16[3,320,128]{2,1,0:T(8,128)(2,1)S(1)} %get-tuple-element.35), channel_id=1, source_target_pairs={{0,8},{4,12},{8,0},{12,4},{16,24},{20,28},{24,16},{28,20},{1,9},{5... | collective-permute-start | bytes 737288 | tf_op jit(solution)/shard_map/ppermute | solution.py:412
  123.6 10.4 %collective-permute-start.15 = (bf16[2,320,128]{2,1,0:T(8,128)(2,1)S(1)}, bf16[2,320,128]{2,1,0:T(8,128)(2,1)S(1)}, u32[]{:S(2)}, u32[]{:S(2)}) collective-permute-start(bf16[2,320,128]{2,1,0:T(8,128)(2,1)S(1)} %get-tuple-element.39), channel_id=1, source_target_pairs={{0,8},{4,12},{8,0},{12,4},{16,24},{20,28},{24,16},{28,20},{1,9},{5... | collective-permute-start | bytes 491528 | tf_op jit(solution)/shard_map/ppermute | solution.py:412
Sparse Core Ops, SparseCore 0:
  9.9 50.4 all-gather.2
  92.7 32.4 reduce-scatter.1
